TPU v7x, 32 devices: a whole 2x2x4 slice. The times are simulated.
32 devices in a mesh: slab: 16 (over z, x, core), view: 2 (over y).
Axes of the slice: x: 2, y: 2, z: 4, core: 2. Of those that a mesh axis runs over, the one named last changes fastest.
Arguments:
- fine_volume: float32 [64, 4096], P('slab'), may hold values from 0 to 1
- coarse_volume: float32 [256, 4096], P('slab'), may hold values from 0 to 1
- fine_rays: bfloat16 [4, 4096, 128], P('view'), may hold values from -0.09375 to 0.09375
- coarse_rays: bfloat16 [4, 4096, 128], P('view'), may hold values from -0.09375 to 0.09375
- fine_axial: bfloat16 [4, 64, 128], P('view', 'slab'), may hold values from -0.4375 to 0.4375
- coarse_axial: bfloat16 [4, 256, 128], P('view', 'slab'), may hold values from -0.3125 to 0.3125
- measured: float32 [128, 4, 128], P('slab', 'view'), may hold values from 0 to 2
- ray_weight: float32 [128, 4, 128], P('slab', 'view'), may hold values from 0.25 to 0.5
- fine_cell_weight: float32 [64, 4096], P('slab'), may hold values from 0.3 to 0.6
- coarse_cell_weight: float32 [256, 4096], P('slab'), may hold values from 0.3 to 0.6
- margin_blocks: int32 [16, 8], P('slab'), may hold values from 0 to 31, as said below
- ray_hits: int32 [4, 16, 8], P('view', 'slab'), may hold values 0 or 1
Outputs:
- fine_result: float32 [64, 4096], P('slab')
- coarse_result: float32 [256, 4096], P('slab')
Inputs may be any that keep to these rules, and one draw needn't show every extreme that they name: `margin_blocks`: each row lists 8 different block numbers.
All inputs are finite; a program needn't handle non-finite values. No bound on the sum of `ray_hits` on one device may be relied on, other than what follows from the above.
Results may differ from a plain program's by a relative error of at most 0.005.
Values may be sent and summed in bfloat16 or wider, within the bound.
No kernel may reach another device: no remote copies, remote signals or barrier semaphores. Data moves between devices by JAX's collectives and lax.ppermute only.
A program may use at most 64 MiB of HBM per device.

v0:
```python
import jax
import jax.numpy as jnp
from jax import lax
from jax.sharding import PartitionSpec as P

ITERS = 3
BLOCK = 128


def body(
    fine_volume,
    coarse_volume,
    fine_rays,
    coarse_rays,
    fine_axial,
    coarse_axial,
    measured,
    ray_weight,
    fine_cell_weight,
    coarse_cell_weight,
    margin_blocks,
    ray_hits,
):
    view_count = fine_rays.shape[0]
    detector_rows = fine_axial.shape[2]
    tile_count = ray_hits.shape[2]
    coarse_cells = coarse_volume.shape[1]
    block_ids = jnp.arange(coarse_cells, dtype=jnp.int32) // BLOCK
    listed = jnp.any(margin_blocks[0][:, None] == block_ids[None, :], axis=0)
    keep_mask = jnp.where(listed, 0.0, 1.0).astype(jnp.float32)[None, :]
    hit_rows = jnp.broadcast_to(
        ray_hits[:, 0, :, None], (view_count, tile_count, detector_rows // tile_count)
    )
    hit_rows = hit_rows.reshape(view_count, detector_rows).astype(jnp.bfloat16)
    fine_depth = fine_axial * hit_rows[:, None, :]
    coarse_depth = coarse_axial * hit_rows[:, None, :]
    fine = fine_volume
    coarse = coarse_volume * keep_mask
    whole_measured, whole_weight = (
        lax.all_gather(measured, "slab", axis=0, tiled=True),
        lax.all_gather(ray_weight, "slab", axis=0, tiled=True),
    )
    for iteration in range(ITERS):
        fine_moment = jnp.einsum(
            "zx,vxu->vzu", fine.astype(jnp.bfloat16), fine_rays, preferred_element_type=jnp.float32
        ).astype(jnp.bfloat16)
        coarse_moment = jnp.einsum(
            "zx,vxu->vzu",
            coarse.astype(jnp.bfloat16),
            coarse_rays,
            preferred_element_type=jnp.float32,
        ).astype(jnp.bfloat16)
        total = jnp.einsum(
            "vzw,vzu->wvu", fine_depth, fine_moment, preferred_element_type=jnp.float32
        )
        projection = lax.psum(
            (
                total
                + jnp.einsum(
                    "vzw,vzu->wvu", coarse_depth, coarse_moment, preferred_element_type=jnp.float32
                )
            ).astype(jnp.bfloat16),
            "slab",
        ).astype(jnp.float32)
        residual = (whole_weight * (whole_measured - projection)).astype(jnp.bfloat16)
        fine_spread = jnp.einsum(
            "vzw,wvu->vzu", fine_depth, residual, preferred_element_type=jnp.float32
        ).astype(jnp.bfloat16)
        coarse_spread = jnp.einsum(
            "vzw,wvu->vzu", coarse_depth, residual, preferred_element_type=jnp.float32
        ).astype(jnp.bfloat16)
        fine_term = jnp.einsum(
            "vzu,vxu->zx", fine_spread, fine_rays, preferred_element_type=jnp.float32
        )
        coarse_term = jnp.einsum(
            "vzu,vxu->zx", coarse_spread, coarse_rays, preferred_element_type=jnp.float32
        )
        fine_back, coarse_back = (
            lax.psum(fine_term.astype(jnp.bfloat16), "view").astype(jnp.float32),
            lax.psum(coarse_term.astype(jnp.bfloat16), "view").astype(jnp.float32),
        )
        fine = fine + fine_cell_weight * fine_back
        coarse = (coarse + coarse_cell_weight * coarse_back) * keep_mask
    return (fine, coarse)


def solution(mesh):
    return jax.shard_map(
        body,
        mesh=mesh,
        in_specs=(
            P("slab", None),
            P("slab", None),
            P("view", None, None),
            P("view", None, None),
            P("view", "slab", None),
            P("view", "slab", None),
            P("slab", "view", None),
            P("slab", "view", None),
            P("slab", None),
            P("slab", None),
            P("slab", None),
            P("view", "slab", None),
        ),
        out_specs=(P("slab", None), P("slab", None)),
        check_vma=False,
    )
```

profile of v0, /device:TPU:0, one launch (start us, length us, event | category | flops | bytes accessed | tf_op | source)
XLA Modules:
  0.0 391.6 jit_solution(1872113554489010287)
XLA Ops:
  7.3 0.8 convert_element_type.156
  8.3 0.8 compare_reduce_fusion
  9.1 2.3 fusion.15
  11.4 1.3 fusion.11
  12.8 23.4 %all_gather.7 = f32[128,2,128]{2,1,0:T(2,128)S(1)} all-gather(f32[8,2,128]{2,1,0:T(2,128)S(1)} %copy-done.9), channel_id=1, replica_groups=mesh['slab'=16,'view'=2] {'slab'}, dimensions={0}, use_global_device_ids=true | all-gather | bytes 139264 | tf_op jit(solution)/shard_map/all_gather | solution.py:40
  36.2 0.1 copy.22
  36.3 17.8 %all_gather.6 = f32[128,2,128]{2,1,0:T(2,128)S(1)} all-gather(f32[8,2,128]{2,1,0:T(2,128)S(1)} %copy-done.10), channel_id=1, replica_groups=mesh['slab'=16,'view'=2] {'slab'}, dimensions={0}, use_global_device_ids=true | all-gather | bytes 139264 | tf_op jit(solution)/shard_map/all_gather | solution.py:41
  54.1 0.1 copy.23
  54.2 45.8 %all-reduce.7.cloned.1.call-done = bf16[128,2,128]{0,2,1:T(8,128)(2,1)} async-done(((bf16[128,2,128]{0,2,1:T(8,128)(2,1)}), bf16[128,2,128]{0,2,1:T(8,128)(2,1)}) %all-reduce.7.cloned.1.call-update) | async-done | bytes 65552 | tf_op jit(solution)/shard_map/psum | solution.py:56
  100.0 0.9 multiply_convert_fusion.3
  100.9 2.4 fusion.3
  103.3 1.4 fusion
  104.7 8.3 %psum.64 = bf16[4,4096]{1,0:T(4,128)(2,1)S(1)} all-reduce(bf16[4,4096]{1,0:T(4,128)(2,1)S(1)} %fusion.3), channel_id=1, replica_groups=mesh['slab'=16,'view'=2] {'view'}, use_global_device_ids=true, to_apply=%region_2.3 | all-reduce | flops 16384 | bytes 65536 | tf_op jit(solution)/shard_map/psum | solution.py:79
  113.1 2.2 fusion.17
  115.3 19.9 %all-reduce.9.cloned.1.call-done = bf16[16,4096]{1,0:T(8,128)(2,1)} async-done(((bf16[16,4096]{1,0:T(8,128)(2,1)}), bf16[16,4096]{1,0:T(8,128)(2,1)}) %all-reduce.9.cloned.1.call-update) | async-done | bytes 131088 | tf_op jit(solution)/shard_map/psum | solution.py:80
  135.3 2.2 fusion.10
  137.6 86.6 %all-reduce.11.cloned.1.call-done = bf16[128,2,128]{0,2,1:T(8,128)(2,1)} async-done(((bf16[128,2,128]{0,2,1:T(8,128)(2,1)}), bf16[128,2,128]{0,2,1:T(8,128)(2,1)}) %all-reduce.11.cloned.1.call-update) | async-done | bytes 65552 | tf_op jit(solution)/shard_map/psum | solution.py:56
  224.1 0.9 multiply_convert_fusion.2
  225.0 2.3 fusion.4
  227.3 1.4 fusion.1
  228.7 8.3 %psum.67 = bf16[4,4096]{1,0:T(4,128)(2,1)S(1)} all-reduce(bf16[4,4096]{1,0:T(4,128)(2,1)S(1)} %fusion.4), channel_id=1, replica_groups=mesh['slab'=16,'view'=2] {'view'}, use_global_device_ids=true, to_apply=%region_5.6 | all-reduce | flops 16384 | bytes 65536 | tf_op jit(solution)/shard_map/psum | solution.py:79
  237.1 2.3 fusion.19
  239.4 20.0 %all-reduce.13.cloned.1.call-done = bf16[16,4096]{1,0:T(8,128)(2,1)} async-done(((bf16[16,4096]{1,0:T(8,128)(2,1)}), bf16[16,4096]{1,0:T(8,128)(2,1)}) %all-reduce.13.cloned.1.call-update) | async-done | bytes 131088 | tf_op jit(solution)/shard_map/psum | solution.py:80
  259.4 2.2 fusion.9
  261.7 86.1 %all-reduce.15.cloned.1.call-done = bf16[128,2,128]{0,2,1:T(8,128)(2,1)} async-done(((bf16[128,2,128]{0,2,1:T(8,128)(2,1)}), bf16[128,2,128]{0,2,1:T(8,128)(2,1)}) %all-reduce.15.cloned.1.call-update) | async-done | bytes 65552 | tf_op jit(solution)/shard_map/psum | solution.py:56
  347.8 0.9 multiply_convert_fusion.1
  348.6 2.4 fusion.5
  351.0 1.4 fusion.2
  352.4 8.3 %psum.70 = bf16[4,4096]{1,0:T(4,128)(2,1)S(1)} all-reduce(bf16[4,4096]{1,0:T(4,128)(2,1)S(1)} %fusion.5), channel_id=1, replica_groups=mesh['slab'=16,'view'=2] {'view'}, use_global_device_ids=true, to_apply=%region_8.9 | all-reduce | flops 16384 | bytes 65536 | tf_op jit(solution)/shard_map/psum | solution.py:79
  360.8 0.7 multiply_add_fusion
  361.4 21.6 %all-reduce.17.cloned.1.call-done = bf16[16,4096]{1,0:T(8,128)(2,1)} async-done(((bf16[16,4096]{1,0:T(8,128)(2,1)}), bf16[16,4096]{1,0:T(8,128)(2,1)}) %all-reduce.17.cloned.1.call-update) | async-done | bytes 131088 | tf_op jit(solution)/shard_map/psum | solution.py:80
  383.0 1.7 add_multiply_fusion
  (39 shorter events, 0.6 us)
Async XLA Ops:
  7.2 4.2 %copy-start = (bf16[2,4096,128]{2,1,0:T(8,128)(2,1)S(1)}, bf16[2,4096,128]{2,1,0:T(8,128)(2,1)}, u32[]{:S(2)}) copy-start(bf16[2,4096,128]{2,1,0:T(8,128)(2,1)} %param.15) | copy-start | bytes 6291460
  7.2 4.2 %copy-start.7 = (bf16[2,16,128]{2,1,0:T(8,128)(2,1)S(1)}, bf16[2,16,128]{2,1,0:T(8,128)(2,1)}, u32[]{:S(2)}) copy-start(bf16[2,16,128]{2,1,0:T(8,128)(2,1)} %param.17) | copy-start | bytes 24580
  7.2 4.2 %copy-start.1 = (f32[16,4096]{1,0:T(8,128)S(1)}, f32[16,4096]{1,0:T(8,128)}, u32[]{:S(2)}) copy-start(f32[16,4096]{1,0:T(8,128)} %param.13) | copy-start | bytes 786436
  7.2 92.8 %all-reduce.7.cloned.1.call-start = ((), (), s32[]{:S(2)}) async-start(), calls=%async_computation | async-start | bytes 131072 | tf_op jit(solution)/shard_map/psum | solution.py:56
  9.1 3.7 copy-start.9
  11.4 24.9 %copy-start.10 = (f32[8,2,128]{2,1,0:T(2,128)S(1)}, f32[8,2,128]{2,1,0:T(2,128)}, u32[]{:S(2)}) copy-start(f32[8,2,128]{2,1,0:T(2,128)} %param.19) | copy-start | bytes 24580
  11.4 89.5 %copy-start.8 = (bf16[2,4,128]{2,1,0:T(4,128)(2,1)S(1)}, bf16[2,4,128]{2,1,0:T(4,128)(2,1)}, u32[]{:S(2)}) copy-start(bf16[2,4,128]{2,1,0:T(4,128)(2,1)} %param.16) | copy-start | bytes 6148
  12.7 122.6 %all-reduce.9.cloned.1.call-start = ((), (), s32[]{:S(2)}) async-start(), calls=%async_computation.1 | async-start | bytes 262144 | tf_op jit(solution)/shard_map/psum | solution.py:80
  100.9 12.2 %copy-start.4 = (f32[4,4096]{1,0:T(4,128)S(1)}, f32[4,4096]{1,0:T(4,128)}, u32[]{:S(2)}) copy-start(f32[4,4096]{1,0:T(4,128)} %param.12) | copy-start | bytes 196612
  100.9 12.2 %copy-start.5 = (f32[4,4096]{1,0:T(4,128)S(1)}, f32[4,4096]{1,0:T(4,128)}, u32[]{:S(2)}) copy-start(f32[4,4096]{1,0:T(4,128)} %param.20) | copy-start | bytes 196612
  103.2 32.0 %copy-start.2 = (f32[16,4096]{1,0:T(8,128)S(1)}, f32[16,4096]{1,0:T(8,128)}, u32[]{:S(2)}) copy-start(f32[16,4096]{1,0:T(8,128)} %param.21) | copy-start | bytes 786436
  113.0 111.1 %all-reduce.11.cloned.1.call-start = ((), (), s32[]{:S(2)}) async-start(), calls=%async_computation.2 | async-start | bytes 131072 | tf_op jit(solution)/shard_map/psum | solution.py:56
  137.5 121.9 %all-reduce.13.cloned.1.call-start = ((), (), s32[]{:S(2)}) async-start(), calls=%async_computation.3 | async-start | bytes 262144 | tf_op jit(solution)/shard_map/psum | solution.py:80
  227.3 32.1 %copy-start.3 = (bf16[16,4096]{1,0:T(8,128)(2,1)S(1)}, bf16[16,4096]{1,0:T(8,128)(2,1)}, u32[]{:S(2)}) copy-start(bf16[16,4096]{1,0:T(8,128)(2,1)} %all-reduce.9.cloned.1.call-done) | copy-start | bytes 393220
  237.1 110.7 %all-reduce.15.cloned.1.call-start = ((), (), s32[]{:S(2)}) async-start(), calls=%async_computation.4 | async-start | bytes 131072 | tf_op jit(solution)/shard_map/psum | solution.py:56
  261.6 121.4 %all-reduce.17.cloned.1.call-start = ((), (), s32[]{:S(2)}) async-start(), calls=%async_computation.5 | async-start | bytes 262144 | tf_op jit(solution)/shard_map/psum | solution.py:80
  348.6 34.4 %copy-start.6 = (bf16[16,4096]{1,0:T(8,128)(2,1)S(1)}, bf16[16,4096]{1,0:T(8,128)(2,1)}, u32[]{:S(2)}) copy-start(bf16[16,4096]{1,0:T(8,128)(2,1)} %all-reduce.13.cloned.1.call-done) | copy-start | bytes 393220
Sparse Core Ops, SparseCore 0:
  12.8 87.1 all-reduce.6
  113.1 22.0 all-reduce.8
  139.7 84.3 all-reduce.10
  237.2 22.1 all-reduce.12
  263.3 84.4 all-reduce.14
  360.9 22.0 all-reduce.16
where the time goes:
time: 392 us
  waiting for transfers between devices  280 us (71%)
  blocking collectives  66.2 us (17%)
  matrix products  23.8 us (6%)
  between operations  14.3 us (4%)
  other arithmetic  6.64 us (2%)
    psum x3, waiting for transfers between devices, body(): lax.psum((total + jnp.einsum('vzw,vzu->wvu', coarse_depth, coarse_moment,...  218 us
    psum x3, waiting for transfers between devices, body(): lax.psum(coarse_term.astype(jnp.bfloat16), 'view').astype(jnp.float32)  61.5 us
    psum x3, blocking collectives, body(): lax.psum(fine_term.astype(jnp.bfloat16), 'view').astype(jnp.float32)  25 us
    all_gather x1, blocking collectives, body(): lax.all_gather(measured, 'slab', axis=0, tiled=True)  23.4 us
    all_gather x1, blocking collectives, body(): lax.all_gather(ray_weight, 'slab', axis=0, tiled=True)  17.8 us
  transfers between devices with their start and end apart: 6, of which 6 were waited for; matrix products, arithmetic and copies ran while one was open for 1% of the time, Pallas kernels for 0%

commit v1 on v0

v1 whole, which is shorter than its diff:
```python
import jax
import jax.numpy as jnp
from jax import lax
from jax.sharding import PartitionSpec as P

ITERS = 3
BLOCK = 128


def swap(value, axis, size, bit):
    return lax.ppermute(value, axis, [(i, i ^ bit) for i in range(size)])


def bits_of(size):
    return [1 << k for k in range(size.bit_length() - 1)]


def pair_sum(value, axis, size):
    for bit in bits_of(size):
        value = value + swap(value, axis, size, bit)
    return value


def pair_gather(value, axis, size):
    me = lax.axis_index(axis)
    for bit in bits_of(size):
        other = swap(value, axis, size, bit)
        upper = (me & bit) != 0
        value = jnp.where(
            upper, jnp.concatenate([other, value]), jnp.concatenate([value, other])
        )
    return value


def make_body(slabs, groups):
    def body(
        fine_volume,
        coarse_volume,
        fine_rays,
        coarse_rays,
        fine_axial,
        coarse_axial,
        measured,
        ray_weight,
        fine_cell_weight,
        coarse_cell_weight,
        margin_blocks,
        ray_hits,
    ):
        view_count = fine_rays.shape[0]
        detector_rows = fine_axial.shape[2]
        tile_count = ray_hits.shape[2]
        coarse_cells = coarse_volume.shape[1]
        block_ids = jnp.arange(coarse_cells, dtype=jnp.int32) // BLOCK
        listed = jnp.any(margin_blocks[0][:, None] == block_ids[None, :], axis=0)
        keep_mask = jnp.where(listed, 0.0, 1.0).astype(jnp.float32)[None, :]
        hit_rows = jnp.broadcast_to(
            ray_hits[:, 0, :, None], (view_count, tile_count, detector_rows // tile_count)
        )
        hit_rows = hit_rows.reshape(view_count, detector_rows).astype(jnp.bfloat16)
        fine_depth = fine_axial * hit_rows[:, None, :]
        coarse_depth = coarse_axial * hit_rows[:, None, :]
        fine_rows = fine_volume.shape[0]
        fine = fine_volume
        coarse = coarse_volume * keep_mask
        gathered = pair_gather(jnp.stack([measured, ray_weight], axis=1), "slab", slabs)
        whole_measured, whole_weight = gathered[:, 0], gathered[:, 1]
        for iteration in range(ITERS):
            fine_moment = jnp.einsum(
                "zx,vxu->vzu",
                fine.astype(jnp.bfloat16),
                fine_rays,
                preferred_element_type=jnp.float32,
            ).astype(jnp.bfloat16)
            coarse_moment = jnp.einsum(
                "zx,vxu->vzu",
                coarse.astype(jnp.bfloat16),
                coarse_rays,
                preferred_element_type=jnp.float32,
            ).astype(jnp.bfloat16)
            total = jnp.einsum(
                "vzw,vzu->wvu", fine_depth, fine_moment, preferred_element_type=jnp.float32
            ) + jnp.einsum(
                "vzw,vzu->wvu", coarse_depth, coarse_moment, preferred_element_type=jnp.float32
            )
            projection = pair_sum(total.astype(jnp.bfloat16), "slab", slabs).astype(jnp.float32)
            residual = (whole_weight * (whole_measured - projection)).astype(jnp.bfloat16)
            fine_spread = jnp.einsum(
                "vzw,wvu->vzu", fine_depth, residual, preferred_element_type=jnp.float32
            ).astype(jnp.bfloat16)
            coarse_spread = jnp.einsum(
                "vzw,wvu->vzu", coarse_depth, residual, preferred_element_type=jnp.float32
            ).astype(jnp.bfloat16)
            fine_term = jnp.einsum(
                "vzu,vxu->zx", fine_spread, fine_rays, preferred_element_type=jnp.float32
            ).astype(jnp.bfloat16)
            coarse_term = jnp.einsum(
                "vzu,vxu->zx", coarse_spread, coarse_rays, preferred_element_type=jnp.float32
            ).astype(jnp.bfloat16)
            term = jnp.concatenate([fine_term, coarse_term])
            back = pair_sum(term, "view", groups).astype(jnp.float32)
            fine = fine + fine_cell_weight * back[:fine_rows]
            coarse = (coarse + coarse_cell_weight * back[fine_rows:]) * keep_mask
        return (fine, coarse)

    return body


def solution(mesh):
    return jax.shard_map(
        make_body(mesh.shape["slab"], mesh.shape["view"]),
        mesh=mesh,
        in_specs=(
            P("slab", None),
            P("slab", None),
            P("view", None, None),
            P("view", None, None),
            P("view", "slab", None),
            P("view", "slab", None),
            P("slab", "view", None),
            P("slab", "view", None),
            P("slab", None),
            P("slab", None),
            P("slab", None),
            P("view", "slab", None),
        ),
        out_specs=(P("slab", None), P("slab", None)),
        check_vma=False,
    )
```

time: 392 us -> 114 us (0.29)
  waiting for transfers between devices: 280 us -> 60.6 us
  blocking collectives: 66.2 us -> 0 us
  starting transfers between devices: 0.25 us -> 17 us
  between operations: 14.3 us -> 1.01 us
    psum x6 -> x0, waiting for transfers between devices: 280 us -> none  [the longest x3 218 us: body(): lax.psum((total + jnp.einsum('vzw,vzu->wvu', coarse_depth, coarse_moment,...]
    ppermute x0 -> x19, waiting for transfers between devices: none -> 60.6 us  [swap(): return lax.ppermute(value, axis, [(i, i ^ bit) for i in range(size)])]
    all_gather x2 -> x0, blocking collectives: 41.2 us -> none  [the longest x1 23.4 us: body(): lax.all_gather(measured, 'slab', axis=0, tiled=True)]
    psum x3 -> x0, blocking collectives: 25 us -> none  [body(): lax.psum(fine_term.astype(jnp.bfloat16), 'view').astype(jnp.float32)]
    ppermute x0 -> x19, starting transfers between devices: none -> 17 us  [swap(): return lax.ppermute(value, axis, [(i, i ^ bit) for i in range(size)])]
  transfers between devices with their start and end apart: 6 -> 19, of which waited for: 6 -> 16; matrix products, arithmetic and copies ran while one was open for 1% -> 5% of each run, Pallas kernels for 0% -> 0%
where the time goes in v1:
time: 114 us; the launch traced here: 113 us
  waiting for transfers between devices  60.6 us (53%)
  matrix products  22.5 us (20%)
  starting transfers between devices  17 us (15%)
  other arithmetic  9.79 us (9%)
  local copies, waits for them, and re-layouts  2.02 us (2%)
    ppermute x19, waiting for transfers between devices, swap(): return lax.ppermute(value, axis, [(i, i ^ bit) for i in range(size)])  60.6 us
    ppermute x19, starting transfers between devices, swap(): return lax.ppermute(value, axis, [(i, i ^ bit) for i in range(size)])  17 us
    dot_general x3, matrix products, body(): jnp.einsum('vzu,vxu->zx', fine_spread, fine_rays, preferred_element_type=...  7.6 us
    dot_general x3, matrix products, body(): jnp.einsum('vzw,vzu->wvu', fine_depth, fine_moment, preferred_element_typ...  6.89 us
    dot_general x3, matrix products, body(): jnp.einsum('vzw,vzu->wvu', coarse_depth, coarse_moment, preferred_element...  4.3 us
    dot_general x3, matrix products, body(): jnp.einsum('vzu,vxu->zx', coarse_spread, coarse_rays, preferred_element_t...  3.71 us
    convert_element_type x3, other arithmetic, body(): back = pair_sum(term, 'view', groups).astype(jnp.float32)  2.51 us
  transfers between devices with their start and end apart: 19, of which 16 were waited for; matrix products, arithmetic and copies ran while one was open for 5% of the time, Pallas kernels for 0%

profile of v1, /device:TPU:0, one launch (start us, length us, event | category | flops | bytes accessed | tf_op | source)
XLA Modules:
  0.0 112.9 jit_solution(3742523493771004148)
XLA Ops:
  3.6 2.3 %fusion.15 = f32[2,128,128]{2,1,0:T(8,128)S(1)} fusion(bf16[2,4096,128]{2,1,0:T(8,128)(2,1)} %param.14, f32[4,4096]{1,0:T(4,128)} %param.12, bf16[2,4,128]{2,1,0:T(4,128)(2,1)} %param.16, bf16[2,128]{1,0:T(2,128)(2,1)S(1)} %convert_element_type.149), kind=kOutput, calls=%fused_computation.36 | convolution fusion | flops 8672256 | bytes 2296320 | tf_op jit(solution)/shard_map/vzw,vzu->wvu/dot_general | solution.py:81
  6.0 2.6 %collective-permute-start.1 = (f32[16,2,2,128]{3,0,2,1:T(8,128)S(1)}, f32[16,2,2,128]{3,0,2,1:T(8,128)S(1)}, u32[]{:S(2)}, u32[]{:S(2)}) collective-permute-start(f32[16,2,2,128]{3,0,2,1:T(8,128)S(1)} %maximum_select_fusion.2), channel_id=1, source_target_pairs={{0,4},{2,6},{4,0},{6,2},{8,12},{10,14},{12,8},{14,10},{16,20},{18,... | collective-permute-start | bytes 98312 | tf_op jit(solution)/shard_map/ppermute | solution.py:11
  10.9 2.0 %collective-permute-start.2 = (f32[32,2,2,128]{0,3,2,1:T(8,128)S(1)}, f32[32,2,2,128]{0,3,2,1:T(8,128)S(1)}, u32[]{:S(2)}, u32[]{:S(2)}) collective-permute-start(f32[32,2,2,128]{0,3,2,1:T(8,128)S(1)} %broadcast_select_fusion), channel_id=1, source_target_pairs={{0,8},{2,10},{4,12},{6,14},{8,0},{10,2},{12,4},{14,6},{16,24},{18,... | collective-permute-start | bytes 196616 | tf_op jit(solution)/shard_map/ppermute | solution.py:11
  13.8 1.6 %collective-permute-start.5 = (bf16[128,2,128]{0,2,1:T(8,128)(2,1)S(1)}, bf16[128,2,128]{0,2,1:T(8,128)(2,1)S(1)}, u32[]{:S(2)}, u32[]{:S(2)}) collective-permute-start(bf16[128,2,128]{0,2,1:T(8,128)(2,1)S(1)} %add.81), channel_id=1, source_target_pairs={{0,4},{2,6},{4,0},{6,2},{8,12},{10,14},{12,8},{14,10},{16,20},{18,... | collective-permute-start | bytes 196616 | tf_op jit(solution)/shard_map/ppermute | solution.py:11
  15.3 3.8 %collective-permute-done.2 = f32[32,2,2,128]{0,3,2,1:T(8,128)S(1)} collective-permute-done((f32[32,2,2,128]{0,3,2,1:T(8,128)S(1)}, f32[32,2,2,128]{0,3,2,1:T(8,128)S(1)}, u32[]{:S(2)}, u32[]{:S(2)}) %collective-permute-start.2) | collective-permute-done | bytes 65568 | tf_op jit(solution)/shard_map/ppermute | solution.py:11
  19.3 2.4 %collective-permute-start.3 = (f32[64,2,2,128]{0,3,2,1:T(8,128)S(1)}, f32[64,2,2,128]{0,3,2,1:T(8,128)S(1)}, u32[]{:S(2)}, u32[]{:S(2)}) collective-permute-start(f32[64,2,2,128]{0,3,2,1:T(8,128)S(1)} %maximum_select_fusion), channel_id=1, source_target_pairs={{0,16},{2,18},{4,20},{6,22},{8,24},{10,26},{12,28},{14,30},{16,0},... | collective-permute-start | bytes 393224 | tf_op jit(solution)/shard_map/ppermute | solution.py:11
  21.8 1.6 %collective-permute-start.6 = (bf16[128,2,128]{0,2,1:T(8,128)(2,1)S(1)}, bf16[128,2,128]{0,2,1:T(8,128)(2,1)S(1)}, u32[]{:S(2)}, u32[]{:S(2)}) collective-permute-start(bf16[128,2,128]{0,2,1:T(8,128)(2,1)S(1)} %add.82), channel_id=1, source_target_pairs={{0,8},{2,10},{4,12},{6,14},{8,0},{10,2},{12,4},{14,6},{16,24},{18,... | collective-permute-start | bytes 196616 | tf_op jit(solution)/shard_map/ppermute | solution.py:11
  23.4 3.9 %collective-permute-done.6 = bf16[128,2,128]{0,2,1:T(8,128)(2,1)S(1)} collective-permute-done((bf16[128,2,128]{0,2,1:T(8,128)(2,1)S(1)}, bf16[128,2,128]{0,2,1:T(8,128)(2,1)S(1)}, u32[]{:S(2)}, u32[]{:S(2)}) %collective-permute-start.6) | collective-permute-done | bytes 65568 | tf_op jit(solution)/shard_map/ppermute | solution.py:11
  27.4 2.4 %collective-permute-start.7 = (bf16[128,2,128]{0,2,1:T(8,128)(2,1)S(1)}, bf16[128,2,128]{0,2,1:T(8,128)(2,1)S(1)}, u32[]{:S(2)}, u32[]{:S(2)}) collective-permute-start(bf16[128,2,128]{0,2,1:T(8,128)(2,1)S(1)} %add.83), channel_id=1, source_target_pairs={{0,16},{2,18},{4,20},{6,22},{8,24},{10,26},{12,28},{14,30},{16,0},... | collective-permute-start | bytes 196616 | tf_op jit(solution)/shard_map/ppermute | solution.py:11
  29.8 5.0 %collective-permute-done.3 = f32[64,2,2,128]{0,3,2,1:T(8,128)S(1)} collective-permute-done((f32[64,2,2,128]{0,3,2,1:T(8,128)S(1)}, f32[64,2,2,128]{0,3,2,1:T(8,128)S(1)}, u32[]{:S(2)}, u32[]{:S(2)}) %collective-permute-start.3) | collective-permute-done | bytes 131104 | tf_op jit(solution)/shard_map/ppermute | solution.py:11
  36.1 2.3 %fusion.3 = bf16[4,4096]{1,0:T(4,128)(2,1)S(1)} fusion(bf16[2,4096,128]{2,1,0:T(8,128)(2,1)} %param.14, bf16[128,2,128]{0,2,1:T(8,128)(2,1)S(1)} %multiply_convert_fusion.3, bf16[2,4,128]{2,1,0:T(4,128)(2,1)S(1)} %copy-done.14, bf16[2,128]{1,0:T(2,128)(2,1)S(1)} %convert_element_type.149), kind=kOutput, calls=%fused_computation.9 | convolution fusion | flops 8672256 | bytes 2198016 | tf_op jit(solution)/shard_map/vzu,vxu->zx/dot_general | solution.py:94
  38.4 1.4 %fusion = bf16[16,4096]{1,0:T(8,128)(2,1)S(1)} fusion(bf16[2,4096,128]{2,1,0:T(8,128)(2,1)S(1)} %copy-done, bf16[128,2,128]{0,2,1:T(8,128)(2,1)S(1)} %multiply_convert_fusion.3, bf16[2,16,128]{2,1,0:T(8,128)(2,1)S(1)} %copy-done.7, bf16[2,128]{1,0:T(2,128)(2,1)} %copy-done.11), kind=kOutput, calls=%fused_computation.3 | convolution fusion | flops 34676736 | bytes 2302464 | tf_op jit(solution)/shard_map/vzu,vxu->zx/dot_general | solution.py:97
  40.6 6.0 %collective-permute-done.8 = bf16[20,4096]{1,0:T(8,128)(2,1)S(1)} collective-permute-done((bf16[20,4096]{1,0:T(8,128)(2,1)S(1)}, bf16[20,4096]{1,0:T(8,128)(2,1)S(1)}, u32[]{:S(2)}, u32[]{:S(2)}) %collective-permute-start.8) | collective-permute-done | bytes 163872 | tf_op jit(solution)/shard_map/ppermute | solution.py:11
  47.4 2.3 %fusion.17 = f32[2,128,128]{2,1,0:T(8,128)S(1)} fusion(bf16[2,4096,128]{2,1,0:T(8,128)(2,1)} %param.14, f32[4,4096]{1,0:T(4,128)S(1)} %copy-done.4, f32[4,4096]{1,0:T(4,128)S(1)} %copy-done.6, f32[20,4096]{1,0:T(8,128)S(1)} %add_convert_fusion.2, bf16[2,4,128]{2,1,0:T(4,128)(2,1)} %param.16, bf16[2,128]{1,0:T(2,128)(2,1)} %copy-done.11), kind=kOutput, calls=%fused_computation.38 | convolution fusion | flops 8705024 | bytes 2427392 | tf_op jit(solution)/shard_map/vzw,vzu->wvu/dot_general | solution.py:81
  49.7 1.4 %fusion.10 = bf16[128,2,128]{0,2,1:T(8,128)(2,1)S(1)} fusion(f32[2,128,128]{2,1,0:T(8,128)S(1)} %fusion.17, bf16[2,4096,128]{2,1,0:T(8,128)(2,1)S(1)} %copy-done, bf16[2,16,128]{2,1,0:T(8,128)(2,1)} %param.17, bf16[2,128]{1,0:T(2,128)(2,1)} %copy-done.11, f32[16,4096]{1,0:T(8,128)S(1)} %copy-done.2, f32[20,4096]{1,0:T(8,128)S(1)} %add_convert_fusion.2, ...), kind=kOutput, calls=%fused_computation.19 | convolution fusion | flops 35004416 | bytes 3105280 | tf_op jit(solution)/shard_map/vzw,vzu->wvu/dot_general | solution.py:83
  51.2 1.2 %collective-permute-done.9 = bf16[128,2,128]{0,2,1:T(8,128)(2,1)S(1)} collective-permute-done((bf16[128,2,128]{0,2,1:T(8,128)(2,1)S(1)}, bf16[128,2,128]{0,2,1:T(8,128)(2,1)S(1)}, u32[]{:S(2)}, u32[]{:S(2)}) %collective-permute-start.9) | collective-permute-done | bytes 65568 | tf_op jit(solution)/shard_map/ppermute | solution.py:11
  52.5 4.3 %collective-permute-done.10 = bf16[128,2,128]{0,2,1:T(8,128)(2,1)S(1)} collective-permute-done((bf16[128,2,128]{0,2,1:T(8,128)(2,1)S(1)}, bf16[128,2,128]{0,2,1:T(8,128)(2,1)S(1)}, u32[]{:S(2)}, u32[]{:S(2)}) %collective-permute-start.10) | collective-permute-done | bytes 65568 | tf_op jit(solution)/shard_map/ppermute | solution.py:11
  56.9 4.3 %collective-permute-done.11 = bf16[128,2,128]{0,2,1:T(8,128)(2,1)S(1)} collective-permute-done((bf16[128,2,128]{0,2,1:T(8,128)(2,1)S(1)}, bf16[128,2,128]{0,2,1:T(8,128)(2,1)S(1)}, u32[]{:S(2)}, u32[]{:S(2)}) %collective-permute-start.11) | collective-permute-done | bytes 65568 | tf_op jit(solution)/shard_map/ppermute | solution.py:11
  61.2 1.4 %collective-permute-start.12 = (bf16[128,2,128]{0,2,1:T(8,128)(2,1)S(1)}, bf16[128,2,128]{0,2,1:T(8,128)(2,1)S(1)}, u32[]{:S(2)}, u32[]{:S(2)}) collective-permute-start(bf16[128,2,128]{0,2,1:T(8,128)(2,1)S(1)} %add.91), channel_id=1, source_target_pairs={{0,16},{2,18},{4,20},{6,22},{8,24},{10,26},{12,28},{14,30},{16,0},... | collective-permute-start | bytes 196616 | tf_op jit(solution)/shard_map/ppermute | solution.py:11
  62.6 4.4 %collective-permute-done.12 = bf16[128,2,128]{0,2,1:T(8,128)(2,1)S(1)} collective-permute-done((bf16[128,2,128]{0,2,1:T(8,128)(2,1)S(1)}, bf16[128,2,128]{0,2,1:T(8,128)(2,1)S(1)}, u32[]{:S(2)}, u32[]{:S(2)}) %collective-permute-start.12) | collective-permute-done | bytes 65568 | tf_op jit(solution)/shard_map/ppermute | solution.py:11
  67.1 2.3 %fusion.4 = bf16[4,4096]{1,0:T(4,128)(2,1)S(1)} fusion(bf16[2,4096,128]{2,1,0:T(8,128)(2,1)} %param.14, bf16[128,2,128]{0,2,1:T(8,128)(2,1)S(1)} %multiply_convert_fusion.2, bf16[2,4,128]{2,1,0:T(4,128)(2,1)S(1)} %copy-done.15, bf16[2,128]{1,0:T(2,128)(2,1)S(1)} %copy-done.12), kind=kOutput, calls=%fused_computation.10 | convolution fusion | flops 8672256 | bytes 2198016 | tf_op jit(solution)/shard_map/vzu,vxu->zx/dot_general | solution.py:94
  70.3 5.6 %collective-permute-done.13 = bf16[20,4096]{1,0:T(8,128)(2,1)S(1)} collective-permute-done((bf16[20,4096]{1,0:T(8,128)(2,1)S(1)}, bf16[20,4096]{1,0:T(8,128)(2,1)S(1)}, u32[]{:S(2)}, u32[]{:S(2)}) %collective-permute-start.13) | collective-permute-done | bytes 163872 | tf_op jit(solution)/shard_map/ppermute | solution.py:11
  76.8 2.3 %fusion.19 = f32[2,128,128]{2,1,0:T(8,128)S(1)} fusion(bf16[2,4096,128]{2,1,0:T(8,128)(2,1)} %param.14, bf16[2,4,128]{2,1,0:T(4,128)(2,1)} %param.16, bf16[2,128]{1,0:T(2,128)(2,1)} %copy-done.11, f32[4,4096]{1,0:T(4,128)} %param.20, f32[20,4096]{1,0:T(8,128)S(1)} %add_convert_fusion.1, f32[4,4096]{1,0:T(4,128)} %param.12, f32[20,4096]{1,0:T(8,128)S(1)} %add_convert_fusion.2), kind=kOutput, calls=%fused_computation.40 | convolution fusion | flops 8737792 | bytes 2492928 | tf_op jit(solution)/shard_map/vzw,vzu->wvu/dot_general | solution.py:81
  79.1 2.3 %fusion.9 = bf16[128,2,128]{0,2,1:T(8,128)(2,1)} fusion(f32[2,128,128]{2,1,0:T(8,128)S(1)} %fusion.19, bf16[2,4096,128]{2,1,0:T(8,128)(2,1)S(1)} %copy-done, f32[16,4096]{1,0:T(8,128)} %param.21, f32[20,4096]{1,0:T(8,128)S(1)} %add_convert_fusion.1, f32[4096]{0:T(1024)S(1)} %broadcast_select_fusion.1, bf16[2,16,128]{2,1,0:T(8,128)(2,1)} %param.17, ...), kind=kOutput, calls=%fused_computation.18 | convolution fusion | flops 35201024 | bytes 3367424 | tf_op jit(solution)/shard_map/vzw,vzu->wvu/dot_general | solution.py:83
  81.4 1.5 %collective-permute-done.14 = bf16[128,2,128]{0,2,1:T(8,128)(2,1)S(1)} collective-permute-done((bf16[128,2,128]{0,2,1:T(8,128)(2,1)}, bf16[128,2,128]{0,2,1:T(8,128)(2,1)S(1)}, u32[]{:S(2)}, u32[]{:S(2)}) %collective-permute-start.14) | collective-permute-done | bytes 65568 | tf_op jit(solution)/shard_map/ppermute | solution.py:11
  83.8 4.3 %collective-permute-done.15 = bf16[128,2,128]{0,2,1:T(8,128)(2,1)S(1)} collective-permute-done((bf16[128,2,128]{0,2,1:T(8,128)(2,1)S(1)}, bf16[128,2,128]{0,2,1:T(8,128)(2,1)S(1)}, u32[]{:S(2)}, u32[]{:S(2)}) %collective-permute-start.15) | collective-permute-done | bytes 65568 | tf_op jit(solution)/shard_map/ppermute | solution.py:11
  88.2 4.3 %collective-permute-done.16 = bf16[128,2,128]{0,2,1:T(8,128)(2,1)S(1)} collective-permute-done((bf16[128,2,128]{0,2,1:T(8,128)(2,1)S(1)}, bf16[128,2,128]{0,2,1:T(8,128)(2,1)S(1)}, u32[]{:S(2)}, u32[]{:S(2)}) %collective-permute-start.16) | collective-permute-done | bytes 65568 | tf_op jit(solution)/shard_map/ppermute | solution.py:11
  93.4 4.4 %collective-permute-done.17 = bf16[128,2,128]{0,2,1:T(8,128)(2,1)S(1)} collective-permute-done((bf16[128,2,128]{0,2,1:T(8,128)(2,1)S(1)}, bf16[128,2,128]{0,2,1:T(8,128)(2,1)S(1)}, u32[]{:S(2)}, u32[]{:S(2)}) %collective-permute-start.17) | collective-permute-done | bytes 65568 | tf_op jit(solution)/shard_map/ppermute | solution.py:11
  98.5 3.0 %fusion.5 = bf16[4,4096]{1,0:T(4,128)(2,1)} fusion(bf16[2,4096,128]{2,1,0:T(8,128)(2,1)} %param.14, bf16[128,2,128]{0,2,1:T(8,128)(2,1)S(1)} %multiply_convert_fusion.1, bf16[2,4,128]{2,1,0:T(4,128)(2,1)} %param.16, bf16[2,128]{1,0:T(2,128)(2,1)} %copy-done.11), kind=kOutput, calls=%fused_computation.11 | convolution fusion | flops 8672256 | bytes 2198016 | tf_op jit(solution)/shard_map/vzu,vxu->zx/dot_general | solution.py:94
  101.5 1.6 %fusion.2 = bf16[16,4096]{1,0:T(8,128)(2,1)S(1)} fusion(bf16[2,4096,128]{2,1,0:T(8,128)(2,1)S(1)} %copy-done, bf16[128,2,128]{0,2,1:T(8,128)(2,1)} %copy-done.5, bf16[2,16,128]{2,1,0:T(8,128)(2,1)} %param.17, bf16[2,128]{1,0:T(2,128)(2,1)} %copy-done.11), kind=kOutput, calls=%fused_computation.5 | convolution fusion | flops 34676736 | bytes 2302464 | tf_op jit(solution)/shard_map/vzu,vxu->zx/dot_general | solution.py:97
  104.0 5.7 %collective-permute-done.18 = bf16[20,4096]{1,0:T(8,128)(2,1)S(1)} collective-permute-done((bf16[20,4096]{1,0:T(8,128)(2,1)S(1)}, bf16[20,4096]{1,0:T(8,128)(2,1)S(1)}, u32[]{:S(2)}, u32[]{:S(2)}) %collective-permute-start.18) | collective-permute-done | bytes 163872 | tf_op jit(solution)/shard_map/ppermute | solution.py:11
  110.5 1.5 %fusion.41 = f32[4,4096]{1,0:T(4,128)} fusion(f32[4,4096]{1,0:T(4,128)} %param.20, f32[20,4096]{1,0:T(8,128)S(1)} %add_convert_fusion, f32[20,4096]{1,0:T(8,128)S(1)} %add_convert_fusion.1, f32[4,4096]{1,0:T(4,128)} %param.12, f32[20,4096]{1,0:T(8,128)S(1)} %add_convert_fusion.2), kind=kLoop, calls=%fused_computation.73 | loop fusion | flops 98304 | bytes 393216 | tf_op jit(solution)/shard_map/add | solution.py:102
  (86 shorter events, 16.6 us)
Async XLA Ops:
  0.6 7.9 %copy-start = (bf16[2,4096,128]{2,1,0:T(8,128)(2,1)S(1)}, bf16[2,4096,128]{2,1,0:T(8,128)(2,1)}, u32[]{:S(2)}) copy-start(bf16[2,4096,128]{2,1,0:T(8,128)(2,1)} %param.15) | copy-start | bytes 6291460
  0.6 7.9 %copy-start.7 = (bf16[2,16,128]{2,1,0:T(8,128)(2,1)S(1)}, bf16[2,16,128]{2,1,0:T(8,128)(2,1)}, u32[]{:S(2)}) copy-start(bf16[2,16,128]{2,1,0:T(8,128)(2,1)} %param.17) | copy-start | bytes 24580
  0.7 7.9 %copy-start.1 = (f32[16,4096]{1,0:T(8,128)S(1)}, f32[16,4096]{1,0:T(8,128)}, u32[]{:S(2)}) copy-start(f32[16,4096]{1,0:T(8,128)} %param.13) | copy-start | bytes 786436
  1.5 4.4 %collective-permute-start = (f32[8,2,2,128]{3,0,2,1:T(8,128)S(1)}, f32[8,2,2,128]{3,0,2,1:T(8,128)S(1)}, u32[]{:S(2)}, u32[]{:S(2)}) collective-permute-start(f32[8,2,2,128]{3,0,2,1:T(8,128)S(1)} %pad_maximum_fusion.5), channel_id=1, source_target_pairs={{0,2},{2,0},{4,6},{6,4},{8,10},{10,8},{12,14},{14,12},{16,18},{18,... | collective-permute-start | bytes 49160 | tf_op jit(solution)/shard_map/ppermute | solution.py:11
  2.9 33.2 %copy-start.11 = (bf16[2,128]{1,0:T(2,128)(2,1)}, bf16[2,128]{1,0:T(2,128)(2,1)S(1)}, u32[]{:S(2)}) copy-start(bf16[2,128]{1,0:T(2,128)(2,1)S(1)} %convert_element_type.149) | copy-start | bytes 1540
  6.0 4.6 %collective-permute-start.1 = (f32[16,2,2,128]{3,0,2,1:T(8,128)S(1)}, f32[16,2,2,128]{3,0,2,1:T(8,128)S(1)}, u32[]{:S(2)}, u32[]{:S(2)}) collective-permute-start(f32[16,2,2,128]{3,0,2,1:T(8,128)S(1)} %maximum_select_fusion.2), channel_id=1, source_target_pairs={{0,4},{2,6},{4,0},{6,2},{8,12},{10,14},{12,8},{14,10},{16,20},{18,... | collective-permute-start | bytes 98312 | tf_op jit(solution)/shard_map/ppermute | solution.py:11
  9.2 3.7 %collective-permute-start.4 = (bf16[128,2,128]{0,2,1:T(8,128)(2,1)S(1)}, bf16[128,2,128]{0,2,1:T(8,128)(2,1)}, u32[]{:S(2)}, u32[]{:S(2)}) collective-permute-start(bf16[128,2,128]{0,2,1:T(8,128)(2,1)S(1)} %fusion.11), channel_id=1, source_target_pairs={{0,2},{2,0},{4,6},{6,4},{8,10},{10,8},{12,14},{14,12},{16,18},{18,... | collective-permute-start | bytes 196616 | tf_op jit(solution)/shard_map/ppermute | solution.py:11
  9.5 26.6 %copy-start.14 = (bf16[2,4,128]{2,1,0:T(4,128)(2,1)S(1)}, bf16[2,4,128]{2,1,0:T(4,128)(2,1)}, u32[]{:S(2)}) copy-start(bf16[2,4,128]{2,1,0:T(4,128)(2,1)} %param.16) | copy-start | bytes 6148
  10.9 8.2 %collective-permute-start.2 = (f32[32,2,2,128]{0,3,2,1:T(8,128)S(1)}, f32[32,2,2,128]{0,3,2,1:T(8,128)S(1)}, u32[]{:S(2)}, u32[]{:S(2)}) collective-permute-start(f32[32,2,2,128]{0,3,2,1:T(8,128)S(1)} %broadcast_select_fusion), channel_id=1, source_target_pairs={{0,8},{2,10},{4,12},{6,14},{8,0},{10,2},{12,4},{14,6},{16,24},{18,... | collective-permute-start | bytes 196616 | tf_op jit(solution)/shard_map/ppermute | solution.py:11
  13.8 8.0 %collective-permute-start.5 = (bf16[128,2,128]{0,2,1:T(8,128)(2,1)S(1)}, bf16[128,2,128]{0,2,1:T(8,128)(2,1)S(1)}, u32[]{:S(2)}, u32[]{:S(2)}) collective-permute-start(bf16[128,2,128]{0,2,1:T(8,128)(2,1)S(1)} %add.81), channel_id=1, source_target_pairs={{0,4},{2,6},{4,0},{6,2},{8,12},{10,14},{12,8},{14,10},{16,20},{18,... | collective-permute-start | bytes 196616 | tf_op jit(solution)/shard_map/ppermute | solution.py:11
  19.3 15.5 %collective-permute-start.3 = (f32[64,2,2,128]{0,3,2,1:T(8,128)S(1)}, f32[64,2,2,128]{0,3,2,1:T(8,128)S(1)}, u32[]{:S(2)}, u32[]{:S(2)}) collective-permute-start(f32[64,2,2,128]{0,3,2,1:T(8,128)S(1)} %maximum_select_fusion), channel_id=1, source_target_pairs={{0,16},{2,18},{4,20},{6,22},{8,24},{10,26},{12,28},{14,30},{16,0},... | collective-permute-start | bytes 393224 | tf_op jit(solution)/shard_map/ppermute | solution.py:11
  21.8 5.6 %collective-permute-start.6 = (bf16[128,2,128]{0,2,1:T(8,128)(2,1)S(1)}, bf16[128,2,128]{0,2,1:T(8,128)(2,1)S(1)}, u32[]{:S(2)}, u32[]{:S(2)}) collective-permute-start(bf16[128,2,128]{0,2,1:T(8,128)(2,1)S(1)} %add.82), channel_id=1, source_target_pairs={{0,8},{2,10},{4,12},{6,14},{8,0},{10,2},{12,4},{14,6},{16,24},{18,... | collective-permute-start | bytes 196616 | tf_op jit(solution)/shard_map/ppermute | solution.py:11
  27.4 8.6 %collective-permute-start.7 = (bf16[128,2,128]{0,2,1:T(8,128)(2,1)S(1)}, bf16[128,2,128]{0,2,1:T(8,128)(2,1)S(1)}, u32[]{:S(2)}, u32[]{:S(2)}) collective-permute-start(bf16[128,2,128]{0,2,1:T(8,128)(2,1)S(1)} %add.83), channel_id=1, source_target_pairs={{0,16},{2,18},{4,20},{6,22},{8,24},{10,26},{12,28},{14,30},{16,0},... | collective-permute-start | bytes 196616 | tf_op jit(solution)/shard_map/ppermute | solution.py:11
  38.4 9.0 %copy-start.4 = (f32[4,4096]{1,0:T(4,128)S(1)}, f32[4,4096]{1,0:T(4,128)}, u32[]{:S(2)}) copy-start(f32[4,4096]{1,0:T(4,128)} %param.12) | copy-start | bytes 196612
  38.4 9.0 %copy-start.6 = (f32[4,4096]{1,0:T(4,128)S(1)}, f32[4,4096]{1,0:T(4,128)}, u32[]{:S(2)}) copy-start(f32[4,4096]{1,0:T(4,128)} %param.20) | copy-start | bytes 196612
  39.8 9.9 %copy-start.2 = (f32[16,4096]{1,0:T(8,128)S(1)}, f32[16,4096]{1,0:T(8,128)}, u32[]{:S(2)}) copy-start(f32[16,4096]{1,0:T(8,128)} %param.21) | copy-start | bytes 786436
  39.8 6.7 %collective-permute-start.8 = (bf16[20,4096]{1,0:T(8,128)(2,1)S(1)}, bf16[20,4096]{1,0:T(8,128)(2,1)S(1)}, u32[]{:S(2)}, u32[]{:S(2)}) collective-permute-start(bf16[20,4096]{1,0:T(8,128)(2,1)S(1)} %pad_maximum_fusion), channel_id=1, source_target_pairs={{0,1},{1,0},{2,3},{3,2},{4,5},{5,4},{6,7},{7,6},{8,9},{9,8},{10,11... | collective-permute-start | bytes 491528 | tf_op jit(solution)/shard_map/ppermute | solution.py:11
  49.7 17.3 %copy-start.12 = (bf16[2,128]{1,0:T(2,128)(2,1)S(1)}, bf16[2,128]{1,0:T(2,128)(2,1)}, u32[]{:S(2)}) copy-start(bf16[2,128]{1,0:T(2,128)(2,1)} %copy-done.11) | copy-start | bytes 1540
  49.7 17.3 %copy-start.15 = (bf16[2,4,128]{2,1,0:T(4,128)(2,1)S(1)}, bf16[2,4,128]{2,1,0:T(4,128)(2,1)}, u32[]{:S(2)}) copy-start(bf16[2,4,128]{2,1,0:T(4,128)(2,1)} %param.16) | copy-start | bytes 6148
  51.1 18.3 %copy-start.8 = (bf16[2,16,128]{2,1,0:T(8,128)(2,1)S(1)}, bf16[2,16,128]{2,1,0:T(8,128)(2,1)}, u32[]{:S(2)}) copy-start(bf16[2,16,128]{2,1,0:T(8,128)(2,1)} %param.17) | copy-start | bytes 24580
  51.1 18.3 %copy-start.13 = (bf16[2,128]{1,0:T(2,128)(2,1)S(1)}, bf16[2,128]{1,0:T(2,128)(2,1)}, u32[]{:S(2)}) copy-start(bf16[2,128]{1,0:T(2,128)(2,1)} %copy-done.11) | copy-start | bytes 1540
  51.1 1.3 %collective-permute-start.9 = (bf16[128,2,128]{0,2,1:T(8,128)(2,1)S(1)}, bf16[128,2,128]{0,2,1:T(8,128)(2,1)S(1)}, u32[]{:S(2)}, u32[]{:S(2)}) collective-permute-start(bf16[128,2,128]{0,2,1:T(8,128)(2,1)S(1)} %fusion.10), channel_id=1, source_target_pairs={{0,2},{2,0},{4,6},{6,4},{8,10},{10,8},{12,14},{14,12},{16,18},{18,... | collective-permute-start | bytes 196616 | tf_op jit(solution)/shard_map/ppermute | solution.py:11
  52.5 4.3 %collective-permute-start.10 = (bf16[128,2,128]{0,2,1:T(8,128)(2,1)S(1)}, bf16[128,2,128]{0,2,1:T(8,128)(2,1)S(1)}, u32[]{:S(2)}, u32[]{:S(2)}) collective-permute-start(bf16[128,2,128]{0,2,1:T(8,128)(2,1)S(1)} %add.89), channel_id=1, source_target_pairs={{0,4},{2,6},{4,0},{6,2},{8,12},{10,14},{12,8},{14,10},{16,20},{18,... | collective-permute-start | bytes 196616 | tf_op jit(solution)/shard_map/ppermute | solution.py:11
  56.8 4.3 %collective-permute-start.11 = (bf16[128,2,128]{0,2,1:T(8,128)(2,1)S(1)}, bf16[128,2,128]{0,2,1:T(8,128)(2,1)S(1)}, u32[]{:S(2)}, u32[]{:S(2)}) collective-permute-start(bf16[128,2,128]{0,2,1:T(8,128)(2,1)S(1)} %add.90), channel_id=1, source_target_pairs={{0,8},{2,10},{4,12},{6,14},{8,0},{10,2},{12,4},{14,6},{16,24},{18,... | collective-permute-start | bytes 196616 | tf_op jit(solution)/shard_map/ppermute | solution.py:11
  61.2 5.8 %collective-permute-start.12 = (bf16[128,2,128]{0,2,1:T(8,128)(2,1)S(1)}, bf16[128,2,128]{0,2,1:T(8,128)(2,1)S(1)}, u32[]{:S(2)}, u32[]{:S(2)}) collective-permute-start(bf16[128,2,128]{0,2,1:T(8,128)(2,1)S(1)} %add.91), channel_id=1, source_target_pairs={{0,16},{2,18},{4,20},{6,22},{8,24},{10,26},{12,28},{14,30},{16,0},... | collective-permute-start | bytes 196616 | tf_op jit(solution)/shard_map/ppermute | solution.py:11
  70.2 5.7 %collective-permute-start.13 = (bf16[20,4096]{1,0:T(8,128)(2,1)S(1)}, bf16[20,4096]{1,0:T(8,128)(2,1)S(1)}, u32[]{:S(2)}, u32[]{:S(2)}) collective-permute-start(bf16[20,4096]{1,0:T(8,128)(2,1)S(1)} %pad_maximum_fusion.1), channel_id=1, source_target_pairs={{0,1},{1,0},{2,3},{3,2},{4,5},{5,4},{6,7},{7,6},{8,9},{9,8},{10,11... | collective-permute-start | bytes 491528 | tf_op jit(solution)/shard_map/ppermute | solution.py:11
  81.4 1.5 %collective-permute-start.14 = (bf16[128,2,128]{0,2,1:T(8,128)(2,1)}, bf16[128,2,128]{0,2,1:T(8,128)(2,1)S(1)}, u32[]{:S(2)}, u32[]{:S(2)}) collective-permute-start(bf16[128,2,128]{0,2,1:T(8,128)(2,1)} %fusion.9), channel_id=1, source_target_pairs={{0,2},{2,0},{4,6},{6,4},{8,10},{10,8},{12,14},{14,12},{16,18},{18,... | collective-permute-start | bytes 196616 | tf_op jit(solution)/shard_map/ppermute | solution.py:11
  83.7 4.3 %collective-permute-start.15 = (bf16[128,2,128]{0,2,1:T(8,128)(2,1)S(1)}, bf16[128,2,128]{0,2,1:T(8,128)(2,1)S(1)}, u32[]{:S(2)}, u32[]{:S(2)}) collective-permute-start(bf16[128,2,128]{0,2,1:T(8,128)(2,1)S(1)} %add.97), channel_id=1, source_target_pairs={{0,4},{2,6},{4,0},{6,2},{8,12},{10,14},{12,8},{14,10},{16,20},{18,... | collective-permute-start | bytes 196616 | tf_op jit(solution)/shard_map/ppermute | solution.py:11
  88.1 4.3 %collective-permute-start.16 = (bf16[128,2,128]{0,2,1:T(8,128)(2,1)S(1)}, bf16[128,2,128]{0,2,1:T(8,128)(2,1)S(1)}, u32[]{:S(2)}, u32[]{:S(2)}) collective-permute-start(bf16[128,2,128]{0,2,1:T(8,128)(2,1)S(1)} %add.98), channel_id=1, source_target_pairs={{0,8},{2,10},{4,12},{6,14},{8,0},{10,2},{12,4},{14,6},{16,24},{18,... | collective-permute-start | bytes 196616 | tf_op jit(solution)/shard_map/ppermute | solution.py:11
  92.5 5.4 %collective-permute-start.17 = (bf16[128,2,128]{0,2,1:T(8,128)(2,1)S(1)}, bf16[128,2,128]{0,2,1:T(8,128)(2,1)S(1)}, u32[]{:S(2)}, u32[]{:S(2)}) collective-permute-start(bf16[128,2,128]{0,2,1:T(8,128)(2,1)S(1)} %add.99), channel_id=1, source_target_pairs={{0,16},{2,18},{4,20},{6,22},{8,24},{10,26},{12,28},{14,30},{16,0},... | collective-permute-start | bytes 196616 | tf_op jit(solution)/shard_map/ppermute | solution.py:11
  101.5 10.6 %copy-start.3 = (f32[16,4096]{1,0:T(8,128)S(1)}, f32[16,4096]{1,0:T(8,128)}, u32[]{:S(2)}) copy-start(f32[16,4096]{1,0:T(8,128)} %param.21) | copy-start | bytes 786436
  103.9 5.7 %collective-permute-start.18 = (bf16[20,4096]{1,0:T(8,128)(2,1)S(1)}, bf16[20,4096]{1,0:T(8,128)(2,1)S(1)}, u32[]{:S(2)}, u32[]{:S(2)}) collective-permute-start(bf16[20,4096]{1,0:T(8,128)(2,1)S(1)} %pad_maximum_fusion.2), channel_id=1, source_target_pairs={{0,1},{1,0},{2,3},{3,2},{4,5},{5,4},{6,7},{7,6},{8,9},{9,8},{10,11... | collective-permute-start | bytes 491528 | tf_op jit(solution)/shard_map/ppermute | solution.py:11
  (3 other events, 3.8 us)

commit v2 on v1

v2 whole, which is shorter than its diff:
```python
import functools
import jax
import jax.numpy as jnp
from jax import lax
from jax.experimental import pallas as pl
from jax.experimental.pallas import tpu as pltpu
from jax.sharding import PartitionSpec as P

BLOCK = 128
PACK = 16
F32 = jnp.float32
BF16 = jnp.bfloat16
PARAMS = pltpu.CompilerParams(vmem_limit_bytes=24 * 1024 * 1024)
VMEM = pl.BlockSpec(memory_space=pltpu.VMEM)
SMEM = pl.BlockSpec(memory_space=pltpu.SMEM)
HBM = pl.BlockSpec(memory_space=pltpu.HBM)
QUICK = pl.CostEstimate(flops=1, bytes_accessed=1, transcendentals=0)


def fetch(source, target, sem):
    copy = pltpu.make_async_copy(source, target, sem)
    copy.start()
    return copy


def swap(value, axis, size, bits):
    return lax.ppermute(value, axis, [(i, i ^ bits) for i in range(size)])


def dot(a, b, dims):
    return lax.dot_general(a, b, (dims, ((), ())), preferred_element_type=F32)


def keep_row(blocks_ref, start, width):
    ids = (lax.broadcasted_iota(jnp.int32, (1, width), 1) + start) // BLOCK
    keep = jnp.ones((1, width), F32)
    for k in range(blocks_ref.shape[1]):
        keep = jnp.where(ids == blocks_ref[0, k], 0.0, keep)
    return keep


def prepare_kernel(
    fine_rays,
    coarse_rays,
    fine_weight_in,
    coarse_weight_in,
    fine_axial_in,
    coarse_axial_in,
    ray_weight_in,
    blocks,
    hits,
    rays,
    mine,
    theirs,
    rows,
    fine_weight,
    coarse_weight,
    fine_axial,
    coarse_axial,
    ray_weight,
    sems,
):
    core = lax.axis_index("slab") % 2
    half = coarse_weight.shape[1] // 2
    cut = pl.ds(pl.multiple_of(core * half, half), half)
    copies = [
        fetch(source, target, sems.at[i])
        for i, (source, target) in enumerate(
            (
                (fine_weight_in, fine_weight),
                (coarse_weight_in, coarse_weight),
                (fine_axial_in, fine_axial),
                (coarse_axial_in, coarse_axial),
                (ray_weight_in, ray_weight),
                (fine_rays.at[:, cut, :], rays.at[0]),
                (coarse_rays.at[:, cut, :], rays.at[1]),
            )
        )
    ]
    for copy in copies[:5]:
        copy.wait()
    fz = fine_weight.shape[0]
    parts = PACK // fz
    width = half // parts
    for out, side in ((mine, core), (theirs, 1 - core)):
        start = pl.multiple_of(side * half, half)
        keep = keep_row(blocks, start, half)
        out[:, :half] = (coarse_weight[:, pl.ds(start, half)] * keep).astype(BF16)
        fine = fine_weight[:, pl.ds(start, half)]
        pieces = [
            fine[i : i + 1, k * width : (k + 1) * width] for i in range(fz) for k in range(parts)
        ]
        out[:, half:] = jnp.concatenate(pieces, axis=0).astype(BF16)
    views, _, det = fine_axial.shape
    columns = ray_weight.shape[2]
    tiles = hits.shape[2]
    tile = lax.broadcasted_iota(jnp.int32, (1, det), 1) // (det // tiles)
    span = views * det
    own = ray_weight.shape[0]
    rows[...] = jnp.zeros(rows.shape, BF16)
    side = []
    for v in range(views):
        hit = jnp.zeros((1, det), F32)
        for t in range(tiles):
            hit = jnp.where(tile == t, hits[v, 0, t].astype(F32), hit)
        rows[:, v * det : (v + 1) * det] = (coarse_axial[v].astype(F32) * hit).astype(BF16)
        side.append(fine_axial[v].astype(F32) * hit)
    wide = rows.shape[1] - span
    weight = jnp.concatenate([ray_weight[:, v, :] for v in range(views)], axis=1)
    fine = jnp.concatenate(side, axis=1)
    if wide > weight.shape[1]:
        weight = jnp.concatenate([weight, jnp.zeros((own, wide - weight.shape[1]), F32)], axis=1)
    if wide > span:
        fine = jnp.concatenate([fine, jnp.zeros((fz, wide - span), F32)], axis=1)
    stack = [weight, fine]
    if own + fz < PACK:
        stack.append(jnp.zeros((PACK - own - fz, wide), F32))
    rows[:, span:] = jnp.concatenate(stack, axis=0).astype(BF16)
    for copy in copies[5:]:
        copy.wait()


def forward_kernel(
    fine_in,
    coarse_in,
    fine_rays_in,
    coarse_rays_in,
    measured_in,
    rows,
    blocks,
    out,
    fine,
    coarse,
    fine_rays,
    coarse_rays,
    measured,
    sems,
):
    steps = sems.shape[0] - 1
    fz, cells = fine.shape
    chunk = cells // steps
    views, _, columns = fine_rays.shape
    given_copy = fetch(measured_in, measured, sems.at[steps, 0])
    copies = []
    for i in range(steps):
        cut = pl.ds(i * chunk, chunk)
        copies.append(
            [
                fetch(fine_in.at[:, cut], fine.at[:, cut], sems.at[i, 0]),
                fetch(fine_rays_in.at[:, cut, :], fine_rays.at[:, cut, :], sems.at[i, 1]),
                fetch(coarse_in.at[:, cut], coarse.at[:, cut], sems.at[i, 2]),
                fetch(coarse_rays_in.at[:, cut, :], coarse_rays.at[:, cut, :], sems.at[i, 3]),
            ]
        )
    fine_sum = coarse_sum = None
    for i in range(steps):
        cut = slice(i * chunk, (i + 1) * chunk)
        for copy in copies[i]:
            copy.wait()
        keep = keep_row(blocks, i * chunk, chunk)
        fine_rows = fine[:, cut].astype(BF16)
        coarse_rows = (coarse[:, cut] * keep).astype(BF16)
        fine_wide = jnp.concatenate([fine_rays[v, cut, :] for v in range(views)], axis=1)
        coarse_wide = jnp.concatenate([coarse_rays[v, cut, :] for v in range(views)], axis=1)
        fine_part = dot(fine_rows, fine_wide, ((1,), (0,)))
        coarse_part = dot(coarse_rows, coarse_wide, ((1,), (0,)))
        fine_sum = fine_part if fine_sum is None else fine_sum + fine_part
        coarse_sum = coarse_part if coarse_sum is None else coarse_sum + coarse_part
    given_copy.wait()
    own = measured.shape[0]
    det = out.shape[0]
    span = views * det
    total = views * columns
    stack = [jnp.zeros((own, total), F32), fine_sum]
    if own + fz < PACK:
        stack.append(jnp.zeros((PACK - own - fz, total), F32))
    moment = jnp.concatenate([coarse_sum] + stack, axis=0).astype(BF16)
    start = lax.axis_index("slab") * own
    row = lax.broadcasted_iota(jnp.int32, (det, columns), 0) - start
    for v in range(views):
        depth = jnp.concatenate(
            [
                rows[:, v * det : (v + 1) * det],
                rows[:, span + v * det : span + (v + 1) * det],
            ],
            axis=0,
        )
        cut = slice(v * columns, (v + 1) * columns)
        projection = dot(depth, moment[:, cut], ((0,), (0,)))
        given = jnp.zeros((det, columns), F32)
        for i in range(own):
            given = jnp.where(row == i, measured[i : i + 1, v, :], given)
        out[:, cut] = given - projection


def unpack_rays(rows, groups, slabs, own, fz, det, total):
    core = lax.axis_index("slab") % 2
    me = lax.axis_index("slab")
    count = slabs * PACK
    half_groups = rows.shape[1]
    span = rows.shape[4] // 2
    shape = (slabs * own, count)
    w = lax.broadcasted_iota(jnp.int32, shape, 0)
    column = lax.broadcasted_iota(jnp.int32, shape, 1)
    block, row = column // PACK, column % PACK
    across, along = (block // 2) // (slabs // 4), (block // 2) % (slabs // 4)
    slab = ((me - core) ^ (across * 2 + along * 4)) + block % 2
    to_weight = jnp.where((row < own) & (w == slab * own + row), 1.0, 0.0).astype(BF16)
    shape = (slabs * fz, count)
    z = lax.broadcasted_iota(jnp.int32, shape, 0)
    column = lax.broadcasted_iota(jnp.int32, shape, 1)
    to_fine = jnp.where(column == (z // fz) * PACK + own + z % fz, 1.0, 0.0).astype(BF16)
    result = []
    for g in range(groups):
        one = rows[(g // half_groups) ^ core, g % half_groups]
        coarse = one[:, :, :span].reshape(count, span)
        side = one[:, :, span:].reshape(count, span)
        fine = dot(to_fine, side, ((1,), (0,))).astype(BF16)
        weight = dot(to_weight, side, ((1,), (0,)))[:, :total]
        result.append((coarse, fine, weight))
    return result


def residuals(q, deltas, weights, groups):
    current = [q[g] for g in range(groups)]
    results = [[weights[g] * current[g] for g in range(groups)]]
    for pair in deltas:
        current = [
            current[g] - (pair[0][g].astype(F32) + pair[1][g].astype(F32)) for g in range(groups)
        ]
        results.append([weights[g] * current[g] for g in range(groups)])
    return results


def in_two(value):
    high = value.astype(BF16)
    return high, (value - high.astype(F32)).astype(BF16)


def loop_kernel(slabs, groups, views, own, fz, rounds, q, *refs):
    deltas = [(refs[2 * i], refs[2 * i + 1]) for i in range(rounds)]
    refs = refs[2 * rounds :]
    weights, rows = refs[0], refs[1]
    held = refs[2 : 2 + groups]
    out = refs[2 + groups]
    det = q.shape[1]
    total = q.shape[2]
    columns = total // views
    half = held[0].shape[2]
    chunk = min(half, 512)
    unpacked = unpack_rays(rows, groups, slabs, own, fz, det, total)
    residual = residuals(q, deltas, [u[2] for u in unpacked], groups)[-1]
    residual = [r.astype(BF16) for r in residual]
    count = slabs * PACK
    parts = PACK // fz
    width = half // parts
    shape = (slabs * fz, count)
    z = lax.broadcasted_iota(jnp.int32, shape, 0)
    column = lax.broadcasted_iota(jnp.int32, shape, 1)
    projections = [None] * groups
    for part in range(2):
        depths = [unpacked[g][1 - part] for g in range(groups)]
        spreads = []
        for g in range(groups):
            pieces = [
                dot(
                    depths[g][:, v * det : (v + 1) * det],
                    residual[g][:, v * columns : (v + 1) * columns],
                    ((1,), (0,)),
                ).astype(BF16)
                for v in range(views)
            ]
            spreads.append(jnp.concatenate(pieces, axis=1))
        moments = [None] * groups
        for c in range(half // chunk):
            cut = slice(c * chunk, (c + 1) * chunk)
            if part == 1:
                weight = weights[:, :, cut].reshape(count, chunk).astype(F32)
            else:
                which = (c * chunk) // width
                low = c * chunk - which * width
                source = weights[:, :, half + low : half + low + chunk].reshape(count, chunk)
                choose = jnp.where(
                    column == (z // fz) * PACK + (z % fz) * parts + which, 1.0, 0.0
                ).astype(BF16)
                weight = dot(choose, source, ((1,), (0,)))
            rays = [
                jnp.concatenate([held[g][part, v, cut, :] for v in range(views)], axis=1)
                for g in range(groups)
            ]
            back = dot(spreads[0], rays[0], ((1,), (1,)))
            for g in range(1, groups):
                back = back + dot(spreads[g], rays[g], ((1,), (1,)))
            change = (weight * back).astype(BF16)
            for g in range(groups):
                moment = dot(change, rays[g], ((1,), (0,)))
                moments[g] = moment if moments[g] is None else moments[g] + moment
        for g in range(groups):
            moment = moments[g].astype(BF16)
            pieces = [
                dot(
                    depths[g][:, v * det : (v + 1) * det],
                    moment[:, v * columns : (v + 1) * columns],
                    ((0,), (0,)),
                )
                for v in range(views)
            ]
            value = jnp.concatenate(pieces, axis=1)
            projections[g] = value if projections[g] is None else projections[g] + value
    for g in range(groups):
        out[g] = projections[g].astype(BF16)


def tail_kernel(slabs, groups, views, own, fz, rounds, q, *refs):
    deltas = [(refs[2 * i], refs[2 * i + 1]) for i in range(rounds)]
    refs = refs[2 * rounds :]
    rows = refs[0]
    held = refs[1 : 1 + groups]
    mine, theirs = refs[1 + groups : 3 + groups]
    det = q.shape[1]
    total = q.shape[2]
    columns = total // views
    half = held[0].shape[2]
    chunk = min(half, 512)
    core = lax.axis_index("slab") % 2
    unpacked = unpack_rays(rows, groups, slabs, own, fz, det, total)
    history = residuals(q, deltas, [u[2] for u in unpacked], groups)
    half_groups = rows.shape[1]
    span = rows.shape[4] // 2
    spreads = []
    for g in range(groups):
        value = history[0][g]
        for other in history[1:]:
            value = value + other[g]
        high, low = in_two(value)
        pieces = []
        for v in range(views):
            depth = jnp.concatenate(
                [
                    rows[(g // half_groups) ^ core, g % half_groups, side ^ core, :, cut]
                    for side in range(2)
                    for cut in (
                        slice(v * det, (v + 1) * det),
                        slice(span + v * det, span + (v + 1) * det),
                    )
                ],
                axis=0,
            )
            cut = slice(v * columns, (v + 1) * columns)
            pieces.append(
                dot(depth, high[:, cut], ((1,), (0,))) + dot(depth, low[:, cut], ((1,), (0,)))
            )
        spreads.append(in_two(jnp.concatenate(pieces, axis=1)))
    for part in range(2):
        first = slice(PACK * (1 - part), PACK * (2 - part))
        second = slice(PACK * (3 - part), PACK * (4 - part))
        chosen = [
            jnp.concatenate([s[first] for s in pair] + [s[second] for s in pair], axis=0)
            for pair in spreads
        ]
        for c in range(half // chunk):
            cut = slice(c * chunk, (c + 1) * chunk)
            back = None
            for g in range(groups):
                rays = jnp.concatenate([held[g][part, v, cut, :] for v in range(views)], axis=1)
                value = dot(chosen[g], rays, ((1,), (1,)))
                back = value if back is None else back + value
            mine[part, :, cut] = back[:PACK] + back[PACK : 2 * PACK]
            theirs[part, :, cut] = back[2 * PACK : 3 * PACK] + back[3 * PACK :]


def final_kernel(own, mine, received, fine, coarse, fw, cw, blocks, fine_out, coarse_out):
    core = lax.axis_index("slab") % 2
    half = mine.shape[2]
    fz = fine.shape[0]
    for source, side in ((mine, core), (received, 1 - core)):
        start = pl.multiple_of(side * half, half)
        where = pl.ds(start, half)
        keep = keep_row(blocks, start, half)
        change = source[0, own : own + fz]
        fine_out[:, where] = fine[:, where] + fw[:, where] * change
        coarse_out[:, where] = (
            coarse[:, where] + cw[:, where] * source[1]
        ) * keep


def make_body(slabs, groups):
    def body(
        fine_volume,
        coarse_volume,
        fine_rays,
        coarse_rays,
        fine_axial,
        coarse_axial,
        measured,
        ray_weight,
        fine_cell_weight,
        coarse_cell_weight,
        margin_blocks,
        ray_hits,
    ):
        views, cells, columns = fine_rays.shape
        det = fine_axial.shape[2]
        fz, cz = fine_volume.shape[0], coarse_volume.shape[0]
        own = measured.shape[0]
        total = views * columns
        span = max(views * det, total)
        half = cells // 2
        core = lax.axis_index("slab") % 2
        width = half + half * fz // PACK

        own_rays, weights_mine, weights_theirs, rows = pl.pallas_call(
            prepare_kernel,
            out_shape=(
                jax.ShapeDtypeStruct((2, views, half, columns), BF16),
                jax.ShapeDtypeStruct((PACK, width), BF16),
                jax.ShapeDtypeStruct((PACK, width), BF16),
                jax.ShapeDtypeStruct((PACK, views * det + span), BF16),
            ),
            in_specs=[HBM] * 7 + [SMEM] * 2,
            out_specs=(VMEM,) * 4,
            scratch_shapes=[
                pltpu.VMEM(a.shape, a.dtype)
                for a in (
                    fine_cell_weight,
                    coarse_cell_weight,
                    fine_axial,
                    coarse_axial,
                    ray_weight,
                )
            ]
            + [pltpu.SemaphoreType.DMA((7,))],
            compiler_params=PARAMS,
            cost_estimate=QUICK,
            name="prepare",
        )(
            fine_rays,
            coarse_rays,
            fine_cell_weight,
            coarse_cell_weight,
            fine_axial,
            coarse_axial,
            ray_weight,
            margin_blocks,
            ray_hits,
        )

        ray_list = [own_rays]
        all_rows = rows[None]
        bit = 1
        while bit < groups:
            all_rows = jnp.concatenate([all_rows, swap(all_rows, "view", groups, bit)])
            ray_list += [swap(value, "view", groups, bit) for value in ray_list]
            bit *= 2

        half_groups = groups // 2
        first, second = all_rows[:half_groups], all_rows[half_groups:]
        lead = core == 0
        rows_mine = jnp.where(lead, first, second)
        rows_theirs = jnp.where(lead, second, first)
        weights_other = swap(weights_theirs, "slab", slabs, 1)
        rows_other = swap(rows_theirs, "slab", slabs, 1)

        def pair(a, b):
            return jnp.where(lead, jnp.stack([a, b]), jnp.stack([b, a]))

        held_weights = pair(weights_mine, weights_other)
        held_rows = pair(rows_mine, rows_other)
        far = [4 * k for k in range(1, slabs // 4)]
        held_weights = jnp.concatenate(
            [held_weights] + [swap(held_weights, "slab", slabs, k) for k in far]
        )
        held_rows = jnp.concatenate(
            [held_rows] + [swap(held_rows, "slab", slabs, k) for k in far]
        )
        held_weights = jnp.concatenate([held_weights, swap(held_weights, "slab", slabs, 2)])
        held_rows = jnp.concatenate([held_rows, swap(held_rows, "slab", slabs, 2)])
        held_rows = jnp.swapaxes(held_rows, 0, 1)
        held_rows = jnp.stack([held_rows, swap(held_rows, "slab", slabs, 1)])

        steps = 4
        q = pl.pallas_call(
            forward_kernel,
            out_shape=jax.ShapeDtypeStruct((det, total), F32),
            in_specs=[HBM] * 5 + [VMEM, SMEM],
            out_specs=VMEM,
            scratch_shapes=[
                pltpu.VMEM(a.shape, a.dtype)
                for a in (fine_volume, coarse_volume, fine_rays, coarse_rays, measured)
            ]
            + [pltpu.SemaphoreType.DMA((steps + 1, 4))],
            compiler_params=PARAMS,
            cost_estimate=QUICK,
            name="forward",
        )(fine_volume, coarse_volume, fine_rays, coarse_rays, measured, rows, margin_blocks)
        bit = 1
        while bit < slabs:
            q = q + swap(q.astype(BF16), "slab", slabs, bit).astype(F32)
            bit *= 2
        q = q[None]
        bit = 1
        while bit < groups:
            q = jnp.concatenate([q, swap(q, "view", groups, bit)])
            bit *= 2

        deltas = []
        for rounds in range(2):
            delta = pl.pallas_call(
                functools.partial(loop_kernel, slabs, groups, views, own, fz, rounds),
                out_shape=jax.ShapeDtypeStruct((groups, det, total), BF16),
                in_specs=[VMEM] * (3 + 2 * rounds + groups),
                out_specs=VMEM,
                compiler_params=PARAMS,
                name="ray_space_step",
            )(q, *deltas, held_weights, held_rows, *ray_list)
            deltas += [delta, swap(delta, "slab", slabs, 1)]
        mine, theirs = pl.pallas_call(
            functools.partial(tail_kernel, slabs, groups, views, own, fz, 2),
            out_shape=(jax.ShapeDtypeStruct((2, PACK, half), F32),) * 2,
            in_specs=[VMEM] * (2 + len(deltas) + groups),
            out_specs=(VMEM, VMEM),
            compiler_params=PARAMS,
            name="back_projection",
        )(q, *deltas, held_rows, *ray_list)
        received = swap(theirs, "slab", slabs, 1)
        return pl.pallas_call(
            functools.partial(final_kernel, own),
            out_shape=(
                jax.ShapeDtypeStruct(fine_volume.shape, F32),
                jax.ShapeDtypeStruct(coarse_volume.shape, F32),
            ),
            in_specs=[VMEM] * 6 + [SMEM],
            out_specs=(VMEM, VMEM),
            compiler_params=PARAMS,
            name="update",
        )(
            mine,
            received,
            fine_volume,
            coarse_volume,
            fine_cell_weight,
            coarse_cell_weight,
            margin_blocks,
        )

    return body


def solution(mesh):
    return jax.shard_map(
        make_body(mesh.shape["slab"], mesh.shape["view"]),
        mesh=mesh,
        in_specs=(
            P("slab", None),
            P("slab", None),
            P("view", None, None),
            P("view", None, None),
            P("view", "slab", None),
            P("view", "slab", None),
            P("slab", "view", None),
            P("slab", "view", None),
            P("slab", None),
            P("slab", None),
            P("slab", None),
            P("view", "slab", None),
        ),
        out_specs=(P("slab", None), P("slab", None)),
        check_vma=False,
    )
```

time: 114 us -> 87.6 us (0.77)
  waiting for transfers between devices: 60.6 us -> 35.9 us
  matrix products: 22.5 us -> 0 us
  Pallas kernels: 0 us -> 13.8 us
  local copies, waits for them, and re-layouts: 2.02 us -> 11.7 us
  other arithmetic: 9.79 us -> 0.35 us
  starting transfers between devices: 17 us -> 24.6 us
    ppermute x19 -> x21, waiting for transfers between devices: 60.6 us -> 35.9 us  [swap(): return lax.ppermute(value, axis, [(i, i ^ bits) for i in range(size)])]
    dot_general x12 -> x0, matrix products: 22.5 us -> none  [the longest x3 7.6 us: body(): jnp.einsum('vzu,vxu->zx', fine_spread, fine_rays, preferred_element_type=...]
    pallas_call x0 -> x6, Pallas kernels: none -> 13.8 us  [the longest x2 7.32 us: body(): pl.pallas_call(functools.partial(loop_kernel, slabs, groups, views, own,...]
    unnamed x33 -> x40, local copies, waits for them, and re-layouts: 0.73 us -> 11.6 us
    ppermute x19 -> x21, starting transfers between devices: 17 us -> 24.6 us  [swap(): return lax.ppermute(value, axis, [(i, i ^ bits) for i in range(size)])]
    add x10 -> x0, other arithmetic: 3.41 us -> none  [the longest x9 1.87 us: pair_sum(): value = value + swap(value, axis, size, bit)]
    convert_element_type x7 -> x4, other arithmetic: 3.3 us -> 0.09 us  [body(): q = q + swap(q.astype(BF16), 'slab', slabs, bit).astype(F32)]
  transfers between devices with their start and end apart: 19 -> 21, of which waited for: 16 -> 10; matrix products, arithmetic and copies ran while one was open for 5% -> 1% of each run, Pallas kernels for 0% -> 3%
where the time goes in v2:
time: 87.6 us; the launch traced here: 87.1 us
  waiting for transfers between devices  35.9 us (41%)
  starting transfers between devices  24.6 us (28%)
  Pallas kernels  13.8 us (16%)
  local copies, waits for them, and re-layouts  11.7 us (13%)
    ppermute x21, waiting for transfers between devices, swap(): return lax.ppermute(value, axis, [(i, i ^ bits) for i in range(size)])  35.9 us
    ppermute x21, starting transfers between devices, swap(): return lax.ppermute(value, axis, [(i, i ^ bits) for i in range(size)])  24.6 us
    unnamed x40, local copies, waits for them, and re-layouts  11.6 us
    pallas_call x2, Pallas kernels, body(): pl.pallas_call(functools.partial(loop_kernel, slabs, groups, views, own,...  7.32 us
    pallas_call x1, Pallas kernels, body(): pl.pallas_call(forward_kernel, out_shape=jax.ShapeDtypeStruct((det, total...  2.23 us
  transfers between devices with their start and end apart: 21, of which 10 were waited for; matrix products, arithmetic and copies ran while one was open for 1% of the time, Pallas kernels for 3%

profile of v2, /device:TPU:0, one launch (start us, length us, event | category | flops | bytes accessed | tf_op | source)
XLA Modules:
  0.0 87.1 jit_solution(12903417249592482736)
XLA Ops:
  0.6 1.6 %copy-done = bf16[2,4096,128]{2,1,0:T(8,128)(2,1)S(1)} copy-done((bf16[2,4096,128]{2,1,0:T(8,128)(2,1)S(1)}, bf16[2,4096,128]{2,1,0:T(8,128)(2,1)}, u32[]{:S(2)}) %copy-start) | copy-done | bytes 2097176
  2.2 1.6 %copy-done.2 = bf16[2,4096,128]{2,1,0:T(8,128)(2,1)S(1)} copy-done((bf16[2,4096,128]{2,1,0:T(8,128)(2,1)S(1)}, bf16[2,4096,128]{2,1,0:T(8,128)(2,1)}, u32[]{:S(2)}) %copy-start.2) | copy-done | bytes 2097176
  3.8 0.9 %copy-done.5 = f32[16,4096]{1,0:T(8,128)S(1)} copy-done((f32[16,4096]{1,0:T(8,128)S(1)}, f32[16,4096]{1,0:T(8,128)}, u32[]{:S(2)}) %copy-start.5) | copy-done | bytes 262168
  4.8 0.8 copy-done.8
  5.6 0.7 copy-done.10
  6.3 0.7 copy-done.11
  9.0 1.1 %prepare.1 = (bf16[2,2,2048,128]{3,2,1,0:T(8,128)(2,1)S(1)}, bf16[16,2560]{1,0:T(8,128)(2,1)S(1)}, bf16[16,2560]{1,0:T(8,128)(2,1)S(1)}, bf16[16,512]{1,0:T(8,128)(2,1)S(1)}) custom-call(bf16[2,4096,128]{2,1,0:T(8,128)(2,1)S(1)} %copy-done, bf16[2,4096,128]{2,1,0:T(8,128)(2,1)S(1)} %copy-done.2, f32[4,4096]{1,0:T(4,128)S(1)} %copy-done.8, ...), custom_call_target="tpu_custom_call" | custom-call | flops 1 | bytes 1 | tf_op jit(solution)/shard_map/prepare/pallas_call | solution.py:412
  10.2 3.0 %collective-permute-start.10 = (bf16[1,16,512]{2,1,0:T(8,128)(2,1)S(1)}, bf16[1,16,512]{2,1,0:T(8,128)(2,1)S(1)}, u32[]{:S(2)}, u32[]{:S(2)}) collective-permute-start(bf16[1,16,512]{2,1,0:T(8,128)(2,1)S(1)} %bitcast.14), channel_id=1, source_target_pairs={{0,1},{1,0},{2,3},{3,2},{4,5},{5,4},{6,7},{7,6},{8,9},{9,8},{10,11... | collective-permute-start | bytes 49160 | tf_op jit(solution)/shard_map/ppermute | solution.py:27
  13.2 1.7 %collective-permute-done.10 = bf16[1,16,512]{2,1,0:T(8,128)(2,1)S(1)} collective-permute-done((bf16[1,16,512]{2,1,0:T(8,128)(2,1)S(1)}, bf16[1,16,512]{2,1,0:T(8,128)(2,1)S(1)}, u32[]{:S(2)}, u32[]{:S(2)}) %collective-permute-start.10) | collective-permute-done | bytes 16416 | tf_op jit(solution)/shard_map/ppermute | solution.py:27
  15.5 1.6 %copy-done.1 = bf16[2,4096,128]{2,1,0:T(8,128)(2,1)S(1)} copy-done((bf16[2,4096,128]{2,1,0:T(8,128)(2,1)S(1)}, bf16[2,4096,128]{2,1,0:T(8,128)(2,1)}, u32[]{:S(2)}) %copy-start.1) | copy-done | bytes 2097176
  17.0 1.6 %copy-done.3 = bf16[2,4096,128]{2,1,0:T(8,128)(2,1)S(1)} copy-done((bf16[2,4096,128]{2,1,0:T(8,128)(2,1)S(1)}, bf16[2,4096,128]{2,1,0:T(8,128)(2,1)}, u32[]{:S(2)}) %copy-start.3) | copy-done | bytes 2097176
  18.6 2.2 %forward.1 = f32[128,256]{1,0:T(8,128)S(1)} custom-call(f32[4,4096]{1,0:T(4,128)S(1)} %copy-done.7, f32[16,4096]{1,0:T(8,128)S(1)} %copy-done.4, bf16[2,4096,128]{2,1,0:T(8,128)(2,1)S(1)} %copy-done.1, bf16[2,4096,128]{2,1,0:T(8,128)(2,1)S(1)} %copy-done.3, f32[8,2,128]{2,1,0:T(2,128)S(1)} %copy-done.12, bf16[16,512]{1,0:T(8,128)(2,1)S(1)} %get-tuple-element.8.rows, ...), custom_call_target="tpu_custom_call" | custom-call | flops 1 | bytes 1 | tf_op jit(solution)/shard_map/forward/pallas_call | solution.py:482
  21.0 2.0 %collective-permute-start.17 = (bf16[2,2,2048,128]{3,2,1,0:T(8,128)(2,1)S(1)}, bf16[2,2,2048,128]{3,2,1,0:T(8,128)(2,1)S(1)}, u32[]{:S(2)}, u32[]{:S(2)}) collective-permute-start(bf16[2,2,2048,128]{3,2,1,0:T(8,128)(2,1)S(1)} %get-tuple-element.11.refs_2_.refs_4_.refs_5_), channel_id=1, source_target_pairs={{0,1},{1,0},{2,3},{3,2},{4,5},{5,4},{6,7},{7,6},{8,9},{9,8},{10,11... | collective-permute-start | bytes 6291464 | tf_op jit(solution)/shard_map/ppermute | solution.py:27
  23.1 3.7 %collective-permute-start.14 = (bf16[2,1,16,512]{3,2,0,1:T(8,128)(2,1)S(1)}, bf16[2,1,16,512]{3,2,0,1:T(8,128)(2,1)S(1)}, u32[]{:S(2)}, u32[]{:S(2)}) collective-permute-start(bf16[2,1,16,512]{3,2,0,1:T(8,128)(2,1)S(1)} %get-tuple-element.15), channel_id=1, source_target_pairs={{0,24},{2,26},{4,28},{6,30},{8,16},{10,18},{12,20},{14,22},{16,8},... | collective-permute-start | bytes 98312 | tf_op jit(solution)/shard_map/ppermute | solution.py:27
  26.7 0.8 collective-permute-start.12
  27.5 1.3 %collective-permute-done.14 = bf16[2,1,16,512]{3,2,0,1:T(8,128)(2,1)S(1)} collective-permute-done((bf16[2,1,16,512]{3,2,0,1:T(8,128)(2,1)S(1)}, bf16[2,1,16,512]{3,2,0,1:T(8,128)(2,1)S(1)}, u32[]{:S(2)}, u32[]{:S(2)}) %collective-permute-start.14) | collective-permute-done | bytes 32800 | tf_op jit(solution)/shard_map/ppermute | solution.py:27
  28.8 1.5 %collective-permute-start.1 = (bf16[128,256]{1,0:T(8,128)(2,1)S(1)}, bf16[128,256]{1,0:T(8,128)(2,1)S(1)}, u32[]{:S(2)}, u32[]{:S(2)}) collective-permute-start(bf16[128,256]{1,0:T(8,128)(2,1)S(1)} %fusion), channel_id=1, source_target_pairs={{0,4},{2,6},{4,0},{6,2},{8,12},{10,14},{12,8},{14,10},{16,20},{18,... | collective-permute-start | bytes 196616 | tf_op jit(solution)/shard_map/ppermute | solution.py:27
  30.3 1.2 %collective-permute-done.13 = bf16[2,1,16,512]{3,2,0,1:T(8,128)(2,1)S(1)} collective-permute-done((bf16[2,1,16,512]{3,2,0,1:T(8,128)(2,1)S(1)}, bf16[2,1,16,512]{3,2,0,1:T(8,128)(2,1)S(1)}, u32[]{:S(2)}, u32[]{:S(2)}) %collective-permute-start.13) | collective-permute-done | bytes 32800 | tf_op jit(solution)/shard_map/ppermute | solution.py:27
  31.6 1.6 %collective-permute-start.15 = (bf16[8,1,16,512]{3,2,0,1:T(8,128)(2,1)S(1)}, bf16[8,1,16,512]{3,2,0,1:T(8,128)(2,1)S(1)}, u32[]{:S(2)}, u32[]{:S(2)}) collective-permute-start(bf16[8,1,16,512]{3,2,0,1:T(8,128)(2,1)S(1)} %pad_maximum_fusion.3), channel_id=1, source_target_pairs={{0,4},{2,6},{4,0},{6,2},{8,12},{10,14},{12,8},{14,10},{16,20},{18,... | collective-permute-start | bytes 393224 | tf_op jit(solution)/shard_map/ppermute | solution.py:27
  33.4 4.3 %collective-permute-start.8 = (bf16[2,16,2560]{2,1,0:T(8,128)(2,1)S(1)}, bf16[2,16,2560]{2,1,0:T(8,128)(2,1)S(1)}, u32[]{:S(2)}, u32[]{:S(2)}) collective-permute-start(bf16[2,16,2560]{2,1,0:T(8,128)(2,1)S(1)} %get-tuple-element.17), channel_id=1, source_target_pairs={{0,24},{2,26},{4,28},{6,30},{8,16},{10,18},{12,20},{14,22},{16,8},... | collective-permute-start | bytes 491528 | tf_op jit(solution)/shard_map/ppermute | solution.py:27
  38.3 1.4 %collective-permute-done.2 = bf16[128,256]{1,0:T(8,128)(2,1)S(1)} collective-permute-done((bf16[128,256]{1,0:T(8,128)(2,1)S(1)}, bf16[128,256]{1,0:T(8,128)(2,1)S(1)}, u32[]{:S(2)}, u32[]{:S(2)}) %collective-permute-start.2) | collective-permute-done | bytes 65568 | tf_op jit(solution)/shard_map/ppermute | solution.py:27
  39.8 3.6 %collective-permute-start.3 = (bf16[128,256]{1,0:T(8,128)(2,1)S(1)}, bf16[128,256]{1,0:T(8,128)(2,1)S(1)}, u32[]{:S(2)}, u32[]{:S(2)}) collective-permute-start(bf16[128,256]{1,0:T(8,128)(2,1)S(1)} %fusion.1), channel_id=1, source_target_pairs={{0,16},{2,18},{4,20},{6,22},{8,24},{10,26},{12,28},{14,30},{16,0},... | collective-permute-start | bytes 196616 | tf_op jit(solution)/shard_map/ppermute | solution.py:27
  44.1 8.3 %collective-permute-done.7 = bf16[2,16,2560]{2,1,0:T(8,128)(2,1)S(1)} collective-permute-done((bf16[2,16,2560]{2,1,0:T(8,128)(2,1)S(1)}, bf16[2,16,2560]{2,1,0:T(8,128)(2,1)S(1)}, u32[]{:S(2)}, u32[]{:S(2)}) %collective-permute-start.7) | collective-permute-done | bytes 163872 | tf_op jit(solution)/shard_map/ppermute | solution.py:27
  52.5 1.6 %collective-permute-start.9 = (bf16[8,16,2560]{2,1,0:T(8,128)(2,1)S(1)}, bf16[8,16,2560]{2,1,0:T(8,128)(2,1)S(1)}, u32[]{:S(2)}, u32[]{:S(2)}) collective-permute-start(bf16[8,16,2560]{2,1,0:T(8,128)(2,1)S(1)} %pad_maximum_fusion), channel_id=1, source_target_pairs={{0,4},{2,6},{4,0},{6,2},{8,12},{10,14},{12,8},{14,10},{16,20},{18,... | collective-permute-start | bytes 1966088 | tf_op jit(solution)/shard_map/ppermute | solution.py:27
  54.7 17.4 %collective-permute-done.4 = f32[1,128,256]{2,1,0:T(8,128)S(1)} collective-permute-done((f32[1,128,256]{2,1,0:T(8,128)S(1)}, f32[1,128,256]{2,1,0:T(8,128)S(1)}, u32[]{:S(2)}, u32[]{:S(2)}) %collective-permute-start.4) | collective-permute-done | bytes 131104 | tf_op jit(solution)/shard_map/ppermute | solution.py:27
  72.2 3.7 %ray_space_step.2.refs_0_ = bf16[2,128,256]{2,1,0:T(8,128)(2,1)S(1)} custom-call(f32[2,128,256]{2,1,0:T(8,128)S(1)} %pad_maximum_fusion.2.q, bf16[16,16,2560]{2,1,0:T(8,128)(2,1)S(1)} %constant_dynamic-update-slice_fusion.refs_0_.refs_2_, bf16[2,1,16,16,512]{4,3,2,1,0:T(8,128)(2,1)S(1)} %pad_maximum_fusion.1.refs_1_.refs_3_.refs_4_, ...), custom_call_target="tpu_custom_call" | custom-call | tf_op jit(solution)/shard_map/ray_space_step/pallas_call | solution.py:508
  76.0 1.3 %collective-permute-done.18.refs_1_ = bf16[2,128,256]{2,1,0:T(8,128)(2,1)S(1)} collective-permute-done((bf16[2,128,256]{2,1,0:T(8,128)(2,1)S(1)}, bf16[2,128,256]{2,1,0:T(8,128)(2,1)S(1)}, u32[]{:S(2)}, u32[]{:S(2)}) %collective-permute-start.18) | collective-permute-done | bytes 131104 | tf_op jit(solution)/shard_map/ppermute | solution.py:27
  77.3 3.7 %ray_space_step.3.refs_2_ = bf16[2,128,256]{2,1,0:T(8,128)(2,1)S(1)} custom-call(f32[2,128,256]{2,1,0:T(8,128)S(1)} %pad_maximum_fusion.2.q, bf16[2,128,256]{2,1,0:T(8,128)(2,1)S(1)} %ray_space_step.2.refs_0_, bf16[2,128,256]{2,1,0:T(8,128)(2,1)S(1)} %collective-permute-done.18.refs_1_, ...), custom_call_target="tpu_custom_call" | custom-call | tf_op jit(solution)/shard_map/ray_space_step/pallas_call | solution.py:508
  81.2 1.2 %collective-permute-done.19.refs_3_ = bf16[2,128,256]{2,1,0:T(8,128)(2,1)S(1)} collective-permute-done((bf16[2,128,256]{2,1,0:T(8,128)(2,1)S(1)}, bf16[2,128,256]{2,1,0:T(8,128)(2,1)S(1)}, u32[]{:S(2)}, u32[]{:S(2)}) %collective-permute-start.19) | collective-permute-done | bytes 131104 | tf_op jit(solution)/shard_map/ppermute | solution.py:27
  82.4 1.6 %back_projection.1 = (f32[2,16,2048]{2,1,0:T(8,128)S(1)}, f32[2,16,2048]{2,1,0:T(8,128)S(1)}) custom-call(f32[2,128,256]{2,1,0:T(8,128)S(1)} %pad_maximum_fusion.2.q, bf16[2,128,256]{2,1,0:T(8,128)(2,1)S(1)} %ray_space_step.2.refs_0_, bf16[2,128,256]{2,1,0:T(8,128)(2,1)S(1)} %collective-permute-done.18.refs_1_, ...), custom_call_target="tpu_custom_call" | custom-call | tf_op jit(solution)/shard_map/back_projection/pallas_call | solution.py:517
  84.2 1.4 %collective-permute-done.20.received = f32[2,16,2048]{2,1,0:T(8,128)S(1)} collective-permute-done((f32[2,16,2048]{2,1,0:T(8,128)S(1)}, f32[2,16,2048]{2,1,0:T(8,128)S(1)}, u32[]{:S(2)}, u32[]{:S(2)}) %collective-permute-start.20) | collective-permute-done | bytes 262176 | tf_op jit(solution)/shard_map/ppermute | solution.py:27
  85.6 1.5 %update.1 = (f32[4,4096]{1,0:T(4,128)}, f32[16,4096]{1,0:T(8,128)}) custom-call(f32[2,16,2048]{2,1,0:T(8,128)S(1)} %get-tuple-element.12.mine, f32[2,16,2048]{2,1,0:T(8,128)S(1)} %collective-permute-done.20.received, f32[4,4096]{1,0:T(4,128)S(1)} %copy-done.7, f32[16,4096]{1,0:T(8,128)S(1)} %copy-done.4, f32[4,4096]{1,0:T(4,128)S(1)} %copy-done.9, ...), custom_call_target="tpu_custom_call" | custom-call | tf_op jit(solution)/shard_map/update/pallas_call | solution.py:526
  (70 shorter events, 5.6 us)
Async XLA Ops:
  0.6 1.6 %copy-start = (bf16[2,4096,128]{2,1,0:T(8,128)(2,1)S(1)}, bf16[2,4096,128]{2,1,0:T(8,128)(2,1)}, u32[]{:S(2)}) copy-start(bf16[2,4096,128]{2,1,0:T(8,128)(2,1)} %fine_rays_in.1) | copy-start | bytes 6291460
  2.2 1.6 %copy-start.2 = (bf16[2,4096,128]{2,1,0:T(8,128)(2,1)S(1)}, bf16[2,4096,128]{2,1,0:T(8,128)(2,1)}, u32[]{:S(2)}) copy-start(bf16[2,4096,128]{2,1,0:T(8,128)(2,1)} %coarse_rays_in.1) | copy-start | bytes 6291460
  3.8 0.9 %copy-start.5 = (f32[16,4096]{1,0:T(8,128)S(1)}, f32[16,4096]{1,0:T(8,128)}, u32[]{:S(2)}) copy-start(f32[16,4096]{1,0:T(8,128)} %cw.1) | copy-start | bytes 786436
  9.0 6.4 %copy-start.4 = (f32[16,4096]{1,0:T(8,128)S(1)}, f32[16,4096]{1,0:T(8,128)}, u32[]{:S(2)}) copy-start(f32[16,4096]{1,0:T(8,128)} %coarse.1) | copy-start | bytes 786436
  9.0 6.4 %copy-start.7 = (f32[4,4096]{1,0:T(4,128)S(1)}, f32[4,4096]{1,0:T(4,128)}, u32[]{:S(2)}) copy-start(f32[4,4096]{1,0:T(4,128)} %fine.1) | copy-start | bytes 196612
  9.0 6.4 %copy-start.12 = (f32[8,2,128]{2,1,0:T(2,128)S(1)}, f32[8,2,128]{2,1,0:T(2,128)}, u32[]{:S(2)}) copy-start(f32[8,2,128]{2,1,0:T(2,128)} %measured_in.1) | copy-start | bytes 24580
  9.0 6.4 %copy-start.14 = (s32[1,8]{1,0:T(1,128)S(1)}, s32[1,8]{1,0:T(1,128)}, u32[]{:S(2)}) copy-start(s32[1,8]{1,0:T(1,128)} %blocks.5) | copy-start | bytes 100
  10.2 4.8 %collective-permute-start.10 = (bf16[1,16,512]{2,1,0:T(8,128)(2,1)S(1)}, bf16[1,16,512]{2,1,0:T(8,128)(2,1)S(1)}, u32[]{:S(2)}, u32[]{:S(2)}) collective-permute-start(bf16[1,16,512]{2,1,0:T(8,128)(2,1)S(1)} %bitcast.14), channel_id=1, source_target_pairs={{0,1},{1,0},{2,3},{3,2},{4,5},{5,4},{6,7},{7,6},{8,9},{9,8},{10,11... | collective-permute-start | bytes 49160 | tf_op jit(solution)/shard_map/ppermute | solution.py:27
  14.9 8.1 %collective-permute-start.11 = (bf16[1,16,512]{2,1,0:T(8,128)(2,1)S(1)}, bf16[1,16,512]{2,1,0:T(8,128)(2,1)S(1)}, u32[]{:S(2)}, u32[]{:S(2)}) collective-permute-start(bf16[1,16,512]{2,1,0:T(8,128)(2,1)S(1)} %get-tuple-element.18), channel_id=1, source_target_pairs={{0,2},{2,0},{4,6},{6,4},{8,10},{10,8},{12,14},{14,12},{16,18},{18,... | collective-permute-start | bytes 49160 | tf_op jit(solution)/shard_map/ppermute | solution.py:27
  14.9 18.4 %collective-permute-start.5 = (bf16[16,2560]{1,0:T(8,128)(2,1)S(1)}, bf16[16,2560]{1,0:T(8,128)(2,1)S(1)}, u32[]{:S(2)}, u32[]{:S(2)}) collective-permute-start(bf16[16,2560]{1,0:T(8,128)(2,1)S(1)} %get-tuple-element.10), channel_id=1, source_target_pairs={{0,2},{2,0},{4,6},{6,4},{8,10},{10,8},{12,14},{14,12},{16,18},{18,... | collective-permute-start | bytes 245768 | tf_op jit(solution)/shard_map/ppermute | solution.py:27
  15.4 1.6 %copy-start.1 = (bf16[2,4096,128]{2,1,0:T(8,128)(2,1)S(1)}, bf16[2,4096,128]{2,1,0:T(8,128)(2,1)}, u32[]{:S(2)}) copy-start(bf16[2,4096,128]{2,1,0:T(8,128)(2,1)} %fine_rays_in.1) | copy-start | bytes 6291460
  17.0 1.6 %copy-start.3 = (bf16[2,4096,128]{2,1,0:T(8,128)(2,1)S(1)}, bf16[2,4096,128]{2,1,0:T(8,128)(2,1)}, u32[]{:S(2)}) copy-start(bf16[2,4096,128]{2,1,0:T(8,128)(2,1)} %coarse_rays_in.1) | copy-start | bytes 6291460
  20.9 5.9 %collective-permute-start = (bf16[128,256]{1,0:T(8,128)(2,1)S(1)}, bf16[128,256]{1,0:T(8,128)(2,1)S(1)}, u32[]{:S(2)}, u32[]{:S(2)}) collective-permute-start(bf16[128,256]{1,0:T(8,128)(2,1)S(1)} %convert_element_type.24), channel_id=1, source_target_pairs={{0,2},{2,0},{4,6},{6,4},{8,10},{10,8},{12,14},{14,12},{16,18},{18,... | collective-permute-start | bytes 196616 | tf_op jit(solution)/shard_map/ppermute | solution.py:27
  21.0 51.2 %collective-permute-start.17 = (bf16[2,2,2048,128]{3,2,1,0:T(8,128)(2,1)S(1)}, bf16[2,2,2048,128]{3,2,1,0:T(8,128)(2,1)S(1)}, u32[]{:S(2)}, u32[]{:S(2)}) collective-permute-start(bf16[2,2,2048,128]{3,2,1,0:T(8,128)(2,1)S(1)} %get-tuple-element.11.refs_2_.refs_4_.refs_5_), channel_id=1, source_target_pairs={{0,1},{1,0},{2,3},{3,2},{4,5},{5,4},{6,7},{7,6},{8,9},{9,8},{10,11... | collective-permute-start | bytes 6291464 | tf_op jit(solution)/shard_map/ppermute | solution.py:27
  23.1 5.8 %collective-permute-start.14 = (bf16[2,1,16,512]{3,2,0,1:T(8,128)(2,1)S(1)}, bf16[2,1,16,512]{3,2,0,1:T(8,128)(2,1)S(1)}, u32[]{:S(2)}, u32[]{:S(2)}) collective-permute-start(bf16[2,1,16,512]{3,2,0,1:T(8,128)(2,1)S(1)} %get-tuple-element.15), channel_id=1, source_target_pairs={{0,24},{2,26},{4,28},{6,30},{8,16},{10,18},{12,20},{14,22},{16,8},... | collective-permute-start | bytes 98312 | tf_op jit(solution)/shard_map/ppermute | solution.py:27
  26.7 4.8 %collective-permute-start.13 = (bf16[2,1,16,512]{3,2,0,1:T(8,128)(2,1)S(1)}, bf16[2,1,16,512]{3,2,0,1:T(8,128)(2,1)S(1)}, u32[]{:S(2)}, u32[]{:S(2)}) collective-permute-start(bf16[2,1,16,512]{3,2,0,1:T(8,128)(2,1)S(1)} %get-tuple-element.15), channel_id=1, source_target_pairs={{0,16},{2,18},{4,20},{6,22},{8,24},{10,26},{12,28},{14,30},{16,0},... | collective-permute-start | bytes 98312 | tf_op jit(solution)/shard_map/ppermute | solution.py:27
  26.7 4.8 %collective-permute-start.12 = (bf16[2,1,16,512]{3,2,0,1:T(8,128)(2,1)S(1)}, bf16[2,1,16,512]{3,2,0,1:T(8,128)(2,1)S(1)}, u32[]{:S(2)}, u32[]{:S(2)}) collective-permute-start(bf16[2,1,16,512]{3,2,0,1:T(8,128)(2,1)S(1)} %get-tuple-element.15), channel_id=1, source_target_pairs={{0,8},{2,10},{4,12},{6,14},{8,0},{10,2},{12,4},{14,6},{16,24},{18,... | collective-permute-start | bytes 98312 | tf_op jit(solution)/shard_map/ppermute | solution.py:27
  28.8 4.3 %collective-permute-start.1 = (bf16[128,256]{1,0:T(8,128)(2,1)S(1)}, bf16[128,256]{1,0:T(8,128)(2,1)S(1)}, u32[]{:S(2)}, u32[]{:S(2)}) collective-permute-start(bf16[128,256]{1,0:T(8,128)(2,1)S(1)} %fusion), channel_id=1, source_target_pairs={{0,4},{2,6},{4,0},{6,2},{8,12},{10,14},{12,8},{14,10},{16,20},{18,... | collective-permute-start | bytes 196616 | tf_op jit(solution)/shard_map/ppermute | solution.py:27
  31.6 8.2 %collective-permute-start.15 = (bf16[8,1,16,512]{3,2,0,1:T(8,128)(2,1)S(1)}, bf16[8,1,16,512]{3,2,0,1:T(8,128)(2,1)S(1)}, u32[]{:S(2)}, u32[]{:S(2)}) collective-permute-start(bf16[8,1,16,512]{3,2,0,1:T(8,128)(2,1)S(1)} %pad_maximum_fusion.3), channel_id=1, source_target_pairs={{0,4},{2,6},{4,0},{6,2},{8,12},{10,14},{12,8},{14,10},{16,20},{18,... | collective-permute-start | bytes 393224 | tf_op jit(solution)/shard_map/ppermute | solution.py:27
  33.2 6.6 %collective-permute-start.2 = (bf16[128,256]{1,0:T(8,128)(2,1)S(1)}, bf16[128,256]{1,0:T(8,128)(2,1)S(1)}, u32[]{:S(2)}, u32[]{:S(2)}) collective-permute-start(bf16[128,256]{1,0:T(8,128)(2,1)S(1)} %fusion.2), channel_id=1, source_target_pairs={{0,8},{2,10},{4,12},{6,14},{8,0},{10,2},{12,4},{14,6},{16,24},{18,... | collective-permute-start | bytes 196616 | tf_op jit(solution)/shard_map/ppermute | solution.py:27
  33.4 10.7 %collective-permute-start.8 = (bf16[2,16,2560]{2,1,0:T(8,128)(2,1)S(1)}, bf16[2,16,2560]{2,1,0:T(8,128)(2,1)S(1)}, u32[]{:S(2)}, u32[]{:S(2)}) collective-permute-start(bf16[2,16,2560]{2,1,0:T(8,128)(2,1)S(1)} %get-tuple-element.17), channel_id=1, source_target_pairs={{0,24},{2,26},{4,28},{6,30},{8,16},{10,18},{12,20},{14,22},{16,8},... | collective-permute-start | bytes 491528 | tf_op jit(solution)/shard_map/ppermute | solution.py:27
  37.7 14.7 %collective-permute-start.7 = (bf16[2,16,2560]{2,1,0:T(8,128)(2,1)S(1)}, bf16[2,16,2560]{2,1,0:T(8,128)(2,1)S(1)}, u32[]{:S(2)}, u32[]{:S(2)}) collective-permute-start(bf16[2,16,2560]{2,1,0:T(8,128)(2,1)S(1)} %get-tuple-element.17), channel_id=1, source_target_pairs={{0,16},{2,18},{4,20},{6,22},{8,24},{10,26},{12,28},{14,30},{16,0},... | collective-permute-start | bytes 491528 | tf_op jit(solution)/shard_map/ppermute | solution.py:27
  39.8 12.6 %collective-permute-start.6 = (bf16[2,16,2560]{2,1,0:T(8,128)(2,1)S(1)}, bf16[2,16,2560]{2,1,0:T(8,128)(2,1)S(1)}, u32[]{:S(2)}, u32[]{:S(2)}) collective-permute-start(bf16[2,16,2560]{2,1,0:T(8,128)(2,1)S(1)} %get-tuple-element.17), channel_id=1, source_target_pairs={{0,8},{2,10},{4,12},{6,14},{8,0},{10,2},{12,4},{14,6},{16,24},{18,... | collective-permute-start | bytes 491528 | tf_op jit(solution)/shard_map/ppermute | solution.py:27
  39.8 14.3 %collective-permute-start.3 = (bf16[128,256]{1,0:T(8,128)(2,1)S(1)}, bf16[128,256]{1,0:T(8,128)(2,1)S(1)}, u32[]{:S(2)}, u32[]{:S(2)}) collective-permute-start(bf16[128,256]{1,0:T(8,128)(2,1)S(1)} %fusion.1), channel_id=1, source_target_pairs={{0,16},{2,18},{4,20},{6,22},{8,24},{10,26},{12,28},{14,30},{16,0},... | collective-permute-start | bytes 196616 | tf_op jit(solution)/shard_map/ppermute | solution.py:27
  44.1 28.0 %collective-permute-start.16 = (bf16[1,16,16,512]{3,2,1,0:T(8,128)(2,1)S(1)}, bf16[1,16,16,512]{3,2,1,0:T(8,128)(2,1)S(1)}, u32[]{:S(2)}, u32[]{:S(2)}) collective-permute-start(bf16[1,16,16,512]{3,2,1,0:T(8,128)(2,1)S(1)} %bitcast.15), channel_id=1, source_target_pairs={{0,2},{2,0},{4,6},{6,4},{8,10},{10,8},{12,14},{14,12},{16,18},{18,... | collective-permute-start | bytes 786440 | tf_op jit(solution)/shard_map/ppermute | solution.py:27
  52.5 19.7 %collective-permute-start.9 = (bf16[8,16,2560]{2,1,0:T(8,128)(2,1)S(1)}, bf16[8,16,2560]{2,1,0:T(8,128)(2,1)S(1)}, u32[]{:S(2)}, u32[]{:S(2)}) collective-permute-start(bf16[8,16,2560]{2,1,0:T(8,128)(2,1)S(1)} %pad_maximum_fusion), channel_id=1, source_target_pairs={{0,4},{2,6},{4,0},{6,2},{8,12},{10,14},{12,8},{14,10},{16,20},{18,... | collective-permute-start | bytes 1966088 | tf_op jit(solution)/shard_map/ppermute | solution.py:27
  54.1 17.9 %collective-permute-start.4 = (f32[1,128,256]{2,1,0:T(8,128)S(1)}, f32[1,128,256]{2,1,0:T(8,128)S(1)}, u32[]{:S(2)}, u32[]{:S(2)}) collective-permute-start(f32[1,128,256]{2,1,0:T(8,128)S(1)} %add_bitcast_fusion), channel_id=1, source_target_pairs={{0,1},{1,0},{2,3},{3,2},{4,5},{5,4},{6,7},{7,6},{8,9},{9,8},{10,11... | collective-permute-start | bytes 393224 | tf_op jit(solution)/shard_map/ppermute | solution.py:27
  75.9 1.4 %collective-permute-start.18 = (bf16[2,128,256]{2,1,0:T(8,128)(2,1)S(1)}, bf16[2,128,256]{2,1,0:T(8,128)(2,1)S(1)}, u32[]{:S(2)}, u32[]{:S(2)}) collective-permute-start(bf16[2,128,256]{2,1,0:T(8,128)(2,1)S(1)} %ray_space_step.2.refs_0_), channel_id=1, source_target_pairs={{0,2},{2,0},{4,6},{6,4},{8,10},{10,8},{12,14},{14,12},{16,18},{18,... | collective-permute-start | bytes 393224 | tf_op jit(solution)/shard_map/ppermute | solution.py:27
  81.0 4.7 %copy-start.6 = (f32[16,4096]{1,0:T(8,128)S(1)}, f32[16,4096]{1,0:T(8,128)}, u32[]{:S(2)}) copy-start(f32[16,4096]{1,0:T(8,128)} %cw.1) | copy-start | bytes 786436
  81.0 4.6 %copy-start.9 = (f32[4,4096]{1,0:T(4,128)S(1)}, f32[4,4096]{1,0:T(4,128)}, u32[]{:S(2)}) copy-start(f32[4,4096]{1,0:T(4,128)} %fw.1) | copy-start | bytes 196612
  81.0 1.4 %collective-permute-start.19 = (bf16[2,128,256]{2,1,0:T(8,128)(2,1)S(1)}, bf16[2,128,256]{2,1,0:T(8,128)(2,1)S(1)}, u32[]{:S(2)}, u32[]{:S(2)}) collective-permute-start(bf16[2,128,256]{2,1,0:T(8,128)(2,1)S(1)} %ray_space_step.3.refs_2_), channel_id=1, source_target_pairs={{0,2},{2,0},{4,6},{6,4},{8,10},{10,8},{12,14},{14,12},{16,18},{18,... | collective-permute-start | bytes 393224 | tf_op jit(solution)/shard_map/ppermute | solution.py:27
  84.1 1.6 %collective-permute-start.20 = (f32[2,16,2048]{2,1,0:T(8,128)S(1)}, f32[2,16,2048]{2,1,0:T(8,128)S(1)}, u32[]{:S(2)}, u32[]{:S(2)}) collective-permute-start(f32[2,16,2048]{2,1,0:T(8,128)S(1)} %get-tuple-element.13), channel_id=1, source_target_pairs={{0,2},{2,0},{4,6},{6,4},{8,10},{10,8},{12,14},{14,12},{16,18},{18,... | collective-permute-start | bytes 786440 | tf_op jit(solution)/shard_map/ppermute | solution.py:27
  (6 other events, 4.2 us)

commit v3 on v1

v3 whole, which is shorter than its diff:
```python
import functools
import jax
import jax.numpy as jnp
from jax import lax
from jax.experimental import pallas as pl
from jax.experimental.pallas import tpu as pltpu
from jax.sharding import PartitionSpec as P

BLOCK = 128
LANES = 128
PACK = 16
F32 = jnp.float32
BF16 = jnp.bfloat16
PARAMS = pltpu.CompilerParams(vmem_limit_bytes=24 * 1024 * 1024)
VMEM = pl.BlockSpec(memory_space=pltpu.VMEM)
SMEM = pl.BlockSpec(memory_space=pltpu.SMEM)
HBM = pl.BlockSpec(memory_space=pltpu.HBM)
QUICK = pl.CostEstimate(flops=1, bytes_accessed=1, transcendentals=0)


def fetch(source, target, sem):
    copy = pltpu.make_async_copy(source, target, sem)
    copy.start()
    return copy


def in_hbm(*arrays):
    return [pltpu.with_memory_space_constraint(a, pltpu.HBM) for a in arrays]


def scratch_like(*arrays):
    return [pltpu.VMEM(a.shape, a.dtype) for a in arrays]


def shaped(shape, dtype):
    return jax.ShapeDtypeStruct(shape, dtype)


def call(kernel, name, out_shape, in_specs, scratch=()):
    many = isinstance(out_shape, tuple)
    return pl.pallas_call(
        kernel,
        out_shape=out_shape,
        in_specs=in_specs,
        out_specs=(VMEM,) * len(out_shape) if many else VMEM,
        scratch_shapes=list(scratch),
        compiler_params=PARAMS,
        cost_estimate=QUICK,
        name=name,
    )


def swap(value, axis, size, bits):
    return lax.ppermute(value, axis, [(i, i ^ bits) for i in range(size)])


def dot(a, b, dims):
    return lax.dot_general(a, b, (dims, ((), ())), preferred_element_type=F32)


def in_two(value):
    high = value.astype(BF16)
    return high, (value - high.astype(F32)).astype(BF16)


def keep_row(blocks_ref, start, width):
    ids = (lax.broadcasted_iota(jnp.int32, (1, width), 1) + start) // BLOCK
    keep = jnp.ones((1, width), F32)
    for k in range(blocks_ref.shape[1]):
        keep = jnp.where(ids == blocks_ref[0, k], 0.0, keep)
    return keep


def packed_tiles(cells, fz):
    parts = PACK // fz
    return -(-(cells // LANES) // parts)


def hit_depths(axial, hits):
    views, _, det = axial.shape
    tiles = hits.shape[2]
    tile = lax.broadcasted_iota(jnp.int32, (1, det), 1) // (det // tiles)
    result = []
    for v in range(views):
        hit = jnp.zeros((1, det), F32)
        for t in range(tiles):
            hit = jnp.where(tile == t, hits[v, 0, t].astype(F32), hit)
        result.append(axial[v].astype(F32) * hit)
    return result


def prepare_kernel(
    cut,
    fine_rays,
    coarse_rays,
    fine_weight_in,
    coarse_weight_in,
    fine_axial_in,
    coarse_axial_in,
    ray_weight_in,
    blocks,
    hits,
    near,
    rest,
    mine,
    theirs,
    rows,
    fine_weight,
    coarse_weight,
    fine_axial,
    coarse_axial,
    ray_weight,
    sems,
):
    me = lax.axis_index("slab")
    core, across = me % 2, (me // 2) % 2
    fz, cells = fine_weight.shape
    half = cells // 2
    base = pl.multiple_of(core * half, half)
    here = pl.ds(pl.multiple_of(base + across * cut, LANES), cut)
    tail = pl.ds(pl.multiple_of(base + 2 * cut, LANES), half - 2 * cut)
    sources = (
        (fine_axial_in, fine_axial),
        (coarse_axial_in, coarse_axial),
        (ray_weight_in, ray_weight),
        (fine_weight_in, fine_weight),
        (coarse_weight_in, coarse_weight),
        (fine_rays.at[:, here, :], near.at[0]),
        (coarse_rays.at[:, here, :], near.at[1]),
        (fine_rays.at[:, tail, :], rest.at[0]),
        (coarse_rays.at[:, tail, :], rest.at[1]),
    )
    copies = [fetch(a, b, sems.at[i]) for i, (a, b) in enumerate(sources)]
    for copy in copies[:3]:
        copy.wait()

    views, _, det = fine_axial.shape
    total = views * ray_weight.shape[2]
    span = views * det
    own = ray_weight.shape[0]
    coarse_depth = hit_depths(coarse_axial, hits)
    fine_depth = hit_depths(fine_axial, hits)
    for v in range(views):
        rows[:, v * det : (v + 1) * det] = coarse_depth[v].astype(BF16)
    wide = rows.shape[1] - span
    weight = jnp.concatenate([ray_weight[:, v, :] for v in range(views)], axis=1)
    fine_wide = jnp.concatenate(fine_depth, axis=1)
    if wide > total:
        weight = jnp.concatenate([weight, jnp.zeros((own, wide - total), F32)], axis=1)
    if wide > span:
        fine_wide = jnp.concatenate([fine_wide, jnp.zeros((fz, wide - span), F32)], axis=1)
    stack = [weight, fine_wide]
    if own + fz < PACK:
        stack.append(jnp.zeros((PACK - own - fz, wide), F32))
    rows[:, span:] = jnp.concatenate(stack, axis=0).astype(BF16)

    for copy in copies[3:5]:
        copy.wait()
    parts = PACK // fz
    empty = jnp.zeros((1, LANES), F32)
    for target, side in ((mine, core), (theirs, 1 - core)):
        column = 0
        begin = pl.multiple_of(side * half, half)
        for first, size in ((0, 2 * cut), (2 * cut, half - 2 * cut)):
            start = pl.multiple_of(begin + first, LANES)
            keep = keep_row(blocks, start, size)
            target[:, column : column + size] = (
                coarse_weight[:, pl.ds(start, size)] * keep
            ).astype(BF16)
            column += size
            fine = fine_weight[:, pl.ds(start, size)]
            for c in range(packed_tiles(size, fz)):
                pieces = []
                for i in range(fz):
                    for k in range(parts):
                        t = c * parts + k
                        inside = t * LANES < size
                        piece = fine[i : i + 1, t * LANES : (t + 1) * LANES] if inside else empty
                        pieces.append(piece)
                target[:, column : column + LANES] = jnp.concatenate(pieces, axis=0).astype(BF16)
                column += LANES
    for copy in copies[5:]:
        copy.wait()


def forward_kernel(
    fine_rays_in,
    coarse_rays_in,
    fine_in,
    coarse_in,
    fine_axial_in,
    coarse_axial_in,
    measured_in,
    blocks,
    hits,
    out,
    own_rays,
    fine_rays,
    coarse_rays,
    fine,
    coarse,
    fine_axial,
    coarse_axial,
    measured,
    sems,
    chunk_sems,
):
    core = lax.axis_index("slab") % 2
    fz, cells = fine.shape
    half = cells // 2
    steps = chunk_sems.shape[0]
    chunk = cells // steps
    copies = []
    for i in range(steps):
        part = pl.ds(i * chunk, chunk)
        copies.append(
            [
                fetch(fine_in.at[:, part], fine.at[:, part], chunk_sems.at[i, 0]),
                fetch(coarse_in.at[:, part], coarse.at[:, part], chunk_sems.at[i, 1]),
                fetch(fine_rays_in.at[:, part, :], fine_rays.at[:, part, :], chunk_sems.at[i, 2]),
                fetch(
                    coarse_rays_in.at[:, part, :], coarse_rays.at[:, part, :], chunk_sems.at[i, 3]
                ),
            ]
        )
    others = [
        fetch(fine_axial_in, fine_axial, sems.at[0]),
        fetch(coarse_axial_in, coarse_axial, sems.at[1]),
        fetch(measured_in, measured, sems.at[2]),
    ]
    views, _, columns = fine_rays.shape
    total = views * columns
    fine_sum = coarse_sum = None
    for i in range(steps):
        part = slice(i * chunk, (i + 1) * chunk)
        for copy in copies[i]:
            copy.wait()
        keep = keep_row(blocks, i * chunk, chunk)
        fine_rows = fine[:, part].astype(BF16)
        coarse_rows = (coarse[:, part] * keep).astype(BF16)
        fine_wide = jnp.concatenate([fine_rays[v, part, :] for v in range(views)], axis=1)
        coarse_wide = jnp.concatenate([coarse_rays[v, part, :] for v in range(views)], axis=1)
        fine_part = dot(fine_rows, fine_wide, ((1,), (0,)))
        coarse_part = dot(coarse_rows, coarse_wide, ((1,), (0,)))
        fine_sum = fine_part if fine_sum is None else fine_sum + fine_part
        coarse_sum = coarse_part if coarse_sum is None else coarse_sum + coarse_part
    held = pl.ds(pl.multiple_of(core * half, half), half)
    outgoing = [
        fetch(fine_rays.at[:, held, :], own_rays.at[0], sems.at[3]),
        fetch(coarse_rays.at[:, held, :], own_rays.at[1], sems.at[4]),
    ]
    for copy in others:
        copy.wait()
    coarse_depth = hit_depths(coarse_axial, hits)
    fine_depth = hit_depths(fine_axial, hits)
    own = measured.shape[0]
    det = out.shape[0]
    pad = jnp.zeros((PACK - fz, total), F32)
    moment = jnp.concatenate([coarse_sum, fine_sum, pad], axis=0).astype(BF16)
    pad = jnp.zeros((PACK - fz, det), F32)
    row = lax.broadcasted_iota(jnp.int32, (det, columns), 0) - lax.axis_index("slab") * own
    for v in range(views):
        depth = jnp.concatenate([coarse_depth[v], fine_depth[v], pad], axis=0).astype(BF16)
        where = slice(v * columns, (v + 1) * columns)
        projection = dot(depth, moment[:, where], ((0,), (0,)))
        given = jnp.zeros((det, columns), F32)
        for i in range(own):
            given = jnp.where(row == i, measured[i : i + 1, v, :], given)
        out[:, where] = given - projection
    for copy in outgoing:
        copy.wait()


def slab_of(block, bits):
    me = lax.axis_index("slab")
    apart = jnp.zeros_like(block)
    for place, bit in enumerate(bits):
        apart = apart + ((block >> (place + 1)) & 1) * bit
    return ((me - me % 2) ^ apart) + (block & 1)


def rows_kernel(own, fz, total, bits, rows, coarse_out, fine_out, coarse_turned, fine_turned, out):
    core = lax.axis_index("slab") % 2
    _, half_groups, slabs, _, width = rows.shape
    groups = 2 * half_groups
    span = width // 2
    det = out.shape[1]
    count = slabs * PACK
    shape = (slabs * own, count)
    w = lax.broadcasted_iota(jnp.int32, shape, 0)
    column = lax.broadcasted_iota(jnp.int32, shape, 1)
    block, row = column // PACK, column % PACK
    match = (row < own) & (w == slab_of(block, bits) * own + row)
    to_weight = jnp.where(match, 1.0, 0.0).astype(BF16)
    shape = (slabs * fz, count)
    z = lax.broadcasted_iota(jnp.int32, shape, 0)
    column = lax.broadcasted_iota(jnp.int32, shape, 1)
    to_fine = jnp.where(column == (z // fz) * PACK + own + z % fz, 1.0, 0.0).astype(BF16)
    for g in range(groups):
        one = rows[(g // half_groups) ^ core, g % half_groups]
        coarse = one[:, :, :span].reshape(count, span)
        side = one[:, :, span:].reshape(count, span)
        fine = dot(to_fine, side, ((1,), (0,)))
        coarse_out[g] = coarse
        fine_out[g] = fine.astype(BF16)
        wide = coarse.astype(F32)
        for v in range(span // det):
            where = slice(v * det, (v + 1) * det)
            coarse_turned[g, v] = wide[:, where].T.astype(BF16)
            fine_turned[g, v] = fine[:, where].T.astype(BF16)
        out[g] = dot(to_weight, side, ((1,), (0,)))[:, :total]


def weights_kernel(fz, cut, order, first, second, fine_out):
    slabs = first.shape[0]
    count = slabs * PACK
    parts = PACK // fz
    shape = (slabs * fz, count)
    z = lax.broadcasted_iota(jnp.int32, shape, 0)
    column = lax.broadcasted_iota(jnp.int32, shape, 1)
    where = z // fz
    moved = jnp.zeros_like(where)
    for j, k in enumerate(order):
        moved = jnp.where(where == j, k, moved)
    done = 0
    half = fine_out.shape[1]
    for source, block, size in ((first, where, 2 * cut), (second, moved, half - 2 * cut)):
        tiles = packed_tiles(size, fz)
        packed = source[:, :, size : size + tiles * LANES].reshape(count, tiles * LANES)
        for k in range(parts):
            choose = column == block * PACK + (z % fz) * parts + k
            chosen = dot(jnp.where(choose, 1.0, 0.0).astype(BF16), packed, ((1,), (0,)))
            for c in range(tiles):
                t = c * parts + k
                if t * LANES < size:
                    fine_out[:, done + t * LANES : done + (t + 1) * LANES] = chosen[
                        :, c * LANES : (c + 1) * LANES
                    ].astype(BF16)
        done += size


def residuals(q, deltas, weights):
    groups = q.shape[0]
    current = [q[g] for g in range(groups)]
    results = [[weights[g] * current[g] for g in range(groups)]]
    for mine, theirs in deltas:
        current = [
            current[g] - (mine[g].astype(F32) + theirs[g].astype(F32)) for g in range(groups)
        ]
        results.append([weights[g] * current[g] for g in range(groups)])
    return results


def spread(depth, residual, views):
    det, columns = residual.shape[0], residual.shape[1] // views
    pieces = [
        dot(
            depth[:, v * det : (v + 1) * det],
            residual[:, v * columns : (v + 1) * columns],
            ((1,), (0,)),
        )
        for v in range(views)
    ]
    return jnp.concatenate(pieces, axis=1)


def spread_kernel(views, q, weights, fine_depth, coarse_depth, fine_out, coarse_out):
    for g in range(q.shape[0]):
        residual = (weights[g] * q[g]).astype(BF16)
        fine_out[g] = spread(fine_depth[g], residual, views).astype(BF16)
        coarse_out[g] = spread(coarse_depth[g], residual, views).astype(BF16)


def segments(cut, half, groups, own_rays, near, far, rest):
    across = (lax.axis_index("slab") // 2) % 2
    views = own_rays.shape[1]

    def reader(start, size, others):
        def read(part, g):
            if g == 0:
                pieces = [own_rays[part, v, pl.ds(start, size), :] for v in range(views)]
            else:
                pieces = [others[g - 1][part, v] for v in range(views)]
            return jnp.concatenate(pieces, axis=1)

        return read

    here = pl.multiple_of(across * cut, LANES)
    there = pl.multiple_of((1 - across) * cut, LANES)
    last = half - 2 * cut
    return (
        (here, cut, reader(here, cut, near)),
        (there, cut, reader(there, cut, far)),
        (2 * cut, last, reader(2 * cut, last, rest)),
    )


def step_kernel(cut, order, groups, views, ready, *refs):
    refs = list(refs)
    if ready:
        spreads = [refs.pop(0), refs.pop(0)]
    else:
        q, mine, theirs, weights, fine_depth, coarse_depth = refs[:6]
        refs = refs[6:]
        residual = residuals(q, [(mine, theirs)], weights)[-1]
        residual = [r.astype(BF16) for r in residual]
        spreads = [
            [spread(depth[g], residual[g], views).astype(BF16) for g in range(groups)]
            for depth in (fine_depth, coarse_depth)
        ]
    turned = refs[:2]
    first, second, fine_weights, own_rays = refs[2:6]
    out = refs[-1]
    others = refs[6:-1]
    n = groups - 1
    near, far, rest = others[:n], others[n : 2 * n], others[2 * n :]
    slabs = first.shape[0]
    count = slabs * PACK
    half = own_rays.shape[2]
    columns = own_rays.shape[3]
    runs = segments(cut, half, groups, own_rays, near, far, rest)
    results = [None] * groups
    for part in range(2):
        moments = [None] * groups
        for index, (start, size, read) in enumerate(runs):
            if part == 0:
                weight = fine_weights[:, pl.ds(start, size)]
            elif index < 2:
                weight = first[:, :, pl.ds(start, size)].reshape(count, size)
            else:
                weight = jnp.concatenate([second[k, :, :size] for k in order], axis=0)
            rays = [read(part, g) for g in range(groups)]
            back = dot(spreads[part][0], rays[0], ((1,), (1,)))
            for g in range(1, groups):
                back = back + dot(spreads[part][g], rays[g], ((1,), (1,)))
            change = (weight.astype(F32) * back).astype(BF16)
            for g in range(groups):
                moment = dot(change, rays[g], ((1,), (0,)))
                moments[g] = moment if moments[g] is None else moments[g] + moment
        for g in range(groups):
            moment = moments[g].astype(BF16)
            pieces = [
                dot(turned[part][g, v], moment[:, v * columns : (v + 1) * columns], ((1,), (0,)))
                for v in range(views)
            ]
            value = jnp.concatenate(pieces, axis=1)
            results[g] = value if results[g] is None else results[g] + value
    for g in range(groups):
        out[g] = results[g].astype(BF16)


def tail_kernel(cut, groups, views, q, *refs):
    deltas = [(refs[0], refs[1]), (refs[2], refs[3])]
    weights, fine_depth, coarse_depth, own_rays = refs[4:8]
    mine, theirs = refs[-2:]
    others = refs[8:-2]
    n = groups - 1
    near, far, rest = others[:n], others[n : 2 * n], others[2 * n :]
    core = lax.axis_index("slab") % 2
    half = own_rays.shape[2]
    fz = mine.shape[0] - PACK
    history = residuals(q, deltas, weights)
    spreads = ([], [])
    for g in range(groups):
        value = history[0][g]
        for other in history[1:]:
            value = value + other[g]
        high, low = in_two(value)
        for part, depth in ((0, fine_depth[g, : 2 * fz]), (1, coarse_depth[g, : 2 * PACK])):
            pair = in_two(spread(depth, high, views) + spread(depth, low, views))
            spreads[part].append(jnp.concatenate(pair, axis=0))
    for part, size in ((0, fz), (1, PACK)):
        place = slice(PACK, PACK + fz) if part == 0 else slice(0, PACK)
        for start, width, read in segments(cut, half, groups, own_rays, near, far, rest):
            back = None
            for g in range(groups):
                value = dot(spreads[part][g], read(part, g), ((1,), (1,)))
                back = value if back is None else back + value
            back = back[: 2 * size] + back[2 * size :]
            lower, upper = back[:size], back[size:]
            where = pl.ds(start, width)
            mine[place, where] = jnp.where(core == 0, lower, upper)
            theirs[place, where] = jnp.where(core == 0, upper, lower)


def final_kernel(mine, received, fine, coarse, fw, cw, blocks, fine_out, coarse_out):
    core = lax.axis_index("slab") % 2
    half = mine.shape[1]
    for source, side in ((mine, core), (received, 1 - core)):
        start = pl.multiple_of(side * half, half)
        where = pl.ds(start, half)
        keep = keep_row(blocks, start, half)
        fine_out[:, where] = fine[:, where] + fw[:, where] * source[PACK:, :]
        coarse_out[:, where] = (coarse[:, where] + cw[:, where] * source[:PACK, :]) * keep


def make_body(slabs, groups):
    far_bits = [1 << k for k in range(slabs.bit_length() - 2, 1, -1)]
    view_bits = [1 << k for k in range(groups.bit_length() - 1)]

    def along_slab(value, bit):
        return swap(value, "slab", slabs, bit)

    def body(
        fine_volume,
        coarse_volume,
        fine_rays,
        coarse_rays,
        fine_axial,
        coarse_axial,
        measured,
        ray_weight,
        fine_cell_weight,
        coarse_cell_weight,
        margin_blocks,
        ray_hits,
    ):
        views, cells, columns = fine_rays.shape
        det = fine_axial.shape[2]
        fz, cz = fine_volume.shape[0], coarse_volume.shape[0]
        own = measured.shape[0]
        total = views * columns
        span = max(views * det, total)
        half = cells // 2
        cut = half * 5 // 16 // LANES * LANES
        last = half - 2 * cut
        core = lax.axis_index("slab") % 2
        lead = core == 0
        width = 2 * cut + packed_tiles(2 * cut, fz) * LANES
        width_two = last + packed_tiles(last, fz) * LANES

        small = in_hbm(
            fine_cell_weight, coarse_cell_weight, fine_axial, coarse_axial, ray_weight
        )
        near, rest, mine, theirs, rows = call(
            functools.partial(prepare_kernel, cut),
            "prepare",
            (
                shaped((2, views, cut, columns), BF16),
                shaped((2, views, last, columns), BF16),
                shaped((PACK, width + width_two), BF16),
                shaped((PACK, width + width_two), BF16),
                shaped((PACK, views * det + span), BF16),
            ),
            [HBM] * 7 + [SMEM] * 2,
            scratch_like(*small) + [pltpu.SemaphoreType.DMA((9,))],
        )(*in_hbm(fine_rays, coarse_rays), *small, *in_hbm(margin_blocks, ray_hits))

        near_list, rest_list, row_list = [near], [rest], [rows]
        for bit in view_bits:
            for held in (near_list, rest_list, row_list):
                held += [swap(value, "view", groups, bit) for value in held]
        near_list, rest_list = near_list[1:], rest_list[1:]
        far_list = [along_slab(value, 2) for value in near_list]

        def pair(a, b):
            return jnp.where(lead, jnp.stack([a, b]), jnp.stack([b, a]))

        both = pair(mine, along_slab(theirs, 1))
        first, second = both[:, :, :width], both[:, :, width:]
        half_groups = groups // 2
        low, high = jnp.stack(row_list[:half_groups]), jnp.stack(row_list[half_groups:])
        kept = jnp.where(lead, low, high)
        given = along_slab(jnp.where(lead, high, low), 1)
        shares = pair(kept, given)
        shares = shares.transpose(0, 2, 1, 3).reshape(2, PACK, -1)
        first = jnp.concatenate([first, shares], axis=2)
        second = jnp.concatenate([second, along_slab(second, 2)])
        for bit in far_bits:
            first = jnp.concatenate([first, along_slab(first, bit)])
            second = jnp.concatenate([second, along_slab(second, bit)])
        first = jnp.concatenate([first, along_slab(first, 2)])
        shares = first[:, :, width:]
        shares = jnp.stack([shares, along_slab(shares, 1)])
        shares = shares.reshape(2, slabs, PACK, half_groups, -1).transpose(0, 3, 1, 2, 4)
        count = len(far_bits)
        order = tuple(
            (j & 1) + 2 * (j >> (count + 1)) + 4 * ((j >> 1) & ((1 << count) - 1))
            for j in range(slabs)
        )

        coarse_depth, fine_depth, coarse_turned, fine_turned, weights = call(
            functools.partial(rows_kernel, own, fz, total, far_bits + [2]),
            "unpack_rows",
            (
                shaped((groups, slabs * PACK, span), BF16),
                shaped((groups, slabs * fz, span), BF16),
                shaped((groups, views, det, slabs * PACK), BF16),
                shaped((groups, views, det, slabs * fz), BF16),
                shaped((groups, det, total), F32),
            ),
            [VMEM],
        )(shares)
        fine_weights = call(
            functools.partial(weights_kernel, fz, cut, order),
            "unpack_weights",
            shaped((slabs * fz, half), BF16),
            [VMEM] * 2,
        )(first, second)

        taken = in_hbm(
            fine_rays,
            coarse_rays,
            fine_volume,
            coarse_volume,
            fine_axial,
            coarse_axial,
            measured,
        )
        q, own_rays = call(
            forward_kernel,
            "forward",
            (shaped((det, total), F32), shaped((2, views, half, columns), BF16)),
            [HBM] * 7 + [SMEM] * 2,
            scratch_like(*taken)
            + [pltpu.SemaphoreType.DMA((5,)), pltpu.SemaphoreType.DMA((4, 4))],
        )(*taken, *in_hbm(margin_blocks, ray_hits))
        for bit in [1, 2] + far_bits:
            q = q + along_slab(q.astype(BF16), bit).astype(F32)
        q = q[None]
        for bit in view_bits:
            q = jnp.concatenate([q, swap(q, "view", groups, bit)])

        spreads = call(
            functools.partial(spread_kernel, views),
            "spread",
            (
                shaped((groups, slabs * fz, total), BF16),
                shaped((groups, slabs * PACK, total), BF16),
            ),
            [VMEM] * 4,
        )(q, weights, fine_depth, coarse_depth)
        others = near_list + far_list + rest_list
        held = (fine_turned, coarse_turned, first, second, fine_weights, own_rays, *others)
        deltas = []
        for ready, inputs in ((True, spreads), (False, None)):
            if not ready:
                inputs = (q, *deltas, weights, fine_depth, coarse_depth)
            delta = call(
                functools.partial(step_kernel, cut, order, groups, views, ready),
                "ray_space_step",
                shaped((groups, det, total), BF16),
                [VMEM] * (len(inputs) + len(held)),
            )(*inputs, *held)
            deltas += [delta, along_slab(delta, 1)]
        result = shaped((PACK + fz, half), F32)
        inputs = (q, *deltas, weights, fine_depth, coarse_depth, own_rays, *others)
        ours, theirs = call(
            functools.partial(tail_kernel, cut, groups, views),
            "back_projection",
            (result, result),
            [VMEM] * len(inputs),
        )(*inputs)
        received = along_slab(theirs, 1)
        return call(
            final_kernel,
            "update",
            (shaped(fine_volume.shape, F32), shaped(coarse_volume.shape, F32)),
            [VMEM] * 6 + [SMEM],
        )(
            ours,
            received,
            fine_volume,
            coarse_volume,
            fine_cell_weight,
            coarse_cell_weight,
            margin_blocks,
        )

    return body


def solution(mesh):
    return jax.shard_map(
        make_body(mesh.shape["slab"], mesh.shape["view"]),
        mesh=mesh,
        in_specs=(
            P("slab", None),
            P("slab", None),
            P("view", None, None),
            P("view", None, None),
            P("view", "slab", None),
            P("view", "slab", None),
            P("slab", "view", None),
            P("slab", "view", None),
            P("slab", None),
            P("slab", None),
            P("slab", None),
            P("view", "slab", None),
        ),
        out_specs=(P("slab", None), P("slab", None)),
        check_vma=False,
    )
```

time: 114 us -> 71.7 us (0.63)
  waiting for transfers between devices: 60.6 us -> 30.5 us
  matrix products: 22.5 us -> 0 us
  Pallas kernels: 0 us -> 16 us
  other arithmetic: 9.79 us -> 0.53 us
  starting transfers between devices: 17 us -> 23.4 us
  local copies, waits for them, and re-layouts: 2.02 us -> 0.1 us
    ppermute x19 -> x21, waiting for transfers between devices: 60.6 us -> 30.5 us  [swap(): return lax.ppermute(value, axis, [(i, i ^ bits) for i in range(size)])]
    dot_general x12 -> x0, matrix products: 22.5 us -> none  [the longest x3 7.6 us: body(): jnp.einsum('vzu,vxu->zx', fine_spread, fine_rays, preferred_element_type=...]
    pallas_call x0 -> x9, Pallas kernels: none -> 16 us  [the longest x2 6.12 us: body(): call(functools.partial(step_kernel, cut, order, groups, views, ready), 'r...]
    ppermute x19 -> x21, starting transfers between devices: 17 us -> 23.4 us  [swap(): return lax.ppermute(value, axis, [(i, i ^ bits) for i in range(size)])]
    add x10 -> x0, other arithmetic: 3.41 us -> none  [the longest x9 1.87 us: pair_sum(): value = value + swap(value, axis, size, bit)]
    convert_element_type x7 -> x4, other arithmetic: 3.3 us -> 0.09 us  [body(): q = q + along_slab(q.astype(BF16), bit).astype(F32)]
  transfers between devices with their start and end apart: 19 -> 21, of which waited for: 16 -> 14; matrix products, arithmetic and copies ran while one was open for 5% -> 1% of each run, Pallas kernels for 0% -> 7%
where the time goes in v3:
time: 71.7 us; the launch traced here: 71.4 us
  waiting for transfers between devices  30.5 us (43%)
  starting transfers between devices  23.4 us (33%)
  Pallas kernels  16 us (22%)
  between operations  0.87 us (1%)
    ppermute x21, waiting for transfers between devices, swap(): return lax.ppermute(value, axis, [(i, i ^ bits) for i in range(size)])  30.5 us
    ppermute x21, starting transfers between devices, swap(): return lax.ppermute(value, axis, [(i, i ^ bits) for i in range(size)])  23.4 us
    pallas_call x2, Pallas kernels, body(): call(functools.partial(step_kernel, cut, order, groups, views, ready), 'r...  6.12 us
    pallas_call x1, Pallas kernels, body(): call(forward_kernel, 'forward', (shaped((det, total), F32), shaped((2, vi...  3.8 us
    pallas_call x1, Pallas kernels, body(): call(functools.partial(prepare_kernel, cut), 'prepare', (shaped((2, views...  2.26 us
    pallas_call x1, Pallas kernels, body(): call(final_kernel, 'update', (shaped(fine_volume.shape, F32), shaped(coar...  1.46 us
    pallas_call x1, Pallas kernels, body(): call(functools.partial(tail_kernel, cut, groups, views), 'back_projection...  1.45 us
  transfers between devices with their start and end apart: 21, of which 14 were waited for; matrix products, arithmetic and copies ran while one was open for 1% of the time, Pallas kernels for 7%

profile of v3, /device:TPU:0, one launch (start us, length us, event | category | flops | bytes accessed | tf_op | source)
XLA Modules:
  0.0 71.4 jit_solution(11567792732678954001)
XLA Ops:
  0.6 2.3 %prepare.1 = (bf16[2,2,640,128]{3,2,1,0:T(8,128)(2,1)S(1)}, bf16[2,2,768,128]{3,2,1,0:T(8,128)(2,1)S(1)}, bf16[16,2688]{1,0:T(8,128)(2,1)S(1)}, bf16[16,2688]{1,0:T(8,128)(2,1)S(1)}, bf16[16,512]{1,0:T(8,128)(2,1)S(1)}) custom-call(bf16[2,4096,128]{2,1,0:T(8,128)(2,1)} %fine_rays.1, bf16[2,4096,128]{2,1,0:T(8,128)(2,1)} %coarse_rays.1, f32[4,4096]{1,0:T(4,128)} %fw.1, ...), custom_call_target="tpu_custom_call" | custom-call | flops 1 | bytes 1 | tf_op jit(solution)/shard_map/prepare/pallas_call | solution.py:535
  2.9 3.0 %collective-permute-start.6 = (bf16[16,512]{1,0:T(8,128)(2,1)S(1)}, bf16[16,512]{1,0:T(8,128)(2,1)S(1)}, u32[]{:S(2)}, u32[]{:S(2)}) collective-permute-start(bf16[16,512]{1,0:T(8,128)(2,1)S(1)} %get-tuple-element.21), channel_id=1, source_target_pairs={{0,1},{1,0},{2,3},{3,2},{4,5},{5,4},{6,7},{7,6},{8,9},{9,8},{10,11... | collective-permute-start | bytes 49160 | tf_op jit(solution)/shard_map/ppermute | solution.py:54
  5.9 1.7 %collective-permute-done.6 = bf16[16,512]{1,0:T(8,128)(2,1)S(1)} collective-permute-done((bf16[16,512]{1,0:T(8,128)(2,1)S(1)}, bf16[16,512]{1,0:T(8,128)(2,1)S(1)}, u32[]{:S(2)}, u32[]{:S(2)}) %collective-permute-start.6) | collective-permute-done | bytes 16416 | tf_op jit(solution)/shard_map/ppermute | solution.py:54
  7.7 0.5 collective-permute-start.5
  8.2 0.7 collective-permute-done.7
  9.2 3.2 %collective-permute-start.8 = (bf16[2,16,2176]{2,1,0:T(8,128)(2,1)S(1)}, bf16[2,16,2176]{2,1,0:T(8,128)(2,1)S(1)}, u32[]{:S(2)}, u32[]{:S(2)}) collective-permute-start(bf16[2,16,2176]{2,1,0:T(8,128)(2,1)S(1)} %pad_maximum_fusion.6), channel_id=1, source_target_pairs={{0,16},{2,18},{4,20},{6,22},{8,24},{10,26},{12,28},{14,30},{16,0},... | collective-permute-start | bytes 417800 | tf_op jit(solution)/shard_map/ppermute | solution.py:54
  12.3 3.8 %forward.1 = (f32[128,256]{1,0:T(8,128)S(1)}, bf16[2,2,2048,128]{3,2,1,0:T(8,128)(2,1)S(1)}) custom-call(bf16[2,4096,128]{2,1,0:T(8,128)(2,1)} %fine_rays.1, bf16[2,4096,128]{2,1,0:T(8,128)(2,1)} %coarse_rays.1, f32[4,4096]{1,0:T(4,128)} %fine.1, f32[16,4096]{1,0:T(8,128)} %coarse.1, bf16[2,4,128]{2,1,0:T(4,128)(2,1)} %fine_axial_in.3, ...), custom_call_target="tpu_custom_call" | custom-call | flops 1 | bytes 1 | tf_op jit(solution)/shard_map/forward/pallas_call | solution.py:610
  16.3 3.2 %collective-permute-done.8 = bf16[2,16,2176]{2,1,0:T(8,128)(2,1)S(1)} collective-permute-done((bf16[2,16,2176]{2,1,0:T(8,128)(2,1)S(1)}, bf16[2,16,2176]{2,1,0:T(8,128)(2,1)S(1)}, u32[]{:S(2)}, u32[]{:S(2)}) %collective-permute-start.8) | collective-permute-done | bytes 139296 | tf_op jit(solution)/shard_map/ppermute | solution.py:54
  19.5 0.8 %collective-permute-start.9 = (bf16[4,16,2176]{2,1,0:T(8,128)(2,1)S(1)}, bf16[4,16,2176]{2,1,0:T(8,128)(2,1)S(1)}, u32[]{:S(2)}, u32[]{:S(2)}) collective-permute-start(bf16[4,16,2176]{2,1,0:T(8,128)(2,1)S(1)} %pad_maximum_fusion.3), channel_id=1, source_target_pairs={{0,8},{2,10},{4,12},{6,14},{8,0},{10,2},{12,4},{14,6},{16,24},{18,... | collective-permute-start | bytes 835592 | tf_op jit(solution)/shard_map/ppermute | solution.py:54
  20.3 1.5 %collective-permute-start.15 = (bf16[2,2,640,128]{3,2,1,0:T(8,128)(2,1)S(1)}, bf16[2,2,640,128]{3,2,1,0:T(8,128)(2,1)S(1)}, u32[]{:S(2)}, u32[]{:S(2)}) collective-permute-start(bf16[2,2,640,128]{3,2,1,0:T(8,128)(2,1)S(1)} %get-tuple-element.30), channel_id=1, source_target_pairs={{0,1},{1,0},{2,3},{3,2},{4,5},{5,4},{6,7},{7,6},{8,9},{9,8},{10,11... | collective-permute-start | bytes 1966088 | tf_op jit(solution)/shard_map/ppermute | solution.py:54
  21.9 0.5 collective-permute-start.17
  22.4 1.6 %collective-permute-start.1 = (bf16[128,256]{1,0:T(8,128)(2,1)S(1)}, bf16[128,256]{1,0:T(8,128)(2,1)S(1)}, u32[]{:S(2)}, u32[]{:S(2)}) collective-permute-start(bf16[128,256]{1,0:T(8,128)(2,1)S(1)} %fusion), channel_id=1, source_target_pairs={{0,4},{2,6},{4,0},{6,2},{8,12},{10,14},{12,8},{14,10},{16,20},{18,... | collective-permute-start | bytes 196616 | tf_op jit(solution)/shard_map/ppermute | solution.py:54
  23.9 0.5 collective-permute-start.12
  24.5 3.4 %collective-permute-done.9 = bf16[4,16,2176]{2,1,0:T(8,128)(2,1)S(1)} collective-permute-done((bf16[4,16,2176]{2,1,0:T(8,128)(2,1)S(1)}, bf16[4,16,2176]{2,1,0:T(8,128)(2,1)S(1)}, u32[]{:S(2)}, u32[]{:S(2)}) %collective-permute-start.9) | collective-permute-done | bytes 278560 | tf_op jit(solution)/shard_map/ppermute | solution.py:54
  28.0 1.4 %collective-permute-start.10 = (bf16[8,16,2176]{2,1,0:T(8,128)(2,1)S(1)}, bf16[8,16,2176]{2,1,0:T(8,128)(2,1)S(1)}, u32[]{:S(2)}, u32[]{:S(2)}) collective-permute-start(bf16[8,16,2176]{2,1,0:T(8,128)(2,1)S(1)} %pad_maximum_fusion.1), channel_id=1, source_target_pairs={{0,4},{2,6},{4,0},{6,2},{8,12},{10,14},{12,8},{14,10},{16,20},{18,... | collective-permute-start | bytes 1671176 | tf_op jit(solution)/shard_map/ppermute | solution.py:54
  29.4 2.9 %collective-permute-start.2 = (bf16[128,256]{1,0:T(8,128)(2,1)S(1)}, bf16[128,256]{1,0:T(8,128)(2,1)S(1)}, u32[]{:S(2)}, u32[]{:S(2)}) collective-permute-start(bf16[128,256]{1,0:T(8,128)(2,1)S(1)} %fusion.2), channel_id=1, source_target_pairs={{0,16},{2,18},{4,20},{6,22},{8,24},{10,26},{12,28},{14,30},{16,0},... | collective-permute-start | bytes 196616 | tf_op jit(solution)/shard_map/ppermute | solution.py:54
  32.5 2.2 %collective-permute-done.2 = bf16[128,256]{1,0:T(8,128)(2,1)S(1)} collective-permute-done((bf16[128,256]{1,0:T(8,128)(2,1)S(1)}, bf16[128,256]{1,0:T(8,128)(2,1)S(1)}, u32[]{:S(2)}, u32[]{:S(2)}) %collective-permute-start.2) | collective-permute-done | bytes 65568 | tf_op jit(solution)/shard_map/ppermute | solution.py:54
  34.7 4.2 %collective-permute-start.3 = (bf16[128,256]{1,0:T(8,128)(2,1)S(1)}, bf16[128,256]{1,0:T(8,128)(2,1)S(1)}, u32[]{:S(2)}, u32[]{:S(2)}) collective-permute-start(bf16[128,256]{1,0:T(8,128)(2,1)S(1)} %fusion.1), channel_id=1, source_target_pairs={{0,8},{2,10},{4,12},{6,14},{8,0},{10,2},{12,4},{14,6},{16,24},{18,... | collective-permute-start | bytes 196616 | tf_op jit(solution)/shard_map/ppermute | solution.py:54
  38.9 2.3 %collective-permute-done.13 = bf16[4,16,1024]{2,1,0:T(8,128)(2,1)S(1)} collective-permute-done((bf16[4,16,1024]{2,1,0:T(8,128)(2,1)S(1)}, bf16[4,16,1024]{2,1,0:T(8,128)(2,1)S(1)}, u32[]{:S(2)}, u32[]{:S(2)}) %collective-permute-start.13) | collective-permute-done | bytes 131104 | tf_op jit(solution)/shard_map/ppermute | solution.py:54
  41.6 0.5 collective-permute-start.16
  42.6 1.6 %collective-permute-start.4 = (f32[1,128,256]{2,1,0:T(8,128)S(1)}, f32[1,128,256]{2,1,0:T(8,128)S(1)}, u32[]{:S(2)}, u32[]{:S(2)}) collective-permute-start(f32[1,128,256]{2,1,0:T(8,128)S(1)} %add_bitcast_fusion), channel_id=1, source_target_pairs={{0,1},{1,0},{2,3},{3,2},{4,5},{5,4},{6,7},{7,6},{8,9},{9,8},{10,11... | collective-permute-start | bytes 393224 | tf_op jit(solution)/shard_map/ppermute | solution.py:54
  44.2 5.1 %collective-permute-done.14 = bf16[8,16,1024]{2,1,0:T(8,128)(2,1)S(1)} collective-permute-done((bf16[8,16,1024]{2,1,0:T(8,128)(2,1)S(1)}, bf16[8,16,1024]{2,1,0:T(8,128)(2,1)S(1)}, u32[]{:S(2)}, u32[]{:S(2)}) %collective-permute-start.14) | collective-permute-done | bytes 262176 | tf_op jit(solution)/shard_map/ppermute | solution.py:54
  49.4 6.9 %collective-permute-done.4 = f32[1,128,256]{2,1,0:T(8,128)S(1)} collective-permute-done((f32[1,128,256]{2,1,0:T(8,128)S(1)}, f32[1,128,256]{2,1,0:T(8,128)S(1)}, u32[]{:S(2)}, u32[]{:S(2)}) %collective-permute-start.4) | collective-permute-done | bytes 131104 | tf_op jit(solution)/shard_map/ppermute | solution.py:54
  56.4 0.3 unpack_weights.1.refs_6_.refs_10_
  57.3 0.6 collective-permute-done.16.refs_9_.refs_13_
  57.9 3.0 %ray_space_step.2.refs_1_.refs_0_ = bf16[2,128,256]{2,1,0:T(8,128)(2,1)S(1)} custom-call(bf16[2,64,256]{2,1,0:T(8,128)(2,1)S(1)} %get-tuple-element.25.refs_0_, bf16[2,256,256]{2,1,0:T(8,128)(2,1)S(1)} %get-tuple-element.26.refs_1_, bf16[2,2,128,64]{3,2,1,0:T(8,128)(2,1)S(1)} %get-tuple-element.27.refs_2_.refs_6_, ...), custom_call_target="tpu_custom_call" | custom-call | flops 1 | bytes 1 | tf_op jit(solution)/shard_map/ray_space_step/pallas_call | solution.py:639
  61.0 1.3 %collective-permute-done.18.refs_2_.refs_1_ = bf16[2,128,256]{2,1,0:T(8,128)(2,1)S(1)} collective-permute-done((bf16[2,128,256]{2,1,0:T(8,128)(2,1)S(1)}, bf16[2,128,256]{2,1,0:T(8,128)(2,1)S(1)}, u32[]{:S(2)}, u32[]{:S(2)}) %collective-permute-start.18) | collective-permute-done | bytes 131104 | tf_op jit(solution)/shard_map/ppermute | solution.py:54
  62.3 3.1 %ray_space_step.3.refs_2_ = bf16[2,128,256]{2,1,0:T(8,128)(2,1)S(1)} custom-call(f32[2,128,256]{2,1,0:T(8,128)S(1)} %pad_maximum_fusion.4.q.refs_0_, bf16[2,128,256]{2,1,0:T(8,128)(2,1)S(1)} %ray_space_step.2.refs_1_.refs_0_, bf16[2,128,256]{2,1,0:T(8,128)(2,1)S(1)} %collective-permute-done.18.refs_2_.refs_1_, ...), custom_call_target="tpu_custom_call" | custom-call | flops 1 | bytes 1 | tf_op jit(solution)/shard_map/ray_space_step/pallas_call | solution.py:639
  65.7 1.2 %collective-permute-done.19.refs_3_ = bf16[2,128,256]{2,1,0:T(8,128)(2,1)S(1)} collective-permute-done((bf16[2,128,256]{2,1,0:T(8,128)(2,1)S(1)}, bf16[2,128,256]{2,1,0:T(8,128)(2,1)S(1)}, u32[]{:S(2)}, u32[]{:S(2)}) %collective-permute-start.19) | collective-permute-done | bytes 131104 | tf_op jit(solution)/shard_map/ppermute | solution.py:54
  66.9 1.5 %back_projection.1 = (f32[20,2048]{1,0:T(8,128)S(1)}, f32[20,2048]{1,0:T(8,128)S(1)}) custom-call(f32[2,128,256]{2,1,0:T(8,128)S(1)} %pad_maximum_fusion.4.q.refs_0_, bf16[2,128,256]{2,1,0:T(8,128)(2,1)S(1)} %ray_space_step.2.refs_1_.refs_0_, bf16[2,128,256]{2,1,0:T(8,128)(2,1)S(1)} %collective-permute-done.18.refs_2_.refs_1_, ...), custom_call_target="tpu_custom_call" | custom-call | flops 1 | bytes 1 | tf_op jit(solution)/shard_map/back_projection/pallas_call | solution.py:648
  68.6 1.3 %collective-permute-done.20.received = f32[20,2048]{1,0:T(8,128)S(1)} collective-permute-done((f32[20,2048]{1,0:T(8,128)S(1)}, f32[20,2048]{1,0:T(8,128)S(1)}, u32[]{:S(2)}, u32[]{:S(2)}) %collective-permute-start.20) | collective-permute-done | bytes 163872 | tf_op jit(solution)/shard_map/ppermute | solution.py:54
  69.9 1.5 %update.1 = (f32[4,4096]{1,0:T(4,128)}, f32[16,4096]{1,0:T(8,128)}) custom-call(f32[20,2048]{1,0:T(8,128)S(1)} %get-tuple-element.32.mine, f32[20,2048]{1,0:T(8,128)S(1)} %collective-permute-done.20.received, f32[4,4096]{1,0:T(4,128)S(1)} %copy-done.2, f32[16,4096]{1,0:T(8,128)S(1)} %copy-done, f32[4,4096]{1,0:T(4,128)S(1)} %copy-done.3, ...), custom_call_target="tpu_custom_call" | custom-call | flops 1 | bytes 1 | tf_op jit(solution)/shard_map/update/pallas_call | solution.py:655
  (49 shorter events, 2.9 us)
Async XLA Ops:
  2.9 4.8 %collective-permute-start.6 = (bf16[16,512]{1,0:T(8,128)(2,1)S(1)}, bf16[16,512]{1,0:T(8,128)(2,1)S(1)}, u32[]{:S(2)}, u32[]{:S(2)}) collective-permute-start(bf16[16,512]{1,0:T(8,128)(2,1)S(1)} %get-tuple-element.21), channel_id=1, source_target_pairs={{0,1},{1,0},{2,3},{3,2},{4,5},{5,4},{6,7},{7,6},{8,9},{9,8},{10,11... | collective-permute-start | bytes 49160 | tf_op jit(solution)/shard_map/ppermute | solution.py:54
  7.7 1.2 %collective-permute-start.7 = (bf16[1,16,512]{2,1,0:T(8,128)(2,1)S(1)}, bf16[1,16,512]{2,1,0:T(8,128)(2,1)S(1)}, u32[]{:S(2)}, u32[]{:S(2)}) collective-permute-start(bf16[1,16,512]{2,1,0:T(8,128)(2,1)S(1)} %get-tuple-element.37), channel_id=1, source_target_pairs={{0,2},{2,0},{4,6},{6,4},{8,10},{10,8},{12,14},{14,12},{16,18},{18,... | collective-permute-start | bytes 49160 | tf_op jit(solution)/shard_map/ppermute | solution.py:54
  7.7 1.4 %collective-permute-start.5 = (bf16[16,2688]{1,0:T(8,128)(2,1)S(1)}, bf16[16,2688]{1,0:T(8,128)(2,1)S(1)}, u32[]{:S(2)}, u32[]{:S(2)}) collective-permute-start(bf16[16,2688]{1,0:T(8,128)(2,1)S(1)} %get-tuple-element.20), channel_id=1, source_target_pairs={{0,2},{2,0},{4,6},{6,4},{8,10},{10,8},{12,14},{14,12},{16,18},{18,... | collective-permute-start | bytes 258056 | tf_op jit(solution)/shard_map/ppermute | solution.py:54
  9.2 10.3 %collective-permute-start.8 = (bf16[2,16,2176]{2,1,0:T(8,128)(2,1)S(1)}, bf16[2,16,2176]{2,1,0:T(8,128)(2,1)S(1)}, u32[]{:S(2)}, u32[]{:S(2)}) collective-permute-start(bf16[2,16,2176]{2,1,0:T(8,128)(2,1)S(1)} %pad_maximum_fusion.6), channel_id=1, source_target_pairs={{0,16},{2,18},{4,20},{6,22},{8,24},{10,26},{12,28},{14,30},{16,0},... | collective-permute-start | bytes 417800 | tf_op jit(solution)/shard_map/ppermute | solution.py:54
  16.1 6.2 %collective-permute-start = (bf16[128,256]{1,0:T(8,128)(2,1)S(1)}, bf16[128,256]{1,0:T(8,128)(2,1)S(1)}, u32[]{:S(2)}, u32[]{:S(2)}) collective-permute-start(bf16[128,256]{1,0:T(8,128)(2,1)S(1)} %convert_element_type.24), channel_id=1, source_target_pairs={{0,2},{2,0},{4,6},{6,4},{8,10},{10,8},{12,14},{14,12},{16,18},{18,... | collective-permute-start | bytes 196616 | tf_op jit(solution)/shard_map/ppermute | solution.py:54
  19.5 8.4 %collective-permute-start.9 = (bf16[4,16,2176]{2,1,0:T(8,128)(2,1)S(1)}, bf16[4,16,2176]{2,1,0:T(8,128)(2,1)S(1)}, u32[]{:S(2)}, u32[]{:S(2)}) collective-permute-start(bf16[4,16,2176]{2,1,0:T(8,128)(2,1)S(1)} %pad_maximum_fusion.3), channel_id=1, source_target_pairs={{0,8},{2,10},{4,12},{6,14},{8,0},{10,2},{12,4},{14,6},{16,24},{18,... | collective-permute-start | bytes 835592 | tf_op jit(solution)/shard_map/ppermute | solution.py:54
  20.3 21.3 %collective-permute-start.15 = (bf16[2,2,640,128]{3,2,1,0:T(8,128)(2,1)S(1)}, bf16[2,2,640,128]{3,2,1,0:T(8,128)(2,1)S(1)}, u32[]{:S(2)}, u32[]{:S(2)}) collective-permute-start(bf16[2,2,640,128]{3,2,1,0:T(8,128)(2,1)S(1)} %get-tuple-element.30), channel_id=1, source_target_pairs={{0,1},{1,0},{2,3},{3,2},{4,5},{5,4},{6,7},{7,6},{8,9},{9,8},{10,11... | collective-permute-start | bytes 1966088 | tf_op jit(solution)/shard_map/ppermute | solution.py:54
  21.9 35.5 %collective-permute-start.17 = (bf16[2,2,768,128]{3,2,1,0:T(8,128)(2,1)S(1)}, bf16[2,2,768,128]{3,2,1,0:T(8,128)(2,1)S(1)}, u32[]{:S(2)}, u32[]{:S(2)}) collective-permute-start(bf16[2,2,768,128]{3,2,1,0:T(8,128)(2,1)S(1)} %get-tuple-element.31), channel_id=1, source_target_pairs={{0,1},{1,0},{2,3},{3,2},{4,5},{5,4},{6,7},{7,6},{8,9},{9,8},{10,11... | collective-permute-start | bytes 2359304 | tf_op jit(solution)/shard_map/ppermute | solution.py:54
  22.4 7.0 %collective-permute-start.1 = (bf16[128,256]{1,0:T(8,128)(2,1)S(1)}, bf16[128,256]{1,0:T(8,128)(2,1)S(1)}, u32[]{:S(2)}, u32[]{:S(2)}) collective-permute-start(bf16[128,256]{1,0:T(8,128)(2,1)S(1)} %fusion), channel_id=1, source_target_pairs={{0,4},{2,6},{4,0},{6,2},{8,12},{10,14},{12,8},{14,10},{16,20},{18,... | collective-permute-start | bytes 196616 | tf_op jit(solution)/shard_map/ppermute | solution.py:54
  23.9 8.3 %collective-permute-start.12 = (bf16[2,16,1024]{2,1,0:T(8,128)(2,1)S(1)}, bf16[2,16,1024]{2,1,0:T(8,128)(2,1)S(1)}, u32[]{:S(2)}, u32[]{:S(2)}) collective-permute-start(bf16[2,16,1024]{2,1,0:T(8,128)(2,1)S(1)} %slice.14), channel_id=1, source_target_pairs={{0,4},{2,6},{4,0},{6,2},{8,12},{10,14},{12,8},{14,10},{16,20},{18,... | collective-permute-start | bytes 196616 | tf_op jit(solution)/shard_map/ppermute | solution.py:54
  28.0 14.2 %collective-permute-start.10 = (bf16[8,16,2176]{2,1,0:T(8,128)(2,1)S(1)}, bf16[8,16,2176]{2,1,0:T(8,128)(2,1)S(1)}, u32[]{:S(2)}, u32[]{:S(2)}) collective-permute-start(bf16[8,16,2176]{2,1,0:T(8,128)(2,1)S(1)} %pad_maximum_fusion.1), channel_id=1, source_target_pairs={{0,4},{2,6},{4,0},{6,2},{8,12},{10,14},{12,8},{14,10},{16,20},{18,... | collective-permute-start | bytes 1671176 | tf_op jit(solution)/shard_map/ppermute | solution.py:54
  29.4 5.3 %collective-permute-start.2 = (bf16[128,256]{1,0:T(8,128)(2,1)S(1)}, bf16[128,256]{1,0:T(8,128)(2,1)S(1)}, u32[]{:S(2)}, u32[]{:S(2)}) collective-permute-start(bf16[128,256]{1,0:T(8,128)(2,1)S(1)} %fusion.2), channel_id=1, source_target_pairs={{0,16},{2,18},{4,20},{6,22},{8,24},{10,26},{12,28},{14,30},{16,0},... | collective-permute-start | bytes 196616 | tf_op jit(solution)/shard_map/ppermute | solution.py:54
  32.3 9.0 %collective-permute-start.13 = (bf16[4,16,1024]{2,1,0:T(8,128)(2,1)S(1)}, bf16[4,16,1024]{2,1,0:T(8,128)(2,1)S(1)}, u32[]{:S(2)}, u32[]{:S(2)}) collective-permute-start(bf16[4,16,1024]{2,1,0:T(8,128)(2,1)S(1)} %pad_maximum_fusion.7), channel_id=1, source_target_pairs={{0,16},{2,18},{4,20},{6,22},{8,24},{10,26},{12,28},{14,30},{16,0},... | collective-permute-start | bytes 393224 | tf_op jit(solution)/shard_map/ppermute | solution.py:54
  34.7 7.9 %collective-permute-start.3 = (bf16[128,256]{1,0:T(8,128)(2,1)S(1)}, bf16[128,256]{1,0:T(8,128)(2,1)S(1)}, u32[]{:S(2)}, u32[]{:S(2)}) collective-permute-start(bf16[128,256]{1,0:T(8,128)(2,1)S(1)} %fusion.1), channel_id=1, source_target_pairs={{0,8},{2,10},{4,12},{6,14},{8,0},{10,2},{12,4},{14,6},{16,24},{18,... | collective-permute-start | bytes 196616 | tf_op jit(solution)/shard_map/ppermute | solution.py:54
  41.3 8.0 %collective-permute-start.14 = (bf16[8,16,1024]{2,1,0:T(8,128)(2,1)S(1)}, bf16[8,16,1024]{2,1,0:T(8,128)(2,1)S(1)}, u32[]{:S(2)}, u32[]{:S(2)}) collective-permute-start(bf16[8,16,1024]{2,1,0:T(8,128)(2,1)S(1)} %pad_maximum_fusion.5), channel_id=1, source_target_pairs={{0,8},{2,10},{4,12},{6,14},{8,0},{10,2},{12,4},{14,6},{16,24},{18,... | collective-permute-start | bytes 786440 | tf_op jit(solution)/shard_map/ppermute | solution.py:54
  41.6 16.3 %collective-permute-start.16 = (bf16[2,2,640,128]{3,2,1,0:T(8,128)(2,1)S(1)}, bf16[2,2,640,128]{3,2,1,0:T(8,128)(2,1)S(1)}, u32[]{:S(2)}, u32[]{:S(2)}) collective-permute-start(bf16[2,2,640,128]{3,2,1,0:T(8,128)(2,1)S(1)} %collective-permute-done.15.refs_8_.refs_12_), channel_id=1, source_target_pairs={{0,4},{2,6},{4,0},{6,2},{8,12},{10,14},{12,8},{14,10},{16,20},{18,... | collective-permute-start | bytes 1966088 | tf_op jit(solution)/shard_map/ppermute | solution.py:54
  42.3 7.1 %collective-permute-start.11 = (bf16[16,16,512]{2,1,0:T(8,128)(2,1)S(1)}, bf16[16,16,512]{2,1,0:T(8,128)(2,1)S(1)}, u32[]{:S(2)}, u32[]{:S(2)}) collective-permute-start(bf16[16,16,512]{2,1,0:T(8,128)(2,1)S(1)} %get-tuple-element.35), channel_id=1, source_target_pairs={{0,2},{2,0},{4,6},{6,4},{8,10},{10,8},{12,14},{14,12},{16,18},{18,... | collective-permute-start | bytes 786440 | tf_op jit(solution)/shard_map/ppermute | solution.py:54
  42.6 13.8 %collective-permute-start.4 = (f32[1,128,256]{2,1,0:T(8,128)S(1)}, f32[1,128,256]{2,1,0:T(8,128)S(1)}, u32[]{:S(2)}, u32[]{:S(2)}) collective-permute-start(f32[1,128,256]{2,1,0:T(8,128)S(1)} %add_bitcast_fusion), channel_id=1, source_target_pairs={{0,1},{1,0},{2,3},{3,2},{4,5},{5,4},{6,7},{7,6},{8,9},{9,8},{10,11... | collective-permute-start | bytes 393224 | tf_op jit(solution)/shard_map/ppermute | solution.py:54
  60.9 1.4 %collective-permute-start.18 = (bf16[2,128,256]{2,1,0:T(8,128)(2,1)S(1)}, bf16[2,128,256]{2,1,0:T(8,128)(2,1)S(1)}, u32[]{:S(2)}, u32[]{:S(2)}) collective-permute-start(bf16[2,128,256]{2,1,0:T(8,128)(2,1)S(1)} %ray_space_step.2.refs_1_.refs_0_), channel_id=1, source_target_pairs={{0,2},{2,0},{4,6},{6,4},{8,10},{10,8},{12,14},{14,12},{16,18},{18,... | collective-permute-start | bytes 393224 | tf_op jit(solution)/shard_map/ppermute | solution.py:54
  65.5 4.4 %copy-start = (f32[16,4096]{1,0:T(8,128)S(1)}, f32[16,4096]{1,0:T(8,128)}, u32[]{:S(2)}) copy-start(f32[16,4096]{1,0:T(8,128)} %coarse.1) | copy-start | bytes 786436
  65.5 4.4 %copy-start.1 = (f32[16,4096]{1,0:T(8,128)S(1)}, f32[16,4096]{1,0:T(8,128)}, u32[]{:S(2)}) copy-start(f32[16,4096]{1,0:T(8,128)} %cw.1) | copy-start | bytes 786436
  65.5 4.4 %copy-start.2 = (f32[4,4096]{1,0:T(4,128)S(1)}, f32[4,4096]{1,0:T(4,128)}, u32[]{:S(2)}) copy-start(f32[4,4096]{1,0:T(4,128)} %fine.1) | copy-start | bytes 196612
  65.5 4.4 %copy-start.3 = (f32[4,4096]{1,0:T(4,128)S(1)}, f32[4,4096]{1,0:T(4,128)}, u32[]{:S(2)}) copy-start(f32[4,4096]{1,0:T(4,128)} %fw.1) | copy-start | bytes 196612
  65.5 4.4 %copy-start.4 = (s32[1,8]{1,0:T(1,128)S(1)}, s32[1,8]{1,0:T(1,128)}, u32[]{:S(2)}) copy-start(s32[1,8]{1,0:T(1,128)} %blocks.5) | copy-start | bytes 100
  65.5 1.4 %collective-permute-start.19 = (bf16[2,128,256]{2,1,0:T(8,128)(2,1)S(1)}, bf16[2,128,256]{2,1,0:T(8,128)(2,1)S(1)}, u32[]{:S(2)}, u32[]{:S(2)}) collective-permute-start(bf16[2,128,256]{2,1,0:T(8,128)(2,1)S(1)} %ray_space_step.3.refs_2_), channel_id=1, source_target_pairs={{0,2},{2,0},{4,6},{6,4},{8,10},{10,8},{12,14},{14,12},{16,18},{18,... | collective-permute-start | bytes 393224 | tf_op jit(solution)/shard_map/ppermute | solution.py:54
  68.4 1.5 %collective-permute-start.20 = (f32[20,2048]{1,0:T(8,128)S(1)}, f32[20,2048]{1,0:T(8,128)S(1)}, u32[]{:S(2)}, u32[]{:S(2)}) collective-permute-start(f32[20,2048]{1,0:T(8,128)S(1)} %get-tuple-element.33), channel_id=1, source_target_pairs={{0,2},{2,0},{4,6},{6,4},{8,10},{10,8},{12,14},{14,12},{16,18},{18,... | collective-permute-start | bytes 491528 | tf_op jit(solution)/shard_map/ppermute | solution.py:54

commit v4 on v3

v4 whole, which is shorter than its diff:
```python
import functools
import jax
import jax.numpy as jnp
from jax import lax
from jax.experimental import pallas as pl
from jax.experimental.pallas import tpu as pltpu
from jax.sharding import PartitionSpec as P

BLOCK = 128
LANES = 128
PACK = 16
F32 = jnp.float32
BF16 = jnp.bfloat16
PARAMS = pltpu.CompilerParams(vmem_limit_bytes=24 * 1024 * 1024)
VMEM = pl.BlockSpec(memory_space=pltpu.VMEM)
SMEM = pl.BlockSpec(memory_space=pltpu.SMEM)
ANY = pl.BlockSpec(memory_space=pl.ANY)
HBM = pl.BlockSpec(memory_space=pltpu.HBM)
SOURCE = {"rays": "start", "weights": "start"}
AWAITED = {"rays": "views"}
QUICK = pl.CostEstimate(flops=1, bytes_accessed=1, transcendentals=0)


def fetch(source, target, sem):
    copy = pltpu.make_async_copy(source, target, sem)
    copy.start()
    return copy


def in_hbm(*arrays):
    return [pltpu.with_memory_space_constraint(a, pltpu.HBM) for a in arrays]


def scratch_like(*arrays):
    return [pltpu.VMEM(a.shape, a.dtype) for a in arrays]


def shaped(shape, dtype):
    return jax.ShapeDtypeStruct(shape, dtype)


def call(kernel, name, out_shape, in_specs, scratch=()):
    many = isinstance(out_shape, tuple)
    return pl.pallas_call(
        kernel,
        out_shape=out_shape,
        in_specs=in_specs,
        out_specs=(VMEM,) * len(out_shape) if many else VMEM,
        scratch_shapes=list(scratch),
        compiler_params=PARAMS,
        cost_estimate=QUICK,
        name=name,
    )


def swap(value, axis, size, bits):
    return lax.ppermute(value, axis, [(i, i ^ bits) for i in range(size)])


def dot(a, b, dims):
    return lax.dot_general(a, b, (dims, ((), ())), preferred_element_type=F32)


def in_two(value):
    high = value.astype(BF16)
    return high, (value - high.astype(F32)).astype(BF16)


def keep_row(blocks_ref, start, width):
    ids = (lax.broadcasted_iota(jnp.int32, (1, width), 1) + start) // BLOCK
    keep = jnp.ones((1, width), F32)
    for k in range(blocks_ref.shape[1]):
        keep = jnp.where(ids == blocks_ref[0, k], 0.0, keep)
    return keep


def share_start(cells, groups, bits=0):
    core = lax.axis_index("slab") % 2
    share = cells // 2 // groups
    return pl.multiple_of(core * (cells // 2) + (lax.axis_index("view") ^ bits) * share, LANES)


def packed_tiles(cells, fz):
    parts = PACK // fz
    return -(-(cells // LANES) // parts)


def hit_depths(axial, hits):
    views, _, det = axial.shape
    tiles = hits.shape[2]
    tile = lax.broadcasted_iota(jnp.int32, (1, det), 1) // (det // tiles)
    result = []
    for v in range(views):
        hit = jnp.zeros((1, det), F32)
        for t in range(tiles):
            hit = jnp.where(tile == t, hits[v, 0, t].astype(F32), hit)
        result.append(axial[v].astype(F32) * hit)
    return result


def take_kernel(groups, bits, fine_rays, coarse_rays, *refs):
    out, sems = refs[-2:]
    cells = pl.ds(share_start(fine_rays.shape[1], groups, bits), out.shape[2])
    copies = [
        fetch(rays.at[:, cells, :], out.at[part], sems.at[part])
        for part, rays in enumerate((fine_rays, coarse_rays))
    ]
    for copy in copies:
        copy.wait()


def pair_kernel(mine, received, *refs):
    out = refs[-1]
    lead = lax.axis_index("slab") % 2 == 0
    own, other = mine[...].astype(F32), received[...].astype(F32)
    out[0] = jnp.where(lead, own, other).astype(BF16)
    out[1] = jnp.where(lead, other, own).astype(BF16)


def join_core_kernel(q, received, rows, *refs):
    total, out = refs[-2:]
    count = q.shape[0]
    value = q[...] + received[...].astype(F32)
    total[...] = value
    out[:count] = value.astype(BF16)
    out[count:] = rows[...]


def join_hop_kernel(last, q, mine, received, *refs):
    total, out = refs[-2:]
    count = q.shape[0]
    value = q[...] + received[:count].astype(F32)
    total[...] = value
    high, low = in_two(value)
    out[:count] = high
    base = count
    if last:
        out[count : 2 * count] = low
        base = 2 * count
    held = mine.shape[0] - count
    out[base : base + held] = mine[count:]
    out[base + held :] = received[count:]


def join_views_kernel(count, *refs):
    q, rows = refs[-2:]
    for g in range(q.shape[0]):
        part = refs[g]
        q[g] = part[:count].astype(F32) + part[count : 2 * count].astype(F32)
        rows[g] = part[2 * count :]


def start_kernel(
    fine_rays_in,
    coarse_rays_in,
    fine_in,
    coarse_in,
    fine_weight_in,
    coarse_weight_in,
    fine_axial_in,
    coarse_axial_in,
    measured_in,
    ray_weight_in,
    blocks,
    hits,
    mine,
    theirs,
    rows,
    out,
    short,
    own_rays,
    fine_rays,
    coarse_rays,
    fine,
    coarse,
    fine_weight,
    coarse_weight,
    fine_axial,
    coarse_axial,
    measured,
    ray_weight,
    scratch,
    sems,
    chunk_sems,
):
    me = lax.axis_index("slab")
    core = me % 2
    fz, cells = fine.shape
    half = cells // 2
    sources = (
        (fine_axial_in, fine_axial),
        (coarse_axial_in, coarse_axial),
        (ray_weight_in, ray_weight),
        (measured_in, measured),
        (fine_weight_in, fine_weight),
        (coarse_weight_in, coarse_weight),
    )
    others = [fetch(a, b, sems.at[i]) for i, (a, b) in enumerate(sources)]
    steps = chunk_sems.shape[0]
    chunk = cells // steps
    copies = []
    for i in range(steps):
        part = pl.ds(i * chunk, chunk)
        copies.append(
            [
                fetch(fine_in.at[:, part], fine.at[:, part], chunk_sems.at[i, 0]),
                fetch(coarse_in.at[:, part], coarse.at[:, part], chunk_sems.at[i, 1]),
                fetch(fine_rays_in.at[:, part, :], fine_rays.at[:, part, :], chunk_sems.at[i, 2]),
                fetch(
                    coarse_rays_in.at[:, part, :], coarse_rays.at[:, part, :], chunk_sems.at[i, 3]
                ),
            ]
        )
    for copy in others:
        copy.wait()

    views, _, det = fine_axial.shape
    columns = ray_weight.shape[2]
    total = views * columns
    span = views * det
    own = ray_weight.shape[0]
    coarse_depth = hit_depths(coarse_axial, hits)
    fine_depth = hit_depths(fine_axial, hits)
    wide = max(span, total)
    weight = jnp.concatenate([ray_weight[:, v, :] for v in range(views)], axis=1)
    fine_wide = jnp.concatenate(fine_depth, axis=1)
    if wide > total:
        weight = jnp.concatenate([weight, jnp.zeros((own, wide - total), F32)], axis=1)
    if wide > span:
        fine_wide = jnp.concatenate([fine_wide, jnp.zeros((fz, wide - span), F32)], axis=1)
    stack = [weight, fine_wide]
    if own + fz < PACK:
        stack.append(jnp.zeros((PACK - own - fz, wide), F32))
    packed = jnp.concatenate(coarse_depth + [jnp.concatenate(stack, axis=0)], axis=1).astype(BF16)
    for p in range((span + wide) // total):
        rows[p * PACK : (p + 1) * PACK] = packed[:, p * total : (p + 1) * total]

    parts = PACK // fz
    empty = jnp.zeros((1, LANES), F32)
    share = own_rays.shape[2]
    groups = half // share
    for target, side in ((mine, core), (theirs, 1 - core)):
        begin = pl.multiple_of(side * half + lax.axis_index("view") * share, LANES)
        keep = keep_row(blocks, begin, share)
        target[:, :share] = (coarse_weight[:, pl.ds(begin, share)] * keep).astype(BF16)
        weight = fine_weight[:, pl.ds(begin, share)]
        for c in range(packed_tiles(share, fz)):
            pieces = []
            for i in range(fz):
                for k in range(parts):
                    t = c * parts + k
                    inside = t * LANES < share
                    piece = weight[i : i + 1, t * LANES : (t + 1) * LANES] if inside else empty
                    pieces.append(piece)
            column = slice(share + c * LANES, share + (c + 1) * LANES)
            target[:, column] = jnp.concatenate(pieces, axis=0).astype(BF16)

    fine_sum = coarse_sum = None
    for i in range(steps):
        part = slice(i * chunk, (i + 1) * chunk)
        for copy in copies[i]:
            copy.wait()
        keep = keep_row(blocks, i * chunk, chunk)
        fine_rows = fine[:, part].astype(BF16)
        coarse_rows = (coarse[:, part] * keep).astype(BF16)
        fine_wide = jnp.concatenate([fine_rays[v, part, :] for v in range(views)], axis=1)
        coarse_wide = jnp.concatenate([coarse_rays[v, part, :] for v in range(views)], axis=1)
        fine_part = dot(fine_rows, fine_wide, ((1,), (0,)))
        coarse_part = dot(coarse_rows, coarse_wide, ((1,), (0,)))
        fine_sum = fine_part if fine_sum is None else fine_sum + fine_part
        coarse_sum = coarse_part if coarse_sum is None else coarse_sum + coarse_part
    held = pl.ds(share_start(cells, groups), share)
    outgoing = [
        fetch(fine_rays.at[:, held, :], own_rays.at[0], sems.at[6]),
        fetch(coarse_rays.at[:, held, :], own_rays.at[1], sems.at[7]),
    ]
    pad = jnp.zeros((PACK - fz, total), F32)
    moment = jnp.concatenate([coarse_sum, fine_sum, pad], axis=0).astype(BF16)
    pad = jnp.zeros((PACK - fz, det), F32)
    row = lax.broadcasted_iota(jnp.int32, (det, columns), 0) - me * own
    for v in range(views):
        depth = jnp.concatenate([coarse_depth[v], fine_depth[v], pad], axis=0).astype(BF16)
        where = slice(v * columns, (v + 1) * columns)
        projection = dot(depth, moment[:, where], ((0,), (0,)))
        given = jnp.zeros((det, columns), F32)
        for i in range(own):
            given = jnp.where(row == i, measured[i : i + 1, v, :], given)
        scratch[:, where] = given - projection
    kept = pl.ds(pl.multiple_of(core * (det // 2), PACK), det // 2)
    sent = pl.ds(pl.multiple_of((1 - core) * (det // 2), PACK), det // 2)
    out[...] = scratch[kept, :]
    short[...] = scratch[sent, :].astype(BF16)
    for copy in outgoing:
        copy.wait()


def slab_of(block, bits):
    me = lax.axis_index("slab")
    apart = jnp.zeros_like(block)
    for place, bit in enumerate(bits):
        apart = apart + ((block >> (place + 1)) & 1) * bit
    return ((me - me % 2) ^ apart) + (block & 1)


def rows_kernel(own, fz, bits, mine, theirs, q_mine, q_theirs, *refs):
    coarse_out, fine_out, coarse_turned, fine_turned, out, q_out = refs
    lead = lax.axis_index("slab") % 2 == 0
    kept = q_mine.shape[1]
    for g in range(q_mine.shape[0]):
        ours, others = q_mine[g], q_theirs[g]
        q_out[g, :kept] = jnp.where(lead, ours, others)
        q_out[g, kept:] = jnp.where(lead, others, ours)
    groups, held, total = mine.shape
    slabs = coarse_out.shape[1] // PACK
    height = 2 * held // slabs
    pieces = height // PACK
    det = out.shape[1]
    count = slabs * PACK
    shape = (slabs * own, count)
    w = lax.broadcasted_iota(jnp.int32, shape, 0)
    column = lax.broadcasted_iota(jnp.int32, shape, 1)
    block, row = column // PACK, column % PACK
    match = (row < own) & (w == slab_of(block, bits) * own + row)
    to_weight = jnp.where(match, 1.0, 0.0).astype(BF16)
    shape = (slabs * fz, count)
    z = lax.broadcasted_iota(jnp.int32, shape, 0)
    column = lax.broadcasted_iota(jnp.int32, shape, 1)
    to_fine = jnp.where(column == (z // fz) * PACK + own + z % fz, 1.0, 0.0).astype(BF16)
    for g in range(groups):
        own_rows, other_rows = mine[g].astype(F32), theirs[g].astype(F32)
        even = jnp.where(lead, own_rows, other_rows).astype(BF16)
        odd = jnp.where(lead, other_rows, own_rows).astype(BF16)
        cuts = []
        for p in range(pieces):
            blocks = [
                (even, odd)[j % 2][(j // 2) * height + p * PACK :][:PACK] for j in range(slabs)
            ]
            cuts.append(jnp.concatenate(blocks, axis=0))
        coarse = jnp.concatenate(cuts[: pieces // 2], axis=1)
        side = jnp.concatenate(cuts[pieces // 2 :], axis=1)
        fine = dot(to_fine, side, ((1,), (0,)))
        coarse_out[g] = coarse
        fine_out[g] = fine.astype(BF16)
        wide = coarse.astype(F32)
        for v in range(coarse.shape[1] // det):
            where = slice(v * det, (v + 1) * det)
            coarse_turned[g, v] = wide[:, where].T.astype(BF16)
            fine_turned[g, v] = fine[:, where].T.astype(BF16)
        out[g] = dot(to_weight, side, ((1,), (0,)))[:, :total]


def weights_kernel(fz, order, mine, received, coarse_out, fine_out):
    held = mine.shape[0]
    slabs = 2 * held
    count = slabs * PACK
    parts = PACK // fz
    size = fine_out.shape[1]
    tiles = packed_tiles(size, fz)
    blocks = [(mine, received)[k // held].at[k % held] for k in order]
    for j, block in enumerate(blocks):
        coarse_out[j * PACK : (j + 1) * PACK] = block[:, :size]
    source = jnp.concatenate([block[:, size : size + tiles * LANES] for block in blocks], axis=0)
    shape = (slabs * fz, count)
    z = lax.broadcasted_iota(jnp.int32, shape, 0)
    column = lax.broadcasted_iota(jnp.int32, shape, 1)
    for k in range(parts):
        choose = jnp.where(column == (z // fz) * PACK + (z % fz) * parts + k, 1.0, 0.0)
        chosen = dot(choose.astype(BF16), source, ((1,), (0,)))
        for c in range(tiles):
            t = c * parts + k
            if t * LANES < size:
                fine_out[:, t * LANES : (t + 1) * LANES] = chosen[
                    :, c * LANES : (c + 1) * LANES
                ].astype(BF16)


def residuals(q, deltas, weights):
    groups = q.shape[0]
    current = [q[g] for g in range(groups)]
    results = [[weights[g] * current[g] for g in range(groups)]]
    for delta in deltas:
        current = [current[g] - delta[g].astype(F32) for g in range(groups)]
        results.append([weights[g] * current[g] for g in range(groups)])
    return results


def spread(depth, residual, views):
    det, columns = residual.shape[0], residual.shape[1] // views
    pieces = [
        dot(
            depth[:, v * det : (v + 1) * det],
            residual[:, v * columns : (v + 1) * columns],
            ((1,), (0,)),
        )
        for v in range(views)
    ]
    return jnp.concatenate(pieces, axis=1)


def spread_kernel(views, q, weights, fine_depth, coarse_depth, fine_out, coarse_out):
    for g in range(q.shape[0]):
        residual = (weights[g] * q[g]).astype(BF16)
        fine_out[g] = spread(fine_depth[g], residual, views).astype(BF16)
        coarse_out[g] = spread(coarse_depth[g], residual, views).astype(BF16)


def group_rays(held, part, g, cut):
    return jnp.concatenate([held[g][part, v, cut, :] for v in range(held[g].shape[1])], axis=1)


def step_kernel(groups, views, ready, *refs):
    refs = list(refs)
    if ready:
        spreads = [refs.pop(0), refs.pop(0)]
    else:
        q, delta, weights, fine_depth, coarse_depth = refs[:5]
        refs = refs[5:]
        residual = residuals(q, [delta], weights)[-1]
        residual = [r.astype(BF16) for r in residual]
        spreads = [
            [spread(depth[g], residual[g], views).astype(BF16) for g in range(groups)]
            for depth in (fine_depth, coarse_depth)
        ]
    turned = refs[:2]
    coarse_weights, fine_weights = refs[2:4]
    held = refs[4:-1]
    out = refs[-1]
    size = fine_weights.shape[1]
    columns = held[0].shape[3]
    chunk = min(size, 512)
    results = [None] * groups
    for part in range(2):
        moments = [None] * groups
        for c in range(size // chunk):
            cut = slice(c * chunk, (c + 1) * chunk)
            if part == 0:
                weight = fine_weights[:, cut]
            else:
                weight = coarse_weights[:, cut]
            rays = [group_rays(held, part, g, cut) for g in range(groups)]
            back = dot(spreads[part][0], rays[0], ((1,), (1,)))
            for g in range(1, groups):
                back = back + dot(spreads[part][g], rays[g], ((1,), (1,)))
            change = (weight.astype(F32) * back).astype(BF16)
            for g in range(groups):
                moment = dot(change, rays[g], ((1,), (0,)))
                moments[g] = moment if moments[g] is None else moments[g] + moment
        for g in range(groups):
            moment = moments[g].astype(BF16)
            pieces = [
                dot(turned[part][g, v], moment[:, v * columns : (v + 1) * columns], ((1,), (0,)))
                for v in range(views)
            ]
            value = jnp.concatenate(pieces, axis=1)
            results[g] = value if results[g] is None else results[g] + value
    for g in range(groups):
        out[g] = results[g].astype(BF16)


def add_kernel(bit, mine, received, out):
    for g in range(mine.shape[0]):
        out[g] = (mine[g].astype(F32) + received[g ^ bit].astype(F32)).astype(BF16)


def tail_kernel(groups, views, q, *refs):
    deltas = refs[:2]
    weights, fine_depth, coarse_depth = refs[2:5]
    held = refs[5:-2]
    fine_out, coarse_out = refs[-2:]
    size = coarse_out.shape[1]
    chunk = min(size, 512)
    history = residuals(q, deltas, weights)
    rows = (fine_out.shape[0], coarse_out.shape[0])
    spreads = ([], [])
    for g in range(groups):
        value = history[0][g]
        for other in history[1:]:
            value = value + other[g]
        high, low = in_two(value)
        for part, depth in enumerate((fine_depth[g, : rows[0]], coarse_depth[g, : rows[1]])):
            pair = in_two(spread(depth, high, views) + spread(depth, low, views))
            spreads[part].append(jnp.concatenate(pair, axis=0))
    for part, out in enumerate((fine_out, coarse_out)):
        for c in range(size // chunk):
            cut = slice(c * chunk, (c + 1) * chunk)
            back = None
            for g in range(groups):
                value = dot(spreads[part][g], group_rays(held, part, g, cut), ((1,), (1,)))
                back = value if back is None else back + value
            out[:, cut] = (back[: rows[part]] + back[rows[part] :]).astype(BF16)


def sort_kernel(groups, *refs):
    pieces, outs = refs[:-4], refs[-4:]
    lead = lax.axis_index("slab") % 2 == 0
    view = lax.axis_index("view")
    for part in range(2):
        mine, theirs = outs[2 * part : 2 * part + 2]
        rows = mine.shape[0]
        size = pieces[part].shape[1]
        for g in range(groups):
            value = pieces[2 * g + part][...].astype(F32)
            lower, upper = value[:rows], value[rows:]
            where = pl.ds(pl.multiple_of((view ^ g) * size, LANES), size)
            mine[:, where] = jnp.where(lead, lower, upper).astype(BF16)
            theirs[:, where] = jnp.where(lead, upper, lower).astype(BF16)


def final_kernel(*refs):
    mine, received = refs[:2], refs[2:4]
    fine, coarse, fw, cw, blocks, fine_out, coarse_out = refs[4:]
    core = lax.axis_index("slab") % 2
    half = mine[0].shape[1]
    for source, side in ((mine, core), (received, 1 - core)):
        start = pl.multiple_of(side * half, half)
        where = pl.ds(start, half)
        keep = keep_row(blocks, start, half)
        fine_out[:, where] = fine[:, where] + fw[:, where] * source[0][...].astype(F32)
        coarse_out[:, where] = (
            coarse[:, where] + cw[:, where] * source[1][...].astype(F32)
        ) * keep


def make_body(slabs, groups):
    far_bits = [1 << k for k in range(slabs.bit_length() - 2, 1, -1)]
    view_bits = [1 << k for k in range(groups.bit_length() - 1)]

    def along_slab(value, bit):
        return swap(value, "slab", slabs, bit)

    def body(
        fine_volume,
        coarse_volume,
        fine_rays,
        coarse_rays,
        fine_axial,
        coarse_axial,
        measured,
        ray_weight,
        fine_cell_weight,
        coarse_cell_weight,
        margin_blocks,
        ray_hits,
    ):
        views, cells, columns = fine_rays.shape
        det = fine_axial.shape[2]
        fz, cz = fine_volume.shape[0], coarse_volume.shape[0]
        own = measured.shape[0]
        total = views * columns
        span = max(views * det, total)
        share = cells // 2 // groups
        lead = lax.axis_index("slab") % 2 == 0
        width = share + packed_tiles(share, fz) * LANES

        taken = in_hbm(
            fine_rays,
            coarse_rays,
            fine_volume,
            coarse_volume,
            fine_cell_weight,
            coarse_cell_weight,
            fine_axial,
            coarse_axial,
            measured,
            ray_weight,
        )
        height = PACK * ((views * det + span) // total)
        mine, theirs, rows, q, short, own_rays = call(
            start_kernel,
            "start",
            (
                shaped((PACK, width), BF16),
                shaped((PACK, width), BF16),
                shaped((height, total), BF16),
                shaped((det // 2, total), F32),
                shaped((det // 2, total), BF16),
                shaped((2, views, share, columns), BF16),
            ),
            [HBM] * len(taken) + [SMEM] * 2,
            scratch_like(*taken)
            + [
                pltpu.VMEM((det, total), F32),
                pltpu.SemaphoreType.DMA((8,)),
                pltpu.SemaphoreType.DMA((4, 4)),
            ],
        )(*taken, *in_hbm(margin_blocks, ray_hits))

        def to_views(value):
            values = [value]
            for bit in view_bits:
                values += [swap(one, "view", groups, bit) for one in values]
            return values

        rows_half = det // 2
        got = {}

        def begin(stage, token):
            waits = [] if token is None else [token]
            if SOURCE["rays"] == stage:
                got["rays"] = []
                for bits in range(1, groups):
                    value = call(
                        functools.partial(take_kernel, groups, bits),
                        "take_rays",
                        shaped((2, views, share, columns), BF16),
                        [HBM] * 2 + [ANY] * len(waits),
                        [pltpu.SemaphoreType.DMA((2,))],
                    )(*in_hbm(fine_rays, coarse_rays), *waits)
                    got["rays"].append(swap(value, "view", groups, bits))
            if SOURCE["weights"] == stage:
                packed = call(
                    pair_kernel,
                    "pair",
                    shaped((2, PACK, width), BF16),
                    [VMEM] * 2 + [ANY] * len(waits),
                )(mine, along_slab(theirs, 1), *waits)
                for index, bit in enumerate(far_bits + [2]):
                    hop = along_slab(packed, bit)
                    got["w%d" % index] = [hop]
                    if bit != 2:
                        packed = jnp.concatenate([packed, hop])
                got["weights"] = (packed, hop)

        def waits_of(stage):
            found = []
            for name, where in AWAITED.items():
                if where == stage:
                    found += got.get(name, [])
            return found

        begin("start", None)
        waits = waits_of("core")
        q, mixed = call(
            join_core_kernel,
            "join_core",
            (shaped((rows_half, total), F32), shaped((rows_half + height, total), BF16)),
            [VMEM] * 3 + [ANY] * len(waits),
        )(q, along_slab(short, 1), rows, *waits)
        begin("core", mixed)
        for index, bit in enumerate([2] + far_bits):
            last = index == len(far_bits)
            name = "last" if last else "hop%d" % index
            waits = waits_of(name)
            size = 2 * mixed.shape[0] - rows_half + (rows_half if last else 0)
            q, mixed = call(
                functools.partial(join_hop_kernel, last),
                "join_hop",
                (shaped(q.shape, F32), shaped((size, total), BF16)),
                [VMEM] * 3 + [ANY] * len(waits),
            )(q, mixed, along_slab(mixed, bit), *waits)
            begin(name, mixed)
        waits = waits_of("views")
        q, rows = call(
            functools.partial(join_views_kernel, rows_half),
            "join_views",
            (
                shaped((groups, rows_half, total), F32),
                shaped((groups, mixed.shape[0] - 2 * rows_half, total), BF16),
            ),
            [VMEM] * groups + [ANY] * len(waits),
        )(*to_views(mixed), *waits)
        count = len(far_bits)
        order = tuple(
            (j & 1) + 2 * (j >> 2) + (((j >> 1) & 1) << (count + 1)) for j in range(slabs)
        )
        coarse_depth, fine_depth, coarse_turned, fine_turned, weights, q = call(
            functools.partial(rows_kernel, own, fz, [2] + far_bits),
            "unpack_rows",
            (
                shaped((groups, slabs * PACK, span), BF16),
                shaped((groups, slabs * fz, span), BF16),
                shaped((groups, views, det, slabs * PACK), BF16),
                shaped((groups, views, det, slabs * fz), BF16),
                shaped((groups, det, total), F32),
                shaped((groups, det, total), F32),
            ),
            [VMEM] * 4,
        )(rows, along_slab(rows, 1), q, along_slab(q, 1))
        coarse_weights, fine_weights = call(
            functools.partial(weights_kernel, fz, order),
            "unpack_weights",
            (shaped((slabs * PACK, share), BF16), shaped((slabs * fz, share), BF16)),
            [VMEM] * 2,
        )(*got["weights"])
        spreads = call(
            functools.partial(spread_kernel, views),
            "spread",
            (
                shaped((groups, slabs * fz, total), BF16),
                shaped((groups, slabs * PACK, total), BF16),
            ),
            [VMEM] * 4,
        )(q, weights, fine_depth, coarse_depth)
        rays = [own_rays] + got["rays"]
        held = (fine_turned, coarse_turned, coarse_weights, fine_weights, *rays)
        def add(mine, received, bit):
            return call(
                functools.partial(add_kernel, bit),
                "add",
                shaped((groups, det, total), BF16),
                [VMEM] * 2,
            )(mine, received)

        deltas = []
        for ready, inputs in ((True, spreads), (False, None)):
            if not ready:
                inputs = (q, *deltas, weights, fine_depth, coarse_depth)
            delta = call(
                functools.partial(step_kernel, groups, views, ready),
                "ray_space_step",
                shaped((groups, det, total), BF16),
                [VMEM] * (len(inputs) + len(held)),
            )(*inputs, *held)
            delta = add(delta, along_slab(delta, 1), 0)
            for bit in view_bits:
                delta = add(delta, swap(delta, "view", groups, bit), bit)
            deltas.append(delta)
        inputs = (q, *deltas, weights, fine_depth, coarse_depth, *rays)
        pieces = call(
            functools.partial(tail_kernel, groups, views),
            "back_projection",
            (shaped((2 * fz, share), BF16), shaped((2 * PACK, share), BF16)),
            [VMEM] * len(inputs),
        )(*inputs)
        pieces = list(pieces)
        for bit in view_bits:
            pieces += [swap(value, "view", groups, bit) for value in pieces]
        fine_ours, fine_theirs, coarse_ours, coarse_theirs = call(
            functools.partial(sort_kernel, groups),
            "sort",
            (shaped((fz, cells // 2), BF16),) * 2 + (shaped((PACK, cells // 2), BF16),) * 2,
            [VMEM] * len(pieces),
        )(*pieces)
        return call(
            final_kernel,
            "update",
            (shaped(fine_volume.shape, F32), shaped(coarse_volume.shape, F32)),
            [VMEM] * 8 + [SMEM],
        )(
            fine_ours,
            coarse_ours,
            along_slab(fine_theirs, 1),
            along_slab(coarse_theirs, 1),
            fine_volume,
            coarse_volume,
            fine_cell_weight,
            coarse_cell_weight,
            margin_blocks,
        )

    return body


def solution(mesh):
    return jax.shard_map(
        make_body(mesh.shape["slab"], mesh.shape["view"]),
        mesh=mesh,
        in_specs=(
            P("slab", None),
            P("slab", None),
            P("view", None, None),
            P("view", None, None),
            P("view", "slab", None),
            P("view", "slab", None),
            P("slab", "view", None),
            P("slab", "view", None),
            P("slab", None),
            P("slab", None),
            P("slab", None),
            P("view", "slab", None),
        ),
        out_specs=(P("slab", None), P("slab", None)),
        check_vma=False,
    )
```

time: 71.7 us -> 64.2 us (0.90)
  starting transfers between devices: 23.4 us -> 19.5 us
  Pallas kernels: 16 us -> 13.2 us
    ppermute x21 -> x20, starting transfers between devices: 23.4 us -> 19.5 us  [swap(): return lax.ppermute(value, axis, [(i, i ^ bits) for i in range(size)])]
    pallas_call x7 -> x18, Pallas kernels: 14.3 us -> 11.5 us  [the longest x1 4.3 us: body(): call(start_kernel, 'start', (shaped((PACK, width), BF16), shaped((PACK, w...]
    ppermute x21 -> x20, waiting for transfers between devices: 30.5 us -> 30.3 us  [swap(): return lax.ppermute(value, axis, [(i, i ^ bits) for i in range(size)])]
  transfers between devices with their start and end apart: 21 -> 20, of which waited for: 14 -> 12; matrix products, arithmetic and copies ran while one was open for 1% -> 0% of each run, Pallas kernels for 7% -> 8%
where the time goes in v4:
time: 64.2 us; the launch traced here: 64 us
  waiting for transfers between devices  30.3 us (47%)
  starting transfers between devices  19.5 us (30%)
  Pallas kernels  13.2 us (21%)
  between operations  0.86 us (1%)
    ppermute x20, waiting for transfers between devices, swap(): return lax.ppermute(value, axis, [(i, i ^ bits) for i in range(size)])  30.3 us
    ppermute x20, starting transfers between devices, swap(): return lax.ppermute(value, axis, [(i, i ^ bits) for i in range(size)])  19.5 us
    pallas_call x1, Pallas kernels, body(): call(start_kernel, 'start', (shaped((PACK, width), BF16), shaped((PACK, w...  4.3 us
    pallas_call x2, Pallas kernels, body(): call(functools.partial(step_kernel, groups, views, ready), 'ray_space_ste...  3.62 us
    pallas_call x1, Pallas kernels, body(): call(final_kernel, 'update', (shaped(fine_volume.shape, F32), shaped(coar...  1.47 us
  transfers between devices with their start and end apart: 20, of which 12 were waited for; matrix products, arithmetic and copies ran while one was open for 0% of the time, Pallas kernels for 8%

profile of v4, /device:TPU:0, one launch (start us, length us, event | category | flops | bytes accessed | tf_op | source)
XLA Modules:
  0.0 64.0 jit_solution(13118543845048698673)
XLA Ops:
  0.6 1.2 %take_rays.1 = bf16[2,2,1024,128]{3,2,1,0:T(8,128)(2,1)S(1)} custom-call(bf16[2,4096,128]{2,1,0:T(8,128)(2,1)} %fine_rays.1, bf16[2,4096,128]{2,1,0:T(8,128)(2,1)} %coarse_rays.1), custom_call_target="tpu_custom_call" | custom-call | flops 1 | bytes 1 | tf_op jit(solution)/shard_map/take_rays/pallas_call | solution.py:602
  1.9 3.0 %collective-permute-start.5 = (bf16[2,2,1024,128]{3,2,1,0:T(8,128)(2,1)S(1)}, bf16[2,2,1024,128]{3,2,1,0:T(8,128)(2,1)S(1)}, u32[]{:S(2)}, u32[]{:S(2)}) collective-permute-start(bf16[2,2,1024,128]{3,2,1,0:T(8,128)(2,1)S(1)} %take_rays.1), channel_id=1, source_target_pairs={{0,1},{1,0},{2,3},{3,2},{4,5},{5,4},{6,7},{7,6},{8,9},{9,8},{10,11... | collective-permute-start | bytes 3145736 | tf_op jit(solution)/shard_map/ppermute | solution.py:57
  4.9 4.3 %start.1 = (bf16[16,1280]{1,0:T(8,128)(2,1)S(1)}, bf16[16,1280]{1,0:T(8,128)(2,1)S(1)}, bf16[32,256]{1,0:T(8,128)(2,1)S(1)}, f32[64,256]{1,0:T(8,128)S(1)}, bf16...) custom-call(bf16[2,4096,128]{2,1,0:T(8,128)(2,1)} %fine_rays.1, bf16[2,4096,128]{2,1,0:T(8,128)(2,1)} %coarse_rays.1, ...), custom_call_target="tpu_custom_call" | custom-call | flops 1 | bytes 1 | tf_op jit(solution)/shard_map/start/pallas_call | solution.py:568
  9.3 0.5 collective-permute-start
  9.8 0.7 %collective-permute-done.8.received = bf16[16,1280]{1,0:T(8,128)(2,1)S(1)} collective-permute-done((bf16[16,1280]{1,0:T(8,128)(2,1)S(1)}, bf16[16,1280]{1,0:T(8,128)(2,1)S(1)}, u32[]{:S(2)}, u32[]{:S(2)}) %collective-permute-start.8) | collective-permute-done | bytes 40992 | tf_op jit(solution)/shard_map/ppermute | solution.py:57
  10.5 2.7 %collective-permute-start.9 = (bf16[2,16,1280]{2,1,0:T(8,128)(2,1)S(1)}, bf16[2,16,1280]{2,1,0:T(8,128)(2,1)S(1)}, u32[]{:S(2)}, u32[]{:S(2)}) collective-permute-start(bf16[2,16,1280]{2,1,0:T(8,128)(2,1)S(1)} %pair.1), channel_id=1, source_target_pairs={{0,16},{2,18},{4,20},{6,22},{8,24},{10,26},{12,28},{14,30},{16,0},... | collective-permute-start | bytes 245768 | tf_op jit(solution)/shard_map/ppermute | solution.py:57
  13.2 1.6 %collective-permute-start.1 = (bf16[96,256]{1,0:T(8,128)(2,1)S(1)}, bf16[96,256]{1,0:T(8,128)(2,1)S(1)}, u32[]{:S(2)}, u32[]{:S(2)}) collective-permute-start(bf16[96,256]{1,0:T(8,128)(2,1)S(1)} %get-tuple-element.37.mine), channel_id=1, source_target_pairs={{0,4},{2,6},{4,0},{6,2},{8,12},{10,14},{12,8},{14,10},{16,20},{18,... | collective-permute-start | bytes 147464 | tf_op jit(solution)/shard_map/ppermute | solution.py:57
  14.7 2.6 %collective-permute-done.1.received = bf16[96,256]{1,0:T(8,128)(2,1)S(1)} collective-permute-done((bf16[96,256]{1,0:T(8,128)(2,1)S(1)}, bf16[96,256]{1,0:T(8,128)(2,1)S(1)}, u32[]{:S(2)}, u32[]{:S(2)}) %collective-permute-start.1) | collective-permute-done | bytes 49184 | tf_op jit(solution)/shard_map/ppermute | solution.py:57
  17.8 1.6 %collective-permute-start.10 = (bf16[4,16,1280]{2,1,0:T(8,128)(2,1)S(1)}, bf16[4,16,1280]{2,1,0:T(8,128)(2,1)S(1)}, u32[]{:S(2)}, u32[]{:S(2)}) collective-permute-start(bf16[4,16,1280]{2,1,0:T(8,128)(2,1)S(1)} %pad_maximum_fusion.1), channel_id=1, source_target_pairs={{0,8},{2,10},{4,12},{6,14},{8,0},{10,2},{12,4},{14,6},{16,24},{18,... | collective-permute-start | bytes 491528 | tf_op jit(solution)/shard_map/ppermute | solution.py:57
  19.4 3.3 %collective-permute-done.2.received = bf16[128,256]{1,0:T(8,128)(2,1)S(1)} collective-permute-done((bf16[128,256]{1,0:T(8,128)(2,1)S(1)}, bf16[128,256]{1,0:T(8,128)(2,1)S(1)}, u32[]{:S(2)}, u32[]{:S(2)}) %collective-permute-start.2) | collective-permute-done | bytes 65568 | tf_op jit(solution)/shard_map/ppermute | solution.py:57
  22.7 2.2 %collective-permute-start.3 = (bf16[192,256]{1,0:T(8,128)(2,1)S(1)}, bf16[192,256]{1,0:T(8,128)(2,1)S(1)}, u32[]{:S(2)}, u32[]{:S(2)}) collective-permute-start(bf16[192,256]{1,0:T(8,128)(2,1)S(1)} %get-tuple-element.41.mine), channel_id=1, source_target_pairs={{0,8},{2,10},{4,12},{6,14},{8,0},{10,2},{12,4},{14,6},{16,24},{18,... | collective-permute-start | bytes 294920 | tf_op jit(solution)/shard_map/ppermute | solution.py:57
  24.9 2.6 %collective-permute-done.3.received = bf16[192,256]{1,0:T(8,128)(2,1)S(1)} collective-permute-done((bf16[192,256]{1,0:T(8,128)(2,1)S(1)}, bf16[192,256]{1,0:T(8,128)(2,1)S(1)}, u32[]{:S(2)}, u32[]{:S(2)}) %collective-permute-start.3) | collective-permute-done | bytes 98336 | tf_op jit(solution)/shard_map/ppermute | solution.py:57
  27.5 0.6 %join_hop.5 = (f32[64,256]{1,0:T(8,128)}, bf16[384,256]{1,0:T(8,128)(2,1)S(1)}) custom-call(f32[64,256]{1,0:T(8,128)S(1)} %get-tuple-element.40.q, bf16[192,256]{1,0:T(8,128)(2,1)S(1)} %get-tuple-element.41.mine, bf16[192,256]{1,0:T(8,128)(2,1)S(1)} %collective-permute-done.3.received), custom_call_target="tpu_custom_call" | custom-call | flops 1 | bytes 1 | tf_op jit(solution)/shard_map/join_hop/pallas_call | solution.py:645
  28.1 0.5 collective-permute-start.4
  28.7 1.6 %collective-permute-start.11 = (bf16[8,16,1280]{2,1,0:T(8,128)(2,1)S(1)}, bf16[8,16,1280]{2,1,0:T(8,128)(2,1)S(1)}, u32[]{:S(2)}, u32[]{:S(2)}) collective-permute-start(bf16[8,16,1280]{2,1,0:T(8,128)(2,1)S(1)} %pad_maximum_fusion.mine), channel_id=1, source_target_pairs={{0,4},{2,6},{4,0},{6,2},{8,12},{10,14},{12,8},{14,10},{16,20},{18,... | collective-permute-start | bytes 983048 | tf_op jit(solution)/shard_map/ppermute | solution.py:57
  30.3 3.6 %collective-permute-done.4.refs_1_ = bf16[384,256]{1,0:T(8,128)(2,1)S(1)} collective-permute-done((bf16[384,256]{1,0:T(8,128)(2,1)S(1)}, bf16[384,256]{1,0:T(8,128)(2,1)S(1)}, u32[]{:S(2)}, u32[]{:S(2)}) %collective-permute-start.4) | collective-permute-done | bytes 196640 | tf_op jit(solution)/shard_map/ppermute | solution.py:57
  33.9 0.5 collective-permute-start.7
  34.4 2.2 %collective-permute-done.11.received = bf16[8,16,1280]{2,1,0:T(8,128)(2,1)S(1)} collective-permute-done((bf16[8,16,1280]{2,1,0:T(8,128)(2,1)S(1)}, bf16[8,16,1280]{2,1,0:T(8,128)(2,1)S(1)}, u32[]{:S(2)}, u32[]{:S(2)}) %collective-permute-start.11) | collective-permute-done | bytes 327712 | tf_op jit(solution)/shard_map/ppermute | solution.py:57
  37.5 1.8 %ray_space_step.2.mine = bf16[2,128,256]{2,1,0:T(8,128)(2,1)S(1)} custom-call(bf16[2,64,256]{2,1,0:T(8,128)(2,1)S(1)} %get-tuple-element.49.refs_0_, bf16[2,256,256]{2,1,0:T(8,128)(2,1)S(1)} %get-tuple-element.50.refs_1_, bf16[2,2,128,64]{3,2,1,0:T(8,128)(2,1)S(1)} %get-tuple-element.51.refs_2_.refs_5_, ...), custom_call_target="tpu_custom_call" | custom-call | flops 1 | bytes 1 | tf_op jit(solution)/shard_map/ray_space_step/pallas_call | solution.py:708
  39.4 1.3 %collective-permute-done.12.received = bf16[2,128,256]{2,1,0:T(8,128)(2,1)S(1)} collective-permute-done((bf16[2,128,256]{2,1,0:T(8,128)(2,1)S(1)}, bf16[2,128,256]{2,1,0:T(8,128)(2,1)S(1)}, u32[]{:S(2)}, u32[]{:S(2)}) %collective-permute-start.12) | collective-permute-done | bytes 131104 | tf_op jit(solution)/shard_map/ppermute | solution.py:57
  40.7 1.0 %collective-permute-start.13 = (bf16[2,128,256]{2,1,0:T(8,128)(2,1)S(1)}, bf16[2,128,256]{2,1,0:T(8,128)(2,1)S(1)}, u32[]{:S(2)}, u32[]{:S(2)}) collective-permute-start(bf16[2,128,256]{2,1,0:T(8,128)(2,1)S(1)} %add.4.mine), channel_id=1, source_target_pairs={{0,1},{1,0},{2,3},{3,2},{4,5},{5,4},{6,7},{7,6},{8,9},{9,8},{10,11... | collective-permute-start | bytes 393224 | tf_op jit(solution)/shard_map/ppermute | solution.py:57
  41.8 4.6 %collective-permute-done.13.received = bf16[2,128,256]{2,1,0:T(8,128)(2,1)S(1)} collective-permute-done((bf16[2,128,256]{2,1,0:T(8,128)(2,1)S(1)}, bf16[2,128,256]{2,1,0:T(8,128)(2,1)S(1)}, u32[]{:S(2)}, u32[]{:S(2)}) %collective-permute-start.13) | collective-permute-done | bytes 131104 | tf_op jit(solution)/shard_map/ppermute | solution.py:57
  46.4 1.9 %ray_space_step.3.mine = bf16[2,128,256]{2,1,0:T(8,128)(2,1)S(1)} custom-call(f32[2,128,256]{2,1,0:T(8,128)S(1)} %get-tuple-element.45.q.refs_0_, bf16[2,128,256]{2,1,0:T(8,128)(2,1)S(1)} %add.5.refs_1_.refs_0_, f32[2,128,256]{2,1,0:T(8,128)S(1)} %get-tuple-element.46.weights.refs_2_, bf16[2,64,256]{2,1,0:T(8,128)(2,1)S(1)} %get-tuple-element.47.fine_depth.refs_3_, ...), custom_call_target="tpu_custom_call" | custom-call | flops 1 | bytes 1 | tf_op jit(solution)/shard_map/ray_space_step/pallas_call | solution.py:708
  48.4 1.3 %collective-permute-done.14.received = bf16[2,128,256]{2,1,0:T(8,128)(2,1)S(1)} collective-permute-done((bf16[2,128,256]{2,1,0:T(8,128)(2,1)S(1)}, bf16[2,128,256]{2,1,0:T(8,128)(2,1)S(1)}, u32[]{:S(2)}, u32[]{:S(2)}) %collective-permute-start.14) | collective-permute-done | bytes 131104 | tf_op jit(solution)/shard_map/ppermute | solution.py:57
  49.8 1.0 %collective-permute-start.15 = (bf16[2,128,256]{2,1,0:T(8,128)(2,1)S(1)}, bf16[2,128,256]{2,1,0:T(8,128)(2,1)S(1)}, u32[]{:S(2)}, u32[]{:S(2)}) collective-permute-start(bf16[2,128,256]{2,1,0:T(8,128)(2,1)S(1)} %add.6.mine), channel_id=1, source_target_pairs={{0,1},{1,0},{2,3},{3,2},{4,5},{5,4},{6,7},{7,6},{8,9},{9,8},{10,11... | collective-permute-start | bytes 393224 | tf_op jit(solution)/shard_map/ppermute | solution.py:57
  50.8 4.6 %collective-permute-done.15.received = bf16[2,128,256]{2,1,0:T(8,128)(2,1)S(1)} collective-permute-done((bf16[2,128,256]{2,1,0:T(8,128)(2,1)S(1)}, bf16[2,128,256]{2,1,0:T(8,128)(2,1)S(1)}, u32[]{:S(2)}, u32[]{:S(2)}) %collective-permute-start.15) | collective-permute-done | bytes 131104 | tf_op jit(solution)/shard_map/ppermute | solution.py:57
  55.4 0.9 %back_projection.1 = (bf16[8,1024]{1,0:T(8,128)(2,1)S(1)}, bf16[32,1024]{1,0:T(8,128)(2,1)S(1)}) custom-call(f32[2,128,256]{2,1,0:T(8,128)S(1)} %get-tuple-element.45.q.refs_0_, bf16[2,128,256]{2,1,0:T(8,128)(2,1)S(1)} %add.5.refs_1_.refs_0_, bf16[2,128,256]{2,1,0:T(8,128)(2,1)S(1)} %add.7.refs_1_, f32[2,128,256]{2,1,0:T(8,128)S(1)} %get-tuple-element.46.weights.refs_2_, ...), custom_call_target="tpu_custom_call" | custom-call | flops 1 | bytes 1 | tf_op jit(solution)/shard_map/back_projection/pallas_call | solution.py:719
  56.3 1.0 %collective-permute-start.17 = (bf16[32,1024]{1,0:T(8,128)(2,1)S(1)}, bf16[32,1024]{1,0:T(8,128)(2,1)S(1)}, u32[]{:S(2)}, u32[]{:S(2)}) collective-permute-start(bf16[32,1024]{1,0:T(8,128)(2,1)S(1)} %get-tuple-element.59.refs_1_), channel_id=1, source_target_pairs={{0,1},{1,0},{2,3},{3,2},{4,5},{5,4},{6,7},{7,6},{8,9},{9,8},{10,11... | collective-permute-start | bytes 196616 | tf_op jit(solution)/shard_map/ppermute | solution.py:57
  57.3 1.1 %collective-permute-start.16 = (bf16[8,1024]{1,0:T(8,128)(2,1)S(1)}, bf16[8,1024]{1,0:T(8,128)(2,1)S(1)}, u32[]{:S(2)}, u32[]{:S(2)}) collective-permute-start(bf16[8,1024]{1,0:T(8,128)(2,1)S(1)} %get-tuple-element.58.refs_0_), channel_id=1, source_target_pairs={{0,1},{1,0},{2,3},{3,2},{4,5},{5,4},{6,7},{7,6},{8,9},{9,8},{10,11... | collective-permute-start | bytes 49160 | tf_op jit(solution)/shard_map/ppermute | solution.py:57
  58.3 2.7 %collective-permute-done.16.refs_2_ = bf16[8,1024]{1,0:T(8,128)(2,1)S(1)} collective-permute-done((bf16[8,1024]{1,0:T(8,128)(2,1)S(1)}, bf16[8,1024]{1,0:T(8,128)(2,1)S(1)}, u32[]{:S(2)}, u32[]{:S(2)}) %collective-permute-start.16) | collective-permute-done | bytes 16416 | tf_op jit(solution)/shard_map/ppermute | solution.py:57
  61.7 0.8 %collective-permute-done.18.refs_2_ = bf16[4,2048]{1,0:T(4,128)(2,1)S(1)} collective-permute-done((bf16[4,2048]{1,0:T(4,128)(2,1)S(1)}, bf16[4,2048]{1,0:T(4,128)(2,1)S(1)}, u32[]{:S(2)}, u32[]{:S(2)}) %collective-permute-start.18) | collective-permute-done | bytes 16416 | tf_op jit(solution)/shard_map/ppermute | solution.py:57
  62.5 1.5 %update.1 = (f32[4,4096]{1,0:T(4,128)}, f32[16,4096]{1,0:T(8,128)}) custom-call(bf16[4,2048]{1,0:T(4,128)(2,1)S(1)} %get-tuple-element.60.refs_0_, bf16[16,2048]{1,0:T(8,128)(2,1)S(1)} %get-tuple-element.61.refs_1_, bf16[4,2048]{1,0:T(4,128)(2,1)S(1)} %collective-permute-done.18.refs_2_, bf16[16,2048]{1,0:T(8,128)(2,1)S(1)} %collective-permute-done.19.refs_3_, ...), custom_call_target="tpu_custom_call" | custom-call | flops 1 | bytes 1 | tf_op jit(solution)/shard_map/update/pallas_call | solution.py:734
  (40 shorter events, 2.5 us)
Async XLA Ops:
  1.9 32.0 %collective-permute-start.5 = (bf16[2,2,1024,128]{3,2,1,0:T(8,128)(2,1)S(1)}, bf16[2,2,1024,128]{3,2,1,0:T(8,128)(2,1)S(1)}, u32[]{:S(2)}, u32[]{:S(2)}) collective-permute-start(bf16[2,2,1024,128]{3,2,1,0:T(8,128)(2,1)S(1)} %take_rays.1), channel_id=1, source_target_pairs={{0,1},{1,0},{2,3},{3,2},{4,5},{5,4},{6,7},{7,6},{8,9},{9,8},{10,11... | collective-permute-start | bytes 3145736 | tf_op jit(solution)/shard_map/ppermute | solution.py:57
  9.2 1.3 %collective-permute-start.8 = (bf16[16,1280]{1,0:T(8,128)(2,1)S(1)}, bf16[16,1280]{1,0:T(8,128)(2,1)S(1)}, u32[]{:S(2)}, u32[]{:S(2)}) collective-permute-start(bf16[16,1280]{1,0:T(8,128)(2,1)S(1)} %get-tuple-element.54), channel_id=1, source_target_pairs={{0,2},{2,0},{4,6},{6,4},{8,10},{10,8},{12,14},{14,12},{16,18},{18,... | collective-permute-start | bytes 122888 | tf_op jit(solution)/shard_map/ppermute | solution.py:57
  9.3 3.9 %collective-permute-start = (bf16[64,256]{1,0:T(8,128)(2,1)S(1)}, bf16[64,256]{1,0:T(8,128)(2,1)S(1)}, u32[]{:S(2)}, u32[]{:S(2)}) collective-permute-start(bf16[64,256]{1,0:T(8,128)(2,1)S(1)} %get-tuple-element.34), channel_id=1, source_target_pairs={{0,2},{2,0},{4,6},{6,4},{8,10},{10,8},{12,14},{14,12},{16,18},{18,... | collective-permute-start | bytes 98312 | tf_op jit(solution)/shard_map/ppermute | solution.py:57
  10.5 7.2 %collective-permute-start.9 = (bf16[2,16,1280]{2,1,0:T(8,128)(2,1)S(1)}, bf16[2,16,1280]{2,1,0:T(8,128)(2,1)S(1)}, u32[]{:S(2)}, u32[]{:S(2)}) collective-permute-start(bf16[2,16,1280]{2,1,0:T(8,128)(2,1)S(1)} %pair.1), channel_id=1, source_target_pairs={{0,16},{2,18},{4,20},{6,22},{8,24},{10,26},{12,28},{14,30},{16,0},... | collective-permute-start | bytes 245768 | tf_op jit(solution)/shard_map/ppermute | solution.py:57
  13.2 4.2 %collective-permute-start.1 = (bf16[96,256]{1,0:T(8,128)(2,1)S(1)}, bf16[96,256]{1,0:T(8,128)(2,1)S(1)}, u32[]{:S(2)}, u32[]{:S(2)}) collective-permute-start(bf16[96,256]{1,0:T(8,128)(2,1)S(1)} %get-tuple-element.37.mine), channel_id=1, source_target_pairs={{0,4},{2,6},{4,0},{6,2},{8,12},{10,14},{12,8},{14,10},{16,20},{18,... | collective-permute-start | bytes 147464 | tf_op jit(solution)/shard_map/ppermute | solution.py:57
  17.4 5.3 %collective-permute-start.2 = (bf16[128,256]{1,0:T(8,128)(2,1)S(1)}, bf16[128,256]{1,0:T(8,128)(2,1)S(1)}, u32[]{:S(2)}, u32[]{:S(2)}) collective-permute-start(bf16[128,256]{1,0:T(8,128)(2,1)S(1)} %get-tuple-element.39.mine), channel_id=1, source_target_pairs={{0,16},{2,18},{4,20},{6,22},{8,24},{10,26},{12,28},{14,30},{16,0},... | collective-permute-start | bytes 196616 | tf_op jit(solution)/shard_map/ppermute | solution.py:57
  17.8 10.9 %collective-permute-start.10 = (bf16[4,16,1280]{2,1,0:T(8,128)(2,1)S(1)}, bf16[4,16,1280]{2,1,0:T(8,128)(2,1)S(1)}, u32[]{:S(2)}, u32[]{:S(2)}) collective-permute-start(bf16[4,16,1280]{2,1,0:T(8,128)(2,1)S(1)} %pad_maximum_fusion.1), channel_id=1, source_target_pairs={{0,8},{2,10},{4,12},{6,14},{8,0},{10,2},{12,4},{14,6},{16,24},{18,... | collective-permute-start | bytes 491528 | tf_op jit(solution)/shard_map/ppermute | solution.py:57
  22.7 4.8 %collective-permute-start.3 = (bf16[192,256]{1,0:T(8,128)(2,1)S(1)}, bf16[192,256]{1,0:T(8,128)(2,1)S(1)}, u32[]{:S(2)}, u32[]{:S(2)}) collective-permute-start(bf16[192,256]{1,0:T(8,128)(2,1)S(1)} %get-tuple-element.41.mine), channel_id=1, source_target_pairs={{0,8},{2,10},{4,12},{6,14},{8,0},{10,2},{12,4},{14,6},{16,24},{18,... | collective-permute-start | bytes 294920 | tf_op jit(solution)/shard_map/ppermute | solution.py:57
  28.1 5.7 %collective-permute-start.4 = (bf16[384,256]{1,0:T(8,128)(2,1)S(1)}, bf16[384,256]{1,0:T(8,128)(2,1)S(1)}, u32[]{:S(2)}, u32[]{:S(2)}) collective-permute-start(bf16[384,256]{1,0:T(8,128)(2,1)S(1)} %get-tuple-element.42.refs_0_), channel_id=1, source_target_pairs={{0,1},{1,0},{2,3},{3,2},{4,5},{5,4},{6,7},{7,6},{8,9},{9,8},{10,11... | collective-permute-start | bytes 589832 | tf_op jit(solution)/shard_map/ppermute | solution.py:57
  28.7 7.9 %collective-permute-start.11 = (bf16[8,16,1280]{2,1,0:T(8,128)(2,1)S(1)}, bf16[8,16,1280]{2,1,0:T(8,128)(2,1)S(1)}, u32[]{:S(2)}, u32[]{:S(2)}) collective-permute-start(bf16[8,16,1280]{2,1,0:T(8,128)(2,1)S(1)} %pad_maximum_fusion.mine), channel_id=1, source_target_pairs={{0,4},{2,6},{4,0},{6,2},{8,12},{10,14},{12,8},{14,10},{16,20},{18,... | collective-permute-start | bytes 983048 | tf_op jit(solution)/shard_map/ppermute | solution.py:57
  33.9 3.0 %collective-permute-start.6 = (bf16[2,256,256]{2,1,0:T(8,128)(2,1)S(1)}, bf16[2,256,256]{2,1,0:T(8,128)(2,1)S(1)}, u32[]{:S(2)}, u32[]{:S(2)}) collective-permute-start(bf16[2,256,256]{2,1,0:T(8,128)(2,1)S(1)} %get-tuple-element.43.mine), channel_id=1, source_target_pairs={{0,2},{2,0},{4,6},{6,4},{8,10},{10,8},{12,14},{14,12},{16,18},{18,... | collective-permute-start | bytes 786440 | tf_op jit(solution)/shard_map/ppermute | solution.py:57
  33.9 2.9 %collective-permute-start.7 = (f32[2,64,256]{2,1,0:T(8,128)S(1)}, f32[2,64,256]{2,1,0:T(8,128)S(1)}, u32[]{:S(2)}, u32[]{:S(2)}) collective-permute-start(f32[2,64,256]{2,1,0:T(8,128)S(1)} %get-tuple-element.44.q_mine), channel_id=1, source_target_pairs={{0,2},{2,0},{4,6},{6,4},{8,10},{10,8},{12,14},{14,12},{16,18},{18,... | collective-permute-start | bytes 393224 | tf_op jit(solution)/shard_map/ppermute | solution.py:57
  39.3 1.4 %collective-permute-start.12 = (bf16[2,128,256]{2,1,0:T(8,128)(2,1)S(1)}, bf16[2,128,256]{2,1,0:T(8,128)(2,1)S(1)}, u32[]{:S(2)}, u32[]{:S(2)}) collective-permute-start(bf16[2,128,256]{2,1,0:T(8,128)(2,1)S(1)} %ray_space_step.2.mine), channel_id=1, source_target_pairs={{0,2},{2,0},{4,6},{6,4},{8,10},{10,8},{12,14},{14,12},{16,18},{18,... | collective-permute-start | bytes 393224 | tf_op jit(solution)/shard_map/ppermute | solution.py:57
  40.7 5.6 %collective-permute-start.13 = (bf16[2,128,256]{2,1,0:T(8,128)(2,1)S(1)}, bf16[2,128,256]{2,1,0:T(8,128)(2,1)S(1)}, u32[]{:S(2)}, u32[]{:S(2)}) collective-permute-start(bf16[2,128,256]{2,1,0:T(8,128)(2,1)S(1)} %add.4.mine), channel_id=1, source_target_pairs={{0,1},{1,0},{2,3},{3,2},{4,5},{5,4},{6,7},{7,6},{8,9},{9,8},{10,11... | collective-permute-start | bytes 393224 | tf_op jit(solution)/shard_map/ppermute | solution.py:57
  48.2 14.3 %copy-start = (f32[16,4096]{1,0:T(8,128)S(1)}, f32[16,4096]{1,0:T(8,128)}, u32[]{:S(2)}) copy-start(f32[16,4096]{1,0:T(8,128)} %refs_5_.1) | copy-start | bytes 786436
  48.3 14.2 %copy-start.1 = (f32[16,4096]{1,0:T(8,128)S(1)}, f32[16,4096]{1,0:T(8,128)}, u32[]{:S(2)}) copy-start(f32[16,4096]{1,0:T(8,128)} %refs_7_.1) | copy-start | bytes 786436
  48.3 14.2 %copy-start.2 = (f32[4,4096]{1,0:T(4,128)S(1)}, f32[4,4096]{1,0:T(4,128)}, u32[]{:S(2)}) copy-start(f32[4,4096]{1,0:T(4,128)} %refs_4_.1) | copy-start | bytes 196612
  48.3 14.2 %copy-start.3 = (f32[4,4096]{1,0:T(4,128)S(1)}, f32[4,4096]{1,0:T(4,128)}, u32[]{:S(2)}) copy-start(f32[4,4096]{1,0:T(4,128)} %refs_6_.1) | copy-start | bytes 196612
  48.3 14.2 %copy-start.4 = (s32[1,8]{1,0:T(1,128)S(1)}, s32[1,8]{1,0:T(1,128)}, u32[]{:S(2)}) copy-start(s32[1,8]{1,0:T(1,128)} %refs_8_.1) | copy-start | bytes 100
  48.3 1.4 %collective-permute-start.14 = (bf16[2,128,256]{2,1,0:T(8,128)(2,1)S(1)}, bf16[2,128,256]{2,1,0:T(8,128)(2,1)S(1)}, u32[]{:S(2)}, u32[]{:S(2)}) collective-permute-start(bf16[2,128,256]{2,1,0:T(8,128)(2,1)S(1)} %ray_space_step.3.mine), channel_id=1, source_target_pairs={{0,2},{2,0},{4,6},{6,4},{8,10},{10,8},{12,14},{14,12},{16,18},{18,... | collective-permute-start | bytes 393224 | tf_op jit(solution)/shard_map/ppermute | solution.py:57
  49.8 5.6 %collective-permute-start.15 = (bf16[2,128,256]{2,1,0:T(8,128)(2,1)S(1)}, bf16[2,128,256]{2,1,0:T(8,128)(2,1)S(1)}, u32[]{:S(2)}, u32[]{:S(2)}) collective-permute-start(bf16[2,128,256]{2,1,0:T(8,128)(2,1)S(1)} %add.6.mine), channel_id=1, source_target_pairs={{0,1},{1,0},{2,3},{3,2},{4,5},{5,4},{6,7},{7,6},{8,9},{9,8},{10,11... | collective-permute-start | bytes 393224 | tf_op jit(solution)/shard_map/ppermute | solution.py:57
  56.3 4.7 %collective-permute-start.17 = (bf16[32,1024]{1,0:T(8,128)(2,1)S(1)}, bf16[32,1024]{1,0:T(8,128)(2,1)S(1)}, u32[]{:S(2)}, u32[]{:S(2)}) collective-permute-start(bf16[32,1024]{1,0:T(8,128)(2,1)S(1)} %get-tuple-element.59.refs_1_), channel_id=1, source_target_pairs={{0,1},{1,0},{2,3},{3,2},{4,5},{5,4},{6,7},{7,6},{8,9},{9,8},{10,11... | collective-permute-start | bytes 196616 | tf_op jit(solution)/shard_map/ppermute | solution.py:57
  57.3 3.7 %collective-permute-start.16 = (bf16[8,1024]{1,0:T(8,128)(2,1)S(1)}, bf16[8,1024]{1,0:T(8,128)(2,1)S(1)}, u32[]{:S(2)}, u32[]{:S(2)}) collective-permute-start(bf16[8,1024]{1,0:T(8,128)(2,1)S(1)} %get-tuple-element.58.refs_0_), channel_id=1, source_target_pairs={{0,1},{1,0},{2,3},{3,2},{4,5},{5,4},{6,7},{7,6},{8,9},{9,8},{10,11... | collective-permute-start | bytes 49160 | tf_op jit(solution)/shard_map/ppermute | solution.py:57
  61.1 1.4 %collective-permute-start.19 = (bf16[16,2048]{1,0:T(8,128)(2,1)S(1)}, bf16[16,2048]{1,0:T(8,128)(2,1)S(1)}, u32[]{:S(2)}, u32[]{:S(2)}) collective-permute-start(bf16[16,2048]{1,0:T(8,128)(2,1)S(1)} %get-tuple-element.63), channel_id=1, source_target_pairs={{0,2},{2,0},{4,6},{6,4},{8,10},{10,8},{12,14},{14,12},{16,18},{18,... | collective-permute-start | bytes 196616 | tf_op jit(solution)/shard_map/ppermute | solution.py:57
  61.2 1.3 %collective-permute-start.18 = (bf16[4,2048]{1,0:T(4,128)(2,1)S(1)}, bf16[4,2048]{1,0:T(4,128)(2,1)S(1)}, u32[]{:S(2)}, u32[]{:S(2)}) collective-permute-start(bf16[4,2048]{1,0:T(4,128)(2,1)S(1)} %get-tuple-element.62), channel_id=1, source_target_pairs={{0,2},{2,0},{4,6},{6,4},{8,10},{10,8},{12,14},{14,12},{16,18},{18,... | collective-permute-start | bytes 49160 | tf_op jit(solution)/shard_map/ppermute | solution.py:57

commit v5 on v4

--- a/solution.py
+++ b/solution.py
@@ -83,6 +83,34 @@
 def packed_tiles(cells, fz):
     parts = PACK // fz
     return -(-(cells // LANES) // parts)
+
+
+def pack_fine(rows):
+    fz, size = rows.shape
+    parts = PACK // fz
+    empty = jnp.zeros((1, LANES), rows.dtype)
+    columns = []
+    for c in range(packed_tiles(size, fz)):
+        pieces = []
+        for i in range(fz):
+            for k in range(parts):
+                t = c * parts + k
+                inside = t * LANES < size
+                pieces.append(rows[i : i + 1, t * LANES : (t + 1) * LANES] if inside else empty)
+        columns.append(jnp.concatenate(pieces, axis=0))
+    return jnp.concatenate(columns, axis=1)
+
+
+def unpack_fine(packed, fz, size):
+    parts = PACK // fz
+    rows = []
+    for i in range(fz):
+        pieces = []
+        for t in range(size // LANES):
+            row, column = i * parts + t % parts, t // parts * LANES
+            pieces.append(packed[row : row + 1, column : column + LANES])
+        rows.append(jnp.concatenate(pieces, axis=1))
+    return jnp.concatenate(rows, axis=0)
 
 
 def hit_depths(axial, hits):
@@ -211,6 +239,13 @@
                 ),
             ]
         )
+    share = own_rays.shape[2]
+    groups = half // share
+    held = pl.ds(share_start(cells, groups), share)
+    outgoing = [
+        fetch(fine_rays_in.at[:, held, :], own_rays.at[0], sems.at[6]),
+        fetch(coarse_rays_in.at[:, held, :], own_rays.at[1], sems.at[7]),
+    ]
     for copy in others:
         copy.wait()
 
@@ -235,25 +270,11 @@
     for p in range((span + wide) // total):
         rows[p * PACK : (p + 1) * PACK] = packed[:, p * total : (p + 1) * total]
 
-    parts = PACK // fz
-    empty = jnp.zeros((1, LANES), F32)
-    share = own_rays.shape[2]
-    groups = half // share
     for target, side in ((mine, core), (theirs, 1 - core)):
         begin = pl.multiple_of(side * half + lax.axis_index("view") * share, LANES)
         keep = keep_row(blocks, begin, share)
         target[:, :share] = (coarse_weight[:, pl.ds(begin, share)] * keep).astype(BF16)
-        weight = fine_weight[:, pl.ds(begin, share)]
-        for c in range(packed_tiles(share, fz)):
-            pieces = []
-            for i in range(fz):
-                for k in range(parts):
-                    t = c * parts + k
-                    inside = t * LANES < share
-                    piece = weight[i : i + 1, t * LANES : (t + 1) * LANES] if inside else empty
-                    pieces.append(piece)
-            column = slice(share + c * LANES, share + (c + 1) * LANES)
-            target[:, column] = jnp.concatenate(pieces, axis=0).astype(BF16)
+        target[:, share:] = pack_fine(fine_weight[:, pl.ds(begin, share)]).astype(BF16)
 
     fine_sum = coarse_sum = None
     for i in range(steps):
@@ -269,11 +290,6 @@
         coarse_part = dot(coarse_rows, coarse_wide, ((1,), (0,)))
         fine_sum = fine_part if fine_sum is None else fine_sum + fine_part
         coarse_sum = coarse_part if coarse_sum is None else coarse_sum + coarse_part
-    held = pl.ds(share_start(cells, groups), share)
-    outgoing = [
-        fetch(fine_rays.at[:, held, :], own_rays.at[0], sems.at[6]),
-        fetch(coarse_rays.at[:, held, :], own_rays.at[1], sems.at[7]),
-    ]
     pad = jnp.zeros((PACK - fz, total), F32)
     moment = jnp.concatenate([coarse_sum, fine_sum, pad], axis=0).astype(BF16)
     pad = jnp.zeros((PACK - fz, det), F32)
@@ -462,63 +478,59 @@
         out[g] = (mine[g].astype(F32) + received[g ^ bit].astype(F32)).astype(BF16)
 
 
-def tail_kernel(groups, views, q, *refs):
+def tail_kernel(fz, groups, views, q, *refs):
     deltas = refs[:2]
     weights, fine_depth, coarse_depth = refs[2:5]
     held = refs[5:-2]
-    fine_out, coarse_out = refs[-2:]
-    size = coarse_out.shape[1]
+    ours, theirs = refs[-2:]
+    size = held[0].shape[2]
     chunk = min(size, 512)
+    lead = lax.axis_index("slab") % 2 == 0
     history = residuals(q, deltas, weights)
-    rows = (fine_out.shape[0], coarse_out.shape[0])
+    rows = (fz, PACK)
     spreads = ([], [])
     for g in range(groups):
         value = history[0][g]
         for other in history[1:]:
             value = value + other[g]
         high, low = in_two(value)
-        for part, depth in enumerate((fine_depth[g, : rows[0]], coarse_depth[g, : rows[1]])):
+        for part, depth in enumerate((fine_depth[g, : 2 * fz], coarse_depth[g, : 2 * PACK])):
             pair = in_two(spread(depth, high, views) + spread(depth, low, views))
             spreads[part].append(jnp.concatenate(pair, axis=0))
-    for part, out in enumerate((fine_out, coarse_out)):
+    backs = ([], [])
+    for part in range(2):
         for c in range(size // chunk):
             cut = slice(c * chunk, (c + 1) * chunk)
             back = None
             for g in range(groups):
                 value = dot(spreads[part][g], group_rays(held, part, g, cut), ((1,), (1,)))
                 back = value if back is None else back + value
-            out[:, cut] = (back[: rows[part]] + back[rows[part] :]).astype(BF16)
-
-
-def sort_kernel(groups, *refs):
-    pieces, outs = refs[:-4], refs[-4:]
-    lead = lax.axis_index("slab") % 2 == 0
+            backs[part].append(back[: 2 * rows[part]] + back[2 * rows[part] :])
+    for out, first in ((ours, lead), (theirs, jnp.logical_not(lead))):
+        parts = []
+        for part in range(2):
+            back = jnp.concatenate(backs[part], axis=1)
+            parts.append(jnp.where(first, back[: rows[part]], back[rows[part] :]))
+        out[:, :size] = parts[1].astype(BF16)
+        out[:, size:] = pack_fine(parts[0]).astype(BF16)
+
+
+def final_kernel(groups, size, *refs):
+    pieces = refs[: 2 * groups]
+    fine, coarse, fw, cw, blocks, fine_out, coarse_out = refs[2 * groups :]
+    core = lax.axis_index("slab") % 2
     view = lax.axis_index("view")
-    for part in range(2):
-        mine, theirs = outs[2 * part : 2 * part + 2]
-        rows = mine.shape[0]
-        size = pieces[part].shape[1]
-        for g in range(groups):
-            value = pieces[2 * g + part][...].astype(F32)
-            lower, upper = value[:rows], value[rows:]
-            where = pl.ds(pl.multiple_of((view ^ g) * size, LANES), size)
-            mine[:, where] = jnp.where(lead, lower, upper).astype(BF16)
-            theirs[:, where] = jnp.where(lead, upper, lower).astype(BF16)
-
-
-def final_kernel(*refs):
-    mine, received = refs[:2], refs[2:4]
-    fine, coarse, fw, cw, blocks, fine_out, coarse_out = refs[4:]
-    core = lax.axis_index("slab") % 2
-    half = mine[0].shape[1]
-    for source, side in ((mine, core), (received, 1 - core)):
-        start = pl.multiple_of(side * half, half)
-        where = pl.ds(start, half)
-        keep = keep_row(blocks, start, half)
-        fine_out[:, where] = fine[:, where] + fw[:, where] * source[0][...].astype(F32)
-        coarse_out[:, where] = (
-            coarse[:, where] + cw[:, where] * source[1][...].astype(F32)
-        ) * keep
+    fz, cells = fine.shape
+    for index, piece in enumerate(pieces):
+        side = core if index < groups else 1 - core
+        start = side * (cells // 2) + (view ^ (index % groups)) * size
+        start = pl.multiple_of(start, LANES)
+        where = pl.ds(start, size)
+        keep = keep_row(blocks, start, size)
+        change = piece[:, :size].astype(F32)
+        coarse_out[:, where] = (coarse[:, where] + cw[:, where] * change) * keep
+        change = unpack_fine(piece[:, size:].astype(F32), fz, size)
+        fine_out[:, where] = fine[:, where] + fw[:, where] * change
 
 
 def make_body(slabs, groups):
@@ -716,31 +728,22 @@
                 delta = add(delta, swap(delta, "view", groups, bit), bit)
             deltas.append(delta)
         inputs = (q, *deltas, weights, fine_depth, coarse_depth, *rays)
-        pieces = call(
-            functools.partial(tail_kernel, groups, views),
+        ours, theirs = call(
+            functools.partial(tail_kernel, fz, groups, views),
             "back_projection",
-            (shaped((2 * fz, share), BF16), shaped((2 * PACK, share), BF16)),
+            (shaped((PACK, width), BF16),) * 2,
             [VMEM] * len(inputs),
         )(*inputs)
-        pieces = list(pieces)
-        for bit in view_bits:
-            pieces += [swap(value, "view", groups, bit) for value in pieces]
-        fine_ours, fine_theirs, coarse_ours, coarse_theirs = call(
-            functools.partial(sort_kernel, groups),
-            "sort",
-            (shaped((fz, cells // 2), BF16),) * 2 + (shaped((PACK, cells // 2), BF16),) * 2,
-            [VMEM] * len(pieces),
-        )(*pieces)
+        both = ("slab", "view")
+        pieces = [ours] + [swap(ours, "view", groups, bits) for bits in range(1, groups)]
+        pieces += [swap(theirs, both, slabs * groups, groups | bits) for bits in range(groups)]
         return call(
-            final_kernel,
+            functools.partial(final_kernel, groups, share),
             "update",
             (shaped(fine_volume.shape, F32), shaped(coarse_volume.shape, F32)),
-            [VMEM] * 8 + [SMEM],
+            [VMEM] * (2 * groups + 4) + [SMEM],
         )(
-            fine_ours,
-            coarse_ours,
-            along_slab(fine_theirs, 1),
-            along_slab(coarse_theirs, 1),
+            *pieces,
             fine_volume,
             coarse_volume,
             fine_cell_weight,

time: 64.2 us -> 62.5 us (0.974)
  waiting for transfers between devices: 30.3 us -> 29.4 us
    ppermute x20 -> x19, waiting for transfers between devices: 30.3 us -> 29.4 us  [swap(): return lax.ppermute(value, axis, [(i, i ^ bits) for i in range(size)])]
    ppermute x20 -> x19, starting transfers between devices: 19.5 us -> 19.1 us  [swap(): return lax.ppermute(value, axis, [(i, i ^ bits) for i in range(size)])]
    pallas_call x3 -> x2, Pallas kernels: 2.39 us -> 2.34 us  [the longest x1 1.48 us: body(): call(functools.partial(final_kernel, groups, share), 'update', (shaped(fi...]
  transfers between devices with their start and end apart: 20 -> 19, of which waited for: 12 -> 12; matrix products, arithmetic and copies ran while one was open for 0% -> 0% of each run, Pallas kernels for 8% -> 8%
where the time goes in v5:
time: 62.5 us; the launch traced here: 62.3 us
  waiting for transfers between devices  29.4 us (47%)
  starting transfers between devices  19.1 us (31%)
  Pallas kernels  12.9 us (21%)
  between operations  0.85 us (1%)
    ppermute x19, waiting for transfers between devices, swap(): return lax.ppermute(value, axis, [(i, i ^ bits) for i in range(size)])  29.4 us
    ppermute x19, starting transfers between devices, swap(): return lax.ppermute(value, axis, [(i, i ^ bits) for i in range(size)])  19.1 us
    pallas_call x1, Pallas kernels, body(): call(start_kernel, 'start', (shaped((PACK, width), BF16), shaped((PACK, w...  4 us
    pallas_call x2, Pallas kernels, body(): call(functools.partial(step_kernel, groups, views, ready), 'ray_space_ste...  3.62 us
    pallas_call x1, Pallas kernels, body(): call(functools.partial(final_kernel, groups, share), 'update', (shaped(fi...  1.48 us
  transfers between devices with their start and end apart: 19, of which 12 were waited for; matrix products, arithmetic and copies ran while one was open for 0% of the time, Pallas kernels for 8%

profile of v5, /device:TPU:0, one launch (start us, length us, event | category | flops | bytes accessed | tf_op | source)
XLA Modules:
  0.0 62.3 jit_solution(10071161240131903821)
XLA Ops:
  0.6 1.2 %take_rays.1 = bf16[2,2,1024,128]{3,2,1,0:T(8,128)(2,1)S(1)} custom-call(bf16[2,4096,128]{2,1,0:T(8,128)(2,1)} %fine_rays.1, bf16[2,4096,128]{2,1,0:T(8,128)(2,1)} %coarse_rays.1), custom_call_target="tpu_custom_call" | custom-call | flops 1 | bytes 1 | tf_op jit(solution)/shard_map/take_rays/pallas_call | solution.py:614
  1.9 3.0 %collective-permute-start.5 = (bf16[2,2,1024,128]{3,2,1,0:T(8,128)(2,1)S(1)}, bf16[2,2,1024,128]{3,2,1,0:T(8,128)(2,1)S(1)}, u32[]{:S(2)}, u32[]{:S(2)}) collective-permute-start(bf16[2,2,1024,128]{3,2,1,0:T(8,128)(2,1)S(1)} %take_rays.1), channel_id=1, source_target_pairs={{0,1},{1,0},{2,3},{3,2},{4,5},{5,4},{6,7},{7,6},{8,9},{9,8},{10,11... | collective-permute-start | bytes 3145736 | tf_op jit(solution)/shard_map/ppermute | solution.py:57
  4.9 4.0 %start.1 = (bf16[16,1280]{1,0:T(8,128)(2,1)S(1)}, bf16[16,1280]{1,0:T(8,128)(2,1)S(1)}, bf16[32,256]{1,0:T(8,128)(2,1)S(1)}, f32[64,256]{1,0:T(8,128)S(1)}, bf16...) custom-call(bf16[2,4096,128]{2,1,0:T(8,128)(2,1)} %fine_rays.1, bf16[2,4096,128]{2,1,0:T(8,128)(2,1)} %coarse_rays.1, ...), custom_call_target="tpu_custom_call" | custom-call | flops 1 | bytes 1 | tf_op jit(solution)/shard_map/start/pallas_call | solution.py:580
  9.0 0.5 collective-permute-start
  9.5 0.7 %collective-permute-done.8.received = bf16[16,1280]{1,0:T(8,128)(2,1)S(1)} collective-permute-done((bf16[16,1280]{1,0:T(8,128)(2,1)S(1)}, bf16[16,1280]{1,0:T(8,128)(2,1)S(1)}, u32[]{:S(2)}, u32[]{:S(2)}) %collective-permute-start.8) | collective-permute-done | bytes 40992 | tf_op jit(solution)/shard_map/ppermute | solution.py:57
  10.2 2.7 %collective-permute-start.9 = (bf16[2,16,1280]{2,1,0:T(8,128)(2,1)S(1)}, bf16[2,16,1280]{2,1,0:T(8,128)(2,1)S(1)}, u32[]{:S(2)}, u32[]{:S(2)}) collective-permute-start(bf16[2,16,1280]{2,1,0:T(8,128)(2,1)S(1)} %pair.1), channel_id=1, source_target_pairs={{0,16},{2,18},{4,20},{6,22},{8,24},{10,26},{12,28},{14,30},{16,0},... | collective-permute-start | bytes 245768 | tf_op jit(solution)/shard_map/ppermute | solution.py:57
  12.9 1.6 %collective-permute-start.1 = (bf16[96,256]{1,0:T(8,128)(2,1)S(1)}, bf16[96,256]{1,0:T(8,128)(2,1)S(1)}, u32[]{:S(2)}, u32[]{:S(2)}) collective-permute-start(bf16[96,256]{1,0:T(8,128)(2,1)S(1)} %get-tuple-element.33.mine), channel_id=1, source_target_pairs={{0,4},{2,6},{4,0},{6,2},{8,12},{10,14},{12,8},{14,10},{16,20},{18,... | collective-permute-start | bytes 147464 | tf_op jit(solution)/shard_map/ppermute | solution.py:57
  14.4 2.6 %collective-permute-done.1.received = bf16[96,256]{1,0:T(8,128)(2,1)S(1)} collective-permute-done((bf16[96,256]{1,0:T(8,128)(2,1)S(1)}, bf16[96,256]{1,0:T(8,128)(2,1)S(1)}, u32[]{:S(2)}, u32[]{:S(2)}) %collective-permute-start.1) | collective-permute-done | bytes 49184 | tf_op jit(solution)/shard_map/ppermute | solution.py:57
  17.5 1.6 %collective-permute-start.10 = (bf16[4,16,1280]{2,1,0:T(8,128)(2,1)S(1)}, bf16[4,16,1280]{2,1,0:T(8,128)(2,1)S(1)}, u32[]{:S(2)}, u32[]{:S(2)}) collective-permute-start(bf16[4,16,1280]{2,1,0:T(8,128)(2,1)S(1)} %pad_maximum_fusion.1), channel_id=1, source_target_pairs={{0,8},{2,10},{4,12},{6,14},{8,0},{10,2},{12,4},{14,6},{16,24},{18,... | collective-permute-start | bytes 491528 | tf_op jit(solution)/shard_map/ppermute | solution.py:57
  19.1 3.3 %collective-permute-done.2.received = bf16[128,256]{1,0:T(8,128)(2,1)S(1)} collective-permute-done((bf16[128,256]{1,0:T(8,128)(2,1)S(1)}, bf16[128,256]{1,0:T(8,128)(2,1)S(1)}, u32[]{:S(2)}, u32[]{:S(2)}) %collective-permute-start.2) | collective-permute-done | bytes 65568 | tf_op jit(solution)/shard_map/ppermute | solution.py:57
  22.4 2.2 %collective-permute-start.3 = (bf16[192,256]{1,0:T(8,128)(2,1)S(1)}, bf16[192,256]{1,0:T(8,128)(2,1)S(1)}, u32[]{:S(2)}, u32[]{:S(2)}) collective-permute-start(bf16[192,256]{1,0:T(8,128)(2,1)S(1)} %get-tuple-element.37.mine), channel_id=1, source_target_pairs={{0,8},{2,10},{4,12},{6,14},{8,0},{10,2},{12,4},{14,6},{16,24},{18,... | collective-permute-start | bytes 294920 | tf_op jit(solution)/shard_map/ppermute | solution.py:57
  24.6 2.6 %collective-permute-done.3.received = bf16[192,256]{1,0:T(8,128)(2,1)S(1)} collective-permute-done((bf16[192,256]{1,0:T(8,128)(2,1)S(1)}, bf16[192,256]{1,0:T(8,128)(2,1)S(1)}, u32[]{:S(2)}, u32[]{:S(2)}) %collective-permute-start.3) | collective-permute-done | bytes 98336 | tf_op jit(solution)/shard_map/ppermute | solution.py:57
  27.2 0.6 %join_hop.5 = (f32[64,256]{1,0:T(8,128)}, bf16[384,256]{1,0:T(8,128)(2,1)S(1)}) custom-call(f32[64,256]{1,0:T(8,128)S(1)} %get-tuple-element.36.q, bf16[192,256]{1,0:T(8,128)(2,1)S(1)} %get-tuple-element.37.mine, bf16[192,256]{1,0:T(8,128)(2,1)S(1)} %collective-permute-done.3.received), custom_call_target="tpu_custom_call" | custom-call | flops 1 | bytes 1 | tf_op jit(solution)/shard_map/join_hop/pallas_call | solution.py:657
  27.9 0.5 collective-permute-start.4
  28.4 1.6 %collective-permute-start.11 = (bf16[8,16,1280]{2,1,0:T(8,128)(2,1)S(1)}, bf16[8,16,1280]{2,1,0:T(8,128)(2,1)S(1)}, u32[]{:S(2)}, u32[]{:S(2)}) collective-permute-start(bf16[8,16,1280]{2,1,0:T(8,128)(2,1)S(1)} %pad_maximum_fusion.mine), channel_id=1, source_target_pairs={{0,4},{2,6},{4,0},{6,2},{8,12},{10,14},{12,8},{14,10},{16,20},{18,... | collective-permute-start | bytes 983048 | tf_op jit(solution)/shard_map/ppermute | solution.py:57
  30.0 3.6 %collective-permute-done.4.refs_1_ = bf16[384,256]{1,0:T(8,128)(2,1)S(1)} collective-permute-done((bf16[384,256]{1,0:T(8,128)(2,1)S(1)}, bf16[384,256]{1,0:T(8,128)(2,1)S(1)}, u32[]{:S(2)}, u32[]{:S(2)}) %collective-permute-start.4) | collective-permute-done | bytes 196640 | tf_op jit(solution)/shard_map/ppermute | solution.py:57
  33.6 0.5 collective-permute-start.7
  34.1 2.2 %collective-permute-done.11.received = bf16[8,16,1280]{2,1,0:T(8,128)(2,1)S(1)} collective-permute-done((bf16[8,16,1280]{2,1,0:T(8,128)(2,1)S(1)}, bf16[8,16,1280]{2,1,0:T(8,128)(2,1)S(1)}, u32[]{:S(2)}, u32[]{:S(2)}) %collective-permute-start.11) | collective-permute-done | bytes 327712 | tf_op jit(solution)/shard_map/ppermute | solution.py:57
  37.2 1.8 %ray_space_step.2.mine = bf16[2,128,256]{2,1,0:T(8,128)(2,1)S(1)} custom-call(bf16[2,64,256]{2,1,0:T(8,128)(2,1)S(1)} %get-tuple-element.45.refs_0_, bf16[2,256,256]{2,1,0:T(8,128)(2,1)S(1)} %get-tuple-element.46.refs_1_, bf16[2,2,128,64]{3,2,1,0:T(8,128)(2,1)S(1)} %get-tuple-element.47.refs_2_.refs_5_, ...), custom_call_target="tpu_custom_call" | custom-call | flops 1 | bytes 1 | tf_op jit(solution)/shard_map/ray_space_step/pallas_call | solution.py:720
  39.0 1.3 %collective-permute-done.12.received = bf16[2,128,256]{2,1,0:T(8,128)(2,1)S(1)} collective-permute-done((bf16[2,128,256]{2,1,0:T(8,128)(2,1)S(1)}, bf16[2,128,256]{2,1,0:T(8,128)(2,1)S(1)}, u32[]{:S(2)}, u32[]{:S(2)}) %collective-permute-start.12) | collective-permute-done | bytes 131104 | tf_op jit(solution)/shard_map/ppermute | solution.py:57
  40.4 1.0 %collective-permute-start.13 = (bf16[2,128,256]{2,1,0:T(8,128)(2,1)S(1)}, bf16[2,128,256]{2,1,0:T(8,128)(2,1)S(1)}, u32[]{:S(2)}, u32[]{:S(2)}) collective-permute-start(bf16[2,128,256]{2,1,0:T(8,128)(2,1)S(1)} %add.4.mine), channel_id=1, source_target_pairs={{0,1},{1,0},{2,3},{3,2},{4,5},{5,4},{6,7},{7,6},{8,9},{9,8},{10,11... | collective-permute-start | bytes 393224 | tf_op jit(solution)/shard_map/ppermute | solution.py:57
  41.5 4.6 %collective-permute-done.13.received = bf16[2,128,256]{2,1,0:T(8,128)(2,1)S(1)} collective-permute-done((bf16[2,128,256]{2,1,0:T(8,128)(2,1)S(1)}, bf16[2,128,256]{2,1,0:T(8,128)(2,1)S(1)}, u32[]{:S(2)}, u32[]{:S(2)}) %collective-permute-start.13) | collective-permute-done | bytes 131104 | tf_op jit(solution)/shard_map/ppermute | solution.py:57
  46.1 1.9 %ray_space_step.3.mine = bf16[2,128,256]{2,1,0:T(8,128)(2,1)S(1)} custom-call(f32[2,128,256]{2,1,0:T(8,128)S(1)} %get-tuple-element.41.q.refs_0_, bf16[2,128,256]{2,1,0:T(8,128)(2,1)S(1)} %add.5.refs_1_.refs_0_, f32[2,128,256]{2,1,0:T(8,128)S(1)} %get-tuple-element.42.weights.refs_2_, bf16[2,64,256]{2,1,0:T(8,128)(2,1)S(1)} %get-tuple-element.43.fine_depth.refs_3_, ...), custom_call_target="tpu_custom_call" | custom-call | flops 1 | bytes 1 | tf_op jit(solution)/shard_map/ray_space_step/pallas_call | solution.py:720
  48.1 1.3 %collective-permute-done.14.received = bf16[2,128,256]{2,1,0:T(8,128)(2,1)S(1)} collective-permute-done((bf16[2,128,256]{2,1,0:T(8,128)(2,1)S(1)}, bf16[2,128,256]{2,1,0:T(8,128)(2,1)S(1)}, u32[]{:S(2)}, u32[]{:S(2)}) %collective-permute-start.14) | collective-permute-done | bytes 131104 | tf_op jit(solution)/shard_map/ppermute | solution.py:57
  49.5 1.0 %collective-permute-start.15 = (bf16[2,128,256]{2,1,0:T(8,128)(2,1)S(1)}, bf16[2,128,256]{2,1,0:T(8,128)(2,1)S(1)}, u32[]{:S(2)}, u32[]{:S(2)}) collective-permute-start(bf16[2,128,256]{2,1,0:T(8,128)(2,1)S(1)} %add.6.mine), channel_id=1, source_target_pairs={{0,1},{1,0},{2,3},{3,2},{4,5},{5,4},{6,7},{7,6},{8,9},{9,8},{10,11... | collective-permute-start | bytes 393224 | tf_op jit(solution)/shard_map/ppermute | solution.py:57
  50.5 4.6 %collective-permute-done.15.received = bf16[2,128,256]{2,1,0:T(8,128)(2,1)S(1)} collective-permute-done((bf16[2,128,256]{2,1,0:T(8,128)(2,1)S(1)}, bf16[2,128,256]{2,1,0:T(8,128)(2,1)S(1)}, u32[]{:S(2)}, u32[]{:S(2)}) %collective-permute-start.15) | collective-permute-done | bytes 131104 | tf_op jit(solution)/shard_map/ppermute | solution.py:57
  55.1 0.9 %back_projection.1 = (bf16[16,1280]{1,0:T(8,128)(2,1)S(1)}, bf16[16,1280]{1,0:T(8,128)(2,1)S(1)}) custom-call(f32[2,128,256]{2,1,0:T(8,128)S(1)} %get-tuple-element.41.q.refs_0_, bf16[2,128,256]{2,1,0:T(8,128)(2,1)S(1)} %add.5.refs_1_.refs_0_, bf16[2,128,256]{2,1,0:T(8,128)(2,1)S(1)} %add.7.refs_1_, f32[2,128,256]{2,1,0:T(8,128)S(1)} %get-tuple-element.42.weights.refs_2_, ...), custom_call_target="tpu_custom_call" | custom-call | flops 1 | bytes 1 | tf_op jit(solution)/shard_map/back_projection/pallas_call | solution.py:731
  56.0 1.0 %collective-permute-start.16 = (bf16[16,1280]{1,0:T(8,128)(2,1)S(1)}, bf16[16,1280]{1,0:T(8,128)(2,1)S(1)}, u32[]{:S(2)}, u32[]{:S(2)}) collective-permute-start(bf16[16,1280]{1,0:T(8,128)(2,1)S(1)} %get-tuple-element.54.refs_0_), channel_id=1, source_target_pairs={{0,1},{1,0},{2,3},{3,2},{4,5},{5,4},{6,7},{7,6},{8,9},{9,8},{10,11... | collective-permute-start | bytes 122888 | tf_op jit(solution)/shard_map/ppermute | solution.py:57
  57.0 1.2 %collective-permute-start.17 = (bf16[16,1280]{1,0:T(8,128)(2,1)S(1)}, bf16[16,1280]{1,0:T(8,128)(2,1)S(1)}, u32[]{:S(2)}, u32[]{:S(2)}) collective-permute-start(bf16[16,1280]{1,0:T(8,128)(2,1)S(1)} %get-tuple-element.55), channel_id=1, source_target_pairs={{0,2},{1,3},{2,0},{3,1},{4,6},{5,7},{6,4},{7,5},{8,10},{9,11},{10,... | collective-permute-start | bytes 122888 | tf_op jit(solution)/shard_map/ppermute | solution.py:57
  58.2 2.0 %collective-permute-done.16.refs_1_ = bf16[16,1280]{1,0:T(8,128)(2,1)S(1)} collective-permute-done((bf16[16,1280]{1,0:T(8,128)(2,1)S(1)}, bf16[16,1280]{1,0:T(8,128)(2,1)S(1)}, u32[]{:S(2)}, u32[]{:S(2)}) %collective-permute-start.16) | collective-permute-done | bytes 40992 | tf_op jit(solution)/shard_map/ppermute | solution.py:57
  60.1 0.6 collective-permute-done.18.refs_3_
  60.8 1.5 %update.1 = (f32[4,4096]{1,0:T(4,128)}, f32[16,4096]{1,0:T(8,128)}) custom-call(bf16[16,1280]{1,0:T(8,128)(2,1)S(1)} %get-tuple-element.54.refs_0_, bf16[16,1280]{1,0:T(8,128)(2,1)S(1)} %collective-permute-done.16.refs_1_, bf16[16,1280]{1,0:T(8,128)(2,1)S(1)} %collective-permute-done.17.refs_2_, bf16[16,1280]{1,0:T(8,128)(2,1)S(1)} %collective-permute-done.18.refs_3_, ...), custom_call_target="tpu_custom_call" | custom-call | flops 1 | bytes 1 | tf_op jit(solution)/shard_map/update/pallas_call | solution.py:740
  (37 shorter events, 1.8 us)
Async XLA Ops:
  1.9 31.7 %collective-permute-start.5 = (bf16[2,2,1024,128]{3,2,1,0:T(8,128)(2,1)S(1)}, bf16[2,2,1024,128]{3,2,1,0:T(8,128)(2,1)S(1)}, u32[]{:S(2)}, u32[]{:S(2)}) collective-permute-start(bf16[2,2,1024,128]{3,2,1,0:T(8,128)(2,1)S(1)} %take_rays.1), channel_id=1, source_target_pairs={{0,1},{1,0},{2,3},{3,2},{4,5},{5,4},{6,7},{7,6},{8,9},{9,8},{10,11... | collective-permute-start | bytes 3145736 | tf_op jit(solution)/shard_map/ppermute | solution.py:57
  8.9 1.3 %collective-permute-start.8 = (bf16[16,1280]{1,0:T(8,128)(2,1)S(1)}, bf16[16,1280]{1,0:T(8,128)(2,1)S(1)}, u32[]{:S(2)}, u32[]{:S(2)}) collective-permute-start(bf16[16,1280]{1,0:T(8,128)(2,1)S(1)} %get-tuple-element.50), channel_id=1, source_target_pairs={{0,2},{2,0},{4,6},{6,4},{8,10},{10,8},{12,14},{14,12},{16,18},{18,... | collective-permute-start | bytes 122888 | tf_op jit(solution)/shard_map/ppermute | solution.py:57
  9.0 3.9 %collective-permute-start = (bf16[64,256]{1,0:T(8,128)(2,1)S(1)}, bf16[64,256]{1,0:T(8,128)(2,1)S(1)}, u32[]{:S(2)}, u32[]{:S(2)}) collective-permute-start(bf16[64,256]{1,0:T(8,128)(2,1)S(1)} %get-tuple-element.30), channel_id=1, source_target_pairs={{0,2},{2,0},{4,6},{6,4},{8,10},{10,8},{12,14},{14,12},{16,18},{18,... | collective-permute-start | bytes 98312 | tf_op jit(solution)/shard_map/ppermute | solution.py:57
  10.2 7.2 %collective-permute-start.9 = (bf16[2,16,1280]{2,1,0:T(8,128)(2,1)S(1)}, bf16[2,16,1280]{2,1,0:T(8,128)(2,1)S(1)}, u32[]{:S(2)}, u32[]{:S(2)}) collective-permute-start(bf16[2,16,1280]{2,1,0:T(8,128)(2,1)S(1)} %pair.1), channel_id=1, source_target_pairs={{0,16},{2,18},{4,20},{6,22},{8,24},{10,26},{12,28},{14,30},{16,0},... | collective-permute-start | bytes 245768 | tf_op jit(solution)/shard_map/ppermute | solution.py:57
  12.9 4.2 %collective-permute-start.1 = (bf16[96,256]{1,0:T(8,128)(2,1)S(1)}, bf16[96,256]{1,0:T(8,128)(2,1)S(1)}, u32[]{:S(2)}, u32[]{:S(2)}) collective-permute-start(bf16[96,256]{1,0:T(8,128)(2,1)S(1)} %get-tuple-element.33.mine), channel_id=1, source_target_pairs={{0,4},{2,6},{4,0},{6,2},{8,12},{10,14},{12,8},{14,10},{16,20},{18,... | collective-permute-start | bytes 147464 | tf_op jit(solution)/shard_map/ppermute | solution.py:57
  17.1 5.3 %collective-permute-start.2 = (bf16[128,256]{1,0:T(8,128)(2,1)S(1)}, bf16[128,256]{1,0:T(8,128)(2,1)S(1)}, u32[]{:S(2)}, u32[]{:S(2)}) collective-permute-start(bf16[128,256]{1,0:T(8,128)(2,1)S(1)} %get-tuple-element.35.mine), channel_id=1, source_target_pairs={{0,16},{2,18},{4,20},{6,22},{8,24},{10,26},{12,28},{14,30},{16,0},... | collective-permute-start | bytes 196616 | tf_op jit(solution)/shard_map/ppermute | solution.py:57
  17.5 10.9 %collective-permute-start.10 = (bf16[4,16,1280]{2,1,0:T(8,128)(2,1)S(1)}, bf16[4,16,1280]{2,1,0:T(8,128)(2,1)S(1)}, u32[]{:S(2)}, u32[]{:S(2)}) collective-permute-start(bf16[4,16,1280]{2,1,0:T(8,128)(2,1)S(1)} %pad_maximum_fusion.1), channel_id=1, source_target_pairs={{0,8},{2,10},{4,12},{6,14},{8,0},{10,2},{12,4},{14,6},{16,24},{18,... | collective-permute-start | bytes 491528 | tf_op jit(solution)/shard_map/ppermute | solution.py:57
  22.4 4.8 %collective-permute-start.3 = (bf16[192,256]{1,0:T(8,128)(2,1)S(1)}, bf16[192,256]{1,0:T(8,128)(2,1)S(1)}, u32[]{:S(2)}, u32[]{:S(2)}) collective-permute-start(bf16[192,256]{1,0:T(8,128)(2,1)S(1)} %get-tuple-element.37.mine), channel_id=1, source_target_pairs={{0,8},{2,10},{4,12},{6,14},{8,0},{10,2},{12,4},{14,6},{16,24},{18,... | collective-permute-start | bytes 294920 | tf_op jit(solution)/shard_map/ppermute | solution.py:57
  27.9 5.7 %collective-permute-start.4 = (bf16[384,256]{1,0:T(8,128)(2,1)S(1)}, bf16[384,256]{1,0:T(8,128)(2,1)S(1)}, u32[]{:S(2)}, u32[]{:S(2)}) collective-permute-start(bf16[384,256]{1,0:T(8,128)(2,1)S(1)} %get-tuple-element.38.refs_0_), channel_id=1, source_target_pairs={{0,1},{1,0},{2,3},{3,2},{4,5},{5,4},{6,7},{7,6},{8,9},{9,8},{10,11... | collective-permute-start | bytes 589832 | tf_op jit(solution)/shard_map/ppermute | solution.py:57
  28.4 7.9 %collective-permute-start.11 = (bf16[8,16,1280]{2,1,0:T(8,128)(2,1)S(1)}, bf16[8,16,1280]{2,1,0:T(8,128)(2,1)S(1)}, u32[]{:S(2)}, u32[]{:S(2)}) collective-permute-start(bf16[8,16,1280]{2,1,0:T(8,128)(2,1)S(1)} %pad_maximum_fusion.mine), channel_id=1, source_target_pairs={{0,4},{2,6},{4,0},{6,2},{8,12},{10,14},{12,8},{14,10},{16,20},{18,... | collective-permute-start | bytes 983048 | tf_op jit(solution)/shard_map/ppermute | solution.py:57
  33.6 3.0 %collective-permute-start.6 = (bf16[2,256,256]{2,1,0:T(8,128)(2,1)S(1)}, bf16[2,256,256]{2,1,0:T(8,128)(2,1)S(1)}, u32[]{:S(2)}, u32[]{:S(2)}) collective-permute-start(bf16[2,256,256]{2,1,0:T(8,128)(2,1)S(1)} %get-tuple-element.39.mine), channel_id=1, source_target_pairs={{0,2},{2,0},{4,6},{6,4},{8,10},{10,8},{12,14},{14,12},{16,18},{18,... | collective-permute-start | bytes 786440 | tf_op jit(solution)/shard_map/ppermute | solution.py:57
  33.6 2.9 %collective-permute-start.7 = (f32[2,64,256]{2,1,0:T(8,128)S(1)}, f32[2,64,256]{2,1,0:T(8,128)S(1)}, u32[]{:S(2)}, u32[]{:S(2)}) collective-permute-start(f32[2,64,256]{2,1,0:T(8,128)S(1)} %get-tuple-element.40.q_mine), channel_id=1, source_target_pairs={{0,2},{2,0},{4,6},{6,4},{8,10},{10,8},{12,14},{14,12},{16,18},{18,... | collective-permute-start | bytes 393224 | tf_op jit(solution)/shard_map/ppermute | solution.py:57
  39.0 1.4 %collective-permute-start.12 = (bf16[2,128,256]{2,1,0:T(8,128)(2,1)S(1)}, bf16[2,128,256]{2,1,0:T(8,128)(2,1)S(1)}, u32[]{:S(2)}, u32[]{:S(2)}) collective-permute-start(bf16[2,128,256]{2,1,0:T(8,128)(2,1)S(1)} %ray_space_step.2.mine), channel_id=1, source_target_pairs={{0,2},{2,0},{4,6},{6,4},{8,10},{10,8},{12,14},{14,12},{16,18},{18,... | collective-permute-start | bytes 393224 | tf_op jit(solution)/shard_map/ppermute | solution.py:57
  40.4 5.6 %collective-permute-start.13 = (bf16[2,128,256]{2,1,0:T(8,128)(2,1)S(1)}, bf16[2,128,256]{2,1,0:T(8,128)(2,1)S(1)}, u32[]{:S(2)}, u32[]{:S(2)}) collective-permute-start(bf16[2,128,256]{2,1,0:T(8,128)(2,1)S(1)} %add.4.mine), channel_id=1, source_target_pairs={{0,1},{1,0},{2,3},{3,2},{4,5},{5,4},{6,7},{7,6},{8,9},{9,8},{10,11... | collective-permute-start | bytes 393224 | tf_op jit(solution)/shard_map/ppermute | solution.py:57
  47.9 12.8 %copy-start = (f32[16,4096]{1,0:T(8,128)S(1)}, f32[16,4096]{1,0:T(8,128)}, u32[]{:S(2)}) copy-start(f32[16,4096]{1,0:T(8,128)} %refs_5_.1) | copy-start | bytes 786436
  48.0 12.8 %copy-start.1 = (f32[16,4096]{1,0:T(8,128)S(1)}, f32[16,4096]{1,0:T(8,128)}, u32[]{:S(2)}) copy-start(f32[16,4096]{1,0:T(8,128)} %refs_7_.1) | copy-start | bytes 786436
  48.0 12.8 %copy-start.2 = (f32[4,4096]{1,0:T(4,128)S(1)}, f32[4,4096]{1,0:T(4,128)}, u32[]{:S(2)}) copy-start(f32[4,4096]{1,0:T(4,128)} %refs_4_.1) | copy-start | bytes 196612
  48.0 12.8 %copy-start.3 = (f32[4,4096]{1,0:T(4,128)S(1)}, f32[4,4096]{1,0:T(4,128)}, u32[]{:S(2)}) copy-start(f32[4,4096]{1,0:T(4,128)} %refs_6_.1) | copy-start | bytes 196612
  48.0 12.8 %copy-start.4 = (s32[1,8]{1,0:T(1,128)S(1)}, s32[1,8]{1,0:T(1,128)}, u32[]{:S(2)}) copy-start(s32[1,8]{1,0:T(1,128)} %refs_8_.1) | copy-start | bytes 100
  48.0 1.4 %collective-permute-start.14 = (bf16[2,128,256]{2,1,0:T(8,128)(2,1)S(1)}, bf16[2,128,256]{2,1,0:T(8,128)(2,1)S(1)}, u32[]{:S(2)}, u32[]{:S(2)}) collective-permute-start(bf16[2,128,256]{2,1,0:T(8,128)(2,1)S(1)} %ray_space_step.3.mine), channel_id=1, source_target_pairs={{0,2},{2,0},{4,6},{6,4},{8,10},{10,8},{12,14},{14,12},{16,18},{18,... | collective-permute-start | bytes 393224 | tf_op jit(solution)/shard_map/ppermute | solution.py:57
  49.5 5.6 %collective-permute-start.15 = (bf16[2,128,256]{2,1,0:T(8,128)(2,1)S(1)}, bf16[2,128,256]{2,1,0:T(8,128)(2,1)S(1)}, u32[]{:S(2)}, u32[]{:S(2)}) collective-permute-start(bf16[2,128,256]{2,1,0:T(8,128)(2,1)S(1)} %add.6.mine), channel_id=1, source_target_pairs={{0,1},{1,0},{2,3},{3,2},{4,5},{5,4},{6,7},{7,6},{8,9},{9,8},{10,11... | collective-permute-start | bytes 393224 | tf_op jit(solution)/shard_map/ppermute | solution.py:57
  56.0 4.2 %collective-permute-start.16 = (bf16[16,1280]{1,0:T(8,128)(2,1)S(1)}, bf16[16,1280]{1,0:T(8,128)(2,1)S(1)}, u32[]{:S(2)}, u32[]{:S(2)}) collective-permute-start(bf16[16,1280]{1,0:T(8,128)(2,1)S(1)} %get-tuple-element.54.refs_0_), channel_id=1, source_target_pairs={{0,1},{1,0},{2,3},{3,2},{4,5},{5,4},{6,7},{7,6},{8,9},{9,8},{10,11... | collective-permute-start | bytes 122888 | tf_op jit(solution)/shard_map/ppermute | solution.py:57
  57.0 3.8 %collective-permute-start.18 = (bf16[16,1280]{1,0:T(8,128)(2,1)S(1)}, bf16[16,1280]{1,0:T(8,128)(2,1)S(1)}, u32[]{:S(2)}, u32[]{:S(2)}) collective-permute-start(bf16[16,1280]{1,0:T(8,128)(2,1)S(1)} %get-tuple-element.55), channel_id=1, source_target_pairs={{0,3},{1,2},{2,1},{3,0},{4,7},{5,6},{6,5},{7,4},{8,11},{9,10},{10,... | collective-permute-start | bytes 122888 | tf_op jit(solution)/shard_map/ppermute | solution.py:57
  57.0 3.8 %collective-permute-start.17 = (bf16[16,1280]{1,0:T(8,128)(2,1)S(1)}, bf16[16,1280]{1,0:T(8,128)(2,1)S(1)}, u32[]{:S(2)}, u32[]{:S(2)}) collective-permute-start(bf16[16,1280]{1,0:T(8,128)(2,1)S(1)} %get-tuple-element.55), channel_id=1, source_target_pairs={{0,2},{1,3},{2,0},{3,1},{4,6},{5,7},{6,4},{7,5},{8,10},{9,11},{10,... | collective-permute-start | bytes 122888 | tf_op jit(solution)/shard_map/ppermute | solution.py:57

commit v6 on v5

--- a/solution.py
+++ b/solution.py
@@ -189,8 +189,8 @@
     coarse_axial_in,
     measured_in,
     ray_weight_in,
-    blocks,
-    hits,
+    blocks_in,
+    hits_in,
     mine,
     theirs,
     rows,
@@ -207,6 +207,8 @@
     coarse_axial,
     measured,
     ray_weight,
+    blocks,
+    hits,
     scratch,
     sems,
     chunk_sems,
@@ -220,6 +222,8 @@
         (coarse_axial_in, coarse_axial),
         (ray_weight_in, ray_weight),
         (measured_in, measured),
+        (blocks_in, blocks),
+        (hits_in, hits),
         (fine_weight_in, fine_weight),
         (coarse_weight_in, coarse_weight),
     )
@@ -243,8 +247,8 @@
     groups = half // share
     held = pl.ds(share_start(cells, groups), share)
     outgoing = [
-        fetch(fine_rays_in.at[:, held, :], own_rays.at[0], sems.at[6]),
-        fetch(coarse_rays_in.at[:, held, :], own_rays.at[1], sems.at[7]),
+        fetch(fine_rays_in.at[:, held, :], own_rays.at[0], sems.at[8]),
+        fetch(coarse_rays_in.at[:, held, :], own_rays.at[1], sems.at[9]),
     ]
     for copy in others:
         copy.wait()
@@ -365,7 +369,8 @@
         out[g] = dot(to_weight, side, ((1,), (0,)))[:, :total]
 
 
-def weights_kernel(fz, order, mine, received, coarse_out, fine_out):
+def weights_kernel(fz, order, mine, received, *refs):
+    coarse_out, fine_out = refs[-2:]
     held = mine.shape[0]
     slabs = 2 * held
     count = slabs * PACK
@@ -390,12 +395,20 @@
                 ].astype(BF16)
 
 
+def whole_rows(mine, received):
+    lead = lax.axis_index("slab") % 2 == 0
+    ours, others = mine.astype(F32), received.astype(F32)
+    return jnp.concatenate(
+        [jnp.where(lead, ours, others), jnp.where(lead, others, ours)], axis=0
+    )
+
+
 def residuals(q, deltas, weights):
     groups = q.shape[0]
     current = [q[g] for g in range(groups)]
     results = [[weights[g] * current[g] for g in range(groups)]]
-    for delta in deltas:
-        current = [current[g] - delta[g].astype(F32) for g in range(groups)]
+    for mine, received in deltas:
+        current = [current[g] - whole_rows(mine[g], received[g]) for g in range(groups)]
         results.append([weights[g] * current[g] for g in range(groups)])
     return results
 
@@ -429,9 +442,9 @@
     if ready:
         spreads = [refs.pop(0), refs.pop(0)]
     else:
-        q, delta, weights, fine_depth, coarse_depth = refs[:5]
-        refs = refs[5:]
-        residual = residuals(q, [delta], weights)[-1]
+        q, mine, received, weights, fine_depth, coarse_depth = refs[:6]
+        refs = refs[6:]
+        residual = residuals(q, [(mine, received)], weights)[-1]
         residual = [r.astype(BF16) for r in residual]
         spreads = [
             [spread(depth[g], residual[g], views).astype(BF16) for g in range(groups)]
@@ -439,11 +452,11 @@
         ]
     turned = refs[:2]
     coarse_weights, fine_weights = refs[2:4]
-    held = refs[4:-1]
-    out = refs[-1]
+    held = refs[4:-3]
+    kept, given, scratch = refs[-3:]
     size = fine_weights.shape[1]
     columns = held[0].shape[3]
-    chunk = min(size, 512)
+    chunk = min(size, 1024)
     results = [None] * groups
     for part in range(2):
         moments = [None] * groups
@@ -469,8 +482,12 @@
             ]
             value = jnp.concatenate(pieces, axis=1)
             results[g] = value if results[g] is None else results[g] + value
+    core = lax.axis_index("slab") % 2
+    rows = kept.shape[1]
     for g in range(groups):
-        out[g] = results[g].astype(BF16)
+        scratch[g] = results[g]
+        kept[g] = scratch[g, pl.ds(pl.multiple_of(core * rows, PACK), rows), :].astype(BF16)
+        given[g] = scratch[g, pl.ds(pl.multiple_of((1 - core) * rows, PACK), rows), :].astype(BF16)
 
 
 def add_kernel(bit, mine, received, out):
@@ -479,12 +496,12 @@
 
 
 def tail_kernel(fz, groups, views, q, *refs):
-    deltas = refs[:2]
-    weights, fine_depth, coarse_depth = refs[2:5]
-    held = refs[5:-2]
+    deltas = [refs[:2], refs[2:4]]
+    weights, fine_depth, coarse_depth = refs[4:7]
+    held = refs[7:-2]
     ours, theirs = refs[-2:]
     size = held[0].shape[2]
-    chunk = min(size, 512)
+    chunk = min(size, 1024)
     lead = lax.axis_index("slab") % 2 == 0
     history = residuals(q, deltas, weights)
     rows = (fz, PACK)
@@ -515,9 +532,13 @@
         out[:, size:] = pack_fine(parts[0]).astype(BF16)
 
 
+def keep_kernel(blocks, out):
+    out[...] = keep_row(blocks, 0, out.shape[1])
+
+
 def final_kernel(groups, size, *refs):
     pieces = refs[: 2 * groups]
-    fine, coarse, fw, cw, blocks, fine_out, coarse_out = refs[2 * groups :]
+    fine, coarse, fw, cw, keep, fine_out, coarse_out = refs[2 * groups :]
     core = lax.axis_index("slab") % 2
     view = lax.axis_index("view")
     fz, cells = fine.shape
@@ -526,9 +547,8 @@
         start = side * (cells // 2) + (view ^ (index % groups)) * size
         start = pl.multiple_of(start, LANES)
         where = pl.ds(start, size)
-        keep = keep_row(blocks, start, size)
         change = piece[:, :size].astype(F32)
-        coarse_out[:, where] = (coarse[:, where] + cw[:, where] * change) * keep
+        coarse_out[:, where] = (coarse[:, where] + cw[:, where] * change) * keep[:, where]
         change = unpack_fine(piece[:, size:].astype(F32), fz, size)
         fine_out[:, where] = fine[:, where] + fw[:, where] * change
 
@@ -588,11 +608,13 @@
                 shaped((det // 2, total), BF16),
                 shaped((2, views, share, columns), BF16),
             ),
-            [HBM] * len(taken) + [SMEM] * 2,
+            [HBM] * (len(taken) + 2),
             scratch_like(*taken)
             + [
+                pltpu.SMEM(margin_blocks.shape, jnp.int32),
+                pltpu.SMEM(ray_hits.shape, jnp.int32),
                 pltpu.VMEM((det, total), F32),
-                pltpu.SemaphoreType.DMA((8,)),
+                pltpu.SemaphoreType.DMA((10,)),
                 pltpu.SemaphoreType.DMA((4, 4)),
             ],
         )(*taken, *in_hbm(margin_blocks, ray_hits))
@@ -688,12 +710,6 @@
             ),
             [VMEM] * 4,
         )(rows, along_slab(rows, 1), q, along_slab(q, 1))
-        coarse_weights, fine_weights = call(
-            functools.partial(weights_kernel, fz, order),
-            "unpack_weights",
-            (shaped((slabs * PACK, share), BF16), shaped((slabs * fz, share), BF16)),
-            [VMEM] * 2,
-        )(*got["weights"])
         spreads = call(
             functools.partial(spread_kernel, views),
             "spread",
@@ -703,13 +719,19 @@
             ),
             [VMEM] * 4,
         )(q, weights, fine_depth, coarse_depth)
+        coarse_weights, fine_weights = call(
+            functools.partial(weights_kernel, fz, order),
+            "unpack_weights",
+            (shaped((slabs * PACK, share), BF16), shaped((slabs * fz, share), BF16)),
+            [VMEM] * 2 + [ANY] * len(spreads),
+        )(*got["weights"], *spreads)
         rays = [own_rays] + got["rays"]
         held = (fine_turned, coarse_turned, coarse_weights, fine_weights, *rays)
         def add(mine, received, bit):
             return call(
                 functools.partial(add_kernel, bit),
                 "add",
-                shaped((groups, det, total), BF16),
+                shaped((groups, rows_half, total), BF16),
                 [VMEM] * 2,
             )(mine, received)
 
@@ -717,16 +739,17 @@
         for ready, inputs in ((True, spreads), (False, None)):
             if not ready:
                 inputs = (q, *deltas, weights, fine_depth, coarse_depth)
-            delta = call(
+            delta, given = call(
                 functools.partial(step_kernel, groups, views, ready),
                 "ray_space_step",
-                shaped((groups, det, total), BF16),
+                (shaped((groups, rows_half, total), BF16),) * 2,
                 [VMEM] * (len(inputs) + len(held)),
+                [pltpu.VMEM((groups, det, total), F32)],
             )(*inputs, *held)
-            delta = add(delta, along_slab(delta, 1), 0)
+            delta = add(delta, along_slab(given, 1), 0)
             for bit in view_bits:
                 delta = add(delta, swap(delta, "view", groups, bit), bit)
-            deltas.append(delta)
+            deltas += [delta, along_slab(delta, 1)]
         inputs = (q, *deltas, weights, fine_depth, coarse_depth, *rays)
         ours, theirs = call(
             functools.partial(tail_kernel, fz, groups, views),
@@ -734,6 +757,7 @@
             (shaped((PACK, width), BF16),) * 2,
             [VMEM] * len(inputs),
         )(*inputs)
+        keep = call(keep_kernel, "keep", shaped((1, cells), F32), [SMEM])(margin_blocks)
         both = ("slab", "view")
         pieces = [ours] + [swap(ours, "view", groups, bits) for bits in range(1, groups)]
         pieces += [swap(theirs, both, slabs * groups, groups | bits) for bits in range(groups)]
@@ -741,14 +765,14 @@
             functools.partial(final_kernel, groups, share),
             "update",
             (shaped(fine_volume.shape, F32), shaped(coarse_volume.shape, F32)),
-            [VMEM] * (2 * groups + 4) + [SMEM],
+            [VMEM] * (2 * groups + 5),
         )(
             *pieces,
             fine_volume,
             coarse_volume,
             fine_cell_weight,
             coarse_cell_weight,
-            margin_blocks,
+            keep,
         )
 
     return body

time: 62.5 us -> 59.8 us (0.957)
  waiting for transfers between devices: 29.4 us -> 27.4 us
  Pallas kernels: 12.9 us -> 11.9 us
    ppermute x19 -> x21, waiting for transfers between devices: 29.4 us -> 27.4 us  [swap(): return lax.ppermute(value, axis, [(i, i ^ bits) for i in range(size)])]
    pallas_call x1, Pallas kernels: 1.48 us -> 0.8 us  [body(): call(functools.partial(final_kernel, groups, share), 'update', (shaped(fi...]
    pallas_call x1, Pallas kernels: 4 us -> 3.33 us  [body(): call(start_kernel, 'start', (shaped((PACK, width), BF16), shaped((PACK, w...]
    ppermute x19 -> x21, starting transfers between devices: 19.1 us -> 19.4 us  [swap(): return lax.ppermute(value, axis, [(i, i ^ bits) for i in range(size)])]
  transfers between devices with their start and end apart: 19 -> 21, of which waited for: 12 -> 15; matrix products, arithmetic and copies ran while one was open for 0% -> 0% of each run, Pallas kernels for 8% -> 9%
where the time goes in v6:
time: 59.8 us; the launch traced here: 59.6 us
  waiting for transfers between devices  27.4 us (46%)
  starting transfers between devices  19.4 us (32%)
  Pallas kernels  11.9 us (20%)
  between operations  0.83 us (1%)
    ppermute x21, waiting for transfers between devices, swap(): return lax.ppermute(value, axis, [(i, i ^ bits) for i in range(size)])  27.4 us
    ppermute x21, starting transfers between devices, swap(): return lax.ppermute(value, axis, [(i, i ^ bits) for i in range(size)])  19.4 us
    pallas_call x2, Pallas kernels, body(): call(functools.partial(step_kernel, groups, views, ready), 'ray_space_ste...  3.41 us
    pallas_call x1, Pallas kernels, body(): call(start_kernel, 'start', (shaped((PACK, width), BF16), shaped((PACK, w...  3.33 us
    pallas_call x1, Pallas kernels, begin(): call(functools.partial(take_kernel, groups, bits), 'take_rays', shaped((2...  1.23 us
  transfers between devices with their start and end apart: 21, of which 15 were waited for; matrix products, arithmetic and copies ran while one was open for 0% of the time, Pallas kernels for 9%

profile of v6, /device:TPU:0, one launch (start us, length us, event | category | flops | bytes accessed | tf_op | source)
XLA Modules:
  0.0 59.6 jit_solution(3896693111738389085)
XLA Ops:
  0.6 1.2 %take_rays.1 = bf16[2,2,1024,128]{3,2,1,0:T(8,128)(2,1)S(1)} custom-call(bf16[2,4096,128]{2,1,0:T(8,128)(2,1)} %fine_rays.1, bf16[2,4096,128]{2,1,0:T(8,128)(2,1)} %coarse_rays.1), custom_call_target="tpu_custom_call" | custom-call | flops 1 | bytes 1 | tf_op jit(solution)/shard_map/take_rays/pallas_call | solution.py:636
  1.9 3.0 %collective-permute-start.5 = (bf16[2,2,1024,128]{3,2,1,0:T(8,128)(2,1)S(1)}, bf16[2,2,1024,128]{3,2,1,0:T(8,128)(2,1)S(1)}, u32[]{:S(2)}, u32[]{:S(2)}) collective-permute-start(bf16[2,2,1024,128]{3,2,1,0:T(8,128)(2,1)S(1)} %take_rays.1), channel_id=1, source_target_pairs={{0,1},{1,0},{2,3},{3,2},{4,5},{5,4},{6,7},{7,6},{8,9},{9,8},{10,11... | collective-permute-start | bytes 3145736 | tf_op jit(solution)/shard_map/ppermute | solution.py:57
  4.9 3.3 %start.1 = (bf16[16,1280]{1,0:T(8,128)(2,1)S(1)}, bf16[16,1280]{1,0:T(8,128)(2,1)S(1)}, bf16[32,256]{1,0:T(8,128)(2,1)S(1)}, f32[64,256]{1,0:T(8,128)S(1)}, bf16...) custom-call(bf16[2,4096,128]{2,1,0:T(8,128)(2,1)} %fine_rays.1, bf16[2,4096,128]{2,1,0:T(8,128)(2,1)} %coarse_rays.1, ...), custom_call_target="tpu_custom_call" | custom-call | flops 1 | bytes 1 | tf_op jit(solution)/shard_map/start/pallas_call | solution.py:600
  8.8 0.7 %collective-permute-done.8.received = bf16[16,1280]{1,0:T(8,128)(2,1)S(1)} collective-permute-done((bf16[16,1280]{1,0:T(8,128)(2,1)S(1)}, bf16[16,1280]{1,0:T(8,128)(2,1)S(1)}, u32[]{:S(2)}, u32[]{:S(2)}) %collective-permute-start.8) | collective-permute-done | bytes 40992 | tf_op jit(solution)/shard_map/ppermute | solution.py:57
  9.6 2.7 %collective-permute-start.9 = (bf16[2,16,1280]{2,1,0:T(8,128)(2,1)S(1)}, bf16[2,16,1280]{2,1,0:T(8,128)(2,1)S(1)}, u32[]{:S(2)}, u32[]{:S(2)}) collective-permute-start(bf16[2,16,1280]{2,1,0:T(8,128)(2,1)S(1)} %pair.1), channel_id=1, source_target_pairs={{0,16},{2,18},{4,20},{6,22},{8,24},{10,26},{12,28},{14,30},{16,0},... | collective-permute-start | bytes 245768 | tf_op jit(solution)/shard_map/ppermute | solution.py:57
  12.2 1.6 %collective-permute-start.1 = (bf16[96,256]{1,0:T(8,128)(2,1)S(1)}, bf16[96,256]{1,0:T(8,128)(2,1)S(1)}, u32[]{:S(2)}, u32[]{:S(2)}) collective-permute-start(bf16[96,256]{1,0:T(8,128)(2,1)S(1)} %get-tuple-element.37.mine), channel_id=1, source_target_pairs={{0,4},{2,6},{4,0},{6,2},{8,12},{10,14},{12,8},{14,10},{16,20},{18,... | collective-permute-start | bytes 147464 | tf_op jit(solution)/shard_map/ppermute | solution.py:57
  13.8 2.6 %collective-permute-done.1.received = bf16[96,256]{1,0:T(8,128)(2,1)S(1)} collective-permute-done((bf16[96,256]{1,0:T(8,128)(2,1)S(1)}, bf16[96,256]{1,0:T(8,128)(2,1)S(1)}, u32[]{:S(2)}, u32[]{:S(2)}) %collective-permute-start.1) | collective-permute-done | bytes 49184 | tf_op jit(solution)/shard_map/ppermute | solution.py:57
  16.8 1.6 %collective-permute-start.10 = (bf16[4,16,1280]{2,1,0:T(8,128)(2,1)S(1)}, bf16[4,16,1280]{2,1,0:T(8,128)(2,1)S(1)}, u32[]{:S(2)}, u32[]{:S(2)}) collective-permute-start(bf16[4,16,1280]{2,1,0:T(8,128)(2,1)S(1)} %pad_maximum_fusion.1), channel_id=1, source_target_pairs={{0,8},{2,10},{4,12},{6,14},{8,0},{10,2},{12,4},{14,6},{16,24},{18,... | collective-permute-start | bytes 491528 | tf_op jit(solution)/shard_map/ppermute | solution.py:57
  18.5 3.3 %collective-permute-done.2.received = bf16[128,256]{1,0:T(8,128)(2,1)S(1)} collective-permute-done((bf16[128,256]{1,0:T(8,128)(2,1)S(1)}, bf16[128,256]{1,0:T(8,128)(2,1)S(1)}, u32[]{:S(2)}, u32[]{:S(2)}) %collective-permute-start.2) | collective-permute-done | bytes 65568 | tf_op jit(solution)/shard_map/ppermute | solution.py:57
  21.8 2.2 %collective-permute-start.3 = (bf16[192,256]{1,0:T(8,128)(2,1)S(1)}, bf16[192,256]{1,0:T(8,128)(2,1)S(1)}, u32[]{:S(2)}, u32[]{:S(2)}) collective-permute-start(bf16[192,256]{1,0:T(8,128)(2,1)S(1)} %get-tuple-element.41.mine), channel_id=1, source_target_pairs={{0,8},{2,10},{4,12},{6,14},{8,0},{10,2},{12,4},{14,6},{16,24},{18,... | collective-permute-start | bytes 294920 | tf_op jit(solution)/shard_map/ppermute | solution.py:57
  23.9 2.6 %collective-permute-done.3.received = bf16[192,256]{1,0:T(8,128)(2,1)S(1)} collective-permute-done((bf16[192,256]{1,0:T(8,128)(2,1)S(1)}, bf16[192,256]{1,0:T(8,128)(2,1)S(1)}, u32[]{:S(2)}, u32[]{:S(2)}) %collective-permute-start.3) | collective-permute-done | bytes 98336 | tf_op jit(solution)/shard_map/ppermute | solution.py:57
  26.5 0.6 %join_hop.5 = (f32[64,256]{1,0:T(8,128)}, bf16[384,256]{1,0:T(8,128)(2,1)S(1)}) custom-call(f32[64,256]{1,0:T(8,128)S(1)} %get-tuple-element.40.q, bf16[192,256]{1,0:T(8,128)(2,1)S(1)} %get-tuple-element.41.mine, bf16[192,256]{1,0:T(8,128)(2,1)S(1)} %collective-permute-done.3.received), custom_call_target="tpu_custom_call" | custom-call | flops 1 | bytes 1 | tf_op jit(solution)/shard_map/join_hop/pallas_call | solution.py:679
  27.2 0.5 collective-permute-start.4
  27.7 1.6 %collective-permute-start.11 = (bf16[8,16,1280]{2,1,0:T(8,128)(2,1)S(1)}, bf16[8,16,1280]{2,1,0:T(8,128)(2,1)S(1)}, u32[]{:S(2)}, u32[]{:S(2)}) collective-permute-start(bf16[8,16,1280]{2,1,0:T(8,128)(2,1)S(1)} %pad_maximum_fusion.mine), channel_id=1, source_target_pairs={{0,4},{2,6},{4,0},{6,2},{8,12},{10,14},{12,8},{14,10},{16,20},{18,... | collective-permute-start | bytes 983048 | tf_op jit(solution)/shard_map/ppermute | solution.py:57
  29.3 3.6 %collective-permute-done.4.refs_1_ = bf16[384,256]{1,0:T(8,128)(2,1)S(1)} collective-permute-done((bf16[384,256]{1,0:T(8,128)(2,1)S(1)}, bf16[384,256]{1,0:T(8,128)(2,1)S(1)}, u32[]{:S(2)}, u32[]{:S(2)}) %collective-permute-start.4) | collective-permute-done | bytes 196640 | tf_op jit(solution)/shard_map/ppermute | solution.py:57
  33.5 1.2 %collective-permute-done.7.q_theirs = f32[2,64,256]{2,1,0:T(8,128)S(1)} collective-permute-done((f32[2,64,256]{2,1,0:T(8,128)S(1)}, f32[2,64,256]{2,1,0:T(8,128)S(1)}, u32[]{:S(2)}, u32[]{:S(2)}) %collective-permute-start.7) | collective-permute-done | bytes 131104 | tf_op jit(solution)/shard_map/ppermute | solution.py:57
  35.9 1.6 %ray_space_step.2 = (bf16[2,64,256]{2,1,0:T(8,128)(2,1)S(1)}, bf16[2,64,256]{2,1,0:T(8,128)(2,1)S(1)}) custom-call(bf16[2,64,256]{2,1,0:T(8,128)(2,1)S(1)} %get-tuple-element.49.refs_0_, bf16[2,256,256]{2,1,0:T(8,128)(2,1)S(1)} %get-tuple-element.50.refs_1_, bf16[2,2,128,64]{3,2,1,0:T(8,128)(2,1)S(1)} %get-tuple-element.51.refs_2_.refs_6_, ...), custom_call_target="tpu_custom_call" | custom-call | flops 1 | bytes 1 | tf_op jit(solution)/shard_map/ray_space_step/pallas_call | solution.py:742
  37.6 1.2 %collective-permute-done.12.received = bf16[2,64,256]{2,1,0:T(8,128)(2,1)S(1)} collective-permute-done((bf16[2,64,256]{2,1,0:T(8,128)(2,1)S(1)}, bf16[2,64,256]{2,1,0:T(8,128)(2,1)S(1)}, u32[]{:S(2)}, u32[]{:S(2)}) %collective-permute-start.12) | collective-permute-done | bytes 65568 | tf_op jit(solution)/shard_map/ppermute | solution.py:57
  38.9 1.0 %collective-permute-start.13 = (bf16[2,64,256]{2,1,0:T(8,128)(2,1)S(1)}, bf16[2,64,256]{2,1,0:T(8,128)(2,1)S(1)}, u32[]{:S(2)}, u32[]{:S(2)}) collective-permute-start(bf16[2,64,256]{2,1,0:T(8,128)(2,1)S(1)} %add.4.mine), channel_id=1, source_target_pairs={{0,1},{1,0},{2,3},{3,2},{4,5},{5,4},{6,7},{7,6},{8,9},{9,8},{10,11... | collective-permute-start | bytes 196616 | tf_op jit(solution)/shard_map/ppermute | solution.py:57
  39.9 3.3 %collective-permute-done.13.received = bf16[2,64,256]{2,1,0:T(8,128)(2,1)S(1)} collective-permute-done((bf16[2,64,256]{2,1,0:T(8,128)(2,1)S(1)}, bf16[2,64,256]{2,1,0:T(8,128)(2,1)S(1)}, u32[]{:S(2)}, u32[]{:S(2)}) %collective-permute-start.13) | collective-permute-done | bytes 65568 | tf_op jit(solution)/shard_map/ppermute | solution.py:57
  43.3 1.2 %collective-permute-done.14.refs_2_.refs_1_ = bf16[2,64,256]{2,1,0:T(8,128)(2,1)S(1)} collective-permute-done((bf16[2,64,256]{2,1,0:T(8,128)(2,1)S(1)}, bf16[2,64,256]{2,1,0:T(8,128)(2,1)S(1)}, u32[]{:S(2)}, u32[]{:S(2)}) %collective-permute-start.14) | collective-permute-done | bytes 65568 | tf_op jit(solution)/shard_map/ppermute | solution.py:57
  44.6 1.8 %ray_space_step.3 = (bf16[2,64,256]{2,1,0:T(8,128)(2,1)S(1)}, bf16[2,64,256]{2,1,0:T(8,128)(2,1)S(1)}) custom-call(f32[2,128,256]{2,1,0:T(8,128)S(1)} %get-tuple-element.45.q.refs_0_, bf16[2,64,256]{2,1,0:T(8,128)(2,1)S(1)} %add.5.refs_1_.refs_0_, bf16[2,64,256]{2,1,0:T(8,128)(2,1)S(1)} %collective-permute-done.14.refs_2_.refs_1_, ...), custom_call_target="tpu_custom_call" | custom-call | flops 1 | bytes 1 | tf_op jit(solution)/shard_map/ray_space_step/pallas_call | solution.py:742
  46.6 1.1 %collective-permute-done.15.received = bf16[2,64,256]{2,1,0:T(8,128)(2,1)S(1)} collective-permute-done((bf16[2,64,256]{2,1,0:T(8,128)(2,1)S(1)}, bf16[2,64,256]{2,1,0:T(8,128)(2,1)S(1)}, u32[]{:S(2)}, u32[]{:S(2)}) %collective-permute-start.15) | collective-permute-done | bytes 65568 | tf_op jit(solution)/shard_map/ppermute | solution.py:57
  47.7 1.0 %collective-permute-start.16 = (bf16[2,64,256]{2,1,0:T(8,128)(2,1)S(1)}, bf16[2,64,256]{2,1,0:T(8,128)(2,1)S(1)}, u32[]{:S(2)}, u32[]{:S(2)}) collective-permute-start(bf16[2,64,256]{2,1,0:T(8,128)(2,1)S(1)} %add.6.mine), channel_id=1, source_target_pairs={{0,1},{1,0},{2,3},{3,2},{4,5},{5,4},{6,7},{7,6},{8,9},{9,8},{10,11... | collective-permute-start | bytes 196616 | tf_op jit(solution)/shard_map/ppermute | solution.py:57
  48.8 3.3 %collective-permute-done.16.received = bf16[2,64,256]{2,1,0:T(8,128)(2,1)S(1)} collective-permute-done((bf16[2,64,256]{2,1,0:T(8,128)(2,1)S(1)}, bf16[2,64,256]{2,1,0:T(8,128)(2,1)S(1)}, u32[]{:S(2)}, u32[]{:S(2)}) %collective-permute-start.16) | collective-permute-done | bytes 65568 | tf_op jit(solution)/shard_map/ppermute | solution.py:57
  52.2 1.2 %collective-permute-done.17.refs_3_ = bf16[2,64,256]{2,1,0:T(8,128)(2,1)S(1)} collective-permute-done((bf16[2,64,256]{2,1,0:T(8,128)(2,1)S(1)}, bf16[2,64,256]{2,1,0:T(8,128)(2,1)S(1)}, u32[]{:S(2)}, u32[]{:S(2)}) %collective-permute-start.17) | collective-permute-done | bytes 65568 | tf_op jit(solution)/shard_map/ppermute | solution.py:57
  53.4 0.9 %back_projection.1 = (bf16[16,1280]{1,0:T(8,128)(2,1)S(1)}, bf16[16,1280]{1,0:T(8,128)(2,1)S(1)}) custom-call(f32[2,128,256]{2,1,0:T(8,128)S(1)} %get-tuple-element.45.q.refs_0_, bf16[2,64,256]{2,1,0:T(8,128)(2,1)S(1)} %add.5.refs_1_.refs_0_, bf16[2,64,256]{2,1,0:T(8,128)(2,1)S(1)} %collective-permute-done.14.refs_2_.refs_1_, ...), custom_call_target="tpu_custom_call" | custom-call | flops 1 | bytes 1 | tf_op jit(solution)/shard_map/back_projection/pallas_call | solution.py:754
  54.3 1.0 %collective-permute-start.18 = (bf16[16,1280]{1,0:T(8,128)(2,1)S(1)}, bf16[16,1280]{1,0:T(8,128)(2,1)S(1)}, u32[]{:S(2)}, u32[]{:S(2)}) collective-permute-start(bf16[16,1280]{1,0:T(8,128)(2,1)S(1)} %get-tuple-element.62.refs_0_), channel_id=1, source_target_pairs={{0,1},{1,0},{2,3},{3,2},{4,5},{5,4},{6,7},{7,6},{8,9},{9,8},{10,11... | collective-permute-start | bytes 122888 | tf_op jit(solution)/shard_map/ppermute | solution.py:57
  55.4 1.2 %collective-permute-start.20 = (bf16[16,1280]{1,0:T(8,128)(2,1)S(1)}, bf16[16,1280]{1,0:T(8,128)(2,1)S(1)}, u32[]{:S(2)}, u32[]{:S(2)}) collective-permute-start(bf16[16,1280]{1,0:T(8,128)(2,1)S(1)} %get-tuple-element.63), channel_id=1, source_target_pairs={{0,3},{1,2},{2,1},{3,0},{4,7},{5,6},{6,5},{7,4},{8,11},{9,10},{10,... | collective-permute-start | bytes 122888 | tf_op jit(solution)/shard_map/ppermute | solution.py:57
  56.5 0.6 %keep.1.refs_8_ = f32[1,4096]{1,0:T(1,128)S(1)} custom-call(s32[1,8]{1,0:T(1,128)S(1)} %copy-done.4), custom_call_target="tpu_custom_call" | custom-call | flops 1 | bytes 1 | tf_op jit(solution)/shard_map/keep/pallas_call | solution.py:760
  57.2 1.3 %collective-permute-done.18.refs_1_ = bf16[16,1280]{1,0:T(8,128)(2,1)S(1)} collective-permute-done((bf16[16,1280]{1,0:T(8,128)(2,1)S(1)}, bf16[16,1280]{1,0:T(8,128)(2,1)S(1)}, u32[]{:S(2)}, u32[]{:S(2)}) %collective-permute-start.18) | collective-permute-done | bytes 40992 | tf_op jit(solution)/shard_map/ppermute | solution.py:57
  58.8 0.8 %update.1 = (f32[4,4096]{1,0:T(4,128)}, f32[16,4096]{1,0:T(8,128)}) custom-call(bf16[16,1280]{1,0:T(8,128)(2,1)S(1)} %get-tuple-element.62.refs_0_, bf16[16,1280]{1,0:T(8,128)(2,1)S(1)} %collective-permute-done.18.refs_1_, bf16[16,1280]{1,0:T(8,128)(2,1)S(1)} %collective-permute-done.19.refs_2_, bf16[16,1280]{1,0:T(8,128)(2,1)S(1)} %collective-permute-done.20.refs_3_, ...), custom_call_target="tpu_custom_call" | custom-call | flops 1 | bytes 1 | tf_op jit(solution)/shard_map/update/pallas_call | solution.py:764
  (42 shorter events, 3.7 us)
Async XLA Ops:
  1.9 31.0 %collective-permute-start.5 = (bf16[2,2,1024,128]{3,2,1,0:T(8,128)(2,1)S(1)}, bf16[2,2,1024,128]{3,2,1,0:T(8,128)(2,1)S(1)}, u32[]{:S(2)}, u32[]{:S(2)}) collective-permute-start(bf16[2,2,1024,128]{3,2,1,0:T(8,128)(2,1)S(1)} %take_rays.1), channel_id=1, source_target_pairs={{0,1},{1,0},{2,3},{3,2},{4,5},{5,4},{6,7},{7,6},{8,9},{9,8},{10,11... | collective-permute-start | bytes 3145736 | tf_op jit(solution)/shard_map/ppermute | solution.py:57
  8.2 1.3 %collective-permute-start.8 = (bf16[16,1280]{1,0:T(8,128)(2,1)S(1)}, bf16[16,1280]{1,0:T(8,128)(2,1)S(1)}, u32[]{:S(2)}, u32[]{:S(2)}) collective-permute-start(bf16[16,1280]{1,0:T(8,128)(2,1)S(1)} %get-tuple-element.54), channel_id=1, source_target_pairs={{0,2},{2,0},{4,6},{6,4},{8,10},{10,8},{12,14},{14,12},{16,18},{18,... | collective-permute-start | bytes 122888 | tf_op jit(solution)/shard_map/ppermute | solution.py:57
  8.3 3.9 %collective-permute-start = (bf16[64,256]{1,0:T(8,128)(2,1)S(1)}, bf16[64,256]{1,0:T(8,128)(2,1)S(1)}, u32[]{:S(2)}, u32[]{:S(2)}) collective-permute-start(bf16[64,256]{1,0:T(8,128)(2,1)S(1)} %get-tuple-element.34), channel_id=1, source_target_pairs={{0,2},{2,0},{4,6},{6,4},{8,10},{10,8},{12,14},{14,12},{16,18},{18,... | collective-permute-start | bytes 98312 | tf_op jit(solution)/shard_map/ppermute | solution.py:57
  9.6 7.2 %collective-permute-start.9 = (bf16[2,16,1280]{2,1,0:T(8,128)(2,1)S(1)}, bf16[2,16,1280]{2,1,0:T(8,128)(2,1)S(1)}, u32[]{:S(2)}, u32[]{:S(2)}) collective-permute-start(bf16[2,16,1280]{2,1,0:T(8,128)(2,1)S(1)} %pair.1), channel_id=1, source_target_pairs={{0,16},{2,18},{4,20},{6,22},{8,24},{10,26},{12,28},{14,30},{16,0},... | collective-permute-start | bytes 245768 | tf_op jit(solution)/shard_map/ppermute | solution.py:57
  12.2 4.2 %collective-permute-start.1 = (bf16[96,256]{1,0:T(8,128)(2,1)S(1)}, bf16[96,256]{1,0:T(8,128)(2,1)S(1)}, u32[]{:S(2)}, u32[]{:S(2)}) collective-permute-start(bf16[96,256]{1,0:T(8,128)(2,1)S(1)} %get-tuple-element.37.mine), channel_id=1, source_target_pairs={{0,4},{2,6},{4,0},{6,2},{8,12},{10,14},{12,8},{14,10},{16,20},{18,... | collective-permute-start | bytes 147464 | tf_op jit(solution)/shard_map/ppermute | solution.py:57
  16.4 5.3 %collective-permute-start.2 = (bf16[128,256]{1,0:T(8,128)(2,1)S(1)}, bf16[128,256]{1,0:T(8,128)(2,1)S(1)}, u32[]{:S(2)}, u32[]{:S(2)}) collective-permute-start(bf16[128,256]{1,0:T(8,128)(2,1)S(1)} %get-tuple-element.39.mine), channel_id=1, source_target_pairs={{0,16},{2,18},{4,20},{6,22},{8,24},{10,26},{12,28},{14,30},{16,0},... | collective-permute-start | bytes 196616 | tf_op jit(solution)/shard_map/ppermute | solution.py:57
  16.8 10.9 %collective-permute-start.10 = (bf16[4,16,1280]{2,1,0:T(8,128)(2,1)S(1)}, bf16[4,16,1280]{2,1,0:T(8,128)(2,1)S(1)}, u32[]{:S(2)}, u32[]{:S(2)}) collective-permute-start(bf16[4,16,1280]{2,1,0:T(8,128)(2,1)S(1)} %pad_maximum_fusion.1), channel_id=1, source_target_pairs={{0,8},{2,10},{4,12},{6,14},{8,0},{10,2},{12,4},{14,6},{16,24},{18,... | collective-permute-start | bytes 491528 | tf_op jit(solution)/shard_map/ppermute | solution.py:57
  21.8 4.8 %collective-permute-start.3 = (bf16[192,256]{1,0:T(8,128)(2,1)S(1)}, bf16[192,256]{1,0:T(8,128)(2,1)S(1)}, u32[]{:S(2)}, u32[]{:S(2)}) collective-permute-start(bf16[192,256]{1,0:T(8,128)(2,1)S(1)} %get-tuple-element.41.mine), channel_id=1, source_target_pairs={{0,8},{2,10},{4,12},{6,14},{8,0},{10,2},{12,4},{14,6},{16,24},{18,... | collective-permute-start | bytes 294920 | tf_op jit(solution)/shard_map/ppermute | solution.py:57
  27.2 5.7 %collective-permute-start.4 = (bf16[384,256]{1,0:T(8,128)(2,1)S(1)}, bf16[384,256]{1,0:T(8,128)(2,1)S(1)}, u32[]{:S(2)}, u32[]{:S(2)}) collective-permute-start(bf16[384,256]{1,0:T(8,128)(2,1)S(1)} %get-tuple-element.42.refs_0_), channel_id=1, source_target_pairs={{0,1},{1,0},{2,3},{3,2},{4,5},{5,4},{6,7},{7,6},{8,9},{9,8},{10,11... | collective-permute-start | bytes 589832 | tf_op jit(solution)/shard_map/ppermute | solution.py:57
  27.7 7.9 %collective-permute-start.11 = (bf16[8,16,1280]{2,1,0:T(8,128)(2,1)S(1)}, bf16[8,16,1280]{2,1,0:T(8,128)(2,1)S(1)}, u32[]{:S(2)}, u32[]{:S(2)}) collective-permute-start(bf16[8,16,1280]{2,1,0:T(8,128)(2,1)S(1)} %pad_maximum_fusion.mine), channel_id=1, source_target_pairs={{0,4},{2,6},{4,0},{6,2},{8,12},{10,14},{12,8},{14,10},{16,20},{18,... | collective-permute-start | bytes 983048 | tf_op jit(solution)/shard_map/ppermute | solution.py:57
  32.9 1.8 %collective-permute-start.6 = (bf16[2,256,256]{2,1,0:T(8,128)(2,1)S(1)}, bf16[2,256,256]{2,1,0:T(8,128)(2,1)S(1)}, u32[]{:S(2)}, u32[]{:S(2)}) collective-permute-start(bf16[2,256,256]{2,1,0:T(8,128)(2,1)S(1)} %get-tuple-element.43.mine), channel_id=1, source_target_pairs={{0,2},{2,0},{4,6},{6,4},{8,10},{10,8},{12,14},{14,12},{16,18},{18,... | collective-permute-start | bytes 786440 | tf_op jit(solution)/shard_map/ppermute | solution.py:57
  33.0 1.7 %collective-permute-start.7 = (f32[2,64,256]{2,1,0:T(8,128)S(1)}, f32[2,64,256]{2,1,0:T(8,128)S(1)}, u32[]{:S(2)}, u32[]{:S(2)}) collective-permute-start(f32[2,64,256]{2,1,0:T(8,128)S(1)} %get-tuple-element.44.q_mine), channel_id=1, source_target_pairs={{0,2},{2,0},{4,6},{6,4},{8,10},{10,8},{12,14},{14,12},{16,18},{18,... | collective-permute-start | bytes 393224 | tf_op jit(solution)/shard_map/ppermute | solution.py:57
  37.6 1.3 %collective-permute-start.12 = (bf16[2,64,256]{2,1,0:T(8,128)(2,1)S(1)}, bf16[2,64,256]{2,1,0:T(8,128)(2,1)S(1)}, u32[]{:S(2)}, u32[]{:S(2)}) collective-permute-start(bf16[2,64,256]{2,1,0:T(8,128)(2,1)S(1)} %get-tuple-element.59), channel_id=1, source_target_pairs={{0,2},{2,0},{4,6},{6,4},{8,10},{10,8},{12,14},{14,12},{16,18},{18,... | collective-permute-start | bytes 196616 | tf_op jit(solution)/shard_map/ppermute | solution.py:57
  38.9 4.3 %collective-permute-start.13 = (bf16[2,64,256]{2,1,0:T(8,128)(2,1)S(1)}, bf16[2,64,256]{2,1,0:T(8,128)(2,1)S(1)}, u32[]{:S(2)}, u32[]{:S(2)}) collective-permute-start(bf16[2,64,256]{2,1,0:T(8,128)(2,1)S(1)} %add.4.mine), channel_id=1, source_target_pairs={{0,1},{1,0},{2,3},{3,2},{4,5},{5,4},{6,7},{7,6},{8,9},{9,8},{10,11... | collective-permute-start | bytes 196616 | tf_op jit(solution)/shard_map/ppermute | solution.py:57
  43.2 1.3 %collective-permute-start.14 = (bf16[2,64,256]{2,1,0:T(8,128)(2,1)S(1)}, bf16[2,64,256]{2,1,0:T(8,128)(2,1)S(1)}, u32[]{:S(2)}, u32[]{:S(2)}) collective-permute-start(bf16[2,64,256]{2,1,0:T(8,128)(2,1)S(1)} %add.5.refs_1_.refs_0_), channel_id=1, source_target_pairs={{0,2},{2,0},{4,6},{6,4},{8,10},{10,8},{12,14},{14,12},{16,18},{18,... | collective-permute-start | bytes 196616 | tf_op jit(solution)/shard_map/ppermute | solution.py:57
  46.3 10.2 %copy-start.4 = (s32[1,8]{1,0:T(1,128)S(1)}, s32[1,8]{1,0:T(1,128)}, u32[]{:S(2)}) copy-start(s32[1,8]{1,0:T(1,128)} %blocks.1) | copy-start | bytes 100
  46.3 12.5 %copy-start = (f32[16,4096]{1,0:T(8,128)S(1)}, f32[16,4096]{1,0:T(8,128)}, u32[]{:S(2)}) copy-start(f32[16,4096]{1,0:T(8,128)} %refs_5_.1) | copy-start | bytes 786436
  46.4 12.5 %copy-start.1 = (f32[16,4096]{1,0:T(8,128)S(1)}, f32[16,4096]{1,0:T(8,128)}, u32[]{:S(2)}) copy-start(f32[16,4096]{1,0:T(8,128)} %refs_7_.1) | copy-start | bytes 786436
  46.4 12.5 %copy-start.2 = (f32[4,4096]{1,0:T(4,128)S(1)}, f32[4,4096]{1,0:T(4,128)}, u32[]{:S(2)}) copy-start(f32[4,4096]{1,0:T(4,128)} %refs_4_.1) | copy-start | bytes 196612
  46.4 12.4 %copy-start.3 = (f32[4,4096]{1,0:T(4,128)S(1)}, f32[4,4096]{1,0:T(4,128)}, u32[]{:S(2)}) copy-start(f32[4,4096]{1,0:T(4,128)} %refs_6_.1) | copy-start | bytes 196612
  46.4 1.3 %collective-permute-start.15 = (bf16[2,64,256]{2,1,0:T(8,128)(2,1)S(1)}, bf16[2,64,256]{2,1,0:T(8,128)(2,1)S(1)}, u32[]{:S(2)}, u32[]{:S(2)}) collective-permute-start(bf16[2,64,256]{2,1,0:T(8,128)(2,1)S(1)} %get-tuple-element.61), channel_id=1, source_target_pairs={{0,2},{2,0},{4,6},{6,4},{8,10},{10,8},{12,14},{14,12},{16,18},{18,... | collective-permute-start | bytes 196616 | tf_op jit(solution)/shard_map/ppermute | solution.py:57
  47.7 4.3 %collective-permute-start.16 = (bf16[2,64,256]{2,1,0:T(8,128)(2,1)S(1)}, bf16[2,64,256]{2,1,0:T(8,128)(2,1)S(1)}, u32[]{:S(2)}, u32[]{:S(2)}) collective-permute-start(bf16[2,64,256]{2,1,0:T(8,128)(2,1)S(1)} %add.6.mine), channel_id=1, source_target_pairs={{0,1},{1,0},{2,3},{3,2},{4,5},{5,4},{6,7},{7,6},{8,9},{9,8},{10,11... | collective-permute-start | bytes 196616 | tf_op jit(solution)/shard_map/ppermute | solution.py:57
  52.1 1.3 %collective-permute-start.17 = (bf16[2,64,256]{2,1,0:T(8,128)(2,1)S(1)}, bf16[2,64,256]{2,1,0:T(8,128)(2,1)S(1)}, u32[]{:S(2)}, u32[]{:S(2)}) collective-permute-start(bf16[2,64,256]{2,1,0:T(8,128)(2,1)S(1)} %add.7.refs_2_), channel_id=1, source_target_pairs={{0,2},{2,0},{4,6},{6,4},{8,10},{10,8},{12,14},{14,12},{16,18},{18,... | collective-permute-start | bytes 196616 | tf_op jit(solution)/shard_map/ppermute | solution.py:57
  54.3 4.2 %collective-permute-start.18 = (bf16[16,1280]{1,0:T(8,128)(2,1)S(1)}, bf16[16,1280]{1,0:T(8,128)(2,1)S(1)}, u32[]{:S(2)}, u32[]{:S(2)}) collective-permute-start(bf16[16,1280]{1,0:T(8,128)(2,1)S(1)} %get-tuple-element.62.refs_0_), channel_id=1, source_target_pairs={{0,1},{1,0},{2,3},{3,2},{4,5},{5,4},{6,7},{7,6},{8,9},{9,8},{10,11... | collective-permute-start | bytes 122888 | tf_op jit(solution)/shard_map/ppermute | solution.py:57
  55.3 3.2 %collective-permute-start.19 = (bf16[16,1280]{1,0:T(8,128)(2,1)S(1)}, bf16[16,1280]{1,0:T(8,128)(2,1)S(1)}, u32[]{:S(2)}, u32[]{:S(2)}) collective-permute-start(bf16[16,1280]{1,0:T(8,128)(2,1)S(1)} %get-tuple-element.63), channel_id=1, source_target_pairs={{0,2},{1,3},{2,0},{3,1},{4,6},{5,7},{6,4},{7,5},{8,10},{9,11},{10,... | collective-permute-start | bytes 122888 | tf_op jit(solution)/shard_map/ppermute | solution.py:57
  55.4 3.5 %collective-permute-start.20 = (bf16[16,1280]{1,0:T(8,128)(2,1)S(1)}, bf16[16,1280]{1,0:T(8,128)(2,1)S(1)}, u32[]{:S(2)}, u32[]{:S(2)}) collective-permute-start(bf16[16,1280]{1,0:T(8,128)(2,1)S(1)} %get-tuple-element.63), channel_id=1, source_target_pairs={{0,3},{1,2},{2,1},{3,0},{4,7},{5,6},{6,5},{7,4},{8,11},{9,10},{10,... | collective-permute-start | bytes 122888 | tf_op jit(solution)/shard_map/ppermute | solution.py:57

commit v7 on v6

--- a/solution.py
+++ b/solution.py
@@ -16,8 +16,8 @@
 SMEM = pl.BlockSpec(memory_space=pltpu.SMEM)
 ANY = pl.BlockSpec(memory_space=pl.ANY)
 HBM = pl.BlockSpec(memory_space=pltpu.HBM)
-SOURCE = {"rays": "start", "weights": "start"}
-AWAITED = {"rays": "views"}
+SOURCE = {'rays': 'start', 'weights': ("start", "core", "hop1")}
+AWAITED = {"rays": "views", "w1": "last"}
 QUICK = pl.CostEstimate(flops=1, bytes_accessed=1, transcendentals=0)
 
 
@@ -145,6 +145,12 @@
     out[1] = jnp.where(lead, other, own).astype(BF16)
 
 
+def join_blocks_kernel(mine, received, *refs):
+    out = refs[-1]
+    out[: mine.shape[0]] = mine[...]
+    out[mine.shape[0] :] = received[...]
+
+
 def join_core_kernel(q, received, rows, *refs):
     total, out = refs[-2:]
     count = q.shape[0]
@@ -154,20 +160,24 @@
     out[count:] = rows[...]
 
 
-def join_hop_kernel(last, q, mine, received, *refs):
+def join_hop_kernel(q, mine, received, *refs):
     total, out = refs[-2:]
     count = q.shape[0]
     value = q[...] + received[:count].astype(F32)
     total[...] = value
-    high, low = in_two(value)
-    out[:count] = high
-    base = count
-    if last:
-        out[count : 2 * count] = low
-        base = 2 * count
+    out[:count] = value.astype(BF16)
     held = mine.shape[0] - count
-    out[base : base + held] = mine[count:]
-    out[base + held :] = received[count:]
+    out[count : count + held] = mine[count:]
+    out[count + held :] = received[count:]
+
+
+def join_last_kernel(q, mine, received, *refs):
+    out = refs[-1]
+    count = q.shape[0]
+    out[:count], out[count : 2 * count] = in_two(q[...] + received[:count].astype(F32))
+    held = mine.shape[0] - count
+    out[2 * count : 2 * count + held] = mine[count:]
+    out[2 * count + held :] = received[count:]
 
 
 def join_views_kernel(count, *refs):
@@ -323,7 +333,7 @@
 
 
 def rows_kernel(own, fz, bits, mine, theirs, q_mine, q_theirs, *refs):
-    coarse_out, fine_out, coarse_turned, fine_turned, out, q_out = refs
+    coarse_out, fine_out, coarse_turned, fine_turned, out, q_out = refs[-6:]
     lead = lax.axis_index("slab") % 2 == 0
     kept = q_mine.shape[1]
     for g in range(q_mine.shape[0]):
@@ -641,19 +651,26 @@
                         [pltpu.SemaphoreType.DMA((2,))],
                     )(*in_hbm(fine_rays, coarse_rays), *waits)
                     got["rays"].append(swap(value, "view", groups, bits))
-            if SOURCE["weights"] == stage:
-                packed = call(
-                    pair_kernel,
-                    "pair",
-                    shaped((2, PACK, width), BF16),
-                    [VMEM] * 2 + [ANY] * len(waits),
-                )(mine, along_slab(theirs, 1), *waits)
-                for index, bit in enumerate(far_bits + [2]):
-                    hop = along_slab(packed, bit)
-                    got["w%d" % index] = [hop]
-                    if bit != 2:
-                        packed = jnp.concatenate([packed, hop])
-                got["weights"] = (packed, hop)
+            for index, bit in enumerate(far_bits + [2]):
+                if SOURCE["weights"][min(index, 2)] != stage:
+                    continue
+                if index == 0:
+                    packed = call(
+                        pair_kernel,
+                        "pair",
+                        shaped((2, PACK, width), BF16),
+                        [VMEM] * 2 + [ANY] * len(waits),
+                    )(mine, along_slab(theirs, 1), *waits)
+                else:
+                    packed, hop = got["weights"]
+                    packed = call(
+                        join_blocks_kernel,
+                        "join_blocks",
+                        shaped((2 * packed.shape[0], PACK, width), BF16),
+                        [VMEM] * 2 + [ANY] * len(waits),
+                    )(packed, hop, *waits)
+                got["w%d" % index] = [along_slab(packed, bit)]
+                got["weights"] = (packed, got["w%d" % index][0])
 
         def waits_of(stage):
             found = []
@@ -675,13 +692,20 @@
             last = index == len(far_bits)
             name = "last" if last else "hop%d" % index
             waits = waits_of(name)
-            size = 2 * mixed.shape[0] - rows_half + (rows_half if last else 0)
-            q, mixed = call(
-                functools.partial(join_hop_kernel, last),
-                "join_hop",
-                (shaped(q.shape, F32), shaped((size, total), BF16)),
-                [VMEM] * 3 + [ANY] * len(waits),
-            )(q, mixed, along_slab(mixed, bit), *waits)
+            inputs = (q, mixed, along_slab(mixed, bit), *waits)
+            specs = [VMEM] * 3 + [ANY] * len(waits)
+            size = 2 * mixed.shape[0]
+            if last:
+                mixed = call(join_last_kernel, "join_last", shaped((size, total), BF16), specs)(
+                    *inputs
+                )
+            else:
+                q, mixed = call(
+                    join_hop_kernel,
+                    "join_hop",
+                    (shaped(q.shape, F32), shaped((size - rows_half, total), BF16)),
+                    specs,
+                )(*inputs)
             begin(name, mixed)
         waits = waits_of("views")
         q, rows = call(
@@ -697,6 +721,7 @@
         order = tuple(
             (j & 1) + 2 * (j >> 2) + (((j >> 1) & 1) << (count + 1)) for j in range(slabs)
         )
+        waits = waits_of("rows")
         coarse_depth, fine_depth, coarse_turned, fine_turned, weights, q = call(
             functools.partial(rows_kernel, own, fz, [2] + far_bits),
             "unpack_rows",
@@ -708,8 +733,8 @@
                 shaped((groups, det, total), F32),
                 shaped((groups, det, total), F32),
             ),
-            [VMEM] * 4,
-        )(rows, along_slab(rows, 1), q, along_slab(q, 1))
+            [VMEM] * 4 + [ANY] * len(waits),
+        )(rows, along_slab(rows, 1), q, along_slab(q, 1), *waits)
         spreads = call(
             functools.partial(spread_kernel, views),
             "spread",

time: 59.8 us -> 59.7 us (level)
  starting transfers between devices: 19.4 us -> 20.3 us
    ppermute x21, starting transfers between devices: 19.4 us -> 20.3 us  [swap(): return lax.ppermute(value, axis, [(i, i ^ bits) for i in range(size)])]
  transfers between devices with their start and end apart: 21 -> 21, of which waited for: 15 -> 15; matrix products, arithmetic and copies ran while one was open for 0% -> 0% of each run, Pallas kernels for 9% -> 8%
where the time goes in v7:
time: 59.7 us; the launch traced here: 59.4 us
  waiting for transfers between devices  26.9 us (45%)
  starting transfers between devices  20.3 us (34%)
  Pallas kernels  11.4 us (19%)
  between operations  0.83 us (1%)
    ppermute x21, waiting for transfers between devices, swap(): return lax.ppermute(value, axis, [(i, i ^ bits) for i in range(size)])  26.9 us
    ppermute x21, starting transfers between devices, swap(): return lax.ppermute(value, axis, [(i, i ^ bits) for i in range(size)])  20.3 us
    pallas_call x2, Pallas kernels, body(): call(functools.partial(step_kernel, groups, views, ready), 'ray_space_ste...  3.41 us
    pallas_call x1, Pallas kernels, body(): call(start_kernel, 'start', (shaped((PACK, width), BF16), shaped((PACK, w...  3.33 us
    pallas_call x1, Pallas kernels, begin(): call(functools.partial(take_kernel, groups, bits), 'take_rays', shaped((2...  1.23 us
  transfers between devices with their start and end apart: 21, of which 15 were waited for; matrix products, arithmetic and copies ran while one was open for 0% of the time, Pallas kernels for 8%

profile of v7, /device:TPU:0, one launch (start us, length us, event | category | flops | bytes accessed | tf_op | source)
XLA Modules:
  0.0 59.4 jit_solution(6848933191222537294)
XLA Ops:
  0.6 1.2 %take_rays.1 = bf16[2,2,1024,128]{3,2,1,0:T(8,128)(2,1)S(1)} custom-call(bf16[2,4096,128]{2,1,0:T(8,128)(2,1)} %fine_rays.1, bf16[2,4096,128]{2,1,0:T(8,128)(2,1)} %coarse_rays.1), custom_call_target="tpu_custom_call" | custom-call | flops 1 | bytes 1 | tf_op jit(solution)/shard_map/take_rays/pallas_call | solution.py:646
  1.9 3.0 %collective-permute-start.8 = (bf16[2,2,1024,128]{3,2,1,0:T(8,128)(2,1)S(1)}, bf16[2,2,1024,128]{3,2,1,0:T(8,128)(2,1)S(1)}, u32[]{:S(2)}, u32[]{:S(2)}) collective-permute-start(bf16[2,2,1024,128]{3,2,1,0:T(8,128)(2,1)S(1)} %take_rays.1), channel_id=1, source_target_pairs={{0,1},{1,0},{2,3},{3,2},{4,5},{5,4},{6,7},{7,6},{8,9},{9,8},{10,11... | collective-permute-start | bytes 3145736 | tf_op jit(solution)/shard_map/ppermute | solution.py:57
  4.9 3.3 %start.1 = (bf16[16,1280]{1,0:T(8,128)(2,1)S(1)}, bf16[16,1280]{1,0:T(8,128)(2,1)S(1)}, bf16[32,256]{1,0:T(8,128)(2,1)S(1)}, f32[64,256]{1,0:T(8,128)S(1)}, bf16...) custom-call(bf16[2,4096,128]{2,1,0:T(8,128)(2,1)} %fine_rays.1, bf16[2,4096,128]{2,1,0:T(8,128)(2,1)} %coarse_rays.1, ...), custom_call_target="tpu_custom_call" | custom-call | flops 1 | bytes 1 | tf_op jit(solution)/shard_map/start/pallas_call | solution.py:610
  8.8 0.7 %collective-permute-done.4.received = bf16[16,1280]{1,0:T(8,128)(2,1)S(1)} collective-permute-done((bf16[16,1280]{1,0:T(8,128)(2,1)S(1)}, bf16[16,1280]{1,0:T(8,128)(2,1)S(1)}, u32[]{:S(2)}, u32[]{:S(2)}) %collective-permute-start.4) | collective-permute-done | bytes 40992 | tf_op jit(solution)/shard_map/ppermute | solution.py:57
  9.6 2.7 %collective-permute-start.5 = (bf16[2,16,1280]{2,1,0:T(8,128)(2,1)S(1)}, bf16[2,16,1280]{2,1,0:T(8,128)(2,1)S(1)}, u32[]{:S(2)}, u32[]{:S(2)}) collective-permute-start(bf16[2,16,1280]{2,1,0:T(8,128)(2,1)S(1)} %pair.1.mine), channel_id=1, source_target_pairs={{0,16},{2,18},{4,20},{6,22},{8,24},{10,26},{12,28},{14,30},{16,0},... | collective-permute-start | bytes 245768 | tf_op jit(solution)/shard_map/ppermute | solution.py:57
  12.2 1.6 %collective-permute-start.1 = (bf16[96,256]{1,0:T(8,128)(2,1)S(1)}, bf16[96,256]{1,0:T(8,128)(2,1)S(1)}, u32[]{:S(2)}, u32[]{:S(2)}) collective-permute-start(bf16[96,256]{1,0:T(8,128)(2,1)S(1)} %get-tuple-element.36.mine.refs_0_), channel_id=1, source_target_pairs={{0,4},{2,6},{4,0},{6,2},{8,12},{10,14},{12,8},{14,10},{16,20},{18,... | collective-permute-start | bytes 147464 | tf_op jit(solution)/shard_map/ppermute | solution.py:57
  13.8 2.6 %collective-permute-done.1.received = bf16[96,256]{1,0:T(8,128)(2,1)S(1)} collective-permute-done((bf16[96,256]{1,0:T(8,128)(2,1)S(1)}, bf16[96,256]{1,0:T(8,128)(2,1)S(1)}, u32[]{:S(2)}, u32[]{:S(2)}) %collective-permute-start.1) | collective-permute-done | bytes 49184 | tf_op jit(solution)/shard_map/ppermute | solution.py:57
  16.8 1.6 %collective-permute-start.6 = (bf16[4,16,1280]{2,1,0:T(8,128)(2,1)S(1)}, bf16[4,16,1280]{2,1,0:T(8,128)(2,1)S(1)}, u32[]{:S(2)}, u32[]{:S(2)}) collective-permute-start(bf16[4,16,1280]{2,1,0:T(8,128)(2,1)S(1)} %join_blocks.2.mine), channel_id=1, source_target_pairs={{0,8},{2,10},{4,12},{6,14},{8,0},{10,2},{12,4},{14,6},{16,24},{18,... | collective-permute-start | bytes 491528 | tf_op jit(solution)/shard_map/ppermute | solution.py:57
  18.5 3.3 %collective-permute-done.2.received = bf16[128,256]{1,0:T(8,128)(2,1)S(1)} collective-permute-done((bf16[128,256]{1,0:T(8,128)(2,1)S(1)}, bf16[128,256]{1,0:T(8,128)(2,1)S(1)}, u32[]{:S(2)}, u32[]{:S(2)}) %collective-permute-start.2) | collective-permute-done | bytes 65568 | tf_op jit(solution)/shard_map/ppermute | solution.py:57
  21.8 2.2 %collective-permute-start.3 = (bf16[192,256]{1,0:T(8,128)(2,1)S(1)}, bf16[192,256]{1,0:T(8,128)(2,1)S(1)}, u32[]{:S(2)}, u32[]{:S(2)}) collective-permute-start(bf16[192,256]{1,0:T(8,128)(2,1)S(1)} %get-tuple-element.40.mine.refs_0_), channel_id=1, source_target_pairs={{0,8},{2,10},{4,12},{6,14},{8,0},{10,2},{12,4},{14,6},{16,24},{18,... | collective-permute-start | bytes 294920 | tf_op jit(solution)/shard_map/ppermute | solution.py:57
  23.9 2.6 %collective-permute-done.3.received = bf16[192,256]{1,0:T(8,128)(2,1)S(1)} collective-permute-done((bf16[192,256]{1,0:T(8,128)(2,1)S(1)}, bf16[192,256]{1,0:T(8,128)(2,1)S(1)}, u32[]{:S(2)}, u32[]{:S(2)}) %collective-permute-start.3) | collective-permute-done | bytes 98336 | tf_op jit(solution)/shard_map/ppermute | solution.py:57
  26.6 0.6 collective-permute-start.7
  27.2 1.6 %collective-permute-start.11 = (bf16[8,16,1280]{2,1,0:T(8,128)(2,1)S(1)}, bf16[8,16,1280]{2,1,0:T(8,128)(2,1)S(1)}, u32[]{:S(2)}, u32[]{:S(2)}) collective-permute-start(bf16[8,16,1280]{2,1,0:T(8,128)(2,1)S(1)} %join_blocks.3.mine), channel_id=1, source_target_pairs={{0,4},{2,6},{4,0},{6,2},{8,12},{10,14},{12,8},{14,10},{16,20},{18,... | collective-permute-start | bytes 983048 | tf_op jit(solution)/shard_map/ppermute | solution.py:57
  28.7 3.6 %collective-permute-done.7.refs_1_ = bf16[384,256]{1,0:T(8,128)(2,1)S(1)} collective-permute-done((bf16[384,256]{1,0:T(8,128)(2,1)S(1)}, bf16[384,256]{1,0:T(8,128)(2,1)S(1)}, u32[]{:S(2)}, u32[]{:S(2)}) %collective-permute-start.7) | collective-permute-done | bytes 196640 | tf_op jit(solution)/shard_map/ppermute | solution.py:57
  32.9 1.2 %collective-permute-done.10.q_theirs = f32[2,64,256]{2,1,0:T(8,128)S(1)} collective-permute-done((f32[2,64,256]{2,1,0:T(8,128)S(1)}, f32[2,64,256]{2,1,0:T(8,128)S(1)}, u32[]{:S(2)}, u32[]{:S(2)}) %collective-permute-start.10) | collective-permute-done | bytes 131104 | tf_op jit(solution)/shard_map/ppermute | solution.py:57
  35.3 1.6 %ray_space_step.2 = (bf16[2,64,256]{2,1,0:T(8,128)(2,1)S(1)}, bf16[2,64,256]{2,1,0:T(8,128)(2,1)S(1)}) custom-call(bf16[2,64,256]{2,1,0:T(8,128)(2,1)S(1)} %get-tuple-element.49.refs_0_, bf16[2,256,256]{2,1,0:T(8,128)(2,1)S(1)} %get-tuple-element.50.refs_1_, bf16[2,2,128,64]{3,2,1,0:T(8,128)(2,1)S(1)} %get-tuple-element.51.refs_2_.refs_6_, ...), custom_call_target="tpu_custom_call" | custom-call | flops 1 | bytes 1 | tf_op jit(solution)/shard_map/ray_space_step/pallas_call | solution.py:767
  37.1 1.2 %collective-permute-done.12.received = bf16[2,64,256]{2,1,0:T(8,128)(2,1)S(1)} collective-permute-done((bf16[2,64,256]{2,1,0:T(8,128)(2,1)S(1)}, bf16[2,64,256]{2,1,0:T(8,128)(2,1)S(1)}, u32[]{:S(2)}, u32[]{:S(2)}) %collective-permute-start.12) | collective-permute-done | bytes 65568 | tf_op jit(solution)/shard_map/ppermute | solution.py:57
  38.3 1.5 %collective-permute-start.13 = (bf16[2,64,256]{2,1,0:T(8,128)(2,1)S(1)}, bf16[2,64,256]{2,1,0:T(8,128)(2,1)S(1)}, u32[]{:S(2)}, u32[]{:S(2)}) collective-permute-start(bf16[2,64,256]{2,1,0:T(8,128)(2,1)S(1)} %add.4.mine), channel_id=1, source_target_pairs={{0,1},{1,0},{2,3},{3,2},{4,5},{5,4},{6,7},{7,6},{8,9},{9,8},{10,11... | collective-permute-start | bytes 196616 | tf_op jit(solution)/shard_map/ppermute | solution.py:57
  39.8 2.9 %collective-permute-done.13.received = bf16[2,64,256]{2,1,0:T(8,128)(2,1)S(1)} collective-permute-done((bf16[2,64,256]{2,1,0:T(8,128)(2,1)S(1)}, bf16[2,64,256]{2,1,0:T(8,128)(2,1)S(1)}, u32[]{:S(2)}, u32[]{:S(2)}) %collective-permute-start.13) | collective-permute-done | bytes 65568 | tf_op jit(solution)/shard_map/ppermute | solution.py:57
  42.8 1.2 %collective-permute-done.14.refs_2_.refs_1_ = bf16[2,64,256]{2,1,0:T(8,128)(2,1)S(1)} collective-permute-done((bf16[2,64,256]{2,1,0:T(8,128)(2,1)S(1)}, bf16[2,64,256]{2,1,0:T(8,128)(2,1)S(1)}, u32[]{:S(2)}, u32[]{:S(2)}) %collective-permute-start.14) | collective-permute-done | bytes 65568 | tf_op jit(solution)/shard_map/ppermute | solution.py:57
  44.0 1.8 %ray_space_step.3 = (bf16[2,64,256]{2,1,0:T(8,128)(2,1)S(1)}, bf16[2,64,256]{2,1,0:T(8,128)(2,1)S(1)}) custom-call(f32[2,128,256]{2,1,0:T(8,128)S(1)} %get-tuple-element.45.q.refs_0_, bf16[2,64,256]{2,1,0:T(8,128)(2,1)S(1)} %add.5.refs_1_.refs_0_, bf16[2,64,256]{2,1,0:T(8,128)(2,1)S(1)} %collective-permute-done.14.refs_2_.refs_1_, ...), custom_call_target="tpu_custom_call" | custom-call | flops 1 | bytes 1 | tf_op jit(solution)/shard_map/ray_space_step/pallas_call | solution.py:767
  46.0 1.1 %collective-permute-done.15.received = bf16[2,64,256]{2,1,0:T(8,128)(2,1)S(1)} collective-permute-done((bf16[2,64,256]{2,1,0:T(8,128)(2,1)S(1)}, bf16[2,64,256]{2,1,0:T(8,128)(2,1)S(1)}, u32[]{:S(2)}, u32[]{:S(2)}) %collective-permute-start.15) | collective-permute-done | bytes 65568 | tf_op jit(solution)/shard_map/ppermute | solution.py:57
  47.2 1.5 %collective-permute-start.16 = (bf16[2,64,256]{2,1,0:T(8,128)(2,1)S(1)}, bf16[2,64,256]{2,1,0:T(8,128)(2,1)S(1)}, u32[]{:S(2)}, u32[]{:S(2)}) collective-permute-start(bf16[2,64,256]{2,1,0:T(8,128)(2,1)S(1)} %add.6.mine), channel_id=1, source_target_pairs={{0,1},{1,0},{2,3},{3,2},{4,5},{5,4},{6,7},{7,6},{8,9},{9,8},{10,11... | collective-permute-start | bytes 196616 | tf_op jit(solution)/shard_map/ppermute | solution.py:57
  48.6 2.9 %collective-permute-done.16.received = bf16[2,64,256]{2,1,0:T(8,128)(2,1)S(1)} collective-permute-done((bf16[2,64,256]{2,1,0:T(8,128)(2,1)S(1)}, bf16[2,64,256]{2,1,0:T(8,128)(2,1)S(1)}, u32[]{:S(2)}, u32[]{:S(2)}) %collective-permute-start.16) | collective-permute-done | bytes 65568 | tf_op jit(solution)/shard_map/ppermute | solution.py:57
  51.6 1.2 %collective-permute-done.17.refs_3_ = bf16[2,64,256]{2,1,0:T(8,128)(2,1)S(1)} collective-permute-done((bf16[2,64,256]{2,1,0:T(8,128)(2,1)S(1)}, bf16[2,64,256]{2,1,0:T(8,128)(2,1)S(1)}, u32[]{:S(2)}, u32[]{:S(2)}) %collective-permute-start.17) | collective-permute-done | bytes 65568 | tf_op jit(solution)/shard_map/ppermute | solution.py:57
  52.8 0.9 %back_projection.1 = (bf16[16,1280]{1,0:T(8,128)(2,1)S(1)}, bf16[16,1280]{1,0:T(8,128)(2,1)S(1)}) custom-call(f32[2,128,256]{2,1,0:T(8,128)S(1)} %get-tuple-element.45.q.refs_0_, bf16[2,64,256]{2,1,0:T(8,128)(2,1)S(1)} %add.5.refs_1_.refs_0_, bf16[2,64,256]{2,1,0:T(8,128)(2,1)S(1)} %collective-permute-done.14.refs_2_.refs_1_, ...), custom_call_target="tpu_custom_call" | custom-call | flops 1 | bytes 1 | tf_op jit(solution)/shard_map/back_projection/pallas_call | solution.py:779
  53.7 1.5 %collective-permute-start.18 = (bf16[16,1280]{1,0:T(8,128)(2,1)S(1)}, bf16[16,1280]{1,0:T(8,128)(2,1)S(1)}, u32[]{:S(2)}, u32[]{:S(2)}) collective-permute-start(bf16[16,1280]{1,0:T(8,128)(2,1)S(1)} %get-tuple-element.60.refs_0_), channel_id=1, source_target_pairs={{0,1},{1,0},{2,3},{3,2},{4,5},{5,4},{6,7},{7,6},{8,9},{9,8},{10,11... | collective-permute-start | bytes 122888 | tf_op jit(solution)/shard_map/ppermute | solution.py:57
  55.2 0.7 %collective-permute-start.20 = (bf16[16,1280]{1,0:T(8,128)(2,1)S(1)}, bf16[16,1280]{1,0:T(8,128)(2,1)S(1)}, u32[]{:S(2)}, u32[]{:S(2)}) collective-permute-start(bf16[16,1280]{1,0:T(8,128)(2,1)S(1)} %get-tuple-element.61), channel_id=1, source_target_pairs={{0,3},{1,2},{2,1},{3,0},{4,7},{5,6},{6,5},{7,4},{8,11},{9,10},{10,... | collective-permute-start | bytes 122888 | tf_op jit(solution)/shard_map/ppermute | solution.py:57
  55.9 0.6 %keep.1.refs_8_ = f32[1,4096]{1,0:T(1,128)S(1)} custom-call(s32[1,8]{1,0:T(1,128)S(1)} %copy-done.4), custom_call_target="tpu_custom_call" | custom-call | flops 1 | bytes 1 | tf_op jit(solution)/shard_map/keep/pallas_call | solution.py:785
  56.6 1.2 %collective-permute-done.18.refs_1_ = bf16[16,1280]{1,0:T(8,128)(2,1)S(1)} collective-permute-done((bf16[16,1280]{1,0:T(8,128)(2,1)S(1)}, bf16[16,1280]{1,0:T(8,128)(2,1)S(1)}, u32[]{:S(2)}, u32[]{:S(2)}) %collective-permute-start.18) | collective-permute-done | bytes 40992 | tf_op jit(solution)/shard_map/ppermute | solution.py:57
  57.8 0.8 %collective-permute-done.20.refs_3_ = bf16[16,1280]{1,0:T(8,128)(2,1)S(1)} collective-permute-done((bf16[16,1280]{1,0:T(8,128)(2,1)S(1)}, bf16[16,1280]{1,0:T(8,128)(2,1)S(1)}, u32[]{:S(2)}, u32[]{:S(2)}) %collective-permute-start.20) | collective-permute-done | bytes 40992 | tf_op jit(solution)/shard_map/ppermute | solution.py:57
  58.6 0.8 %update.1 = (f32[4,4096]{1,0:T(4,128)}, f32[16,4096]{1,0:T(8,128)}) custom-call(bf16[16,1280]{1,0:T(8,128)(2,1)S(1)} %get-tuple-element.60.refs_0_, bf16[16,1280]{1,0:T(8,128)(2,1)S(1)} %collective-permute-done.18.refs_1_, bf16[16,1280]{1,0:T(8,128)(2,1)S(1)} %collective-permute-done.19.refs_2_, bf16[16,1280]{1,0:T(8,128)(2,1)S(1)} %collective-permute-done.20.refs_3_, ...), custom_call_target="tpu_custom_call" | custom-call | flops 1 | bytes 1 | tf_op jit(solution)/shard_map/update/pallas_call | solution.py:789
  (42 shorter events, 3.4 us)
Async XLA Ops:
  1.9 30.4 %collective-permute-start.8 = (bf16[2,2,1024,128]{3,2,1,0:T(8,128)(2,1)S(1)}, bf16[2,2,1024,128]{3,2,1,0:T(8,128)(2,1)S(1)}, u32[]{:S(2)}, u32[]{:S(2)}) collective-permute-start(bf16[2,2,1024,128]{3,2,1,0:T(8,128)(2,1)S(1)} %take_rays.1), channel_id=1, source_target_pairs={{0,1},{1,0},{2,3},{3,2},{4,5},{5,4},{6,7},{7,6},{8,9},{9,8},{10,11... | collective-permute-start | bytes 3145736 | tf_op jit(solution)/shard_map/ppermute | solution.py:57
  8.2 1.3 %collective-permute-start.4 = (bf16[16,1280]{1,0:T(8,128)(2,1)S(1)}, bf16[16,1280]{1,0:T(8,128)(2,1)S(1)}, u32[]{:S(2)}, u32[]{:S(2)}) collective-permute-start(bf16[16,1280]{1,0:T(8,128)(2,1)S(1)} %get-tuple-element.42), channel_id=1, source_target_pairs={{0,2},{2,0},{4,6},{6,4},{8,10},{10,8},{12,14},{14,12},{16,18},{18,... | collective-permute-start | bytes 122888 | tf_op jit(solution)/shard_map/ppermute | solution.py:57
  8.3 3.9 %collective-permute-start = (bf16[64,256]{1,0:T(8,128)(2,1)S(1)}, bf16[64,256]{1,0:T(8,128)(2,1)S(1)}, u32[]{:S(2)}, u32[]{:S(2)}) collective-permute-start(bf16[64,256]{1,0:T(8,128)(2,1)S(1)} %get-tuple-element.33), channel_id=1, source_target_pairs={{0,2},{2,0},{4,6},{6,4},{8,10},{10,8},{12,14},{14,12},{16,18},{18,... | collective-permute-start | bytes 98312 | tf_op jit(solution)/shard_map/ppermute | solution.py:57
  9.6 7.2 %collective-permute-start.5 = (bf16[2,16,1280]{2,1,0:T(8,128)(2,1)S(1)}, bf16[2,16,1280]{2,1,0:T(8,128)(2,1)S(1)}, u32[]{:S(2)}, u32[]{:S(2)}) collective-permute-start(bf16[2,16,1280]{2,1,0:T(8,128)(2,1)S(1)} %pair.1.mine), channel_id=1, source_target_pairs={{0,16},{2,18},{4,20},{6,22},{8,24},{10,26},{12,28},{14,30},{16,0},... | collective-permute-start | bytes 245768 | tf_op jit(solution)/shard_map/ppermute | solution.py:57
  12.2 4.2 %collective-permute-start.1 = (bf16[96,256]{1,0:T(8,128)(2,1)S(1)}, bf16[96,256]{1,0:T(8,128)(2,1)S(1)}, u32[]{:S(2)}, u32[]{:S(2)}) collective-permute-start(bf16[96,256]{1,0:T(8,128)(2,1)S(1)} %get-tuple-element.36.mine.refs_0_), channel_id=1, source_target_pairs={{0,4},{2,6},{4,0},{6,2},{8,12},{10,14},{12,8},{14,10},{16,20},{18,... | collective-permute-start | bytes 147464 | tf_op jit(solution)/shard_map/ppermute | solution.py:57
  16.4 5.3 %collective-permute-start.2 = (bf16[128,256]{1,0:T(8,128)(2,1)S(1)}, bf16[128,256]{1,0:T(8,128)(2,1)S(1)}, u32[]{:S(2)}, u32[]{:S(2)}) collective-permute-start(bf16[128,256]{1,0:T(8,128)(2,1)S(1)} %get-tuple-element.38.mine), channel_id=1, source_target_pairs={{0,16},{2,18},{4,20},{6,22},{8,24},{10,26},{12,28},{14,30},{16,0},... | collective-permute-start | bytes 196616 | tf_op jit(solution)/shard_map/ppermute | solution.py:57
  16.8 9.7 %collective-permute-start.6 = (bf16[4,16,1280]{2,1,0:T(8,128)(2,1)S(1)}, bf16[4,16,1280]{2,1,0:T(8,128)(2,1)S(1)}, u32[]{:S(2)}, u32[]{:S(2)}) collective-permute-start(bf16[4,16,1280]{2,1,0:T(8,128)(2,1)S(1)} %join_blocks.2.mine), channel_id=1, source_target_pairs={{0,8},{2,10},{4,12},{6,14},{8,0},{10,2},{12,4},{14,6},{16,24},{18,... | collective-permute-start | bytes 491528 | tf_op jit(solution)/shard_map/ppermute | solution.py:57
  21.8 4.8 %collective-permute-start.3 = (bf16[192,256]{1,0:T(8,128)(2,1)S(1)}, bf16[192,256]{1,0:T(8,128)(2,1)S(1)}, u32[]{:S(2)}, u32[]{:S(2)}) collective-permute-start(bf16[192,256]{1,0:T(8,128)(2,1)S(1)} %get-tuple-element.40.mine.refs_0_), channel_id=1, source_target_pairs={{0,8},{2,10},{4,12},{6,14},{8,0},{10,2},{12,4},{14,6},{16,24},{18,... | collective-permute-start | bytes 294920 | tf_op jit(solution)/shard_map/ppermute | solution.py:57
  26.6 5.7 %collective-permute-start.7 = (bf16[384,256]{1,0:T(8,128)(2,1)S(1)}, bf16[384,256]{1,0:T(8,128)(2,1)S(1)}, u32[]{:S(2)}, u32[]{:S(2)}) collective-permute-start(bf16[384,256]{1,0:T(8,128)(2,1)S(1)} %join_last.1.refs_0_), channel_id=1, source_target_pairs={{0,1},{1,0},{2,3},{3,2},{4,5},{5,4},{6,7},{7,6},{8,9},{9,8},{10,11... | collective-permute-start | bytes 589832 | tf_op jit(solution)/shard_map/ppermute | solution.py:57
  27.2 7.9 %collective-permute-start.11 = (bf16[8,16,1280]{2,1,0:T(8,128)(2,1)S(1)}, bf16[8,16,1280]{2,1,0:T(8,128)(2,1)S(1)}, u32[]{:S(2)}, u32[]{:S(2)}) collective-permute-start(bf16[8,16,1280]{2,1,0:T(8,128)(2,1)S(1)} %join_blocks.3.mine), channel_id=1, source_target_pairs={{0,4},{2,6},{4,0},{6,2},{8,12},{10,14},{12,8},{14,10},{16,20},{18,... | collective-permute-start | bytes 983048 | tf_op jit(solution)/shard_map/ppermute | solution.py:57
  32.3 1.8 %collective-permute-start.9 = (bf16[2,256,256]{2,1,0:T(8,128)(2,1)S(1)}, bf16[2,256,256]{2,1,0:T(8,128)(2,1)S(1)}, u32[]{:S(2)}, u32[]{:S(2)}) collective-permute-start(bf16[2,256,256]{2,1,0:T(8,128)(2,1)S(1)} %get-tuple-element.43.mine), channel_id=1, source_target_pairs={{0,2},{2,0},{4,6},{6,4},{8,10},{10,8},{12,14},{14,12},{16,18},{18,... | collective-permute-start | bytes 786440 | tf_op jit(solution)/shard_map/ppermute | solution.py:57
  32.4 1.7 %collective-permute-start.10 = (f32[2,64,256]{2,1,0:T(8,128)S(1)}, f32[2,64,256]{2,1,0:T(8,128)S(1)}, u32[]{:S(2)}, u32[]{:S(2)}) collective-permute-start(f32[2,64,256]{2,1,0:T(8,128)S(1)} %get-tuple-element.44.q_mine), channel_id=1, source_target_pairs={{0,2},{2,0},{4,6},{6,4},{8,10},{10,8},{12,14},{14,12},{16,18},{18,... | collective-permute-start | bytes 393224 | tf_op jit(solution)/shard_map/ppermute | solution.py:57
  37.0 1.3 %collective-permute-start.12 = (bf16[2,64,256]{2,1,0:T(8,128)(2,1)S(1)}, bf16[2,64,256]{2,1,0:T(8,128)(2,1)S(1)}, u32[]{:S(2)}, u32[]{:S(2)}) collective-permute-start(bf16[2,64,256]{2,1,0:T(8,128)(2,1)S(1)} %get-tuple-element.57), channel_id=1, source_target_pairs={{0,2},{2,0},{4,6},{6,4},{8,10},{10,8},{12,14},{14,12},{16,18},{18,... | collective-permute-start | bytes 196616 | tf_op jit(solution)/shard_map/ppermute | solution.py:57
  38.3 4.3 %collective-permute-start.13 = (bf16[2,64,256]{2,1,0:T(8,128)(2,1)S(1)}, bf16[2,64,256]{2,1,0:T(8,128)(2,1)S(1)}, u32[]{:S(2)}, u32[]{:S(2)}) collective-permute-start(bf16[2,64,256]{2,1,0:T(8,128)(2,1)S(1)} %add.4.mine), channel_id=1, source_target_pairs={{0,1},{1,0},{2,3},{3,2},{4,5},{5,4},{6,7},{7,6},{8,9},{9,8},{10,11... | collective-permute-start | bytes 196616 | tf_op jit(solution)/shard_map/ppermute | solution.py:57
  42.7 1.3 %collective-permute-start.14 = (bf16[2,64,256]{2,1,0:T(8,128)(2,1)S(1)}, bf16[2,64,256]{2,1,0:T(8,128)(2,1)S(1)}, u32[]{:S(2)}, u32[]{:S(2)}) collective-permute-start(bf16[2,64,256]{2,1,0:T(8,128)(2,1)S(1)} %add.5.refs_1_.refs_0_), channel_id=1, source_target_pairs={{0,2},{2,0},{4,6},{6,4},{8,10},{10,8},{12,14},{14,12},{16,18},{18,... | collective-permute-start | bytes 196616 | tf_op jit(solution)/shard_map/ppermute | solution.py:57
  45.8 10.2 %copy-start.4 = (s32[1,8]{1,0:T(1,128)S(1)}, s32[1,8]{1,0:T(1,128)}, u32[]{:S(2)}) copy-start(s32[1,8]{1,0:T(1,128)} %blocks.1) | copy-start | bytes 100
  45.8 12.9 %copy-start = (f32[16,4096]{1,0:T(8,128)S(1)}, f32[16,4096]{1,0:T(8,128)}, u32[]{:S(2)}) copy-start(f32[16,4096]{1,0:T(8,128)} %refs_5_.1) | copy-start | bytes 786436
  45.8 12.8 %copy-start.1 = (f32[16,4096]{1,0:T(8,128)S(1)}, f32[16,4096]{1,0:T(8,128)}, u32[]{:S(2)}) copy-start(f32[16,4096]{1,0:T(8,128)} %refs_7_.1) | copy-start | bytes 786436
  45.8 12.8 %copy-start.2 = (f32[4,4096]{1,0:T(4,128)S(1)}, f32[4,4096]{1,0:T(4,128)}, u32[]{:S(2)}) copy-start(f32[4,4096]{1,0:T(4,128)} %refs_4_.1) | copy-start | bytes 196612
  45.8 12.8 %copy-start.3 = (f32[4,4096]{1,0:T(4,128)S(1)}, f32[4,4096]{1,0:T(4,128)}, u32[]{:S(2)}) copy-start(f32[4,4096]{1,0:T(4,128)} %refs_6_.1) | copy-start | bytes 196612
  45.8 1.3 %collective-permute-start.15 = (bf16[2,64,256]{2,1,0:T(8,128)(2,1)S(1)}, bf16[2,64,256]{2,1,0:T(8,128)(2,1)S(1)}, u32[]{:S(2)}, u32[]{:S(2)}) collective-permute-start(bf16[2,64,256]{2,1,0:T(8,128)(2,1)S(1)} %get-tuple-element.59), channel_id=1, source_target_pairs={{0,2},{2,0},{4,6},{6,4},{8,10},{10,8},{12,14},{14,12},{16,18},{18,... | collective-permute-start | bytes 196616 | tf_op jit(solution)/shard_map/ppermute | solution.py:57
  47.2 4.3 %collective-permute-start.16 = (bf16[2,64,256]{2,1,0:T(8,128)(2,1)S(1)}, bf16[2,64,256]{2,1,0:T(8,128)(2,1)S(1)}, u32[]{:S(2)}, u32[]{:S(2)}) collective-permute-start(bf16[2,64,256]{2,1,0:T(8,128)(2,1)S(1)} %add.6.mine), channel_id=1, source_target_pairs={{0,1},{1,0},{2,3},{3,2},{4,5},{5,4},{6,7},{7,6},{8,9},{9,8},{10,11... | collective-permute-start | bytes 196616 | tf_op jit(solution)/shard_map/ppermute | solution.py:57
  51.5 1.3 %collective-permute-start.17 = (bf16[2,64,256]{2,1,0:T(8,128)(2,1)S(1)}, bf16[2,64,256]{2,1,0:T(8,128)(2,1)S(1)}, u32[]{:S(2)}, u32[]{:S(2)}) collective-permute-start(bf16[2,64,256]{2,1,0:T(8,128)(2,1)S(1)} %add.7.refs_2_), channel_id=1, source_target_pairs={{0,2},{2,0},{4,6},{6,4},{8,10},{10,8},{12,14},{14,12},{16,18},{18,... | collective-permute-start | bytes 196616 | tf_op jit(solution)/shard_map/ppermute | solution.py:57
  53.7 4.1 %collective-permute-start.18 = (bf16[16,1280]{1,0:T(8,128)(2,1)S(1)}, bf16[16,1280]{1,0:T(8,128)(2,1)S(1)}, u32[]{:S(2)}, u32[]{:S(2)}) collective-permute-start(bf16[16,1280]{1,0:T(8,128)(2,1)S(1)} %get-tuple-element.60.refs_0_), channel_id=1, source_target_pairs={{0,1},{1,0},{2,3},{3,2},{4,5},{5,4},{6,7},{7,6},{8,9},{9,8},{10,11... | collective-permute-start | bytes 122888 | tf_op jit(solution)/shard_map/ppermute | solution.py:57
  55.2 2.6 %collective-permute-start.19 = (bf16[16,1280]{1,0:T(8,128)(2,1)S(1)}, bf16[16,1280]{1,0:T(8,128)(2,1)S(1)}, u32[]{:S(2)}, u32[]{:S(2)}) collective-permute-start(bf16[16,1280]{1,0:T(8,128)(2,1)S(1)} %get-tuple-element.61), channel_id=1, source_target_pairs={{0,2},{1,3},{2,0},{3,1},{4,6},{5,7},{6,4},{7,5},{8,10},{9,11},{10,... | collective-permute-start | bytes 122888 | tf_op jit(solution)/shard_map/ppermute | solution.py:57
  55.2 3.4 %collective-permute-start.20 = (bf16[16,1280]{1,0:T(8,128)(2,1)S(1)}, bf16[16,1280]{1,0:T(8,128)(2,1)S(1)}, u32[]{:S(2)}, u32[]{:S(2)}) collective-permute-start(bf16[16,1280]{1,0:T(8,128)(2,1)S(1)} %get-tuple-element.61), channel_id=1, source_target_pairs={{0,3},{1,2},{2,1},{3,0},{4,7},{5,6},{6,5},{7,4},{8,11},{9,10},{10,... | collective-permute-start | bytes 122888 | tf_op jit(solution)/shard_map/ppermute | solution.py:57

commit v8 on v7

--- a/solution.py
+++ b/solution.py
@@ -195,7 +195,7 @@
     coarse_in,
     fine_weight_in,
     coarse_weight_in,
-    fine_axial_in,
+    fine_axial,
     coarse_axial_in,
     measured_in,
     ray_weight_in,
@@ -213,7 +213,6 @@
     coarse,
     fine_weight,
     coarse_weight,
-    fine_axial,
     coarse_axial,
     measured,
     ray_weight,
@@ -228,7 +227,6 @@
     fz, cells = fine.shape
     half = cells // 2
     sources = (
-        (fine_axial_in, fine_axial),
         (coarse_axial_in, coarse_axial),
         (ray_weight_in, ray_weight),
         (measured_in, measured),
@@ -521,7 +519,8 @@
         for other in history[1:]:
             value = value + other[g]
         high, low = in_two(value)
-        for part, depth in enumerate((fine_depth[g, : 2 * fz], coarse_depth[g, : 2 * PACK])):
+        fine_rows = fine_depth[g, : 2 * PACK].astype(F32)[: 2 * fz].astype(BF16)
+        for part, depth in enumerate((fine_rows, coarse_depth[g, : 2 * PACK])):
             pair = in_two(spread(depth, high, views) + spread(depth, low, views))
             spreads[part].append(jnp.concatenate(pair, axis=0))
     backs = ([], [])
@@ -601,7 +600,6 @@
             coarse_volume,
             fine_cell_weight,
             coarse_cell_weight,
-            fine_axial,
             coarse_axial,
             measured,
             ray_weight,
@@ -618,7 +616,7 @@
                 shaped((det // 2, total), BF16),
                 shaped((2, views, share, columns), BF16),
             ),
-            [HBM] * (len(taken) + 2),
+            [HBM] * 6 + [VMEM] + [HBM] * 5,
             scratch_like(*taken)
             + [
                 pltpu.SMEM(margin_blocks.shape, jnp.int32),
@@ -627,7 +625,7 @@
                 pltpu.SemaphoreType.DMA((10,)),
                 pltpu.SemaphoreType.DMA((4, 4)),
             ],
-        )(*taken, *in_hbm(margin_blocks, ray_hits))
+        )(*taken[:6], fine_axial, *taken[6:], *in_hbm(margin_blocks, ray_hits))
 
         def to_views(value):
             values = [value]

time: 59.7 us -> 59.7 us (level)
  no operation moved by 1% of the time
where the time goes in v8:
time: 59.7 us; the launch traced here: 59.5 us
  waiting for transfers between devices  26.9 us (45%)
  starting transfers between devices  20.3 us (34%)
  Pallas kernels  11.4 us (19%)
  between operations  0.84 us (1%)
    ppermute x21, waiting for transfers between devices, swap(): return lax.ppermute(value, axis, [(i, i ^ bits) for i in range(size)])  26.9 us
    ppermute x21, starting transfers between devices, swap(): return lax.ppermute(value, axis, [(i, i ^ bits) for i in range(size)])  20.3 us
    pallas_call x2, Pallas kernels, body(): call(functools.partial(step_kernel, groups, views, ready), 'ray_space_ste...  3.41 us
    pallas_call x1, Pallas kernels, body(): call(start_kernel, 'start', (shaped((PACK, width), BF16), shaped((PACK, w...  3.33 us
    pallas_call x1, Pallas kernels, begin(): call(functools.partial(take_kernel, groups, bits), 'take_rays', shaped((2...  1.23 us
  transfers between devices with their start and end apart: 21, of which 15 were waited for; matrix products, arithmetic and copies ran while one was open for 0% of the time, Pallas kernels for 8%

profile of v8, /device:TPU:0, one launch (start us, length us, event | category | flops | bytes accessed | tf_op | source)
XLA Modules:
  0.0 59.5 jit_solution(13621719875975041227)
XLA Ops:
  0.6 1.2 %take_rays.1 = bf16[2,2,1024,128]{3,2,1,0:T(8,128)(2,1)S(1)} custom-call(bf16[2,4096,128]{2,1,0:T(8,128)(2,1)} %fine_rays.1, bf16[2,4096,128]{2,1,0:T(8,128)(2,1)} %coarse_rays.1), custom_call_target="tpu_custom_call" | custom-call | flops 1 | bytes 1 | tf_op jit(solution)/shard_map/take_rays/pallas_call | solution.py:644
  1.9 3.0 %collective-permute-start.8 = (bf16[2,2,1024,128]{3,2,1,0:T(8,128)(2,1)S(1)}, bf16[2,2,1024,128]{3,2,1,0:T(8,128)(2,1)S(1)}, u32[]{:S(2)}, u32[]{:S(2)}) collective-permute-start(bf16[2,2,1024,128]{3,2,1,0:T(8,128)(2,1)S(1)} %take_rays.1), channel_id=1, source_target_pairs={{0,1},{1,0},{2,3},{3,2},{4,5},{5,4},{6,7},{7,6},{8,9},{9,8},{10,11... | collective-permute-start | bytes 3145736 | tf_op jit(solution)/shard_map/ppermute | solution.py:57
  4.9 3.3 %start.1 = (bf16[16,1280]{1,0:T(8,128)(2,1)S(1)}, bf16[16,1280]{1,0:T(8,128)(2,1)S(1)}, bf16[32,256]{1,0:T(8,128)(2,1)S(1)}, f32[64,256]{1,0:T(8,128)S(1)}, bf16...) custom-call(bf16[2,4096,128]{2,1,0:T(8,128)(2,1)} %fine_rays.1, bf16[2,4096,128]{2,1,0:T(8,128)(2,1)} %coarse_rays.1, ...), custom_call_target="tpu_custom_call" | custom-call | flops 1 | bytes 1 | tf_op jit(solution)/shard_map/start/pallas_call | solution.py:608
  8.8 0.7 %collective-permute-done.4.received = bf16[16,1280]{1,0:T(8,128)(2,1)S(1)} collective-permute-done((bf16[16,1280]{1,0:T(8,128)(2,1)S(1)}, bf16[16,1280]{1,0:T(8,128)(2,1)S(1)}, u32[]{:S(2)}, u32[]{:S(2)}) %collective-permute-start.4) | collective-permute-done | bytes 40992 | tf_op jit(solution)/shard_map/ppermute | solution.py:57
  9.6 2.7 %collective-permute-start.5 = (bf16[2,16,1280]{2,1,0:T(8,128)(2,1)S(1)}, bf16[2,16,1280]{2,1,0:T(8,128)(2,1)S(1)}, u32[]{:S(2)}, u32[]{:S(2)}) collective-permute-start(bf16[2,16,1280]{2,1,0:T(8,128)(2,1)S(1)} %pair.1.mine), channel_id=1, source_target_pairs={{0,16},{2,18},{4,20},{6,22},{8,24},{10,26},{12,28},{14,30},{16,0},... | collective-permute-start | bytes 245768 | tf_op jit(solution)/shard_map/ppermute | solution.py:57
  12.2 1.6 %collective-permute-start.1 = (bf16[96,256]{1,0:T(8,128)(2,1)S(1)}, bf16[96,256]{1,0:T(8,128)(2,1)S(1)}, u32[]{:S(2)}, u32[]{:S(2)}) collective-permute-start(bf16[96,256]{1,0:T(8,128)(2,1)S(1)} %get-tuple-element.36.mine.refs_0_), channel_id=1, source_target_pairs={{0,4},{2,6},{4,0},{6,2},{8,12},{10,14},{12,8},{14,10},{16,20},{18,... | collective-permute-start | bytes 147464 | tf_op jit(solution)/shard_map/ppermute | solution.py:57
  13.8 2.6 %collective-permute-done.1.received = bf16[96,256]{1,0:T(8,128)(2,1)S(1)} collective-permute-done((bf16[96,256]{1,0:T(8,128)(2,1)S(1)}, bf16[96,256]{1,0:T(8,128)(2,1)S(1)}, u32[]{:S(2)}, u32[]{:S(2)}) %collective-permute-start.1) | collective-permute-done | bytes 49184 | tf_op jit(solution)/shard_map/ppermute | solution.py:57
  16.8 1.6 %collective-permute-start.6 = (bf16[4,16,1280]{2,1,0:T(8,128)(2,1)S(1)}, bf16[4,16,1280]{2,1,0:T(8,128)(2,1)S(1)}, u32[]{:S(2)}, u32[]{:S(2)}) collective-permute-start(bf16[4,16,1280]{2,1,0:T(8,128)(2,1)S(1)} %join_blocks.2.mine), channel_id=1, source_target_pairs={{0,8},{2,10},{4,12},{6,14},{8,0},{10,2},{12,4},{14,6},{16,24},{18,... | collective-permute-start | bytes 491528 | tf_op jit(solution)/shard_map/ppermute | solution.py:57
  18.5 3.3 %collective-permute-done.2.received = bf16[128,256]{1,0:T(8,128)(2,1)S(1)} collective-permute-done((bf16[128,256]{1,0:T(8,128)(2,1)S(1)}, bf16[128,256]{1,0:T(8,128)(2,1)S(1)}, u32[]{:S(2)}, u32[]{:S(2)}) %collective-permute-start.2) | collective-permute-done | bytes 65568 | tf_op jit(solution)/shard_map/ppermute | solution.py:57
  21.8 2.2 %collective-permute-start.3 = (bf16[192,256]{1,0:T(8,128)(2,1)S(1)}, bf16[192,256]{1,0:T(8,128)(2,1)S(1)}, u32[]{:S(2)}, u32[]{:S(2)}) collective-permute-start(bf16[192,256]{1,0:T(8,128)(2,1)S(1)} %get-tuple-element.40.mine.refs_0_), channel_id=1, source_target_pairs={{0,8},{2,10},{4,12},{6,14},{8,0},{10,2},{12,4},{14,6},{16,24},{18,... | collective-permute-start | bytes 294920 | tf_op jit(solution)/shard_map/ppermute | solution.py:57
  24.0 2.6 %collective-permute-done.3.received = bf16[192,256]{1,0:T(8,128)(2,1)S(1)} collective-permute-done((bf16[192,256]{1,0:T(8,128)(2,1)S(1)}, bf16[192,256]{1,0:T(8,128)(2,1)S(1)}, u32[]{:S(2)}, u32[]{:S(2)}) %collective-permute-start.3) | collective-permute-done | bytes 98336 | tf_op jit(solution)/shard_map/ppermute | solution.py:57
  26.6 0.6 collective-permute-start.7
  27.2 1.6 %collective-permute-start.11 = (bf16[8,16,1280]{2,1,0:T(8,128)(2,1)S(1)}, bf16[8,16,1280]{2,1,0:T(8,128)(2,1)S(1)}, u32[]{:S(2)}, u32[]{:S(2)}) collective-permute-start(bf16[8,16,1280]{2,1,0:T(8,128)(2,1)S(1)} %join_blocks.3.mine), channel_id=1, source_target_pairs={{0,4},{2,6},{4,0},{6,2},{8,12},{10,14},{12,8},{14,10},{16,20},{18,... | collective-permute-start | bytes 983048 | tf_op jit(solution)/shard_map/ppermute | solution.py:57
  28.7 3.6 %collective-permute-done.7.refs_1_ = bf16[384,256]{1,0:T(8,128)(2,1)S(1)} collective-permute-done((bf16[384,256]{1,0:T(8,128)(2,1)S(1)}, bf16[384,256]{1,0:T(8,128)(2,1)S(1)}, u32[]{:S(2)}, u32[]{:S(2)}) %collective-permute-start.7) | collective-permute-done | bytes 196640 | tf_op jit(solution)/shard_map/ppermute | solution.py:57
  32.9 1.2 %collective-permute-done.10.q_theirs = f32[2,64,256]{2,1,0:T(8,128)S(1)} collective-permute-done((f32[2,64,256]{2,1,0:T(8,128)S(1)}, f32[2,64,256]{2,1,0:T(8,128)S(1)}, u32[]{:S(2)}, u32[]{:S(2)}) %collective-permute-start.10) | collective-permute-done | bytes 131104 | tf_op jit(solution)/shard_map/ppermute | solution.py:57
  35.3 1.6 %ray_space_step.2 = (bf16[2,64,256]{2,1,0:T(8,128)(2,1)S(1)}, bf16[2,64,256]{2,1,0:T(8,128)(2,1)S(1)}) custom-call(bf16[2,64,256]{2,1,0:T(8,128)(2,1)S(1)} %get-tuple-element.49.refs_0_, bf16[2,256,256]{2,1,0:T(8,128)(2,1)S(1)} %get-tuple-element.50.refs_1_, bf16[2,2,128,64]{3,2,1,0:T(8,128)(2,1)S(1)} %get-tuple-element.51.refs_2_.refs_6_, ...), custom_call_target="tpu_custom_call" | custom-call | flops 1 | bytes 1 | tf_op jit(solution)/shard_map/ray_space_step/pallas_call | solution.py:765
  37.1 1.2 %collective-permute-done.12.received = bf16[2,64,256]{2,1,0:T(8,128)(2,1)S(1)} collective-permute-done((bf16[2,64,256]{2,1,0:T(8,128)(2,1)S(1)}, bf16[2,64,256]{2,1,0:T(8,128)(2,1)S(1)}, u32[]{:S(2)}, u32[]{:S(2)}) %collective-permute-start.12) | collective-permute-done | bytes 65568 | tf_op jit(solution)/shard_map/ppermute | solution.py:57
  38.3 1.4 %collective-permute-start.13 = (bf16[2,64,256]{2,1,0:T(8,128)(2,1)S(1)}, bf16[2,64,256]{2,1,0:T(8,128)(2,1)S(1)}, u32[]{:S(2)}, u32[]{:S(2)}) collective-permute-start(bf16[2,64,256]{2,1,0:T(8,128)(2,1)S(1)} %add.4.mine), channel_id=1, source_target_pairs={{0,1},{1,0},{2,3},{3,2},{4,5},{5,4},{6,7},{7,6},{8,9},{9,8},{10,11... | collective-permute-start | bytes 196616 | tf_op jit(solution)/shard_map/ppermute | solution.py:57
  39.8 2.9 %collective-permute-done.13.received = bf16[2,64,256]{2,1,0:T(8,128)(2,1)S(1)} collective-permute-done((bf16[2,64,256]{2,1,0:T(8,128)(2,1)S(1)}, bf16[2,64,256]{2,1,0:T(8,128)(2,1)S(1)}, u32[]{:S(2)}, u32[]{:S(2)}) %collective-permute-start.13) | collective-permute-done | bytes 65568 | tf_op jit(solution)/shard_map/ppermute | solution.py:57
  42.8 1.2 %collective-permute-done.14.refs_2_.refs_1_ = bf16[2,64,256]{2,1,0:T(8,128)(2,1)S(1)} collective-permute-done((bf16[2,64,256]{2,1,0:T(8,128)(2,1)S(1)}, bf16[2,64,256]{2,1,0:T(8,128)(2,1)S(1)}, u32[]{:S(2)}, u32[]{:S(2)}) %collective-permute-start.14) | collective-permute-done | bytes 65568 | tf_op jit(solution)/shard_map/ppermute | solution.py:57
  44.0 1.8 %ray_space_step.3 = (bf16[2,64,256]{2,1,0:T(8,128)(2,1)S(1)}, bf16[2,64,256]{2,1,0:T(8,128)(2,1)S(1)}) custom-call(f32[2,128,256]{2,1,0:T(8,128)S(1)} %get-tuple-element.45.q.refs_0_, bf16[2,64,256]{2,1,0:T(8,128)(2,1)S(1)} %add.5.refs_1_.refs_0_, bf16[2,64,256]{2,1,0:T(8,128)(2,1)S(1)} %collective-permute-done.14.refs_2_.refs_1_, ...), custom_call_target="tpu_custom_call" | custom-call | flops 1 | bytes 1 | tf_op jit(solution)/shard_map/ray_space_step/pallas_call | solution.py:765
  46.1 1.1 %collective-permute-done.15.received = bf16[2,64,256]{2,1,0:T(8,128)(2,1)S(1)} collective-permute-done((bf16[2,64,256]{2,1,0:T(8,128)(2,1)S(1)}, bf16[2,64,256]{2,1,0:T(8,128)(2,1)S(1)}, u32[]{:S(2)}, u32[]{:S(2)}) %collective-permute-start.15) | collective-permute-done | bytes 65568 | tf_op jit(solution)/shard_map/ppermute | solution.py:57
  47.2 1.4 %collective-permute-start.16 = (bf16[2,64,256]{2,1,0:T(8,128)(2,1)S(1)}, bf16[2,64,256]{2,1,0:T(8,128)(2,1)S(1)}, u32[]{:S(2)}, u32[]{:S(2)}) collective-permute-start(bf16[2,64,256]{2,1,0:T(8,128)(2,1)S(1)} %add.6.mine), channel_id=1, source_target_pairs={{0,1},{1,0},{2,3},{3,2},{4,5},{5,4},{6,7},{7,6},{8,9},{9,8},{10,11... | collective-permute-start | bytes 196616 | tf_op jit(solution)/shard_map/ppermute | solution.py:57
  48.6 2.9 %collective-permute-done.16.received = bf16[2,64,256]{2,1,0:T(8,128)(2,1)S(1)} collective-permute-done((bf16[2,64,256]{2,1,0:T(8,128)(2,1)S(1)}, bf16[2,64,256]{2,1,0:T(8,128)(2,1)S(1)}, u32[]{:S(2)}, u32[]{:S(2)}) %collective-permute-start.16) | collective-permute-done | bytes 65568 | tf_op jit(solution)/shard_map/ppermute | solution.py:57
  51.6 1.2 %collective-permute-done.17.refs_3_ = bf16[2,64,256]{2,1,0:T(8,128)(2,1)S(1)} collective-permute-done((bf16[2,64,256]{2,1,0:T(8,128)(2,1)S(1)}, bf16[2,64,256]{2,1,0:T(8,128)(2,1)S(1)}, u32[]{:S(2)}, u32[]{:S(2)}) %collective-permute-start.17) | collective-permute-done | bytes 65568 | tf_op jit(solution)/shard_map/ppermute | solution.py:57
  52.9 0.9 %back_projection.1 = (bf16[16,1280]{1,0:T(8,128)(2,1)S(1)}, bf16[16,1280]{1,0:T(8,128)(2,1)S(1)}) custom-call(f32[2,128,256]{2,1,0:T(8,128)S(1)} %get-tuple-element.45.q.refs_0_, bf16[2,64,256]{2,1,0:T(8,128)(2,1)S(1)} %add.5.refs_1_.refs_0_, bf16[2,64,256]{2,1,0:T(8,128)(2,1)S(1)} %collective-permute-done.14.refs_2_.refs_1_, ...), custom_call_target="tpu_custom_call" | custom-call | flops 1 | bytes 1 | tf_op jit(solution)/shard_map/back_projection/pallas_call | solution.py:777
  53.8 1.5 %collective-permute-start.18 = (bf16[16,1280]{1,0:T(8,128)(2,1)S(1)}, bf16[16,1280]{1,0:T(8,128)(2,1)S(1)}, u32[]{:S(2)}, u32[]{:S(2)}) collective-permute-start(bf16[16,1280]{1,0:T(8,128)(2,1)S(1)} %get-tuple-element.60.refs_0_), channel_id=1, source_target_pairs={{0,1},{1,0},{2,3},{3,2},{4,5},{5,4},{6,7},{7,6},{8,9},{9,8},{10,11... | collective-permute-start | bytes 122888 | tf_op jit(solution)/shard_map/ppermute | solution.py:57
  55.2 0.8 %collective-permute-start.20 = (bf16[16,1280]{1,0:T(8,128)(2,1)S(1)}, bf16[16,1280]{1,0:T(8,128)(2,1)S(1)}, u32[]{:S(2)}, u32[]{:S(2)}) collective-permute-start(bf16[16,1280]{1,0:T(8,128)(2,1)S(1)} %get-tuple-element.61), channel_id=1, source_target_pairs={{0,3},{1,2},{2,1},{3,0},{4,7},{5,6},{6,5},{7,4},{8,11},{9,10},{10,... | collective-permute-start | bytes 122888 | tf_op jit(solution)/shard_map/ppermute | solution.py:57
  56.0 0.6 %keep.1.refs_8_ = f32[1,4096]{1,0:T(1,128)S(1)} custom-call(s32[1,8]{1,0:T(1,128)S(1)} %copy-done.5), custom_call_target="tpu_custom_call" | custom-call | flops 1 | bytes 1 | tf_op jit(solution)/shard_map/keep/pallas_call | solution.py:783
  56.6 1.2 %collective-permute-done.18.refs_1_ = bf16[16,1280]{1,0:T(8,128)(2,1)S(1)} collective-permute-done((bf16[16,1280]{1,0:T(8,128)(2,1)S(1)}, bf16[16,1280]{1,0:T(8,128)(2,1)S(1)}, u32[]{:S(2)}, u32[]{:S(2)}) %collective-permute-start.18) | collective-permute-done | bytes 40992 | tf_op jit(solution)/shard_map/ppermute | solution.py:57
  57.8 0.8 %collective-permute-done.20.refs_3_ = bf16[16,1280]{1,0:T(8,128)(2,1)S(1)} collective-permute-done((bf16[16,1280]{1,0:T(8,128)(2,1)S(1)}, bf16[16,1280]{1,0:T(8,128)(2,1)S(1)}, u32[]{:S(2)}, u32[]{:S(2)}) %collective-permute-start.20) | collective-permute-done | bytes 40992 | tf_op jit(solution)/shard_map/ppermute | solution.py:57
  58.7 0.8 %update.1 = (f32[4,4096]{1,0:T(4,128)}, f32[16,4096]{1,0:T(8,128)}) custom-call(bf16[16,1280]{1,0:T(8,128)(2,1)S(1)} %get-tuple-element.60.refs_0_, bf16[16,1280]{1,0:T(8,128)(2,1)S(1)} %collective-permute-done.18.refs_1_, bf16[16,1280]{1,0:T(8,128)(2,1)S(1)} %collective-permute-done.19.refs_2_, bf16[16,1280]{1,0:T(8,128)(2,1)S(1)} %collective-permute-done.20.refs_3_, ...), custom_call_target="tpu_custom_call" | custom-call | flops 1 | bytes 1 | tf_op jit(solution)/shard_map/update/pallas_call | solution.py:787
  (44 shorter events, 3.4 us)
Async XLA Ops:
  0.6 4.3 %copy-start.4 = (bf16[2,4,128]{2,1,0:T(4,128)(2,1)S(1)}, bf16[2,4,128]{2,1,0:T(4,128)(2,1)}, u32[]{:S(2)}) copy-start(bf16[2,4,128]{2,1,0:T(4,128)(2,1)} %fine_axial.1) | copy-start | bytes 6148
  1.9 30.4 %collective-permute-start.8 = (bf16[2,2,1024,128]{3,2,1,0:T(8,128)(2,1)S(1)}, bf16[2,2,1024,128]{3,2,1,0:T(8,128)(2,1)S(1)}, u32[]{:S(2)}, u32[]{:S(2)}) collective-permute-start(bf16[2,2,1024,128]{3,2,1,0:T(8,128)(2,1)S(1)} %take_rays.1), channel_id=1, source_target_pairs={{0,1},{1,0},{2,3},{3,2},{4,5},{5,4},{6,7},{7,6},{8,9},{9,8},{10,11... | collective-permute-start | bytes 3145736 | tf_op jit(solution)/shard_map/ppermute | solution.py:57
  8.3 1.3 %collective-permute-start.4 = (bf16[16,1280]{1,0:T(8,128)(2,1)S(1)}, bf16[16,1280]{1,0:T(8,128)(2,1)S(1)}, u32[]{:S(2)}, u32[]{:S(2)}) collective-permute-start(bf16[16,1280]{1,0:T(8,128)(2,1)S(1)} %get-tuple-element.42), channel_id=1, source_target_pairs={{0,2},{2,0},{4,6},{6,4},{8,10},{10,8},{12,14},{14,12},{16,18},{18,... | collective-permute-start | bytes 122888 | tf_op jit(solution)/shard_map/ppermute | solution.py:57
  8.3 3.9 %collective-permute-start = (bf16[64,256]{1,0:T(8,128)(2,1)S(1)}, bf16[64,256]{1,0:T(8,128)(2,1)S(1)}, u32[]{:S(2)}, u32[]{:S(2)}) collective-permute-start(bf16[64,256]{1,0:T(8,128)(2,1)S(1)} %get-tuple-element.33), channel_id=1, source_target_pairs={{0,2},{2,0},{4,6},{6,4},{8,10},{10,8},{12,14},{14,12},{16,18},{18,... | collective-permute-start | bytes 98312 | tf_op jit(solution)/shard_map/ppermute | solution.py:57
  9.6 7.2 %collective-permute-start.5 = (bf16[2,16,1280]{2,1,0:T(8,128)(2,1)S(1)}, bf16[2,16,1280]{2,1,0:T(8,128)(2,1)S(1)}, u32[]{:S(2)}, u32[]{:S(2)}) collective-permute-start(bf16[2,16,1280]{2,1,0:T(8,128)(2,1)S(1)} %pair.1.mine), channel_id=1, source_target_pairs={{0,16},{2,18},{4,20},{6,22},{8,24},{10,26},{12,28},{14,30},{16,0},... | collective-permute-start | bytes 245768 | tf_op jit(solution)/shard_map/ppermute | solution.py:57
  12.2 4.2 %collective-permute-start.1 = (bf16[96,256]{1,0:T(8,128)(2,1)S(1)}, bf16[96,256]{1,0:T(8,128)(2,1)S(1)}, u32[]{:S(2)}, u32[]{:S(2)}) collective-permute-start(bf16[96,256]{1,0:T(8,128)(2,1)S(1)} %get-tuple-element.36.mine.refs_0_), channel_id=1, source_target_pairs={{0,4},{2,6},{4,0},{6,2},{8,12},{10,14},{12,8},{14,10},{16,20},{18,... | collective-permute-start | bytes 147464 | tf_op jit(solution)/shard_map/ppermute | solution.py:57
  16.4 5.3 %collective-permute-start.2 = (bf16[128,256]{1,0:T(8,128)(2,1)S(1)}, bf16[128,256]{1,0:T(8,128)(2,1)S(1)}, u32[]{:S(2)}, u32[]{:S(2)}) collective-permute-start(bf16[128,256]{1,0:T(8,128)(2,1)S(1)} %get-tuple-element.38.mine), channel_id=1, source_target_pairs={{0,16},{2,18},{4,20},{6,22},{8,24},{10,26},{12,28},{14,30},{16,0},... | collective-permute-start | bytes 196616 | tf_op jit(solution)/shard_map/ppermute | solution.py:57
  16.8 9.7 %collective-permute-start.6 = (bf16[4,16,1280]{2,1,0:T(8,128)(2,1)S(1)}, bf16[4,16,1280]{2,1,0:T(8,128)(2,1)S(1)}, u32[]{:S(2)}, u32[]{:S(2)}) collective-permute-start(bf16[4,16,1280]{2,1,0:T(8,128)(2,1)S(1)} %join_blocks.2.mine), channel_id=1, source_target_pairs={{0,8},{2,10},{4,12},{6,14},{8,0},{10,2},{12,4},{14,6},{16,24},{18,... | collective-permute-start | bytes 491528 | tf_op jit(solution)/shard_map/ppermute | solution.py:57
  21.8 4.8 %collective-permute-start.3 = (bf16[192,256]{1,0:T(8,128)(2,1)S(1)}, bf16[192,256]{1,0:T(8,128)(2,1)S(1)}, u32[]{:S(2)}, u32[]{:S(2)}) collective-permute-start(bf16[192,256]{1,0:T(8,128)(2,1)S(1)} %get-tuple-element.40.mine.refs_0_), channel_id=1, source_target_pairs={{0,8},{2,10},{4,12},{6,14},{8,0},{10,2},{12,4},{14,6},{16,24},{18,... | collective-permute-start | bytes 294920 | tf_op jit(solution)/shard_map/ppermute | solution.py:57
  26.6 5.7 %collective-permute-start.7 = (bf16[384,256]{1,0:T(8,128)(2,1)S(1)}, bf16[384,256]{1,0:T(8,128)(2,1)S(1)}, u32[]{:S(2)}, u32[]{:S(2)}) collective-permute-start(bf16[384,256]{1,0:T(8,128)(2,1)S(1)} %join_last.1.refs_0_), channel_id=1, source_target_pairs={{0,1},{1,0},{2,3},{3,2},{4,5},{5,4},{6,7},{7,6},{8,9},{9,8},{10,11... | collective-permute-start | bytes 589832 | tf_op jit(solution)/shard_map/ppermute | solution.py:57
  27.2 7.9 %collective-permute-start.11 = (bf16[8,16,1280]{2,1,0:T(8,128)(2,1)S(1)}, bf16[8,16,1280]{2,1,0:T(8,128)(2,1)S(1)}, u32[]{:S(2)}, u32[]{:S(2)}) collective-permute-start(bf16[8,16,1280]{2,1,0:T(8,128)(2,1)S(1)} %join_blocks.3.mine), channel_id=1, source_target_pairs={{0,4},{2,6},{4,0},{6,2},{8,12},{10,14},{12,8},{14,10},{16,20},{18,... | collective-permute-start | bytes 983048 | tf_op jit(solution)/shard_map/ppermute | solution.py:57
  32.3 1.8 %collective-permute-start.9 = (bf16[2,256,256]{2,1,0:T(8,128)(2,1)S(1)}, bf16[2,256,256]{2,1,0:T(8,128)(2,1)S(1)}, u32[]{:S(2)}, u32[]{:S(2)}) collective-permute-start(bf16[2,256,256]{2,1,0:T(8,128)(2,1)S(1)} %get-tuple-element.43.mine), channel_id=1, source_target_pairs={{0,2},{2,0},{4,6},{6,4},{8,10},{10,8},{12,14},{14,12},{16,18},{18,... | collective-permute-start | bytes 786440 | tf_op jit(solution)/shard_map/ppermute | solution.py:57
  32.4 1.7 %collective-permute-start.10 = (f32[2,64,256]{2,1,0:T(8,128)S(1)}, f32[2,64,256]{2,1,0:T(8,128)S(1)}, u32[]{:S(2)}, u32[]{:S(2)}) collective-permute-start(f32[2,64,256]{2,1,0:T(8,128)S(1)} %get-tuple-element.44.q_mine), channel_id=1, source_target_pairs={{0,2},{2,0},{4,6},{6,4},{8,10},{10,8},{12,14},{14,12},{16,18},{18,... | collective-permute-start | bytes 393224 | tf_op jit(solution)/shard_map/ppermute | solution.py:57
  37.0 1.3 %collective-permute-start.12 = (bf16[2,64,256]{2,1,0:T(8,128)(2,1)S(1)}, bf16[2,64,256]{2,1,0:T(8,128)(2,1)S(1)}, u32[]{:S(2)}, u32[]{:S(2)}) collective-permute-start(bf16[2,64,256]{2,1,0:T(8,128)(2,1)S(1)} %get-tuple-element.57), channel_id=1, source_target_pairs={{0,2},{2,0},{4,6},{6,4},{8,10},{10,8},{12,14},{14,12},{16,18},{18,... | collective-permute-start | bytes 196616 | tf_op jit(solution)/shard_map/ppermute | solution.py:57
  38.3 4.3 %collective-permute-start.13 = (bf16[2,64,256]{2,1,0:T(8,128)(2,1)S(1)}, bf16[2,64,256]{2,1,0:T(8,128)(2,1)S(1)}, u32[]{:S(2)}, u32[]{:S(2)}) collective-permute-start(bf16[2,64,256]{2,1,0:T(8,128)(2,1)S(1)} %add.4.mine), channel_id=1, source_target_pairs={{0,1},{1,0},{2,3},{3,2},{4,5},{5,4},{6,7},{7,6},{8,9},{9,8},{10,11... | collective-permute-start | bytes 196616 | tf_op jit(solution)/shard_map/ppermute | solution.py:57
  42.7 1.3 %collective-permute-start.14 = (bf16[2,64,256]{2,1,0:T(8,128)(2,1)S(1)}, bf16[2,64,256]{2,1,0:T(8,128)(2,1)S(1)}, u32[]{:S(2)}, u32[]{:S(2)}) collective-permute-start(bf16[2,64,256]{2,1,0:T(8,128)(2,1)S(1)} %add.5.refs_1_.refs_0_), channel_id=1, source_target_pairs={{0,2},{2,0},{4,6},{6,4},{8,10},{10,8},{12,14},{14,12},{16,18},{18,... | collective-permute-start | bytes 196616 | tf_op jit(solution)/shard_map/ppermute | solution.py:57
  45.8 10.2 %copy-start.5 = (s32[1,8]{1,0:T(1,128)S(1)}, s32[1,8]{1,0:T(1,128)}, u32[]{:S(2)}) copy-start(s32[1,8]{1,0:T(1,128)} %blocks.1) | copy-start | bytes 100
  45.8 12.8 %copy-start = (f32[16,4096]{1,0:T(8,128)S(1)}, f32[16,4096]{1,0:T(8,128)}, u32[]{:S(2)}) copy-start(f32[16,4096]{1,0:T(8,128)} %refs_5_.1) | copy-start | bytes 786436
  45.8 12.8 %copy-start.1 = (f32[16,4096]{1,0:T(8,128)S(1)}, f32[16,4096]{1,0:T(8,128)}, u32[]{:S(2)}) copy-start(f32[16,4096]{1,0:T(8,128)} %refs_7_.1) | copy-start | bytes 786436
  45.8 12.8 %copy-start.2 = (f32[4,4096]{1,0:T(4,128)S(1)}, f32[4,4096]{1,0:T(4,128)}, u32[]{:S(2)}) copy-start(f32[4,4096]{1,0:T(4,128)} %refs_4_.1) | copy-start | bytes 196612
  45.8 12.8 %copy-start.3 = (f32[4,4096]{1,0:T(4,128)S(1)}, f32[4,4096]{1,0:T(4,128)}, u32[]{:S(2)}) copy-start(f32[4,4096]{1,0:T(4,128)} %refs_6_.1) | copy-start | bytes 196612
  45.8 1.3 %collective-permute-start.15 = (bf16[2,64,256]{2,1,0:T(8,128)(2,1)S(1)}, bf16[2,64,256]{2,1,0:T(8,128)(2,1)S(1)}, u32[]{:S(2)}, u32[]{:S(2)}) collective-permute-start(bf16[2,64,256]{2,1,0:T(8,128)(2,1)S(1)} %get-tuple-element.59), channel_id=1, source_target_pairs={{0,2},{2,0},{4,6},{6,4},{8,10},{10,8},{12,14},{14,12},{16,18},{18,... | collective-permute-start | bytes 196616 | tf_op jit(solution)/shard_map/ppermute | solution.py:57
  47.2 4.3 %collective-permute-start.16 = (bf16[2,64,256]{2,1,0:T(8,128)(2,1)S(1)}, bf16[2,64,256]{2,1,0:T(8,128)(2,1)S(1)}, u32[]{:S(2)}, u32[]{:S(2)}) collective-permute-start(bf16[2,64,256]{2,1,0:T(8,128)(2,1)S(1)} %add.6.mine), channel_id=1, source_target_pairs={{0,1},{1,0},{2,3},{3,2},{4,5},{5,4},{6,7},{7,6},{8,9},{9,8},{10,11... | collective-permute-start | bytes 196616 | tf_op jit(solution)/shard_map/ppermute | solution.py:57
  51.5 1.3 %collective-permute-start.17 = (bf16[2,64,256]{2,1,0:T(8,128)(2,1)S(1)}, bf16[2,64,256]{2,1,0:T(8,128)(2,1)S(1)}, u32[]{:S(2)}, u32[]{:S(2)}) collective-permute-start(bf16[2,64,256]{2,1,0:T(8,128)(2,1)S(1)} %add.7.refs_2_), channel_id=1, source_target_pairs={{0,2},{2,0},{4,6},{6,4},{8,10},{10,8},{12,14},{14,12},{16,18},{18,... | collective-permute-start | bytes 196616 | tf_op jit(solution)/shard_map/ppermute | solution.py:57
  53.8 4.1 %collective-permute-start.18 = (bf16[16,1280]{1,0:T(8,128)(2,1)S(1)}, bf16[16,1280]{1,0:T(8,128)(2,1)S(1)}, u32[]{:S(2)}, u32[]{:S(2)}) collective-permute-start(bf16[16,1280]{1,0:T(8,128)(2,1)S(1)} %get-tuple-element.60.refs_0_), channel_id=1, source_target_pairs={{0,1},{1,0},{2,3},{3,2},{4,5},{5,4},{6,7},{7,6},{8,9},{9,8},{10,11... | collective-permute-start | bytes 122888 | tf_op jit(solution)/shard_map/ppermute | solution.py:57
  55.2 2.6 %collective-permute-start.19 = (bf16[16,1280]{1,0:T(8,128)(2,1)S(1)}, bf16[16,1280]{1,0:T(8,128)(2,1)S(1)}, u32[]{:S(2)}, u32[]{:S(2)}) collective-permute-start(bf16[16,1280]{1,0:T(8,128)(2,1)S(1)} %get-tuple-element.61), channel_id=1, source_target_pairs={{0,2},{1,3},{2,0},{3,1},{4,6},{5,7},{6,4},{7,5},{8,10},{9,11},{10,... | collective-permute-start | bytes 122888 | tf_op jit(solution)/shard_map/ppermute | solution.py:57
  55.2 3.4 %collective-permute-start.20 = (bf16[16,1280]{1,0:T(8,128)(2,1)S(1)}, bf16[16,1280]{1,0:T(8,128)(2,1)S(1)}, u32[]{:S(2)}, u32[]{:S(2)}) collective-permute-start(bf16[16,1280]{1,0:T(8,128)(2,1)S(1)} %get-tuple-element.61), channel_id=1, source_target_pairs={{0,3},{1,2},{2,1},{3,0},{4,7},{5,6},{6,5},{7,4},{8,11},{9,10},{10,... | collective-permute-start | bytes 122888 | tf_op jit(solution)/shard_map/ppermute | solution.py:57

commit v9 on v8

--- a/solution.py
+++ b/solution.py
@@ -189,8 +189,8 @@
 
 
 def start_kernel(
-    fine_rays_in,
-    coarse_rays_in,
+    fine_rays,
+    coarse_rays,
     fine_in,
     coarse_in,
     fine_weight_in,
@@ -207,8 +207,6 @@
     out,
     short,
     own_rays,
-    fine_rays,
-    coarse_rays,
     fine,
     coarse,
     fine_weight,
@@ -245,18 +243,14 @@
             [
                 fetch(fine_in.at[:, part], fine.at[:, part], chunk_sems.at[i, 0]),
                 fetch(coarse_in.at[:, part], coarse.at[:, part], chunk_sems.at[i, 1]),
-                fetch(fine_rays_in.at[:, part, :], fine_rays.at[:, part, :], chunk_sems.at[i, 2]),
-                fetch(
-                    coarse_rays_in.at[:, part, :], coarse_rays.at[:, part, :], chunk_sems.at[i, 3]
-                ),
             ]
         )
     share = own_rays.shape[2]
     groups = half // share
     held = pl.ds(share_start(cells, groups), share)
     outgoing = [
-        fetch(fine_rays_in.at[:, held, :], own_rays.at[0], sems.at[8]),
-        fetch(coarse_rays_in.at[:, held, :], own_rays.at[1], sems.at[9]),
+        fetch(fine_rays.at[:, held, :], own_rays.at[0], sems.at[8]),
+        fetch(coarse_rays.at[:, held, :], own_rays.at[1], sems.at[9]),
     ]
     for copy in others:
         copy.wait()
@@ -330,8 +324,17 @@
     return ((me - me % 2) ^ apart) + (block & 1)
 
 
+def turn_kernel(fine, coarse, fine_out, coarse_out):
+    det = fine_out.shape[2]
+    for source, out in ((fine, fine_out), (coarse, coarse_out)):
+        for g in range(out.shape[0]):
+            wide = source[g].astype(F32)
+            for v in range(out.shape[1]):
+                out[g, v] = wide[:, v * det : (v + 1) * det].T.astype(BF16)
+
+
 def rows_kernel(own, fz, bits, mine, theirs, q_mine, q_theirs, *refs):
-    coarse_out, fine_out, coarse_turned, fine_turned, out, q_out = refs[-6:]
+    coarse_out, fine_out, out, q_out = refs[-4:]
     lead = lax.axis_index("slab") % 2 == 0
     kept = q_mine.shape[1]
     for g in range(q_mine.shape[0]):
@@ -369,11 +372,6 @@
         fine = dot(to_fine, side, ((1,), (0,)))
         coarse_out[g] = coarse
         fine_out[g] = fine.astype(BF16)
-        wide = coarse.astype(F32)
-        for v in range(coarse.shape[1] // det):
-            where = slice(v * det, (v + 1) * det)
-            coarse_turned[g, v] = wide[:, where].T.astype(BF16)
-            fine_turned[g, v] = fine[:, where].T.astype(BF16)
         out[g] = dot(to_weight, side, ((1,), (0,)))[:, :total]
 
 
@@ -594,8 +592,6 @@
         width = share + packed_tiles(share, fz) * LANES
 
         taken = in_hbm(
-            fine_rays,
-            coarse_rays,
             fine_volume,
             coarse_volume,
             fine_cell_weight,
@@ -616,7 +612,7 @@
                 shaped((det // 2, total), BF16),
                 shaped((2, views, share, columns), BF16),
             ),
-            [HBM] * 6 + [VMEM] + [HBM] * 5,
+            [VMEM] * 2 + [HBM] * 4 + [VMEM] + [HBM] * 5,
             scratch_like(*taken)
             + [
                 pltpu.SMEM(margin_blocks.shape, jnp.int32),
@@ -625,7 +621,14 @@
                 pltpu.SemaphoreType.DMA((10,)),
                 pltpu.SemaphoreType.DMA((4, 4)),
             ],
-        )(*taken[:6], fine_axial, *taken[6:], *in_hbm(margin_blocks, ray_hits))
+        )(
+            fine_rays,
+            coarse_rays,
+            *taken[:4],
+            fine_axial,
+            *taken[4:],
+            *in_hbm(margin_blocks, ray_hits),
+        )
 
         def to_views(value):
             values = [value]
@@ -720,14 +723,12 @@
             (j & 1) + 2 * (j >> 2) + (((j >> 1) & 1) << (count + 1)) for j in range(slabs)
         )
         waits = waits_of("rows")
-        coarse_depth, fine_depth, coarse_turned, fine_turned, weights, q = call(
+        coarse_depth, fine_depth, weights, q = call(
             functools.partial(rows_kernel, own, fz, [2] + far_bits),
             "unpack_rows",
             (
                 shaped((groups, slabs * PACK, span), BF16),
                 shaped((groups, slabs * fz, span), BF16),
-                shaped((groups, views, det, slabs * PACK), BF16),
-                shaped((groups, views, det, slabs * fz), BF16),
                 shaped((groups, det, total), F32),
                 shaped((groups, det, total), F32),
             ),
@@ -742,11 +743,20 @@
             ),
             [VMEM] * 4,
         )(q, weights, fine_depth, coarse_depth)
+        fine_turned, coarse_turned = call(
+            turn_kernel,
+            "turn",
+            (
+                shaped((groups, views, det, slabs * fz), BF16),
+                shaped((groups, views, det, slabs * PACK), BF16),
+            ),
+            [VMEM] * 2,
+        )(fine_depth, coarse_depth)
         coarse_weights, fine_weights = call(
             functools.partial(weights_kernel, fz, order),
             "unpack_weights",
             (shaped((slabs * PACK, share), BF16), shaped((slabs * fz, share), BF16)),
-            [VMEM] * 2 + [ANY] * len(spreads),
+            [VMEM] * 2 + [ANY] * 2,
         )(*got["weights"], *spreads)
         rays = [own_rays] + got["rays"]
         held = (fine_turned, coarse_turned, coarse_weights, fine_weights, *rays)

time: 59.7 us -> 60.1 us (level)
  starting transfers between devices: 20.3 us -> 21.7 us
    ppermute x21, starting transfers between devices: 20.3 us -> 21.7 us  [swap(): return lax.ppermute(value, axis, [(i, i ^ bits) for i in range(size)])]
    pallas_call x1, Pallas kernels: 3.33 us -> 2.47 us  [body(): call(start_kernel, 'start', (shaped((PACK, width), BF16), shaped((PACK, w...]
  transfers between devices with their start and end apart: 21 -> 21, of which waited for: 15 -> 14; matrix products, arithmetic and copies ran while one was open for 0% -> 0% of each run, Pallas kernels for 8% -> 7%
where the time goes in v9:
time: 60.1 us; the launch traced here: 59.8 us
  waiting for transfers between devices  26.4 us (44%)
  starting transfers between devices  21.7 us (36%)
  Pallas kernels  10.8 us (18%)
  between operations  0.87 us (1%)
    ppermute x21, waiting for transfers between devices, swap(): return lax.ppermute(value, axis, [(i, i ^ bits) for i in range(size)])  26.4 us
    ppermute x21, starting transfers between devices, swap(): return lax.ppermute(value, axis, [(i, i ^ bits) for i in range(size)])  21.7 us
    pallas_call x2, Pallas kernels, body(): call(functools.partial(step_kernel, groups, views, ready), 'ray_space_ste...  3.45 us
    pallas_call x1, Pallas kernels, body(): call(start_kernel, 'start', (shaped((PACK, width), BF16), shaped((PACK, w...  2.47 us
    pallas_call x1, Pallas kernels, begin(): call(functools.partial(take_kernel, groups, bits), 'take_rays', shaped((2...  1.38 us
  transfers between devices with their start and end apart: 21, of which 14 were waited for; matrix products, arithmetic and copies ran while one was open for 0% of the time, Pallas kernels for 7%

profile of v9, /device:TPU:0, one launch (start us, length us, event | category | flops | bytes accessed | tf_op | source)
XLA Modules:
  0.0 59.8 jit_solution(9955294725994784128)
XLA Ops:
  0.7 1.4 %take_rays.1 = bf16[2,2,1024,128]{3,2,1,0:T(8,128)(2,1)S(1)} custom-call(bf16[2,4096,128]{2,1,0:T(8,128)(2,1)} %fine_rays.3, bf16[2,4096,128]{2,1,0:T(8,128)(2,1)} %coarse_rays.3), custom_call_target="tpu_custom_call" | custom-call | flops 1 | bytes 1 | tf_op jit(solution)/shard_map/take_rays/pallas_call | solution.py:647
  2.1 3.0 %collective-permute-start.8 = (bf16[2,2,1024,128]{3,2,1,0:T(8,128)(2,1)S(1)}, bf16[2,2,1024,128]{3,2,1,0:T(8,128)(2,1)S(1)}, u32[]{:S(2)}, u32[]{:S(2)}) collective-permute-start(bf16[2,2,1024,128]{3,2,1,0:T(8,128)(2,1)S(1)} %take_rays.1), channel_id=1, source_target_pairs={{0,1},{1,0},{2,3},{3,2},{4,5},{5,4},{6,7},{7,6},{8,9},{9,8},{10,11... | collective-permute-start | bytes 3145736 | tf_op jit(solution)/shard_map/ppermute | solution.py:57
  5.1 2.5 %start.1 = (bf16[16,1280]{1,0:T(8,128)(2,1)S(1)}, bf16[16,1280]{1,0:T(8,128)(2,1)S(1)}, bf16[32,256]{1,0:T(8,128)(2,1)S(1)}, f32[64,256]{1,0:T(8,128)S(1)}, bf16...) custom-call(bf16[2,4096,128]{2,1,0:T(8,128)(2,1)S(1)} %copy-done, bf16[2,4096,128]{2,1,0:T(8,128)(2,1)S(1)} %copy-done.1, ...), custom_call_target="tpu_custom_call" | custom-call | flops 1 | bytes 1 | tf_op jit(solution)/shard_map/start/pallas_call | solution.py:604
  7.7 0.5 collective-permute-start
  8.1 0.7 %collective-permute-done.4.received = bf16[16,1280]{1,0:T(8,128)(2,1)S(1)} collective-permute-done((bf16[16,1280]{1,0:T(8,128)(2,1)S(1)}, bf16[16,1280]{1,0:T(8,128)(2,1)S(1)}, u32[]{:S(2)}, u32[]{:S(2)}) %collective-permute-start.4) | collective-permute-done | bytes 40992 | tf_op jit(solution)/shard_map/ppermute | solution.py:57
  8.9 2.7 %collective-permute-start.5 = (bf16[2,16,1280]{2,1,0:T(8,128)(2,1)S(1)}, bf16[2,16,1280]{2,1,0:T(8,128)(2,1)S(1)}, u32[]{:S(2)}, u32[]{:S(2)}) collective-permute-start(bf16[2,16,1280]{2,1,0:T(8,128)(2,1)S(1)} %pair.1.mine), channel_id=1, source_target_pairs={{0,16},{2,18},{4,20},{6,22},{8,24},{10,26},{12,28},{14,30},{16,0},... | collective-permute-start | bytes 245768 | tf_op jit(solution)/shard_map/ppermute | solution.py:57
  11.6 1.6 %collective-permute-start.1 = (bf16[96,256]{1,0:T(8,128)(2,1)S(1)}, bf16[96,256]{1,0:T(8,128)(2,1)S(1)}, u32[]{:S(2)}, u32[]{:S(2)}) collective-permute-start(bf16[96,256]{1,0:T(8,128)(2,1)S(1)} %get-tuple-element.36.mine.refs_0_), channel_id=1, source_target_pairs={{0,4},{2,6},{4,0},{6,2},{8,12},{10,14},{12,8},{14,10},{16,20},{18,... | collective-permute-start | bytes 147464 | tf_op jit(solution)/shard_map/ppermute | solution.py:57
  13.1 2.6 %collective-permute-done.1.received = bf16[96,256]{1,0:T(8,128)(2,1)S(1)} collective-permute-done((bf16[96,256]{1,0:T(8,128)(2,1)S(1)}, bf16[96,256]{1,0:T(8,128)(2,1)S(1)}, u32[]{:S(2)}, u32[]{:S(2)}) %collective-permute-start.1) | collective-permute-done | bytes 49184 | tf_op jit(solution)/shard_map/ppermute | solution.py:57
  16.1 1.6 %collective-permute-start.6 = (bf16[4,16,1280]{2,1,0:T(8,128)(2,1)S(1)}, bf16[4,16,1280]{2,1,0:T(8,128)(2,1)S(1)}, u32[]{:S(2)}, u32[]{:S(2)}) collective-permute-start(bf16[4,16,1280]{2,1,0:T(8,128)(2,1)S(1)} %join_blocks.2.mine), channel_id=1, source_target_pairs={{0,8},{2,10},{4,12},{6,14},{8,0},{10,2},{12,4},{14,6},{16,24},{18,... | collective-permute-start | bytes 491528 | tf_op jit(solution)/shard_map/ppermute | solution.py:57
  17.8 3.3 %collective-permute-done.2.received = bf16[128,256]{1,0:T(8,128)(2,1)S(1)} collective-permute-done((bf16[128,256]{1,0:T(8,128)(2,1)S(1)}, bf16[128,256]{1,0:T(8,128)(2,1)S(1)}, u32[]{:S(2)}, u32[]{:S(2)}) %collective-permute-start.2) | collective-permute-done | bytes 65568 | tf_op jit(solution)/shard_map/ppermute | solution.py:57
  21.1 2.2 %collective-permute-start.3 = (bf16[192,256]{1,0:T(8,128)(2,1)S(1)}, bf16[192,256]{1,0:T(8,128)(2,1)S(1)}, u32[]{:S(2)}, u32[]{:S(2)}) collective-permute-start(bf16[192,256]{1,0:T(8,128)(2,1)S(1)} %get-tuple-element.40.mine.refs_0_), channel_id=1, source_target_pairs={{0,8},{2,10},{4,12},{6,14},{8,0},{10,2},{12,4},{14,6},{16,24},{18,... | collective-permute-start | bytes 294920 | tf_op jit(solution)/shard_map/ppermute | solution.py:57
  23.3 2.6 %collective-permute-done.3.received = bf16[192,256]{1,0:T(8,128)(2,1)S(1)} collective-permute-done((bf16[192,256]{1,0:T(8,128)(2,1)S(1)}, bf16[192,256]{1,0:T(8,128)(2,1)S(1)}, u32[]{:S(2)}, u32[]{:S(2)}) %collective-permute-start.3) | collective-permute-done | bytes 98336 | tf_op jit(solution)/shard_map/ppermute | solution.py:57
  25.9 1.1 %collective-permute-start.7 = (bf16[384,256]{1,0:T(8,128)(2,1)S(1)}, bf16[384,256]{1,0:T(8,128)(2,1)S(1)}, u32[]{:S(2)}, u32[]{:S(2)}) collective-permute-start(bf16[384,256]{1,0:T(8,128)(2,1)S(1)} %join_last.1.refs_0_), channel_id=1, source_target_pairs={{0,1},{1,0},{2,3},{3,2},{4,5},{5,4},{6,7},{7,6},{8,9},{9,8},{10,11... | collective-permute-start | bytes 589832 | tf_op jit(solution)/shard_map/ppermute | solution.py:57
  27.0 1.6 %collective-permute-start.11 = (bf16[8,16,1280]{2,1,0:T(8,128)(2,1)S(1)}, bf16[8,16,1280]{2,1,0:T(8,128)(2,1)S(1)}, u32[]{:S(2)}, u32[]{:S(2)}) collective-permute-start(bf16[8,16,1280]{2,1,0:T(8,128)(2,1)S(1)} %join_blocks.3.mine), channel_id=1, source_target_pairs={{0,4},{2,6},{4,0},{6,2},{8,12},{10,14},{12,8},{14,10},{16,20},{18,... | collective-permute-start | bytes 983048 | tf_op jit(solution)/shard_map/ppermute | solution.py:57
  28.6 3.9 %collective-permute-done.7.refs_1_ = bf16[384,256]{1,0:T(8,128)(2,1)S(1)} collective-permute-done((bf16[384,256]{1,0:T(8,128)(2,1)S(1)}, bf16[384,256]{1,0:T(8,128)(2,1)S(1)}, u32[]{:S(2)}, u32[]{:S(2)}) %collective-permute-start.7) | collective-permute-done | bytes 196640 | tf_op jit(solution)/shard_map/ppermute | solution.py:57
  33.1 1.2 %collective-permute-done.10.q_theirs = f32[2,64,256]{2,1,0:T(8,128)S(1)} collective-permute-done((f32[2,64,256]{2,1,0:T(8,128)S(1)}, f32[2,64,256]{2,1,0:T(8,128)S(1)}, u32[]{:S(2)}, u32[]{:S(2)}) %collective-permute-start.10) | collective-permute-done | bytes 131104 | tf_op jit(solution)/shard_map/ppermute | solution.py:57
  35.3 1.7 %ray_space_step.2 = (bf16[2,64,256]{2,1,0:T(8,128)(2,1)S(1)}, bf16[2,64,256]{2,1,0:T(8,128)(2,1)S(1)}) custom-call(bf16[2,64,256]{2,1,0:T(8,128)(2,1)S(1)} %get-tuple-element.49.refs_0_, bf16[2,256,256]{2,1,0:T(8,128)(2,1)S(1)} %get-tuple-element.50.refs_1_, bf16[2,2,128,64]{3,2,1,0:T(8,128)(2,1)S(1)} %get-tuple-element.51.refs_2_.refs_6_, ...), custom_call_target="tpu_custom_call" | custom-call | flops 1 | bytes 1 | tf_op jit(solution)/shard_map/ray_space_step/pallas_call | solution.py:775
  37.2 1.1 %collective-permute-done.12.received = bf16[2,64,256]{2,1,0:T(8,128)(2,1)S(1)} collective-permute-done((bf16[2,64,256]{2,1,0:T(8,128)(2,1)S(1)}, bf16[2,64,256]{2,1,0:T(8,128)(2,1)S(1)}, u32[]{:S(2)}, u32[]{:S(2)}) %collective-permute-start.12) | collective-permute-done | bytes 65568 | tf_op jit(solution)/shard_map/ppermute | solution.py:57
  38.3 1.8 %collective-permute-start.13 = (bf16[2,64,256]{2,1,0:T(8,128)(2,1)S(1)}, bf16[2,64,256]{2,1,0:T(8,128)(2,1)S(1)}, u32[]{:S(2)}, u32[]{:S(2)}) collective-permute-start(bf16[2,64,256]{2,1,0:T(8,128)(2,1)S(1)} %add.4.mine), channel_id=1, source_target_pairs={{0,1},{1,0},{2,3},{3,2},{4,5},{5,4},{6,7},{7,6},{8,9},{9,8},{10,11... | collective-permute-start | bytes 196616 | tf_op jit(solution)/shard_map/ppermute | solution.py:57
  40.1 2.5 %collective-permute-done.13.received = bf16[2,64,256]{2,1,0:T(8,128)(2,1)S(1)} collective-permute-done((bf16[2,64,256]{2,1,0:T(8,128)(2,1)S(1)}, bf16[2,64,256]{2,1,0:T(8,128)(2,1)S(1)}, u32[]{:S(2)}, u32[]{:S(2)}) %collective-permute-start.13) | collective-permute-done | bytes 65568 | tf_op jit(solution)/shard_map/ppermute | solution.py:57
  42.8 1.2 %collective-permute-done.14.refs_2_.refs_1_ = bf16[2,64,256]{2,1,0:T(8,128)(2,1)S(1)} collective-permute-done((bf16[2,64,256]{2,1,0:T(8,128)(2,1)S(1)}, bf16[2,64,256]{2,1,0:T(8,128)(2,1)S(1)}, u32[]{:S(2)}, u32[]{:S(2)}) %collective-permute-start.14) | collective-permute-done | bytes 65568 | tf_op jit(solution)/shard_map/ppermute | solution.py:57
  44.0 1.8 %ray_space_step.3 = (bf16[2,64,256]{2,1,0:T(8,128)(2,1)S(1)}, bf16[2,64,256]{2,1,0:T(8,128)(2,1)S(1)}) custom-call(f32[2,128,256]{2,1,0:T(8,128)S(1)} %get-tuple-element.45.q.refs_0_, bf16[2,64,256]{2,1,0:T(8,128)(2,1)S(1)} %add.5.refs_1_.refs_0_, bf16[2,64,256]{2,1,0:T(8,128)(2,1)S(1)} %collective-permute-done.14.refs_2_.refs_1_, ...), custom_call_target="tpu_custom_call" | custom-call | flops 1 | bytes 1 | tf_op jit(solution)/shard_map/ray_space_step/pallas_call | solution.py:775
  46.1 1.1 %collective-permute-done.15.received = bf16[2,64,256]{2,1,0:T(8,128)(2,1)S(1)} collective-permute-done((bf16[2,64,256]{2,1,0:T(8,128)(2,1)S(1)}, bf16[2,64,256]{2,1,0:T(8,128)(2,1)S(1)}, u32[]{:S(2)}, u32[]{:S(2)}) %collective-permute-start.15) | collective-permute-done | bytes 65568 | tf_op jit(solution)/shard_map/ppermute | solution.py:57
  47.2 1.8 %collective-permute-start.16 = (bf16[2,64,256]{2,1,0:T(8,128)(2,1)S(1)}, bf16[2,64,256]{2,1,0:T(8,128)(2,1)S(1)}, u32[]{:S(2)}, u32[]{:S(2)}) collective-permute-start(bf16[2,64,256]{2,1,0:T(8,128)(2,1)S(1)} %add.6.mine), channel_id=1, source_target_pairs={{0,1},{1,0},{2,3},{3,2},{4,5},{5,4},{6,7},{7,6},{8,9},{9,8},{10,11... | collective-permute-start | bytes 196616 | tf_op jit(solution)/shard_map/ppermute | solution.py:57
  49.0 2.5 %collective-permute-done.16.received = bf16[2,64,256]{2,1,0:T(8,128)(2,1)S(1)} collective-permute-done((bf16[2,64,256]{2,1,0:T(8,128)(2,1)S(1)}, bf16[2,64,256]{2,1,0:T(8,128)(2,1)S(1)}, u32[]{:S(2)}, u32[]{:S(2)}) %collective-permute-start.16) | collective-permute-done | bytes 65568 | tf_op jit(solution)/shard_map/ppermute | solution.py:57
  51.6 1.2 %collective-permute-done.17.refs_3_ = bf16[2,64,256]{2,1,0:T(8,128)(2,1)S(1)} collective-permute-done((bf16[2,64,256]{2,1,0:T(8,128)(2,1)S(1)}, bf16[2,64,256]{2,1,0:T(8,128)(2,1)S(1)}, u32[]{:S(2)}, u32[]{:S(2)}) %collective-permute-start.17) | collective-permute-done | bytes 65568 | tf_op jit(solution)/shard_map/ppermute | solution.py:57
  52.9 0.9 %back_projection.1 = (bf16[16,1280]{1,0:T(8,128)(2,1)S(1)}, bf16[16,1280]{1,0:T(8,128)(2,1)S(1)}) custom-call(f32[2,128,256]{2,1,0:T(8,128)S(1)} %get-tuple-element.45.q.refs_0_, bf16[2,64,256]{2,1,0:T(8,128)(2,1)S(1)} %add.5.refs_1_.refs_0_, bf16[2,64,256]{2,1,0:T(8,128)(2,1)S(1)} %collective-permute-done.14.refs_2_.refs_1_, ...), custom_call_target="tpu_custom_call" | custom-call | flops 1 | bytes 1 | tf_op jit(solution)/shard_map/back_projection/pallas_call | solution.py:787
  53.8 1.8 %collective-permute-start.18 = (bf16[16,1280]{1,0:T(8,128)(2,1)S(1)}, bf16[16,1280]{1,0:T(8,128)(2,1)S(1)}, u32[]{:S(2)}, u32[]{:S(2)}) collective-permute-start(bf16[16,1280]{1,0:T(8,128)(2,1)S(1)} %get-tuple-element.60.refs_0_), channel_id=1, source_target_pairs={{0,1},{1,0},{2,3},{3,2},{4,5},{5,4},{6,7},{7,6},{8,9},{9,8},{10,11... | collective-permute-start | bytes 122888 | tf_op jit(solution)/shard_map/ppermute | solution.py:57
  56.0 0.6 %keep.1.refs_8_ = f32[1,4096]{1,0:T(1,128)S(1)} custom-call(s32[1,8]{1,0:T(1,128)S(1)} %copy-done.7), custom_call_target="tpu_custom_call" | custom-call | flops 1 | bytes 1 | tf_op jit(solution)/shard_map/keep/pallas_call | solution.py:793
  56.6 1.2 %collective-permute-done.18.refs_1_ = bf16[16,1280]{1,0:T(8,128)(2,1)S(1)} collective-permute-done((bf16[16,1280]{1,0:T(8,128)(2,1)S(1)}, bf16[16,1280]{1,0:T(8,128)(2,1)S(1)}, u32[]{:S(2)}, u32[]{:S(2)}) %collective-permute-start.18) | collective-permute-done | bytes 40992 | tf_op jit(solution)/shard_map/ppermute | solution.py:57
  57.9 1.2 %collective-permute-done.20.refs_3_ = bf16[16,1280]{1,0:T(8,128)(2,1)S(1)} collective-permute-done((bf16[16,1280]{1,0:T(8,128)(2,1)S(1)}, bf16[16,1280]{1,0:T(8,128)(2,1)S(1)}, u32[]{:S(2)}, u32[]{:S(2)}) %collective-permute-start.20) | collective-permute-done | bytes 40992 | tf_op jit(solution)/shard_map/ppermute | solution.py:57
  59.0 0.8 %update.1 = (f32[4,4096]{1,0:T(4,128)}, f32[16,4096]{1,0:T(8,128)}) custom-call(bf16[16,1280]{1,0:T(8,128)(2,1)S(1)} %get-tuple-element.60.refs_0_, bf16[16,1280]{1,0:T(8,128)(2,1)S(1)} %collective-permute-done.18.refs_1_, bf16[16,1280]{1,0:T(8,128)(2,1)S(1)} %collective-permute-done.19.refs_2_, bf16[16,1280]{1,0:T(8,128)(2,1)S(1)} %collective-permute-done.20.refs_3_, ...), custom_call_target="tpu_custom_call" | custom-call | flops 1 | bytes 1 | tf_op jit(solution)/shard_map/update/pallas_call | solution.py:797
  (49 shorter events, 3.3 us)
Async XLA Ops:
  0.6 4.5 %copy-start = (bf16[2,4096,128]{2,1,0:T(8,128)(2,1)S(1)}, bf16[2,4096,128]{2,1,0:T(8,128)(2,1)}, u32[]{:S(2)}) copy-start(bf16[2,4096,128]{2,1,0:T(8,128)(2,1)} %fine_rays.3) | copy-start | bytes 6291460
  0.6 4.4 %copy-start.1 = (bf16[2,4096,128]{2,1,0:T(8,128)(2,1)S(1)}, bf16[2,4096,128]{2,1,0:T(8,128)(2,1)}, u32[]{:S(2)}) copy-start(bf16[2,4096,128]{2,1,0:T(8,128)(2,1)} %coarse_rays.3) | copy-start | bytes 6291460
  0.7 4.4 %copy-start.6 = (bf16[2,4,128]{2,1,0:T(4,128)(2,1)S(1)}, bf16[2,4,128]{2,1,0:T(4,128)(2,1)}, u32[]{:S(2)}) copy-start(bf16[2,4,128]{2,1,0:T(4,128)(2,1)} %fine_axial.1) | copy-start | bytes 6148
  2.1 30.4 %collective-permute-start.8 = (bf16[2,2,1024,128]{3,2,1,0:T(8,128)(2,1)S(1)}, bf16[2,2,1024,128]{3,2,1,0:T(8,128)(2,1)S(1)}, u32[]{:S(2)}, u32[]{:S(2)}) collective-permute-start(bf16[2,2,1024,128]{3,2,1,0:T(8,128)(2,1)S(1)} %take_rays.1), channel_id=1, source_target_pairs={{0,1},{1,0},{2,3},{3,2},{4,5},{5,4},{6,7},{7,6},{8,9},{9,8},{10,11... | collective-permute-start | bytes 3145736 | tf_op jit(solution)/shard_map/ppermute | solution.py:57
  7.6 1.3 %collective-permute-start.4 = (bf16[16,1280]{1,0:T(8,128)(2,1)S(1)}, bf16[16,1280]{1,0:T(8,128)(2,1)S(1)}, u32[]{:S(2)}, u32[]{:S(2)}) collective-permute-start(bf16[16,1280]{1,0:T(8,128)(2,1)S(1)} %get-tuple-element.42), channel_id=1, source_target_pairs={{0,2},{2,0},{4,6},{6,4},{8,10},{10,8},{12,14},{14,12},{16,18},{18,... | collective-permute-start | bytes 122888 | tf_op jit(solution)/shard_map/ppermute | solution.py:57
  7.7 3.9 %collective-permute-start = (bf16[64,256]{1,0:T(8,128)(2,1)S(1)}, bf16[64,256]{1,0:T(8,128)(2,1)S(1)}, u32[]{:S(2)}, u32[]{:S(2)}) collective-permute-start(bf16[64,256]{1,0:T(8,128)(2,1)S(1)} %get-tuple-element.33), channel_id=1, source_target_pairs={{0,2},{2,0},{4,6},{6,4},{8,10},{10,8},{12,14},{14,12},{16,18},{18,... | collective-permute-start | bytes 98312 | tf_op jit(solution)/shard_map/ppermute | solution.py:57
  8.9 7.2 %collective-permute-start.5 = (bf16[2,16,1280]{2,1,0:T(8,128)(2,1)S(1)}, bf16[2,16,1280]{2,1,0:T(8,128)(2,1)S(1)}, u32[]{:S(2)}, u32[]{:S(2)}) collective-permute-start(bf16[2,16,1280]{2,1,0:T(8,128)(2,1)S(1)} %pair.1.mine), channel_id=1, source_target_pairs={{0,16},{2,18},{4,20},{6,22},{8,24},{10,26},{12,28},{14,30},{16,0},... | collective-permute-start | bytes 245768 | tf_op jit(solution)/shard_map/ppermute | solution.py:57
  11.6 4.2 %collective-permute-start.1 = (bf16[96,256]{1,0:T(8,128)(2,1)S(1)}, bf16[96,256]{1,0:T(8,128)(2,1)S(1)}, u32[]{:S(2)}, u32[]{:S(2)}) collective-permute-start(bf16[96,256]{1,0:T(8,128)(2,1)S(1)} %get-tuple-element.36.mine.refs_0_), channel_id=1, source_target_pairs={{0,4},{2,6},{4,0},{6,2},{8,12},{10,14},{12,8},{14,10},{16,20},{18,... | collective-permute-start | bytes 147464 | tf_op jit(solution)/shard_map/ppermute | solution.py:57
  15.7 5.3 %collective-permute-start.2 = (bf16[128,256]{1,0:T(8,128)(2,1)S(1)}, bf16[128,256]{1,0:T(8,128)(2,1)S(1)}, u32[]{:S(2)}, u32[]{:S(2)}) collective-permute-start(bf16[128,256]{1,0:T(8,128)(2,1)S(1)} %get-tuple-element.38.mine), channel_id=1, source_target_pairs={{0,16},{2,18},{4,20},{6,22},{8,24},{10,26},{12,28},{14,30},{16,0},... | collective-permute-start | bytes 196616 | tf_op jit(solution)/shard_map/ppermute | solution.py:57
  16.1 9.7 %collective-permute-start.6 = (bf16[4,16,1280]{2,1,0:T(8,128)(2,1)S(1)}, bf16[4,16,1280]{2,1,0:T(8,128)(2,1)S(1)}, u32[]{:S(2)}, u32[]{:S(2)}) collective-permute-start(bf16[4,16,1280]{2,1,0:T(8,128)(2,1)S(1)} %join_blocks.2.mine), channel_id=1, source_target_pairs={{0,8},{2,10},{4,12},{6,14},{8,0},{10,2},{12,4},{14,6},{16,24},{18,... | collective-permute-start | bytes 491528 | tf_op jit(solution)/shard_map/ppermute | solution.py:57
  21.1 4.8 %collective-permute-start.3 = (bf16[192,256]{1,0:T(8,128)(2,1)S(1)}, bf16[192,256]{1,0:T(8,128)(2,1)S(1)}, u32[]{:S(2)}, u32[]{:S(2)}) collective-permute-start(bf16[192,256]{1,0:T(8,128)(2,1)S(1)} %get-tuple-element.40.mine.refs_0_), channel_id=1, source_target_pairs={{0,8},{2,10},{4,12},{6,14},{8,0},{10,2},{12,4},{14,6},{16,24},{18,... | collective-permute-start | bytes 294920 | tf_op jit(solution)/shard_map/ppermute | solution.py:57
  25.9 6.6 %collective-permute-start.7 = (bf16[384,256]{1,0:T(8,128)(2,1)S(1)}, bf16[384,256]{1,0:T(8,128)(2,1)S(1)}, u32[]{:S(2)}, u32[]{:S(2)}) collective-permute-start(bf16[384,256]{1,0:T(8,128)(2,1)S(1)} %join_last.1.refs_0_), channel_id=1, source_target_pairs={{0,1},{1,0},{2,3},{3,2},{4,5},{5,4},{6,7},{7,6},{8,9},{9,8},{10,11... | collective-permute-start | bytes 589832 | tf_op jit(solution)/shard_map/ppermute | solution.py:57
  27.0 8.1 %collective-permute-start.11 = (bf16[8,16,1280]{2,1,0:T(8,128)(2,1)S(1)}, bf16[8,16,1280]{2,1,0:T(8,128)(2,1)S(1)}, u32[]{:S(2)}, u32[]{:S(2)}) collective-permute-start(bf16[8,16,1280]{2,1,0:T(8,128)(2,1)S(1)} %join_blocks.3.mine), channel_id=1, source_target_pairs={{0,4},{2,6},{4,0},{6,2},{8,12},{10,14},{12,8},{14,10},{16,20},{18,... | collective-permute-start | bytes 983048 | tf_op jit(solution)/shard_map/ppermute | solution.py:57
  32.5 1.8 %collective-permute-start.9 = (bf16[2,256,256]{2,1,0:T(8,128)(2,1)S(1)}, bf16[2,256,256]{2,1,0:T(8,128)(2,1)S(1)}, u32[]{:S(2)}, u32[]{:S(2)}) collective-permute-start(bf16[2,256,256]{2,1,0:T(8,128)(2,1)S(1)} %get-tuple-element.43.mine), channel_id=1, source_target_pairs={{0,2},{2,0},{4,6},{6,4},{8,10},{10,8},{12,14},{14,12},{16,18},{18,... | collective-permute-start | bytes 786440 | tf_op jit(solution)/shard_map/ppermute | solution.py:57
  32.6 1.7 %collective-permute-start.10 = (f32[2,64,256]{2,1,0:T(8,128)S(1)}, f32[2,64,256]{2,1,0:T(8,128)S(1)}, u32[]{:S(2)}, u32[]{:S(2)}) collective-permute-start(f32[2,64,256]{2,1,0:T(8,128)S(1)} %get-tuple-element.44.q_mine), channel_id=1, source_target_pairs={{0,2},{2,0},{4,6},{6,4},{8,10},{10,8},{12,14},{14,12},{16,18},{18,... | collective-permute-start | bytes 393224 | tf_op jit(solution)/shard_map/ppermute | solution.py:57
  37.0 1.3 %collective-permute-start.12 = (bf16[2,64,256]{2,1,0:T(8,128)(2,1)S(1)}, bf16[2,64,256]{2,1,0:T(8,128)(2,1)S(1)}, u32[]{:S(2)}, u32[]{:S(2)}) collective-permute-start(bf16[2,64,256]{2,1,0:T(8,128)(2,1)S(1)} %get-tuple-element.57), channel_id=1, source_target_pairs={{0,2},{2,0},{4,6},{6,4},{8,10},{10,8},{12,14},{14,12},{16,18},{18,... | collective-permute-start | bytes 196616 | tf_op jit(solution)/shard_map/ppermute | solution.py:57
  38.3 4.3 %collective-permute-start.13 = (bf16[2,64,256]{2,1,0:T(8,128)(2,1)S(1)}, bf16[2,64,256]{2,1,0:T(8,128)(2,1)S(1)}, u32[]{:S(2)}, u32[]{:S(2)}) collective-permute-start(bf16[2,64,256]{2,1,0:T(8,128)(2,1)S(1)} %add.4.mine), channel_id=1, source_target_pairs={{0,1},{1,0},{2,3},{3,2},{4,5},{5,4},{6,7},{7,6},{8,9},{9,8},{10,11... | collective-permute-start | bytes 196616 | tf_op jit(solution)/shard_map/ppermute | solution.py:57
  42.7 1.3 %collective-permute-start.14 = (bf16[2,64,256]{2,1,0:T(8,128)(2,1)S(1)}, bf16[2,64,256]{2,1,0:T(8,128)(2,1)S(1)}, u32[]{:S(2)}, u32[]{:S(2)}) collective-permute-start(bf16[2,64,256]{2,1,0:T(8,128)(2,1)S(1)} %add.5.refs_1_.refs_0_), channel_id=1, source_target_pairs={{0,2},{2,0},{4,6},{6,4},{8,10},{10,8},{12,14},{14,12},{16,18},{18,... | collective-permute-start | bytes 196616 | tf_op jit(solution)/shard_map/ppermute | solution.py:57
  45.8 10.2 %copy-start.7 = (s32[1,8]{1,0:T(1,128)S(1)}, s32[1,8]{1,0:T(1,128)}, u32[]{:S(2)}) copy-start(s32[1,8]{1,0:T(1,128)} %blocks.1) | copy-start | bytes 100
  45.8 13.2 %copy-start.2 = (f32[16,4096]{1,0:T(8,128)S(1)}, f32[16,4096]{1,0:T(8,128)}, u32[]{:S(2)}) copy-start(f32[16,4096]{1,0:T(8,128)} %refs_5_.1) | copy-start | bytes 786436
  45.8 13.2 %copy-start.3 = (f32[16,4096]{1,0:T(8,128)S(1)}, f32[16,4096]{1,0:T(8,128)}, u32[]{:S(2)}) copy-start(f32[16,4096]{1,0:T(8,128)} %refs_7_.1) | copy-start | bytes 786436
  45.8 13.2 %copy-start.4 = (f32[4,4096]{1,0:T(4,128)S(1)}, f32[4,4096]{1,0:T(4,128)}, u32[]{:S(2)}) copy-start(f32[4,4096]{1,0:T(4,128)} %refs_4_.1) | copy-start | bytes 196612
  45.8 13.2 %copy-start.5 = (f32[4,4096]{1,0:T(4,128)S(1)}, f32[4,4096]{1,0:T(4,128)}, u32[]{:S(2)}) copy-start(f32[4,4096]{1,0:T(4,128)} %refs_6_.1) | copy-start | bytes 196612
  45.9 1.3 %collective-permute-start.15 = (bf16[2,64,256]{2,1,0:T(8,128)(2,1)S(1)}, bf16[2,64,256]{2,1,0:T(8,128)(2,1)S(1)}, u32[]{:S(2)}, u32[]{:S(2)}) collective-permute-start(bf16[2,64,256]{2,1,0:T(8,128)(2,1)S(1)} %get-tuple-element.59), channel_id=1, source_target_pairs={{0,2},{2,0},{4,6},{6,4},{8,10},{10,8},{12,14},{14,12},{16,18},{18,... | collective-permute-start | bytes 196616 | tf_op jit(solution)/shard_map/ppermute | solution.py:57
  47.2 4.3 %collective-permute-start.16 = (bf16[2,64,256]{2,1,0:T(8,128)(2,1)S(1)}, bf16[2,64,256]{2,1,0:T(8,128)(2,1)S(1)}, u32[]{:S(2)}, u32[]{:S(2)}) collective-permute-start(bf16[2,64,256]{2,1,0:T(8,128)(2,1)S(1)} %add.6.mine), channel_id=1, source_target_pairs={{0,1},{1,0},{2,3},{3,2},{4,5},{5,4},{6,7},{7,6},{8,9},{9,8},{10,11... | collective-permute-start | bytes 196616 | tf_op jit(solution)/shard_map/ppermute | solution.py:57
  51.6 1.3 %collective-permute-start.17 = (bf16[2,64,256]{2,1,0:T(8,128)(2,1)S(1)}, bf16[2,64,256]{2,1,0:T(8,128)(2,1)S(1)}, u32[]{:S(2)}, u32[]{:S(2)}) collective-permute-start(bf16[2,64,256]{2,1,0:T(8,128)(2,1)S(1)} %add.7.refs_2_), channel_id=1, source_target_pairs={{0,2},{2,0},{4,6},{6,4},{8,10},{10,8},{12,14},{14,12},{16,18},{18,... | collective-permute-start | bytes 196616 | tf_op jit(solution)/shard_map/ppermute | solution.py:57
  53.8 4.1 %collective-permute-start.18 = (bf16[16,1280]{1,0:T(8,128)(2,1)S(1)}, bf16[16,1280]{1,0:T(8,128)(2,1)S(1)}, u32[]{:S(2)}, u32[]{:S(2)}) collective-permute-start(bf16[16,1280]{1,0:T(8,128)(2,1)S(1)} %get-tuple-element.60.refs_0_), channel_id=1, source_target_pairs={{0,1},{1,0},{2,3},{3,2},{4,5},{5,4},{6,7},{7,6},{8,9},{9,8},{10,11... | collective-permute-start | bytes 122888 | tf_op jit(solution)/shard_map/ppermute | solution.py:57
  55.6 2.3 %collective-permute-start.19 = (bf16[16,1280]{1,0:T(8,128)(2,1)S(1)}, bf16[16,1280]{1,0:T(8,128)(2,1)S(1)}, u32[]{:S(2)}, u32[]{:S(2)}) collective-permute-start(bf16[16,1280]{1,0:T(8,128)(2,1)S(1)} %get-tuple-element.61), channel_id=1, source_target_pairs={{0,2},{1,3},{2,0},{3,1},{4,6},{5,7},{6,4},{7,5},{8,10},{9,11},{10,... | collective-permute-start | bytes 122888 | tf_op jit(solution)/shard_map/ppermute | solution.py:57
  55.6 3.4 %collective-permute-start.20 = (bf16[16,1280]{1,0:T(8,128)(2,1)S(1)}, bf16[16,1280]{1,0:T(8,128)(2,1)S(1)}, u32[]{:S(2)}, u32[]{:S(2)}) collective-permute-start(bf16[16,1280]{1,0:T(8,128)(2,1)S(1)} %get-tuple-element.61), channel_id=1, source_target_pairs={{0,3},{1,2},{2,1},{3,0},{4,7},{5,6},{6,5},{7,4},{8,11},{9,10},{10,... | collective-permute-start | bytes 122888 | tf_op jit(solution)/shard_map/ppermute | solution.py:57

commit v10 on v8

--- a/solution.py
+++ b/solution.py
@@ -16,7 +16,7 @@
 SMEM = pl.BlockSpec(memory_space=pltpu.SMEM)
 ANY = pl.BlockSpec(memory_space=pl.ANY)
 HBM = pl.BlockSpec(memory_space=pltpu.HBM)
-SOURCE = {'rays': 'start', 'weights': ("start", "core", "hop1")}
+SOURCE = {'rays': 'start', 'weights': ("start", "core", "last")}
 AWAITED = {"rays": "views", "w1": "last"}
 QUICK = pl.CostEstimate(flops=1, bytes_accessed=1, transcendentals=0)
 

time: 59.7 us -> 59.7 us (level)
  no operation moved by 1% of the time
where the time goes in v10:
time: 59.7 us; the launch traced here: 59.5 us
  waiting for transfers between devices  26.9 us (45%)
  starting transfers between devices  20.3 us (34%)
  Pallas kernels  11.4 us (19%)
  between operations  0.84 us (1%)
    ppermute x21, waiting for transfers between devices, swap(): return lax.ppermute(value, axis, [(i, i ^ bits) for i in range(size)])  26.9 us
    ppermute x21, starting transfers between devices, swap(): return lax.ppermute(value, axis, [(i, i ^ bits) for i in range(size)])  20.3 us
    pallas_call x2, Pallas kernels, body(): call(functools.partial(step_kernel, groups, views, ready), 'ray_space_ste...  3.41 us
    pallas_call x1, Pallas kernels, body(): call(start_kernel, 'start', (shaped((PACK, width), BF16), shaped((PACK, w...  3.33 us
    pallas_call x1, Pallas kernels, begin(): call(functools.partial(take_kernel, groups, bits), 'take_rays', shaped((2...  1.23 us
  transfers between devices with their start and end apart: 21, of which 15 were waited for; matrix products, arithmetic and copies ran while one was open for 0% of the time, Pallas kernels for 8%

profile of v10, /device:TPU:0, one launch (start us, length us, event | category | flops | bytes accessed | tf_op | source)
XLA Modules:
  0.0 59.5 jit_solution(2023558356589647290)
XLA Ops:
  0.6 1.2 %take_rays.1 = bf16[2,2,1024,128]{3,2,1,0:T(8,128)(2,1)S(1)} custom-call(bf16[2,4096,128]{2,1,0:T(8,128)(2,1)} %fine_rays.1, bf16[2,4096,128]{2,1,0:T(8,128)(2,1)} %coarse_rays.1), custom_call_target="tpu_custom_call" | custom-call | flops 1 | bytes 1 | tf_op jit(solution)/shard_map/take_rays/pallas_call | solution.py:644
  1.9 3.0 %collective-permute-start.8 = (bf16[2,2,1024,128]{3,2,1,0:T(8,128)(2,1)S(1)}, bf16[2,2,1024,128]{3,2,1,0:T(8,128)(2,1)S(1)}, u32[]{:S(2)}, u32[]{:S(2)}) collective-permute-start(bf16[2,2,1024,128]{3,2,1,0:T(8,128)(2,1)S(1)} %take_rays.1), channel_id=1, source_target_pairs={{0,1},{1,0},{2,3},{3,2},{4,5},{5,4},{6,7},{7,6},{8,9},{9,8},{10,11... | collective-permute-start | bytes 3145736 | tf_op jit(solution)/shard_map/ppermute | solution.py:57
  4.9 3.3 %start.1 = (bf16[16,1280]{1,0:T(8,128)(2,1)S(1)}, bf16[16,1280]{1,0:T(8,128)(2,1)S(1)}, bf16[32,256]{1,0:T(8,128)(2,1)S(1)}, f32[64,256]{1,0:T(8,128)S(1)}, bf16...) custom-call(bf16[2,4096,128]{2,1,0:T(8,128)(2,1)} %fine_rays.1, bf16[2,4096,128]{2,1,0:T(8,128)(2,1)} %coarse_rays.1, ...), custom_call_target="tpu_custom_call" | custom-call | flops 1 | bytes 1 | tf_op jit(solution)/shard_map/start/pallas_call | solution.py:608
  8.8 0.7 %collective-permute-done.4.received = bf16[16,1280]{1,0:T(8,128)(2,1)S(1)} collective-permute-done((bf16[16,1280]{1,0:T(8,128)(2,1)S(1)}, bf16[16,1280]{1,0:T(8,128)(2,1)S(1)}, u32[]{:S(2)}, u32[]{:S(2)}) %collective-permute-start.4) | collective-permute-done | bytes 40992 | tf_op jit(solution)/shard_map/ppermute | solution.py:57
  9.6 2.7 %collective-permute-start.5 = (bf16[2,16,1280]{2,1,0:T(8,128)(2,1)S(1)}, bf16[2,16,1280]{2,1,0:T(8,128)(2,1)S(1)}, u32[]{:S(2)}, u32[]{:S(2)}) collective-permute-start(bf16[2,16,1280]{2,1,0:T(8,128)(2,1)S(1)} %pair.1.mine), channel_id=1, source_target_pairs={{0,16},{2,18},{4,20},{6,22},{8,24},{10,26},{12,28},{14,30},{16,0},... | collective-permute-start | bytes 245768 | tf_op jit(solution)/shard_map/ppermute | solution.py:57
  12.2 1.6 %collective-permute-start.1 = (bf16[96,256]{1,0:T(8,128)(2,1)S(1)}, bf16[96,256]{1,0:T(8,128)(2,1)S(1)}, u32[]{:S(2)}, u32[]{:S(2)}) collective-permute-start(bf16[96,256]{1,0:T(8,128)(2,1)S(1)} %get-tuple-element.36.mine.refs_0_), channel_id=1, source_target_pairs={{0,4},{2,6},{4,0},{6,2},{8,12},{10,14},{12,8},{14,10},{16,20},{18,... | collective-permute-start | bytes 147464 | tf_op jit(solution)/shard_map/ppermute | solution.py:57
  13.8 2.6 %collective-permute-done.1.received = bf16[96,256]{1,0:T(8,128)(2,1)S(1)} collective-permute-done((bf16[96,256]{1,0:T(8,128)(2,1)S(1)}, bf16[96,256]{1,0:T(8,128)(2,1)S(1)}, u32[]{:S(2)}, u32[]{:S(2)}) %collective-permute-start.1) | collective-permute-done | bytes 49184 | tf_op jit(solution)/shard_map/ppermute | solution.py:57
  16.8 1.6 %collective-permute-start.6 = (bf16[4,16,1280]{2,1,0:T(8,128)(2,1)S(1)}, bf16[4,16,1280]{2,1,0:T(8,128)(2,1)S(1)}, u32[]{:S(2)}, u32[]{:S(2)}) collective-permute-start(bf16[4,16,1280]{2,1,0:T(8,128)(2,1)S(1)} %join_blocks.2.mine), channel_id=1, source_target_pairs={{0,8},{2,10},{4,12},{6,14},{8,0},{10,2},{12,4},{14,6},{16,24},{18,... | collective-permute-start | bytes 491528 | tf_op jit(solution)/shard_map/ppermute | solution.py:57
  18.5 3.3 %collective-permute-done.2.received = bf16[128,256]{1,0:T(8,128)(2,1)S(1)} collective-permute-done((bf16[128,256]{1,0:T(8,128)(2,1)S(1)}, bf16[128,256]{1,0:T(8,128)(2,1)S(1)}, u32[]{:S(2)}, u32[]{:S(2)}) %collective-permute-start.2) | collective-permute-done | bytes 65568 | tf_op jit(solution)/shard_map/ppermute | solution.py:57
  21.8 2.2 %collective-permute-start.3 = (bf16[192,256]{1,0:T(8,128)(2,1)S(1)}, bf16[192,256]{1,0:T(8,128)(2,1)S(1)}, u32[]{:S(2)}, u32[]{:S(2)}) collective-permute-start(bf16[192,256]{1,0:T(8,128)(2,1)S(1)} %get-tuple-element.40.mine), channel_id=1, source_target_pairs={{0,8},{2,10},{4,12},{6,14},{8,0},{10,2},{12,4},{14,6},{16,24},{18,... | collective-permute-start | bytes 294920 | tf_op jit(solution)/shard_map/ppermute | solution.py:57
  24.0 2.6 %collective-permute-done.3.received = bf16[192,256]{1,0:T(8,128)(2,1)S(1)} collective-permute-done((bf16[192,256]{1,0:T(8,128)(2,1)S(1)}, bf16[192,256]{1,0:T(8,128)(2,1)S(1)}, u32[]{:S(2)}, u32[]{:S(2)}) %collective-permute-start.3) | collective-permute-done | bytes 98336 | tf_op jit(solution)/shard_map/ppermute | solution.py:57
  26.6 0.6 collective-permute-start.7
  27.2 1.6 %collective-permute-start.11 = (bf16[8,16,1280]{2,1,0:T(8,128)(2,1)S(1)}, bf16[8,16,1280]{2,1,0:T(8,128)(2,1)S(1)}, u32[]{:S(2)}, u32[]{:S(2)}) collective-permute-start(bf16[8,16,1280]{2,1,0:T(8,128)(2,1)S(1)} %join_blocks.3.mine), channel_id=1, source_target_pairs={{0,4},{2,6},{4,0},{6,2},{8,12},{10,14},{12,8},{14,10},{16,20},{18,... | collective-permute-start | bytes 983048 | tf_op jit(solution)/shard_map/ppermute | solution.py:57
  28.7 3.6 %collective-permute-done.7.refs_1_ = bf16[384,256]{1,0:T(8,128)(2,1)S(1)} collective-permute-done((bf16[384,256]{1,0:T(8,128)(2,1)S(1)}, bf16[384,256]{1,0:T(8,128)(2,1)S(1)}, u32[]{:S(2)}, u32[]{:S(2)}) %collective-permute-start.7) | collective-permute-done | bytes 196640 | tf_op jit(solution)/shard_map/ppermute | solution.py:57
  32.9 1.2 %collective-permute-done.10.q_theirs = f32[2,64,256]{2,1,0:T(8,128)S(1)} collective-permute-done((f32[2,64,256]{2,1,0:T(8,128)S(1)}, f32[2,64,256]{2,1,0:T(8,128)S(1)}, u32[]{:S(2)}, u32[]{:S(2)}) %collective-permute-start.10) | collective-permute-done | bytes 131104 | tf_op jit(solution)/shard_map/ppermute | solution.py:57
  35.3 1.6 %ray_space_step.2 = (bf16[2,64,256]{2,1,0:T(8,128)(2,1)S(1)}, bf16[2,64,256]{2,1,0:T(8,128)(2,1)S(1)}) custom-call(bf16[2,64,256]{2,1,0:T(8,128)(2,1)S(1)} %get-tuple-element.49.refs_0_, bf16[2,256,256]{2,1,0:T(8,128)(2,1)S(1)} %get-tuple-element.50.refs_1_, bf16[2,2,128,64]{3,2,1,0:T(8,128)(2,1)S(1)} %get-tuple-element.51.refs_2_.refs_6_, ...), custom_call_target="tpu_custom_call" | custom-call | flops 1 | bytes 1 | tf_op jit(solution)/shard_map/ray_space_step/pallas_call | solution.py:765
  37.1 1.2 %collective-permute-done.12.received = bf16[2,64,256]{2,1,0:T(8,128)(2,1)S(1)} collective-permute-done((bf16[2,64,256]{2,1,0:T(8,128)(2,1)S(1)}, bf16[2,64,256]{2,1,0:T(8,128)(2,1)S(1)}, u32[]{:S(2)}, u32[]{:S(2)}) %collective-permute-start.12) | collective-permute-done | bytes 65568 | tf_op jit(solution)/shard_map/ppermute | solution.py:57
  38.3 1.4 %collective-permute-start.13 = (bf16[2,64,256]{2,1,0:T(8,128)(2,1)S(1)}, bf16[2,64,256]{2,1,0:T(8,128)(2,1)S(1)}, u32[]{:S(2)}, u32[]{:S(2)}) collective-permute-start(bf16[2,64,256]{2,1,0:T(8,128)(2,1)S(1)} %add.4.mine), channel_id=1, source_target_pairs={{0,1},{1,0},{2,3},{3,2},{4,5},{5,4},{6,7},{7,6},{8,9},{9,8},{10,11... | collective-permute-start | bytes 196616 | tf_op jit(solution)/shard_map/ppermute | solution.py:57
  39.8 2.9 %collective-permute-done.13.received = bf16[2,64,256]{2,1,0:T(8,128)(2,1)S(1)} collective-permute-done((bf16[2,64,256]{2,1,0:T(8,128)(2,1)S(1)}, bf16[2,64,256]{2,1,0:T(8,128)(2,1)S(1)}, u32[]{:S(2)}, u32[]{:S(2)}) %collective-permute-start.13) | collective-permute-done | bytes 65568 | tf_op jit(solution)/shard_map/ppermute | solution.py:57
  42.8 1.2 %collective-permute-done.14.refs_2_.refs_1_ = bf16[2,64,256]{2,1,0:T(8,128)(2,1)S(1)} collective-permute-done((bf16[2,64,256]{2,1,0:T(8,128)(2,1)S(1)}, bf16[2,64,256]{2,1,0:T(8,128)(2,1)S(1)}, u32[]{:S(2)}, u32[]{:S(2)}) %collective-permute-start.14) | collective-permute-done | bytes 65568 | tf_op jit(solution)/shard_map/ppermute | solution.py:57
  44.0 1.8 %ray_space_step.3 = (bf16[2,64,256]{2,1,0:T(8,128)(2,1)S(1)}, bf16[2,64,256]{2,1,0:T(8,128)(2,1)S(1)}) custom-call(f32[2,128,256]{2,1,0:T(8,128)S(1)} %get-tuple-element.45.q.refs_0_, bf16[2,64,256]{2,1,0:T(8,128)(2,1)S(1)} %add.5.refs_1_.refs_0_, bf16[2,64,256]{2,1,0:T(8,128)(2,1)S(1)} %collective-permute-done.14.refs_2_.refs_1_, ...), custom_call_target="tpu_custom_call" | custom-call | flops 1 | bytes 1 | tf_op jit(solution)/shard_map/ray_space_step/pallas_call | solution.py:765
  46.1 1.1 %collective-permute-done.15.received = bf16[2,64,256]{2,1,0:T(8,128)(2,1)S(1)} collective-permute-done((bf16[2,64,256]{2,1,0:T(8,128)(2,1)S(1)}, bf16[2,64,256]{2,1,0:T(8,128)(2,1)S(1)}, u32[]{:S(2)}, u32[]{:S(2)}) %collective-permute-start.15) | collective-permute-done | bytes 65568 | tf_op jit(solution)/shard_map/ppermute | solution.py:57
  47.2 1.4 %collective-permute-start.16 = (bf16[2,64,256]{2,1,0:T(8,128)(2,1)S(1)}, bf16[2,64,256]{2,1,0:T(8,128)(2,1)S(1)}, u32[]{:S(2)}, u32[]{:S(2)}) collective-permute-start(bf16[2,64,256]{2,1,0:T(8,128)(2,1)S(1)} %add.6.mine), channel_id=1, source_target_pairs={{0,1},{1,0},{2,3},{3,2},{4,5},{5,4},{6,7},{7,6},{8,9},{9,8},{10,11... | collective-permute-start | bytes 196616 | tf_op jit(solution)/shard_map/ppermute | solution.py:57
  48.6 2.9 %collective-permute-done.16.received = bf16[2,64,256]{2,1,0:T(8,128)(2,1)S(1)} collective-permute-done((bf16[2,64,256]{2,1,0:T(8,128)(2,1)S(1)}, bf16[2,64,256]{2,1,0:T(8,128)(2,1)S(1)}, u32[]{:S(2)}, u32[]{:S(2)}) %collective-permute-start.16) | collective-permute-done | bytes 65568 | tf_op jit(solution)/shard_map/ppermute | solution.py:57
  51.6 1.2 %collective-permute-done.17.refs_3_ = bf16[2,64,256]{2,1,0:T(8,128)(2,1)S(1)} collective-permute-done((bf16[2,64,256]{2,1,0:T(8,128)(2,1)S(1)}, bf16[2,64,256]{2,1,0:T(8,128)(2,1)S(1)}, u32[]{:S(2)}, u32[]{:S(2)}) %collective-permute-start.17) | collective-permute-done | bytes 65568 | tf_op jit(solution)/shard_map/ppermute | solution.py:57
  52.9 0.9 %back_projection.1 = (bf16[16,1280]{1,0:T(8,128)(2,1)S(1)}, bf16[16,1280]{1,0:T(8,128)(2,1)S(1)}) custom-call(f32[2,128,256]{2,1,0:T(8,128)S(1)} %get-tuple-element.45.q.refs_0_, bf16[2,64,256]{2,1,0:T(8,128)(2,1)S(1)} %add.5.refs_1_.refs_0_, bf16[2,64,256]{2,1,0:T(8,128)(2,1)S(1)} %collective-permute-done.14.refs_2_.refs_1_, ...), custom_call_target="tpu_custom_call" | custom-call | flops 1 | bytes 1 | tf_op jit(solution)/shard_map/back_projection/pallas_call | solution.py:777
  53.8 1.5 %collective-permute-start.18 = (bf16[16,1280]{1,0:T(8,128)(2,1)S(1)}, bf16[16,1280]{1,0:T(8,128)(2,1)S(1)}, u32[]{:S(2)}, u32[]{:S(2)}) collective-permute-start(bf16[16,1280]{1,0:T(8,128)(2,1)S(1)} %get-tuple-element.60.refs_0_), channel_id=1, source_target_pairs={{0,1},{1,0},{2,3},{3,2},{4,5},{5,4},{6,7},{7,6},{8,9},{9,8},{10,11... | collective-permute-start | bytes 122888 | tf_op jit(solution)/shard_map/ppermute | solution.py:57
  55.2 0.8 %collective-permute-start.20 = (bf16[16,1280]{1,0:T(8,128)(2,1)S(1)}, bf16[16,1280]{1,0:T(8,128)(2,1)S(1)}, u32[]{:S(2)}, u32[]{:S(2)}) collective-permute-start(bf16[16,1280]{1,0:T(8,128)(2,1)S(1)} %get-tuple-element.61), channel_id=1, source_target_pairs={{0,3},{1,2},{2,1},{3,0},{4,7},{5,6},{6,5},{7,4},{8,11},{9,10},{10,... | collective-permute-start | bytes 122888 | tf_op jit(solution)/shard_map/ppermute | solution.py:57
  56.0 0.6 %keep.1.refs_8_ = f32[1,4096]{1,0:T(1,128)S(1)} custom-call(s32[1,8]{1,0:T(1,128)S(1)} %copy-done.5), custom_call_target="tpu_custom_call" | custom-call | flops 1 | bytes 1 | tf_op jit(solution)/shard_map/keep/pallas_call | solution.py:783
  56.6 1.2 %collective-permute-done.18.refs_1_ = bf16[16,1280]{1,0:T(8,128)(2,1)S(1)} collective-permute-done((bf16[16,1280]{1,0:T(8,128)(2,1)S(1)}, bf16[16,1280]{1,0:T(8,128)(2,1)S(1)}, u32[]{:S(2)}, u32[]{:S(2)}) %collective-permute-start.18) | collective-permute-done | bytes 40992 | tf_op jit(solution)/shard_map/ppermute | solution.py:57
  57.8 0.8 %collective-permute-done.20.refs_3_ = bf16[16,1280]{1,0:T(8,128)(2,1)S(1)} collective-permute-done((bf16[16,1280]{1,0:T(8,128)(2,1)S(1)}, bf16[16,1280]{1,0:T(8,128)(2,1)S(1)}, u32[]{:S(2)}, u32[]{:S(2)}) %collective-permute-start.20) | collective-permute-done | bytes 40992 | tf_op jit(solution)/shard_map/ppermute | solution.py:57
  58.7 0.8 %update.1 = (f32[4,4096]{1,0:T(4,128)}, f32[16,4096]{1,0:T(8,128)}) custom-call(bf16[16,1280]{1,0:T(8,128)(2,1)S(1)} %get-tuple-element.60.refs_0_, bf16[16,1280]{1,0:T(8,128)(2,1)S(1)} %collective-permute-done.18.refs_1_, bf16[16,1280]{1,0:T(8,128)(2,1)S(1)} %collective-permute-done.19.refs_2_, bf16[16,1280]{1,0:T(8,128)(2,1)S(1)} %collective-permute-done.20.refs_3_, ...), custom_call_target="tpu_custom_call" | custom-call | flops 1 | bytes 1 | tf_op jit(solution)/shard_map/update/pallas_call | solution.py:787
  (44 shorter events, 3.4 us)
Async XLA Ops:
  0.6 4.3 %copy-start.4 = (bf16[2,4,128]{2,1,0:T(4,128)(2,1)S(1)}, bf16[2,4,128]{2,1,0:T(4,128)(2,1)}, u32[]{:S(2)}) copy-start(bf16[2,4,128]{2,1,0:T(4,128)(2,1)} %fine_axial.1) | copy-start | bytes 6148
  1.9 30.4 %collective-permute-start.8 = (bf16[2,2,1024,128]{3,2,1,0:T(8,128)(2,1)S(1)}, bf16[2,2,1024,128]{3,2,1,0:T(8,128)(2,1)S(1)}, u32[]{:S(2)}, u32[]{:S(2)}) collective-permute-start(bf16[2,2,1024,128]{3,2,1,0:T(8,128)(2,1)S(1)} %take_rays.1), channel_id=1, source_target_pairs={{0,1},{1,0},{2,3},{3,2},{4,5},{5,4},{6,7},{7,6},{8,9},{9,8},{10,11... | collective-permute-start | bytes 3145736 | tf_op jit(solution)/shard_map/ppermute | solution.py:57
  8.3 1.3 %collective-permute-start.4 = (bf16[16,1280]{1,0:T(8,128)(2,1)S(1)}, bf16[16,1280]{1,0:T(8,128)(2,1)S(1)}, u32[]{:S(2)}, u32[]{:S(2)}) collective-permute-start(bf16[16,1280]{1,0:T(8,128)(2,1)S(1)} %get-tuple-element.42), channel_id=1, source_target_pairs={{0,2},{2,0},{4,6},{6,4},{8,10},{10,8},{12,14},{14,12},{16,18},{18,... | collective-permute-start | bytes 122888 | tf_op jit(solution)/shard_map/ppermute | solution.py:57
  8.3 3.9 %collective-permute-start = (bf16[64,256]{1,0:T(8,128)(2,1)S(1)}, bf16[64,256]{1,0:T(8,128)(2,1)S(1)}, u32[]{:S(2)}, u32[]{:S(2)}) collective-permute-start(bf16[64,256]{1,0:T(8,128)(2,1)S(1)} %get-tuple-element.33), channel_id=1, source_target_pairs={{0,2},{2,0},{4,6},{6,4},{8,10},{10,8},{12,14},{14,12},{16,18},{18,... | collective-permute-start | bytes 98312 | tf_op jit(solution)/shard_map/ppermute | solution.py:57
  9.6 7.2 %collective-permute-start.5 = (bf16[2,16,1280]{2,1,0:T(8,128)(2,1)S(1)}, bf16[2,16,1280]{2,1,0:T(8,128)(2,1)S(1)}, u32[]{:S(2)}, u32[]{:S(2)}) collective-permute-start(bf16[2,16,1280]{2,1,0:T(8,128)(2,1)S(1)} %pair.1.mine), channel_id=1, source_target_pairs={{0,16},{2,18},{4,20},{6,22},{8,24},{10,26},{12,28},{14,30},{16,0},... | collective-permute-start | bytes 245768 | tf_op jit(solution)/shard_map/ppermute | solution.py:57
  12.2 4.2 %collective-permute-start.1 = (bf16[96,256]{1,0:T(8,128)(2,1)S(1)}, bf16[96,256]{1,0:T(8,128)(2,1)S(1)}, u32[]{:S(2)}, u32[]{:S(2)}) collective-permute-start(bf16[96,256]{1,0:T(8,128)(2,1)S(1)} %get-tuple-element.36.mine.refs_0_), channel_id=1, source_target_pairs={{0,4},{2,6},{4,0},{6,2},{8,12},{10,14},{12,8},{14,10},{16,20},{18,... | collective-permute-start | bytes 147464 | tf_op jit(solution)/shard_map/ppermute | solution.py:57
  16.4 5.3 %collective-permute-start.2 = (bf16[128,256]{1,0:T(8,128)(2,1)S(1)}, bf16[128,256]{1,0:T(8,128)(2,1)S(1)}, u32[]{:S(2)}, u32[]{:S(2)}) collective-permute-start(bf16[128,256]{1,0:T(8,128)(2,1)S(1)} %get-tuple-element.38.mine), channel_id=1, source_target_pairs={{0,16},{2,18},{4,20},{6,22},{8,24},{10,26},{12,28},{14,30},{16,0},... | collective-permute-start | bytes 196616 | tf_op jit(solution)/shard_map/ppermute | solution.py:57
  16.8 9.7 %collective-permute-start.6 = (bf16[4,16,1280]{2,1,0:T(8,128)(2,1)S(1)}, bf16[4,16,1280]{2,1,0:T(8,128)(2,1)S(1)}, u32[]{:S(2)}, u32[]{:S(2)}) collective-permute-start(bf16[4,16,1280]{2,1,0:T(8,128)(2,1)S(1)} %join_blocks.2.mine), channel_id=1, source_target_pairs={{0,8},{2,10},{4,12},{6,14},{8,0},{10,2},{12,4},{14,6},{16,24},{18,... | collective-permute-start | bytes 491528 | tf_op jit(solution)/shard_map/ppermute | solution.py:57
  21.8 4.8 %collective-permute-start.3 = (bf16[192,256]{1,0:T(8,128)(2,1)S(1)}, bf16[192,256]{1,0:T(8,128)(2,1)S(1)}, u32[]{:S(2)}, u32[]{:S(2)}) collective-permute-start(bf16[192,256]{1,0:T(8,128)(2,1)S(1)} %get-tuple-element.40.mine), channel_id=1, source_target_pairs={{0,8},{2,10},{4,12},{6,14},{8,0},{10,2},{12,4},{14,6},{16,24},{18,... | collective-permute-start | bytes 294920 | tf_op jit(solution)/shard_map/ppermute | solution.py:57
  26.6 5.7 %collective-permute-start.7 = (bf16[384,256]{1,0:T(8,128)(2,1)S(1)}, bf16[384,256]{1,0:T(8,128)(2,1)S(1)}, u32[]{:S(2)}, u32[]{:S(2)}) collective-permute-start(bf16[384,256]{1,0:T(8,128)(2,1)S(1)} %join_last.1.refs_0_), channel_id=1, source_target_pairs={{0,1},{1,0},{2,3},{3,2},{4,5},{5,4},{6,7},{7,6},{8,9},{9,8},{10,11... | collective-permute-start | bytes 589832 | tf_op jit(solution)/shard_map/ppermute | solution.py:57
  27.2 7.9 %collective-permute-start.11 = (bf16[8,16,1280]{2,1,0:T(8,128)(2,1)S(1)}, bf16[8,16,1280]{2,1,0:T(8,128)(2,1)S(1)}, u32[]{:S(2)}, u32[]{:S(2)}) collective-permute-start(bf16[8,16,1280]{2,1,0:T(8,128)(2,1)S(1)} %join_blocks.3.mine), channel_id=1, source_target_pairs={{0,4},{2,6},{4,0},{6,2},{8,12},{10,14},{12,8},{14,10},{16,20},{18,... | collective-permute-start | bytes 983048 | tf_op jit(solution)/shard_map/ppermute | solution.py:57
  32.3 1.8 %collective-permute-start.9 = (bf16[2,256,256]{2,1,0:T(8,128)(2,1)S(1)}, bf16[2,256,256]{2,1,0:T(8,128)(2,1)S(1)}, u32[]{:S(2)}, u32[]{:S(2)}) collective-permute-start(bf16[2,256,256]{2,1,0:T(8,128)(2,1)S(1)} %get-tuple-element.43.mine), channel_id=1, source_target_pairs={{0,2},{2,0},{4,6},{6,4},{8,10},{10,8},{12,14},{14,12},{16,18},{18,... | collective-permute-start | bytes 786440 | tf_op jit(solution)/shard_map/ppermute | solution.py:57
  32.4 1.7 %collective-permute-start.10 = (f32[2,64,256]{2,1,0:T(8,128)S(1)}, f32[2,64,256]{2,1,0:T(8,128)S(1)}, u32[]{:S(2)}, u32[]{:S(2)}) collective-permute-start(f32[2,64,256]{2,1,0:T(8,128)S(1)} %get-tuple-element.44.q_mine), channel_id=1, source_target_pairs={{0,2},{2,0},{4,6},{6,4},{8,10},{10,8},{12,14},{14,12},{16,18},{18,... | collective-permute-start | bytes 393224 | tf_op jit(solution)/shard_map/ppermute | solution.py:57
  37.0 1.3 %collective-permute-start.12 = (bf16[2,64,256]{2,1,0:T(8,128)(2,1)S(1)}, bf16[2,64,256]{2,1,0:T(8,128)(2,1)S(1)}, u32[]{:S(2)}, u32[]{:S(2)}) collective-permute-start(bf16[2,64,256]{2,1,0:T(8,128)(2,1)S(1)} %get-tuple-element.57), channel_id=1, source_target_pairs={{0,2},{2,0},{4,6},{6,4},{8,10},{10,8},{12,14},{14,12},{16,18},{18,... | collective-permute-start | bytes 196616 | tf_op jit(solution)/shard_map/ppermute | solution.py:57
  38.3 4.3 %collective-permute-start.13 = (bf16[2,64,256]{2,1,0:T(8,128)(2,1)S(1)}, bf16[2,64,256]{2,1,0:T(8,128)(2,1)S(1)}, u32[]{:S(2)}, u32[]{:S(2)}) collective-permute-start(bf16[2,64,256]{2,1,0:T(8,128)(2,1)S(1)} %add.4.mine), channel_id=1, source_target_pairs={{0,1},{1,0},{2,3},{3,2},{4,5},{5,4},{6,7},{7,6},{8,9},{9,8},{10,11... | collective-permute-start | bytes 196616 | tf_op jit(solution)/shard_map/ppermute | solution.py:57
  42.7 1.3 %collective-permute-start.14 = (bf16[2,64,256]{2,1,0:T(8,128)(2,1)S(1)}, bf16[2,64,256]{2,1,0:T(8,128)(2,1)S(1)}, u32[]{:S(2)}, u32[]{:S(2)}) collective-permute-start(bf16[2,64,256]{2,1,0:T(8,128)(2,1)S(1)} %add.5.refs_1_.refs_0_), channel_id=1, source_target_pairs={{0,2},{2,0},{4,6},{6,4},{8,10},{10,8},{12,14},{14,12},{16,18},{18,... | collective-permute-start | bytes 196616 | tf_op jit(solution)/shard_map/ppermute | solution.py:57
  45.8 10.2 %copy-start.5 = (s32[1,8]{1,0:T(1,128)S(1)}, s32[1,8]{1,0:T(1,128)}, u32[]{:S(2)}) copy-start(s32[1,8]{1,0:T(1,128)} %blocks.1) | copy-start | bytes 100
  45.8 12.8 %copy-start = (f32[16,4096]{1,0:T(8,128)S(1)}, f32[16,4096]{1,0:T(8,128)}, u32[]{:S(2)}) copy-start(f32[16,4096]{1,0:T(8,128)} %refs_5_.1) | copy-start | bytes 786436
  45.8 12.8 %copy-start.1 = (f32[16,4096]{1,0:T(8,128)S(1)}, f32[16,4096]{1,0:T(8,128)}, u32[]{:S(2)}) copy-start(f32[16,4096]{1,0:T(8,128)} %refs_7_.1) | copy-start | bytes 786436
  45.8 12.8 %copy-start.2 = (f32[4,4096]{1,0:T(4,128)S(1)}, f32[4,4096]{1,0:T(4,128)}, u32[]{:S(2)}) copy-start(f32[4,4096]{1,0:T(4,128)} %refs_4_.1) | copy-start | bytes 196612
  45.8 12.8 %copy-start.3 = (f32[4,4096]{1,0:T(4,128)S(1)}, f32[4,4096]{1,0:T(4,128)}, u32[]{:S(2)}) copy-start(f32[4,4096]{1,0:T(4,128)} %refs_6_.1) | copy-start | bytes 196612
  45.8 1.3 %collective-permute-start.15 = (bf16[2,64,256]{2,1,0:T(8,128)(2,1)S(1)}, bf16[2,64,256]{2,1,0:T(8,128)(2,1)S(1)}, u32[]{:S(2)}, u32[]{:S(2)}) collective-permute-start(bf16[2,64,256]{2,1,0:T(8,128)(2,1)S(1)} %get-tuple-element.59), channel_id=1, source_target_pairs={{0,2},{2,0},{4,6},{6,4},{8,10},{10,8},{12,14},{14,12},{16,18},{18,... | collective-permute-start | bytes 196616 | tf_op jit(solution)/shard_map/ppermute | solution.py:57
  47.2 4.3 %collective-permute-start.16 = (bf16[2,64,256]{2,1,0:T(8,128)(2,1)S(1)}, bf16[2,64,256]{2,1,0:T(8,128)(2,1)S(1)}, u32[]{:S(2)}, u32[]{:S(2)}) collective-permute-start(bf16[2,64,256]{2,1,0:T(8,128)(2,1)S(1)} %add.6.mine), channel_id=1, source_target_pairs={{0,1},{1,0},{2,3},{3,2},{4,5},{5,4},{6,7},{7,6},{8,9},{9,8},{10,11... | collective-permute-start | bytes 196616 | tf_op jit(solution)/shard_map/ppermute | solution.py:57
  51.5 1.3 %collective-permute-start.17 = (bf16[2,64,256]{2,1,0:T(8,128)(2,1)S(1)}, bf16[2,64,256]{2,1,0:T(8,128)(2,1)S(1)}, u32[]{:S(2)}, u32[]{:S(2)}) collective-permute-start(bf16[2,64,256]{2,1,0:T(8,128)(2,1)S(1)} %add.7.refs_2_), channel_id=1, source_target_pairs={{0,2},{2,0},{4,6},{6,4},{8,10},{10,8},{12,14},{14,12},{16,18},{18,... | collective-permute-start | bytes 196616 | tf_op jit(solution)/shard_map/ppermute | solution.py:57
  53.8 4.1 %collective-permute-start.18 = (bf16[16,1280]{1,0:T(8,128)(2,1)S(1)}, bf16[16,1280]{1,0:T(8,128)(2,1)S(1)}, u32[]{:S(2)}, u32[]{:S(2)}) collective-permute-start(bf16[16,1280]{1,0:T(8,128)(2,1)S(1)} %get-tuple-element.60.refs_0_), channel_id=1, source_target_pairs={{0,1},{1,0},{2,3},{3,2},{4,5},{5,4},{6,7},{7,6},{8,9},{9,8},{10,11... | collective-permute-start | bytes 122888 | tf_op jit(solution)/shard_map/ppermute | solution.py:57
  55.2 2.6 %collective-permute-start.19 = (bf16[16,1280]{1,0:T(8,128)(2,1)S(1)}, bf16[16,1280]{1,0:T(8,128)(2,1)S(1)}, u32[]{:S(2)}, u32[]{:S(2)}) collective-permute-start(bf16[16,1280]{1,0:T(8,128)(2,1)S(1)} %get-tuple-element.61), channel_id=1, source_target_pairs={{0,2},{1,3},{2,0},{3,1},{4,6},{5,7},{6,4},{7,5},{8,10},{9,11},{10,... | collective-permute-start | bytes 122888 | tf_op jit(solution)/shard_map/ppermute | solution.py:57
  55.2 3.4 %collective-permute-start.20 = (bf16[16,1280]{1,0:T(8,128)(2,1)S(1)}, bf16[16,1280]{1,0:T(8,128)(2,1)S(1)}, u32[]{:S(2)}, u32[]{:S(2)}) collective-permute-start(bf16[16,1280]{1,0:T(8,128)(2,1)S(1)} %get-tuple-element.61), channel_id=1, source_target_pairs={{0,3},{1,2},{2,1},{3,0},{4,7},{5,6},{6,5},{7,4},{8,11},{9,10},{10,... | collective-permute-start | bytes 122888 | tf_op jit(solution)/shard_map/ppermute | solution.py:57
